TPU v7x, 32 devices: a whole 2x2x4 slice. The times are simulated.
32 devices in a mesh: hash: 16 (over z, x, core), tm: 2 (over y).
Axes of the slice: x: 2, y: 2, z: 4, core: 2. Of those that a mesh axis runs over, the one named last changes fastest.
Arguments:
- transactions: float32 [32768, 256], P(('hash', 'tm')), may hold values from -6 to 6
- tx_product: int32 [32768], P(('hash', 'tm')), may hold values from 0 to 255
- tx_count: int32 [512], P(('hash', 'tm')), may hold values from 16 to 64, as said below
- products: float32 [4096, 256], P(('hash', 'tm')), may hold values from -6 to 6
- customers: float32 [8192, 256], P(('hash', 'tm')), may hold values from -6 to 6
- send_rows: int32 [8192], P(('hash', 'tm')), may hold values from 0 to 127
- send_count: int32 [512], P(('hash', 'tm')), may hold values from 0 to 16, as said below
- recv_customer: int32 [8192], P(('hash', 'tm')), may hold values from 0 to 255
- w_msg: float32 [256, 256], replicated, may hold values from -0.375 to 0.375
- w_prod_self: float32 [256, 256], replicated, may hold values from -0.375 to 0.375
- w_prod_agg: float32 [256, 256], replicated, may hold values from -0.375 to 0.375
- w_cust_self: float32 [256, 256], replicated, may hold values from -0.375 to 0.375
- w_cust_prod: float32 [256, 256], replicated, may hold values from -0.375 to 0.375
Outputs:
- new_products: float32 [4096, 256], P(('hash', 'tm'))
- new_customers: float32 [8192, 256], P(('hash', 'tm'))
Inputs may be any that keep to these rules, and one draw needn't show every extreme that they name: `tx_count`: each device has at least one product owner for which all 64 slots are used; which one is drawn. `send_count`: uneven counts; each device has at least one customer owner for which all 16 slots are used.
All inputs are finite; a program needn't handle non-finite values.
Results may differ from a plain program's by a relative error of at most 0.000055.
Values sent between devices are 32-bit elements; how exact they have to be, the bound alone decides.
No kernel may reach another device: no remote copies, remote signals or barrier semaphores. Data moves between devices by JAX's collectives and lax.ppermute only.
A program may use at most 64 MiB of HBM per device.

v0:
```python
import jax
import jax.numpy as jnp
from jax import lax
from jax.sharding import PartitionSpec as P

highest = lax.Precision.HIGHEST


def update(table, other, w_self, w_other):
    inner = jnp.dot(table, w_self, precision=highest) + jnp.dot(other, w_other, precision=highest)
    return table + jax.nn.relu(inner)


def local(
    transactions,
    tx_product,
    tx_count,
    products,
    customers,
    send_rows,
    send_count,
    recv_customer,
    w_msg,
    w_prod_self,
    w_prod_agg,
    w_cust_self,
    w_cust_prod,
):
    peers = lax.axis_size("hash")
    width = transactions.shape[1]
    slots = transactions.shape[0] // peers
    mine = products.shape[0]
    owned = mine * lax.axis_size("tm")
    outgoing = jax.nn.relu(jnp.dot(transactions, w_msg, precision=highest))
    outgoing = outgoing.reshape(peers, slots, width)
    product_ids = tx_product.reshape(peers, slots)
    arrived, arrived_ids, arrived_count = (
        lax.all_to_all(outgoing, "hash", split_axis=0, concat_axis=0, tiled=True),
        lax.all_to_all(product_ids, "hash", split_axis=0, concat_axis=0, tiled=True),
        lax.all_to_all(tx_count, "hash", split_axis=0, concat_axis=0, tiled=True),
    )
    slot_index = lax.broadcasted_iota(jnp.int32, (peers, slots), 1)
    used = slot_index < arrived_count[:, None]
    masked = jnp.where(used[:, :, None], arrived, jnp.zeros_like(arrived)).reshape(-1, width)
    flat_ids = arrived_ids.reshape(-1)
    block = min(512, owned)

    def block_sum(offset):
        targets = offset + lax.iota(jnp.int32, block)
        onehot = (flat_ids[None, :] == targets[:, None]).astype(jnp.float32)
        return jnp.dot(onehot, masked, precision=highest)

    offsets = jnp.arange(0, owned, block, dtype=jnp.int32)
    partial_value = lax.map(block_sum, offsets).reshape(owned, width)
    share = lax.psum_scatter(partial_value, "tm", scatter_dimension=0, tiled=True)
    new_products = update(products, share, w_prod_self, w_prod_agg)
    send_slots = send_rows.shape[0] // peers
    listed = jnp.take(new_products, send_rows, axis=0).reshape(peers, send_slots, width)
    customer_self = jnp.dot(customers, w_cust_self, precision=highest)
    incoming, incoming_count = (
        lax.all_to_all(listed, "hash", split_axis=0, concat_axis=0, tiled=True),
        lax.all_to_all(send_count, "hash", split_axis=0, concat_axis=0, tiled=True),
    )
    send_index = lax.broadcasted_iota(jnp.int32, (peers, send_slots), 1)
    live = (send_index < incoming_count[:, None]).reshape(-1)
    rows_in = jnp.where(
        live[:, None],
        incoming.reshape(-1, width),
        jnp.zeros((peers * send_slots, width), jnp.float32),
    )
    customer_rows = lax.iota(jnp.int32, customers.shape[0])
    incidence = (recv_customer[None, :] == customer_rows[:, None]).astype(jnp.float32)
    bought = jnp.dot(incidence, rows_in, precision=highest)
    inner = customer_self + jnp.dot(bought, w_cust_prod, precision=highest)
    new_customers = customers + jax.nn.relu(inner)
    return (new_products, new_customers)


def solution(mesh):
    placed = (
        P(("hash", "tm"), None),
        P(("hash", "tm")),
        P(("hash", "tm")),
        P(("hash", "tm"), None),
        P(("hash", "tm"), None),
        P(("hash", "tm")),
        P(("hash", "tm")),
        P(("hash", "tm")),
        P(),
        P(),
        P(),
        P(),
        P(),
    )
    return jax.shard_map(
        local,
        mesh=mesh,
        in_specs=placed,
        out_specs=(P(("hash", "tm"), None), P(("hash", "tm"), None)),
        check_vma=False,
    )
```

profile of v0, /device:TPU:0, one launch (start us, length us, event | category | flops | bytes accessed | tf_op | source)
XLA Modules:
  0.0 110.2 jit_solution(942641003405517411)
XLA Ops:
  7.2 0.0 copy-start
  7.2 0.0 copy-start.11
  7.2 0.7 copy-done.11
  7.9 0.7 copy.17
  8.6 7.5 %all-to-all-start.1 = ((s32[16,1,1]{2,1,0:T(1,128)}), s32[16,1,1]{2,1,0:T(1,128)S(1)}, u32[]{:S(2)}, u32[]{:S(2)}) async-start(s32[16,1,1]{2,1,0:T(1,128)} %copy.17), calls=%async_computation.1 | async-start | bytes 16384 | tf_op jit(solution)/shard_map/all_to_all | solution.py:40
  16.1 0.0 copy-done.8
  16.1 0.7 all_to_all.24
  16.8 5.6 %all-to-all-done.1 = s32[16,1,1]{2,1,0:T(1,128)S(1)} async-done(((s32[16,1,1]{2,1,0:T(1,128)}), s32[16,1,1]{2,1,0:T(1,128)S(1)}, u32[]{:S(2)}, u32[]{:S(2)}) %all-to-all-start.1) | async-done | bytes 96 | tf_op jit(solution)/shard_map/all_to_all | solution.py:40
  22.4 3.5 %all-to-all-start = ((s32[16,1,64]{2,1,0:T(1,128)}), s32[16,1,64]{2,1,0:T(1,128)S(1)}, u32[]{:S(2)}, u32[]{:S(2)}) async-start(s32[16,1,64]{2,1,0:T(1,128)} %all_to_all.24), calls=%async_computation | async-start | bytes 16384 | tf_op jit(solution)/shard_map/all_to_all | solution.py:39
  25.9 0.0 copy-done
  25.9 2.9 %convolution_maximum_fusion = f32[1024,256]{1,0:T(8,128)} fusion(f32[1024,256]{1,0:T(8,128)S(1)} %copy-done, f32[256,256]{1,0:T(8,128)} %param.21), kind=kOutput, calls=%fused_computation.1 | convolution fusion | flops 805568512 | bytes 2359296 | tf_op jit(solution)/shard_map/dot_general | solution.py:34
  28.8 3.4 %all-to-all-done = s32[16,1,64]{2,1,0:T(1,128)S(1)} async-done(((s32[16,1,64]{2,1,0:T(1,128)}), s32[16,1,64]{2,1,0:T(1,128)S(1)}, u32[]{:S(2)}, u32[]{:S(2)}) %all-to-all-start) | async-done | bytes 4128 | tf_op jit(solution)/shard_map/all_to_all | solution.py:39
  32.2 3.8 %all-to-all-start.2 = ((f32[16,64,256]{2,1,0:T(8,128)}), f32[16,64,256]{2,1,0:T(8,128)S(1)}, u32[]{:S(2)}, u32[]{:S(2)}) async-start(f32[16,64,256]{2,1,0:T(8,128)} %bitcast.1), calls=%async_computation.2 | async-start | bytes 2097152 | tf_op jit(solution)/shard_map/all_to_all | solution.py:38
  36.0 0.1 broadcast_in_dim.50
  36.1 0.7 copy-done.12
  36.8 0.7 copy.18
  37.4 0.4 reduce.1
  37.8 0.1 iota_compare_fusion.5
  37.9 0.5 broadcast.32
  38.4 0.7 reduce.5
  39.1 0.1 eq.35
  39.2 19.7 %all-to-all-done.2 = f32[16,64,256]{2,1,0:T(8,128)S(1)} async-done(((f32[16,64,256]{2,1,0:T(8,128)}), f32[16,64,256]{2,1,0:T(8,128)S(1)}, u32[]{:S(2)}, u32[]{:S(2)}) %all-to-all-start.2) | async-done | bytes 1048608 | tf_op jit(solution)/shard_map/all_to_all | solution.py:38
  58.9 6.8 %all-to-all-start.3 = ((s32[16,1,1]{2,1,0:T(1,128)}), s32[16,1,1]{2,1,0:T(1,128)S(1)}, u32[]{:S(2)}, u32[]{:S(2)}) async-start(s32[16,1,1]{2,1,0:T(1,128)} %copy.18), calls=%async_computation.4 | async-start | bytes 16384 | tf_op jit(solution)/shard_map/all_to_all | solution.py:62
  65.7 0.0 reduce-scatter.2.cloned.1.call-start
  65.8 0.2 broadcast_select_fusion
  66.0 0.0 copy-start.7
  66.0 1.5 %fusion.4 = f32[256,256]{1,0:T(8,128)} fusion(f32[1024,256]{1,0:T(8,128)S(1)} %bitcast.19, s32[1024]{0:T(1024)S(1)} %eq.35), kind=kOutput, calls=%fused_computation.9 | convolution fusion | flops 805568512 | bytes 1314816 | tf_op jit(solution)/shard_map/while/body/eval_jaxpr/dot_general | solution.py:51
  67.5 0.0 reduce-scatter.2.cloned.1.call-update
  67.5 0.8 copy-done.3
  68.4 0.3 fusion.8
  68.7 13.7 %reduce-scatter.2.cloned.1.call-done = f32[128,256]{1,0:T(8,128)} async-done(((f32[256,256]{1,0:T(8,128)}), f32[128,256]{1,0:T(8,128)}) %reduce-scatter.2.cloned.1.call-update) | async-done | bytes 131088 | tf_op jit(solution)/shard_map/reduce_scatter | solution.py:55
  82.4 1.2 %fusion.3 = f32[128,256]{1,0:T(8,128)S(1)} fusion(f32[128,256]{1,0:T(8,128)S(1)} %copy-done.3, f32[128,256]{1,0:T(8,128)S(1)} %fusion.8, f32[128,256]{1,0:T(8,128)} %reduce-scatter.2.cloned.1.call-done, f32[256,256]{1,0:T(8,128)S(1)} %copy-done.4), kind=kOutput, calls=%fused_computation.7 | convolution fusion | flops 100761600 | bytes 786432 | tf_op jit(solution)/shard_map/dot_general | solution.py:10
  83.6 0.0 copy-start.1
  83.6 1.0 gather_fusion
  84.6 0.8 broadcast_select_fusion.1
  85.4 0.0 all-to-all-done.3
  85.4 5.7 %all-to-all-start.4 = ((f32[16,16,256]{2,1,0:T(8,128)}), f32[16,16,256]{2,1,0:T(8,128)S(1)}, u32[]{:S(2)}, u32[]{:S(2)}) async-start(f32[16,16,256]{2,1,0:T(8,128)} %broadcast_select_fusion.1), calls=%async_computation.5 | async-start | bytes 524288 | tf_op jit(solution)/shard_map/all_to_all | solution.py:61
  91.2 0.4 fusion.9
  91.5 0.4 reduce.2
  91.9 0.1 iota_compare_fusion.4
  92.0 0.1 lt.46
  92.1 0.0 copy-start.9
  92.1 9.1 %all-to-all-done.4 = f32[16,16,256]{2,1,0:T(8,128)S(1)} async-done(((f32[16,16,256]{2,1,0:T(8,128)}), f32[16,16,256]{2,1,0:T(8,128)S(1)}, u32[]{:S(2)}, u32[]{:S(2)}) %all-to-all-start.4) | async-done | bytes 262176 | tf_op jit(solution)/shard_map/all_to_all | solution.py:61
  101.2 0.1 bitcast_select_fusion
  101.3 0.0 copy-start.6
  101.3 0.3 fusion.6
  101.6 0.6 copy-done.6
  102.3 1.1 fusion.1
  (17 shorter events, 0.0 us)
Async XLA Ops:
  7.2 18.8 %copy-start = (f32[1024,256]{1,0:T(8,128)S(1)}, f32[1024,256]{1,0:T(8,128)}, u32[]{:S(2)}) copy-start(f32[1024,256]{1,0:T(8,128)} %param.13) | copy-start | bytes 3145732
  7.2 0.7 copy-start.11
  8.6 7.5 %copy-start.8 = (s32[1024]{0:T(1024)S(1)}, s32[1024]{0:T(1024)}, u32[]{:S(2)}) copy-start(s32[1024]{0:T(1024)} %param.14) | copy-start | bytes 12292
  8.6 13.8 %all-to-all-start.1 = ((s32[16,1,1]{2,1,0:T(1,128)}), s32[16,1,1]{2,1,0:T(1,128)S(1)}, u32[]{:S(2)}, u32[]{:S(2)}) async-start(s32[16,1,1]{2,1,0:T(1,128)} %copy.17), calls=%async_computation.1 | async-start | bytes 16384 | tf_op jit(solution)/shard_map/all_to_all | solution.py:40
  22.4 9.8 %all-to-all-start = ((s32[16,1,64]{2,1,0:T(1,128)}), s32[16,1,64]{2,1,0:T(1,128)S(1)}, u32[]{:S(2)}, u32[]{:S(2)}) async-start(s32[16,1,64]{2,1,0:T(1,128)} %all_to_all.24), calls=%async_computation | async-start | bytes 16384 | tf_op jit(solution)/shard_map/all_to_all | solution.py:39
  32.2 3.8 %copy-start.10 = (s32[256]{0:T(256)S(1)}, s32[256]{0:T(256)}, u32[]{:S(2)}) copy-start(s32[256]{0:T(256)} %param.18) | copy-start | bytes 3076
  32.2 26.7 %all-to-all-start.2 = ((f32[16,64,256]{2,1,0:T(8,128)}), f32[16,64,256]{2,1,0:T(8,128)S(1)}, u32[]{:S(2)}, u32[]{:S(2)}) async-start(f32[16,64,256]{2,1,0:T(8,128)} %bitcast.1), calls=%async_computation.2 | async-start | bytes 2097152 | tf_op jit(solution)/shard_map/all_to_all | solution.py:38
  36.1 0.7 copy-start.12
  58.9 26.5 %all-to-all-start.3 = ((s32[16,1,1]{2,1,0:T(1,128)}), s32[16,1,1]{2,1,0:T(1,128)S(1)}, u32[]{:S(2)}, u32[]{:S(2)}) async-start(s32[16,1,1]{2,1,0:T(1,128)} %copy.18), calls=%async_computation.4 | async-start | bytes 16384 | tf_op jit(solution)/shard_map/all_to_all | solution.py:62
  65.7 16.7 %reduce-scatter.2.cloned.1.call-start = ((), (), s32[]{:S(2)}) async-start(), calls=%async_computation.6 | async-start | bytes 393216 | tf_op jit(solution)/shard_map/reduce_scatter | solution.py:55
  66.0 1.5 %copy-start.7 = (f32[256,256]{1,0:T(8,128)S(1)}, f32[256,256]{1,0:T(8,128)}, u32[]{:S(2)}) copy-start(f32[256,256]{1,0:T(8,128)} %param.22) | copy-start | bytes 786436
  67.5 0.9 copy-start.3
  68.4 14.0 %copy-start.4 = (f32[256,256]{1,0:T(8,128)S(1)}, f32[256,256]{1,0:T(8,128)}, u32[]{:S(2)}) copy-start(f32[256,256]{1,0:T(8,128)} %param.23) | copy-start | bytes 786436
  83.6 1.0 copy-start.1
  85.4 5.8 %copy-start.2 = (f32[256,256]{1,0:T(8,128)S(1)}, f32[256,256]{1,0:T(8,128)}, u32[]{:S(2)}) copy-start(f32[256,256]{1,0:T(8,128)} %param.17) | copy-start | bytes 786436
  85.4 5.8 %copy-start.5 = (f32[256,256]{1,0:T(8,128)S(1)}, f32[256,256]{1,0:T(8,128)}, u32[]{:S(2)}) copy-start(f32[256,256]{1,0:T(8,128)} %param.24) | copy-start | bytes 786436
  85.4 15.8 %all-to-all-start.4 = ((f32[16,16,256]{2,1,0:T(8,128)}), f32[16,16,256]{2,1,0:T(8,128)S(1)}, u32[]{:S(2)}, u32[]{:S(2)}) async-start(f32[16,16,256]{2,1,0:T(8,128)} %broadcast_select_fusion.1), calls=%async_computation.5 | async-start | bytes 524288 | tf_op jit(solution)/shard_map/all_to_all | solution.py:61
  92.1 9.2 %copy-start.9 = (s32[256]{0:T(256)S(1)}, s32[256]{0:T(256)}, u32[]{:S(2)}) copy-start(s32[256]{0:T(256)} %param.20) | copy-start | bytes 3076
  101.3 1.0 copy-start.6
Sparse Core Ops, SparseCore 0:
  69.4 12.9 reduce-scatter.1
where the time goes:
time: 111 us; the launch traced here: 110 us
  waiting for transfers between devices  51.6 us (46%)
  starting transfers between devices  27.3 us (25%)
  between operations  14.3 us (13%)
  matrix products  7.64 us (7%)
  local copies, waits for them, and re-layouts  6.69 us (6%)
  other arithmetic  2.7 us (2%)
    all_to_all x1, waiting for transfers between devices, local(): lax.all_to_all(outgoing, 'hash', split_axis=0, concat_axis=0, tiled=True)  19.7 us
    reduce_scatter x1, waiting for transfers between devices, local(): lax.psum_scatter(partial_value, 'tm', scatter_dimension=0, tiled=True)  13.7 us
    all_to_all x1, waiting for transfers between devices, local(): lax.all_to_all(listed, 'hash', split_axis=0, concat_axis=0, tiled=True)  9.08 us
    all_to_all x1, starting transfers between devices, local(): lax.all_to_all(tx_count, 'hash', split_axis=0, concat_axis=0, tiled=True)  7.49 us
    all_to_all x1, starting transfers between devices, local(): lax.all_to_all(send_count, 'hash', split_axis=0, concat_axis=0, tiled=True)  6.81 us
    all_to_all x1, starting transfers between devices, local(): lax.all_to_all(listed, 'hash', split_axis=0, concat_axis=0, tiled=True)  5.75 us
    all_to_all x1, waiting for transfers between devices, local(): lax.all_to_all(tx_count, 'hash', split_axis=0, concat_axis=0, tiled=True)  5.64 us
    all_to_all x1, starting transfers between devices, local(): lax.all_to_all(outgoing, 'hash', split_axis=0, concat_axis=0, tiled=True)  3.78 us
  transfers between devices with their start and end apart: 6, of which 5 were waited for; matrix products, arithmetic and copies ran while one was open for 10% of the time, Pallas kernels for 0%

commit v1 on v0

v1 whole, which is shorter than its diff:
```python
import jax
import jax.numpy as jnp
from jax import lax
from jax.sharding import PartitionSpec as P

high = lax.Precision.HIGH


def swap_bit(blocks, axis, bit, mask, peers):
    keep = lax.dynamic_index_in_dim(blocks, bit, axis, keepdims=True)
    send = lax.dynamic_index_in_dim(blocks, 1 - bit, axis, keepdims=True)
    got = lax.ppermute(send, "hash", [(i, i ^ mask) for i in range(peers)])
    low = jnp.where(bit == 0, keep, got)
    top = jnp.where(bit == 0, got, keep)
    return jnp.concatenate([low, top], axis)


def exchange_ids(ids):
    peers, slots = ids.shape
    if peers != 16:
        return lax.all_to_all(ids, "hash", split_axis=0, concat_axis=0, tiled=True)
    me = lax.axis_index("hash")
    blocks = ids.reshape(4, 2, 2, slots)
    blocks = swap_bit(blocks, 2, me & 1, 1, peers)
    blocks = swap_bit(blocks, 1, (me >> 1) & 1, 2, peers)
    far = me >> 2
    got = [lax.dynamic_index_in_dim(blocks, far, 0, keepdims=False)]
    for k in (1, 2, 3):
        send = lax.dynamic_index_in_dim(blocks, far ^ k, 0, keepdims=False)
        got.append(lax.ppermute(send, "hash", [(i, i ^ (4 * k)) for i in range(peers)]))
    stacked = jnp.stack(got)
    order = [lax.dynamic_index_in_dim(stacked, far ^ k, 0, keepdims=True) for k in range(4)]
    return jnp.concatenate(order, 0).reshape(peers, slots)


def local(
    transactions,
    tx_product,
    tx_count,
    products,
    customers,
    send_rows,
    send_count,
    recv_customer,
    w_msg,
    w_prod_self,
    w_prod_agg,
    w_cust_self,
    w_cust_prod,
):
    peers, pair = lax.axis_size("hash"), lax.axis_size("tm")
    half = lax.axis_index("tm")
    width = transactions.shape[1]
    slots = transactions.shape[0] // peers
    mine = products.shape[0]
    send_slots = send_rows.shape[0] // peers

    slot_index = lax.broadcasted_iota(jnp.int32, (peers, slots), 1)
    ids = jnp.where(slot_index < tx_count[:, None], tx_product.reshape(peers, slots), -1)
    outgoing = jax.nn.relu(jnp.dot(transactions, w_msg, precision=high))
    arrived = lax.all_to_all(
        outgoing.reshape(peers, slots, width), "hash", split_axis=0, concat_axis=0, tiled=True
    ).reshape(-1, width)
    flat_ids = exchange_ids(ids).reshape(-1)

    product_self = jnp.dot(products, w_prod_self, precision=high)
    customer_self = jnp.dot(customers, w_cust_self, precision=high)

    def block_sum(part):
        targets = part * mine + lax.iota(jnp.int32, mine)
        onehot = (flat_ids[None, :] == targets[:, None]).astype(jnp.float32)
        return jnp.dot(onehot, arrived, precision=high)

    if pair == 2:
        other = lax.ppermute(block_sum(1 - half), "tm", [(0, 1), (1, 0)])
        aggregate = block_sum(half) + other
    else:
        parts = lax.map(block_sum, jnp.arange(pair)).reshape(pair * mine, width)
        aggregate = lax.psum_scatter(parts, "tm", scatter_dimension=0, tiled=True)
    inner = product_self + jnp.dot(aggregate, w_prod_agg, precision=high)
    new_products = products + jax.nn.relu(inner)

    send_index = lax.broadcasted_iota(jnp.int32, (peers, send_slots), 1)
    named = jnp.where(send_index < send_count[:, None], send_rows.reshape(peers, send_slots), -1)
    picks = (named.reshape(-1)[:, None] == lax.iota(jnp.int32, mine)[None, :]).astype(jnp.float32)
    listed = jnp.dot(picks, new_products, precision=high).reshape(peers, send_slots, width)
    incoming = lax.all_to_all(listed, "hash", split_axis=0, concat_axis=0, tiled=True)
    customer_rows = lax.iota(jnp.int32, customers.shape[0])
    incidence = (recv_customer[None, :] == customer_rows[:, None]).astype(jnp.float32)
    bought = jnp.dot(incidence, incoming.reshape(-1, width), precision=high)
    inner = customer_self + jnp.dot(bought, w_cust_prod, precision=high)
    return new_products, customers + jax.nn.relu(inner)


def solution(mesh):
    rows, flat = P(("hash", "tm"), None), P(("hash", "tm"))
    placed = (rows, flat, flat, rows, rows, flat, flat, flat, P(), P(), P(), P(), P())
    return jax.shard_map(local, mesh=mesh, in_specs=placed, out_specs=(rows, rows), check_vma=False)
```

time: 111 us -> 62.1 us (0.56)
  waiting for transfers between devices: 51.6 us -> 30.7 us
  between operations: 14.3 us -> 0.85 us
  starting transfers between devices: 27.3 us -> 20.1 us
  local copies, waits for them, and re-layouts: 6.69 us -> 3.59 us
  other arithmetic: 2.7 us -> 0.23 us
  matrix products: 7.64 us -> 6.16 us
    all_to_all x4 -> x1, waiting for transfers between devices: 28.7 us -> 0.01 us  [local(): lax.all_to_all(outgoing.reshape(peers, slots, width), 'hash', split_axis=...]
    ppermute x0 -> x6, waiting for transfers between devices: none -> 21 us  [the longest x3 13.5 us: exchange_ids(): lax.ppermute(send, 'hash', [(i, i ^ 4 * k) for i in range(peers)])]
    all_to_all x4 -> x1, starting transfers between devices: 21.6 us -> 7.49 us  [local(): lax.all_to_all(outgoing.reshape(peers, slots, width), 'hash', split_axis=...]
    reduce_scatter x1 -> x0, waiting for transfers between devices: 13.7 us -> none  [local(): lax.psum_scatter(partial_value, 'tm', scatter_dimension=0, tiled=True)]
    ppermute x0 -> x6, starting transfers between devices: none -> 8.68 us  [the longest x3 4.7 us: exchange_ids(): lax.ppermute(send, 'hash', [(i, i ^ 4 * k) for i in range(peers)])]
    all_to_all x4 -> x0, local copies, waits for them, and re-layouts: 2.55 us -> none  [the longest x2 1.2 us: local(): lax.all_to_all(product_ids, 'hash', split_axis=0, concat_axis=0, tiled=True)]
    all_to_all x1, starting transfers between devices: 5.75 us -> 3.96 us  [local(): lax.all_to_all(listed, 'hash', split_axis=0, concat_axis=0, tiled=True)]
    dot_general x7 -> x9, matrix products: 7.64 us -> 6.16 us  [the longest x1 2.55 us: local(): outgoing = jax.nn.relu(jnp.dot(transactions, w_msg, precision=high))]
  transfers between devices with their start and end apart: 6 -> 8, of which waited for: 5 -> 6; matrix products, arithmetic and copies ran while one was open for 10% -> 2% of each run, Pallas kernels for 0% -> 0%
where the time goes in v1:
time: 62.1 us; the launch traced here: 61.7 us
  waiting for transfers between devices  30.7 us (49%)
  starting transfers between devices  20.1 us (32%)
  matrix products  6.16 us (10%)
  local copies, waits for them, and re-layouts  3.59 us (6%)
  between operations  0.85 us (1%)
    ppermute x3, waiting for transfers between devices, exchange_ids(): lax.ppermute(send, 'hash', [(i, i ^ 4 * k) for i in range(peers)])  13.5 us
    all_to_all x1, waiting for transfers between devices, local(): lax.all_to_all(listed, 'hash', split_axis=0, concat_axis=0, tiled=True)  9.74 us
    all_to_all x1, starting transfers between devices, local(): lax.all_to_all(outgoing.reshape(peers, slots, width), 'hash', split_axis=...  7.49 us
    ppermute x3, starting transfers between devices, exchange_ids(): lax.ppermute(send, 'hash', [(i, i ^ 4 * k) for i in range(peers)])  4.7 us
    ppermute x2, waiting for transfers between devices, swap_bit(): got = lax.ppermute(send, 'hash', [(i, i ^ mask) for i in range(peers)])  4.09 us
    all_to_all x1, starting transfers between devices, local(): lax.all_to_all(listed, 'hash', split_axis=0, concat_axis=0, tiled=True)  3.96 us
    ppermute x1, waiting for transfers between devices, local(): other = lax.ppermute(block_sum(1 - half), 'tm', [(0, 1), (1, 0)])  3.42 us
    unnamed x26, local copies, waits for them, and re-layouts  3.23 us
  transfers between devices with their start and end apart: 8, of which 6 were waited for; matrix products, arithmetic and copies ran while one was open for 2% of the time, Pallas kernels for 0%

profile of v1, /device:TPU:0, one launch (start us, length us, event | category | flops | bytes accessed | tf_op | source)
XLA Modules:
  0.0 61.7 jit_solution(16149945049063923943)
XLA Ops:
  0.6 0.0 copy-start
  0.6 1.2 %copy-done = f32[1024,256]{1,0:T(8,128)S(1)} copy-done((f32[1024,256]{1,0:T(8,128)S(1)}, f32[1024,256]{1,0:T(8,128)}, u32[]{:S(2)}) %copy-start) | copy-done | bytes 1048600
  1.9 2.5 %convolution_maximum_fusion = f32[1024,256]{1,0:T(8,128)} fusion(f32[1024,256]{1,0:T(8,128)S(1)} %copy-done, f32[256,256]{1,0:T(8,128)} %param.21), kind=kOutput, calls=%fused_computation | convolution fusion | flops 402915328 | bytes 2359296 | tf_op jit(solution)/shard_map/dot_general | solution.py:60
  4.4 7.5 %all-to-all-start = ((f32[16,64,256]{2,1,0:T(8,128)}), f32[16,64,256]{2,1,0:T(8,128)S(1)}, u32[]{:S(2)}, u32[]{:S(2)}) async-start(f32[16,64,256]{2,1,0:T(8,128)} %bitcast.6), calls=%async_computation | async-start | bytes 2097152 | tf_op jit(solution)/shard_map/all_to_all | solution.py:61
  11.9 0.0 copy-start.8
  11.9 0.7 %copy-done.8 = s32[1024]{0:T(1024)S(1)} copy-done((s32[1024]{0:T(1024)S(1)}, s32[1024]{0:T(1024)}, u32[]{:S(2)}) %copy-start.8) | copy-done | bytes 4120
  12.6 0.1 reshape.53
  12.7 0.6 copy-done.11
  13.3 0.1 lt.56
  13.4 0.1 compare_select_fusion
  13.4 0.5 collective-permute-start
  13.9 0.0 copy-done.3
  13.9 0.0 copy-done.7
  13.9 0.2 fusion.24
  14.2 0.6 collective-permute-done
  14.8 0.0 copy-start.12
  14.8 1.9 %collective-permute-start.1 = (s32[4,1,2,64]{3,2,1,0:T(2,128)S(1)}, s32[4,1,2,64]{3,2,1,0:T(2,128)S(1)}, u32[]{:S(2)}, u32[]{:S(2)}) collective-permute-start(s32[4,1,2,64]{3,2,1,0:T(2,128)S(1)} %fusion.15), channel_id=1, source_target_pairs={{0,4},{2,6},{4,0},{6,2},{8,12},{10,14},{12,8},{14,10},{16,20},{18,... | collective-permute-start | bytes 6152 | tf_op jit(solution)/shard_map/ppermute | solution.py:12
  16.7 0.0 copy-done.12
  16.7 0.1 iota_compare_fusion.4
  16.8 3.5 %collective-permute-done.1 = s32[4,1,2,64]{3,2,1,0:T(2,128)S(1)} collective-permute-done((s32[4,1,2,64]{3,2,1,0:T(2,128)S(1)}, s32[4,1,2,64]{3,2,1,0:T(2,128)S(1)}, u32[]{:S(2)}, u32[]{:S(2)}) %collective-permute-start.1) | collective-permute-done | bytes 2080 | tf_op jit(solution)/shard_map/ppermute | solution.py:12
  20.4 0.1 collective-permute-start.2
  20.5 4.6 %collective-permute-start.3 = (s32[2,2,64]{2,1,0:T(2,128)S(1)}, s32[2,2,64]{2,1,0:T(2,128)S(1)}, u32[]{:S(2)}, u32[]{:S(2)}) collective-permute-start(s32[2,2,64]{2,1,0:T(2,128)S(1)} %get-tuple-element.12), channel_id=1, source_target_pairs={{0,16},{2,18},{4,20},{6,22},{8,24},{10,26},{12,28},{14,30},{16,0},... | collective-permute-start | bytes 3080 | tf_op jit(solution)/shard_map/ppermute | solution.py:30
  25.1 0.0 collective-permute-start.4
  25.1 0.1 lt.69
  25.1 5.0 %collective-permute-done.2 = s32[2,2,64]{2,1,0:T(2,128)S(1)} collective-permute-done((s32[2,2,64]{2,1,0:T(2,128)S(1)}, s32[2,2,64]{2,1,0:T(2,128)S(1)}, u32[]{:S(2)}, u32[]{:S(2)}) %collective-permute-start.2) | collective-permute-done | bytes 1056 | tf_op jit(solution)/shard_map/ppermute | solution.py:30
  30.1 8.5 %collective-permute-done.3 = s32[2,2,64]{2,1,0:T(2,128)S(1)} collective-permute-done((s32[2,2,64]{2,1,0:T(2,128)S(1)}, s32[2,2,64]{2,1,0:T(2,128)S(1)}, u32[]{:S(2)}, u32[]{:S(2)}) %collective-permute-start.3) | collective-permute-done | bytes 1056 | tf_op jit(solution)/shard_map/ppermute | solution.py:30
  38.6 0.0 collective-permute-done.4
  38.7 0.1 eq.30
  38.7 0.0 all-to-all-done
  38.8 0.3 fusion.4
  39.1 1.6 %collective-permute-start.5 = (f32[128,256]{1,0:T(8,128)S(1)}, f32[128,256]{1,0:T(8,128)S(1)}, u32[]{:S(2)}, u32[]{:S(2)}) collective-permute-start(f32[128,256]{1,0:T(8,128)S(1)} %fusion.4), channel_id=1, source_target_pairs={{0,1},{1,0},{2,3},{3,2},{4,5},{5,4},{6,7},{7,6},{8,9},{9,8},{10,11... | collective-permute-start | bytes 393224 | tf_op jit(solution)/shard_map/ppermute | solution.py:75
  40.7 0.0 copy-done.10
  40.7 0.0 copy-start.4
  40.7 3.4 %collective-permute-done.5 = f32[128,256]{1,0:T(8,128)S(1)} collective-permute-done((f32[128,256]{1,0:T(8,128)S(1)}, f32[128,256]{1,0:T(8,128)S(1)}, u32[]{:S(2)}, u32[]{:S(2)}) %collective-permute-start.5) | collective-permute-done | bytes 131104 | tf_op jit(solution)/shard_map/ppermute | solution.py:75
  44.1 0.3 convolution_add_fusion.2
  44.5 0.0 copy-done.4
  44.5 0.2 fusion.3
  44.7 0.0 copy-start.2
  44.8 1.0 %fusion.13 = f32[256,256]{1,0:T(8,128)} fusion(f32[128,256]{1,0:T(8,128)S(1)} %fusion.3, s32[256]{0:T(256)S(1)} %broadcast_select_fusion.4), kind=kOutput, calls=%fused_computation.19 | convolution fusion | flops 50364416 | bytes 394240 | tf_op jit(solution)/shard_map/dot_general | solution.py:86
  45.7 0.0 copy-done.2
  45.7 4.0 %all-to-all-start.1 = ((f32[16,16,256]{2,1,0:T(8,128)}), f32[16,16,256]{2,1,0:T(8,128)S(1)}, u32[]{:S(2)}, u32[]{:S(2)}) async-start(f32[16,16,256]{2,1,0:T(8,128)} %bitcast.8), calls=%async_computation.1 | async-start | bytes 524288 | tf_op jit(solution)/shard_map/all_to_all | solution.py:87
  49.7 0.0 copy-done.1
  49.7 0.3 fusion.25
  50.0 0.0 copy-start.9
  50.0 9.7 %all-to-all-done.1 = f32[16,16,256]{2,1,0:T(8,128)S(1)} async-done(((f32[16,16,256]{2,1,0:T(8,128)}), f32[16,16,256]{2,1,0:T(8,128)S(1)}, u32[]{:S(2)}, u32[]{:S(2)}) %all-to-all-start.1) | async-done | bytes 262176 | tf_op jit(solution)/shard_map/all_to_all | solution.py:87
  59.8 0.2 fusion.11
  60.0 0.7 %copy-done.6 = f32[256,256]{1,0:T(8,128)S(1)} copy-done((f32[256,256]{1,0:T(8,128)S(1)}, f32[256,256]{1,0:T(8,128)}, u32[]{:S(2)}) %copy-start.6) | copy-done | bytes 262168
  60.7 1.0 %fusion.1 = f32[256,256]{1,0:T(8,128)} fusion(f32[256,256]{1,0:T(8,128)S(1)} %copy-done.1, f32[256,256]{1,0:T(8,128)S(1)} %fusion.25, f32[256,256]{1,0:T(8,128)S(1)} %fusion.11, f32[256,256]{1,0:T(8,128)S(1)} %copy-done.6), kind=kOutput, calls=%fused_computation.3 | convolution fusion | flops 100859904 | bytes 1310720 | tf_op jit(solution)/shard_map/dot_general | solution.py:91
  (20 shorter events, 0.1 us)
Async XLA Ops:
  0.6 1.2 %copy-start = (f32[1024,256]{1,0:T(8,128)S(1)}, f32[1024,256]{1,0:T(8,128)}, u32[]{:S(2)}) copy-start(f32[1024,256]{1,0:T(8,128)} %param.13) | copy-start | bytes 3145732
  4.4 9.5 %copy-start.3 = (f32[128,256]{1,0:T(8,128)S(1)}, f32[128,256]{1,0:T(8,128)}, u32[]{:S(2)}) copy-start(f32[128,256]{1,0:T(8,128)} %param.16) | copy-start | bytes 393220
  4.4 9.5 %copy-start.7 = (f32[256,256]{1,0:T(8,128)S(1)}, f32[256,256]{1,0:T(8,128)}, u32[]{:S(2)}) copy-start(f32[256,256]{1,0:T(8,128)} %param.22) | copy-start | bytes 786436
  4.4 34.3 %all-to-all-start = ((f32[16,64,256]{2,1,0:T(8,128)}), f32[16,64,256]{2,1,0:T(8,128)S(1)}, u32[]{:S(2)}, u32[]{:S(2)}) async-start(f32[16,64,256]{2,1,0:T(8,128)} %bitcast.6), calls=%async_computation | async-start | bytes 2097152 | tf_op jit(solution)/shard_map/all_to_all | solution.py:61
  11.9 0.7 %copy-start.8 = (s32[1024]{0:T(1024)S(1)}, s32[1024]{0:T(1024)}, u32[]{:S(2)}) copy-start(s32[1024]{0:T(1024)} %param.14) | copy-start | bytes 12292
  12.6 0.7 %copy-start.11 = (s32[16]{0:T(128)S(1)}, s32[16]{0:T(128)}, u32[]{:S(2)}) copy-start(s32[16]{0:T(128)} %param.15) | copy-start | bytes 196
  13.4 1.3 %collective-permute-start = (s32[4,2,1,64]{3,2,1,0:T(1,128)S(1)}, s32[4,2,1,64]{3,2,1,0:T(1,128)S(1)}, u32[]{:S(2)}, u32[]{:S(2)}) collective-permute-start(s32[4,2,1,64]{3,2,1,0:T(1,128)S(1)} %constant_dynamic-slice_fusion.4), channel_id=1, source_target_pairs={{0,2},{2,0},{4,6},{6,4},{8,10},{10,8},{12,14},{14,12},{16,18},{18,... | collective-permute-start | bytes 6152 | tf_op jit(solution)/shard_map/ppermute | solution.py:12
  14.8 2.0 %copy-start.12 = (s32[16]{0:T(128)S(1)}, s32[16]{0:T(128)}, u32[]{:S(2)}) copy-start(s32[16]{0:T(128)} %param.19) | copy-start | bytes 196
  14.8 5.5 %collective-permute-start.1 = (s32[4,1,2,64]{3,2,1,0:T(2,128)S(1)}, s32[4,1,2,64]{3,2,1,0:T(2,128)S(1)}, u32[]{:S(2)}, u32[]{:S(2)}) collective-permute-start(s32[4,1,2,64]{3,2,1,0:T(2,128)S(1)} %fusion.15), channel_id=1, source_target_pairs={{0,4},{2,6},{4,0},{6,2},{8,12},{10,14},{12,8},{14,10},{16,20},{18,... | collective-permute-start | bytes 6152 | tf_op jit(solution)/shard_map/ppermute | solution.py:12
  20.4 9.8 %collective-permute-start.2 = (s32[2,2,64]{2,1,0:T(2,128)S(1)}, s32[2,2,64]{2,1,0:T(2,128)S(1)}, u32[]{:S(2)}, u32[]{:S(2)}) collective-permute-start(s32[2,2,64]{2,1,0:T(2,128)S(1)} %get-tuple-element.11), channel_id=1, source_target_pairs={{0,8},{2,10},{4,12},{6,14},{8,0},{10,2},{12,4},{14,6},{16,24},{18,... | collective-permute-start | bytes 3080 | tf_op jit(solution)/shard_map/ppermute | solution.py:30
  20.5 18.1 %collective-permute-start.3 = (s32[2,2,64]{2,1,0:T(2,128)S(1)}, s32[2,2,64]{2,1,0:T(2,128)S(1)}, u32[]{:S(2)}, u32[]{:S(2)}) collective-permute-start(s32[2,2,64]{2,1,0:T(2,128)S(1)} %get-tuple-element.12), channel_id=1, source_target_pairs={{0,16},{2,18},{4,20},{6,22},{8,24},{10,26},{12,28},{14,30},{16,0},... | collective-permute-start | bytes 3080 | tf_op jit(solution)/shard_map/ppermute | solution.py:30
  25.1 13.6 %collective-permute-start.4 = (s32[2,2,64]{2,1,0:T(2,128)S(1)}, s32[2,2,64]{2,1,0:T(2,128)S(1)}, u32[]{:S(2)}, u32[]{:S(2)}) collective-permute-start(s32[2,2,64]{2,1,0:T(2,128)S(1)} %get-tuple-element.13), channel_id=1, source_target_pairs={{0,24},{2,26},{4,28},{6,30},{8,16},{10,18},{12,20},{14,22},{16,8},... | collective-permute-start | bytes 3080 | tf_op jit(solution)/shard_map/ppermute | solution.py:30
  38.8 1.9 %copy-start.10 = (s32[256]{0:T(256)S(1)}, s32[256]{0:T(256)}, u32[]{:S(2)}) copy-start(s32[256]{0:T(256)} %param.18) | copy-start | bytes 3076
  39.1 5.0 %collective-permute-start.5 = (f32[128,256]{1,0:T(8,128)S(1)}, f32[128,256]{1,0:T(8,128)S(1)}, u32[]{:S(2)}, u32[]{:S(2)}) collective-permute-start(f32[128,256]{1,0:T(8,128)S(1)} %fusion.4), channel_id=1, source_target_pairs={{0,1},{1,0},{2,3},{3,2},{4,5},{5,4},{6,7},{7,6},{8,9},{9,8},{10,11... | collective-permute-start | bytes 393224 | tf_op jit(solution)/shard_map/ppermute | solution.py:75
  40.7 3.8 %copy-start.4 = (f32[256,256]{1,0:T(8,128)S(1)}, f32[256,256]{1,0:T(8,128)}, u32[]{:S(2)}) copy-start(f32[256,256]{1,0:T(8,128)} %param.23) | copy-start | bytes 786436
  44.7 1.0 %copy-start.2 = (f32[128,256]{1,0:T(8,128)}, f32[128,256]{1,0:T(8,128)S(1)}, u32[]{:S(2)}) copy-start(f32[128,256]{1,0:T(8,128)S(1)} %fusion.3) | copy-start | bytes 393220
  45.7 4.0 %copy-start.1 = (f32[256,256]{1,0:T(8,128)S(1)}, f32[256,256]{1,0:T(8,128)}, u32[]{:S(2)}) copy-start(f32[256,256]{1,0:T(8,128)} %param.17) | copy-start | bytes 786436
  45.7 4.0 %copy-start.5 = (f32[256,256]{1,0:T(8,128)S(1)}, f32[256,256]{1,0:T(8,128)}, u32[]{:S(2)}) copy-start(f32[256,256]{1,0:T(8,128)} %param.24) | copy-start | bytes 786436
  45.7 14.0 %all-to-all-start.1 = ((f32[16,16,256]{2,1,0:T(8,128)}), f32[16,16,256]{2,1,0:T(8,128)S(1)}, u32[]{:S(2)}, u32[]{:S(2)}) async-start(f32[16,16,256]{2,1,0:T(8,128)} %bitcast.8), calls=%async_computation.1 | async-start | bytes 524288 | tf_op jit(solution)/shard_map/all_to_all | solution.py:87
  50.0 9.8 %copy-start.9 = (s32[256]{0:T(256)S(1)}, s32[256]{0:T(256)}, u32[]{:S(2)}) copy-start(s32[256]{0:T(256)} %param.20) | copy-start | bytes 3076
  59.8 1.0 %copy-start.6 = (f32[256,256]{1,0:T(8,128)S(1)}, f32[256,256]{1,0:T(8,128)}, u32[]{:S(2)}) copy-start(f32[256,256]{1,0:T(8,128)} %param.25) | copy-start | bytes 786436

commit v2 on v1

v2 whole, which is shorter than its diff:
```python
import jax
import jax.numpy as jnp
from jax import lax
from jax.experimental import pallas as pl
from jax.experimental.pallas import tpu as pltpu
from jax.sharding import PartitionSpec as P

high = lax.Precision.HIGH
f32, bf16 = jnp.float32, jnp.bfloat16


def split(x):
    top = x.astype(bf16)
    return top, (x - top.astype(f32)).astype(bf16)


def split_outside(x):
    top = lax.reduce_precision(x, 8, 7)
    return top.astype(bf16), (x - top).astype(bf16)


def mm(a, b):
    return jnp.dot(a, b, preferred_element_type=f32)


def dot3(x, w_top, w_low):
    top, low = split(x)
    return mm(top, w_top) + (mm(low, w_top) + mm(top, w_low))


def dot2(picks, x):
    top, low = split(x)
    return mm(picks, top) + mm(picks, low)


def call(kernel, out, ins):
    vmem = pl.BlockSpec(memory_space=pltpu.VMEM)
    return pl.pallas_call(
        kernel,
        out_shape=[jax.ShapeDtypeStruct(s, f32) for s in out],
        in_specs=[vmem] * len(ins),
        out_specs=[vmem] * len(out),
        compiler_params=pltpu.CompilerParams(vmem_limit_bytes=32 * 1024 * 1024),
    )(*ins)


def message_kernel(x, w, out):
    out[...] = jnp.maximum(dot3(x[...], *split(w[...])), 0.0).reshape(out.shape)


def messages(transactions, w_msg, peers):
    rows, width = transactions.shape
    slots, steps = rows // peers, 4
    return pl.pallas_call(
        message_kernel,
        grid=(steps,),
        out_shape=jax.ShapeDtypeStruct((peers, slots, width), f32),
        in_specs=[
            pl.BlockSpec((rows // steps, width), lambda i: (i, 0)),
            pl.BlockSpec((width, width), lambda i: (0, 0)),
        ],
        out_specs=pl.BlockSpec((peers // steps, slots, width), lambda i: (i, 0, 0)),
        compiler_params=pltpu.CompilerParams(vmem_limit_bytes=32 * 1024 * 1024),
    )(transactions, w_msg)


def sum_kernel(picks, x, out):
    out[...] = dot2(picks[...], x[...])


def update_kernel(kept, got, own, table, w_top, w_low, picks, new, listed):
    fresh = table[...] + jnp.maximum(own[...] + dot3(kept[...] + got[...], w_top[...], w_low[...]), 0.0)
    new[...] = fresh
    listed[...] = dot2(picks[...], fresh).reshape(listed.shape)


def final_kernel(incoming, incidence, own, table, w_top, w_low, new):
    bought = dot2(incidence[...], incoming[...])
    new[...] = table[...] + jnp.maximum(own[...] + dot3(bought, w_top[...], w_low[...]), 0.0)


def swap(x, axis, mask, size):
    return lax.ppermute(x, axis, [(i, i ^ mask) for i in range(size)])


def spread(x):
    return lax.all_to_all(x, "hash", split_axis=0, concat_axis=0, tiled=True)


def pick(x, i, axis=0):
    return lax.dynamic_index_in_dim(x, i, axis, keepdims=True)


def swap_bit(blocks, axis, bit, mask, peers):
    keep = pick(blocks, bit, axis)
    got = swap(pick(blocks, 1 - bit, axis), "hash", mask, peers)
    return jnp.concatenate([jnp.where(bit == 0, keep, got), jnp.where(bit == 0, got, keep)], axis)


def spread_both(outgoing, ids):
    peers, slots = ids.shape
    if peers != 16:
        return spread(outgoing), spread(ids)
    me = lax.axis_index("hash")
    far = me >> 2
    blocks = ids.reshape(4, 2, 2, slots)
    got = [pick(blocks, far)] + [swap(pick(blocks, far ^ k), "hash", 4 * k, peers) for k in (1, 2, 3)]
    outgoing, *got = lax.optimization_barrier((outgoing, *got))
    arrived = spread(outgoing)
    stacked = jnp.concatenate(got, 0)
    blocks = jnp.concatenate([pick(stacked, far ^ k) for k in range(4)], 0)
    blocks = swap_bit(blocks, 2, me & 1, 1, peers)
    blocks = swap_bit(blocks, 1, (me >> 1) & 1, 2, peers)
    return arrived, blocks.reshape(peers, slots)


def local(
    transactions,
    tx_product,
    tx_count,
    products,
    customers,
    send_rows,
    send_count,
    recv_customer,
    w_msg,
    w_prod_self,
    w_prod_agg,
    w_cust_self,
    w_cust_prod,
):
    peers, pair = lax.axis_size("hash"), lax.axis_size("tm")
    half = lax.axis_index("tm")
    width = transactions.shape[1]
    slots = transactions.shape[0] // peers
    mine = products.shape[0]
    send_slots = send_rows.shape[0] // peers

    slot_index = lax.broadcasted_iota(jnp.int32, (peers, slots), 1)
    ids = jnp.where(slot_index < tx_count[:, None], tx_product.reshape(peers, slots), -1)
    arrived, ids = spread_both(messages(transactions, w_msg, peers), ids)
    arrived, ids = arrived.reshape(-1, width), ids.reshape(-1)

    def part_sum(part):
        picks = (ids[None, :] == (part * mine + lax.iota(jnp.int32, mine))[:, None]).astype(bf16)
        return call(sum_kernel, [(mine, width)], (picks, arrived))[0]

    if pair == 2:
        got = swap(part_sum(1 - half), "tm", 1, 2)
        kept = part_sum(half)
    else:
        parts = jnp.concatenate([part_sum(i) for i in range(pair)])
        kept = lax.psum_scatter(parts, "tm", scatter_dimension=0, tiled=True)
        got = jnp.zeros_like(kept)

    product_self = jnp.dot(products, w_prod_self, precision=high)
    customer_self = jnp.dot(customers, w_cust_self, precision=high)
    send_index = lax.broadcasted_iota(jnp.int32, (peers, send_slots), 1)
    named = jnp.where(send_index < send_count[:, None], send_rows.reshape(peers, send_slots), -1).reshape(-1)
    picks = (named[:, None] == lax.iota(jnp.int32, mine)[None, :]).astype(bf16)
    incidence = (recv_customer[None, :] == lax.iota(jnp.int32, customers.shape[0])[:, None]).astype(bf16)

    new_products, listed = call(
        update_kernel,
        [products.shape, (peers, send_slots, width)],
        (kept, got, product_self, products, *split_outside(w_prod_agg), picks),
    )
    incoming = spread(listed).reshape(-1, width)
    (new_customers,) = call(
        final_kernel,
        [customers.shape],
        (incoming, incidence, customer_self, customers, *split_outside(w_cust_prod)),
    )
    return new_products, new_customers


def solution(mesh):
    rows, flat = P(("hash", "tm"), None), P(("hash", "tm"))
    placed = (rows, flat, flat, rows, rows, flat, flat, flat, P(), P(), P(), P(), P())
    return jax.shard_map(local, mesh=mesh, in_specs=placed, out_specs=(rows, rows), check_vma=False)
```

time: 62.1 us -> 68.9 us (1.11)
  Pallas kernels: 0 us -> 5.33 us
  matrix products: 6.16 us -> 1.52 us
  starting transfers between devices: 20.1 us -> 22.5 us
  waiting for transfers between devices: 30.7 us -> 32.8 us
  other arithmetic: 0.23 us -> 1.51 us
    all_to_all x2, waiting for transfers between devices: 9.74 us -> 23 us  [spread(): return lax.all_to_all(x, 'hash', split_axis=0, concat_axis=0, tiled=True)]
    ppermute x6, waiting for transfers between devices: 21 us -> 9.72 us  [swap(): return lax.ppermute(x, axis, [(i, i ^ mask) for i in range(size)])]
    dot_general x7 -> x0, matrix products: 5.66 us -> none  [the longest x1 2.55 us: local(): outgoing = jax.nn.relu(jnp.dot(transactions, w_msg, precision=high))]
    pallas_call x0 -> x5, Pallas kernels: none -> 5.33 us  [the longest x4 3.09 us: call(): pl.pallas_call(kernel, out_shape=[jax.ShapeDtypeStruct(s, f32) for s in o...]
    all_to_all x2, starting transfers between devices: 11.5 us -> 12.8 us  [spread(): return lax.all_to_all(x, 'hash', split_axis=0, concat_axis=0, tiled=True)]
    convert_element_type x0 -> x5, other arithmetic: none -> 1.3 us  [the longest x2 1.02 us: split_outside(): return (top.astype(bf16), (x - top).astype(bf16))]
    unnamed x26 -> x21, local copies, waits for them, and re-layouts: 3.23 us -> 2.08 us
    dot_general x1, matrix products: 0.23 us -> 1.26 us  [local(): product_self = jnp.dot(products, w_prod_self, precision=high)]
  transfers between devices with their start and end apart: 8 -> 8, of which waited for: 6 -> 5; matrix products, arithmetic and copies ran while one was open for 2% -> 5% of each run, Pallas kernels for 0% -> 4%
where the time goes in v2:
time: 68.9 us; the launch traced here: 68.4 us
  waiting for transfers between devices  32.8 us (48%)
  starting transfers between devices  22.5 us (33%)
  Pallas kernels  5.33 us (8%)
  local copies, waits for them, and re-layouts  3.89 us (6%)
  matrix products  1.52 us (2%)
  other arithmetic  1.51 us (2%)
  between operations  0.9 us (1%)
    all_to_all x2, waiting for transfers between devices, spread(): return lax.all_to_all(x, 'hash', split_axis=0, concat_axis=0, tiled=True)  23 us
    all_to_all x2, starting transfers between devices, spread(): return lax.all_to_all(x, 'hash', split_axis=0, concat_axis=0, tiled=True)  12.8 us
    ppermute x6, waiting for transfers between devices, swap(): return lax.ppermute(x, axis, [(i, i ^ mask) for i in range(size)])  9.72 us
    ppermute x6, starting transfers between devices, swap(): return lax.ppermute(x, axis, [(i, i ^ mask) for i in range(size)])  9.65 us
    pallas_call x4, Pallas kernels, call(): pl.pallas_call(kernel, out_shape=[jax.ShapeDtypeStruct(s, f32) for s in o...  3.09 us
    pallas_call x1, Pallas kernels, messages(): pl.pallas_call(message_kernel, grid=(steps,), out_shape=jax.ShapeDtypeStr...  2.25 us
    unnamed x21, local copies, waits for them, and re-layouts  2.08 us
  transfers between devices with their start and end apart: 8, of which 5 were waited for; matrix products, arithmetic and copies ran while one was open for 5% of the time, Pallas kernels for 4%

profile of v2, /device:TPU:0, one launch (start us, length us, event | category | flops | bytes accessed | tf_op | source)
XLA Modules:
  0.0 68.4 jit_solution(11272674304728518945)
XLA Ops:
  0.6 0.0 copy-start
  0.6 0.0 copy-start.1
  0.7 0.9 %reshape.47 = s32[4,2,2,64]{3,2,1,0:T(2,128)S(1)} reshape(s32[1024]{0:T(1024)} %param.14) | data formatting | bytes 8192 | tf_op jit(solution)/shard_map/reshape | solution.py:140
  1.5 0.7 %lt.55 = s32[4,2,2]{2,1,0:T(2,128)S(1)} reshape(s32[16]{0:T(128)} %param.15) | data formatting | bytes 128 | tf_op jit(solution)/shard_map/lt | solution.py:140
  2.3 0.1 compare_select_fusion
  2.4 3.1 %collective-permute-start = (s32[1,2,2,64]{3,2,1,0:T(2,128)S(1)}, s32[1,2,2,64]{3,2,1,0:T(2,128)S(1)}, u32[]{:S(2)}, u32[]{:S(2)}) collective-permute-start(s32[1,2,2,64]{3,2,1,0:T(2,128)S(1)} %get-tuple-element.30), channel_id=1, source_target_pairs={{0,8},{2,10},{4,12},{6,14},{8,0},{10,2},{12,4},{14,6},{16,24},{18,... | collective-permute-start | bytes 3080 | tf_op jit(solution)/shard_map/ppermute | solution.py:83
  5.5 2.6 %collective-permute-start.1 = (s32[1,2,2,64]{3,2,1,0:T(2,128)S(1)}, s32[1,2,2,64]{3,2,1,0:T(2,128)S(1)}, u32[]{:S(2)}, u32[]{:S(2)}) collective-permute-start(s32[1,2,2,64]{3,2,1,0:T(2,128)S(1)} %get-tuple-element.29), channel_id=1, source_target_pairs={{0,16},{2,18},{4,20},{6,22},{8,24},{10,26},{12,28},{14,30},{16,0},... | collective-permute-start | bytes 3080 | tf_op jit(solution)/shard_map/ppermute | solution.py:83
  8.0 0.0 collective-permute-start.2
  8.0 1.0 %fusion = (bf16[256,256]{1,0:T(8,128)(2,1)S(1)}, bf16[256,256]{1,0:T(8,128)(2,1)S(1)}) fusion(f32[256,256]{1,0:T(8,128)} %param.23), kind=kLoop, calls=%fused_computation.6 | loop fusion | flops 262144 | bytes 524288 | tf_op jit(solution)/shard_map/convert_element_type | solution.py:19
  9.0 0.0 copy-start.8
  9.0 1.3 %fusion.6.own = f32[128,256]{1,0:T(8,128)S(1)} fusion(f32[128,256]{1,0:T(8,128)} %table.2, f32[256,256]{1,0:T(8,128)} %param.22), kind=kOutput, calls=%fused_computation.43 | convolution fusion | flops 50331648 | bytes 524288 | tf_op jit(solution)/shard_map/dot_general | solution.py:156
  10.3 0.0 copy-done.8
  10.3 0.1 iota_compare_fusion.2
  10.4 0.1 lt.68
  10.5 0.0 copy-done.1
  10.5 0.0 copy-start.4
  10.5 0.9 %copy-done.4 = f32[256,256]{1,0:T(8,128)S(1)} copy-done((f32[256,256]{1,0:T(8,128)S(1)}, f32[256,256]{1,0:T(8,128)}, u32[]{:S(2)}) %copy-start.4) | copy-done | bytes 262168
  11.4 2.2 %shard_map.140 = f32[16,64,256]{2,1,0:T(8,128)} custom-call(f32[1024,256]{1,0:T(8,128)S(1)} %copy-done.1, f32[256,256]{1,0:T(8,128)S(1)} %copy-done.4), custom_call_target="tpu_custom_call" | custom-call | tf_op jit(solution)/shard_map/pallas_call | solution.py:54
  13.7 0.0 collective-permute-done
  13.7 0.0 collective-permute-done.1
  13.7 0.0 collective-permute-done.2
  13.7 6.1 %all-to-all-start = ((f32[16,64,256]{2,1,0:T(8,128)}), f32[16,64,256]{2,1,0:T(8,128)S(1)}, u32[]{:S(2)}, u32[]{:S(2)}) async-start(f32[16,64,256]{2,1,0:T(8,128)} %shard_map.140), calls=%async_computation | async-start | bytes 2097152 | tf_op jit(solution)/shard_map/all_to_all | solution.py:87
  19.9 0.0 copy-start.7
  20.0 0.5 collective-permute-start.3
  20.4 0.2 copy-done.7
  20.6 0.6 collective-permute-done.3
  21.3 1.9 %collective-permute-start.4 = (s32[4,1,2,64]{3,2,1,0:T(2,128)S(1)}, s32[4,1,2,64]{3,2,1,0:T(2,128)S(1)}, u32[]{:S(2)}, u32[]{:S(2)}) collective-permute-start(s32[4,1,2,64]{3,2,1,0:T(2,128)S(1)} %fusion.4), channel_id=1, source_target_pairs={{0,4},{2,6},{4,0},{6,2},{8,12},{10,14},{12,8},{14,10},{16,20},{18,... | collective-permute-start | bytes 6152 | tf_op jit(solution)/shard_map/ppermute | solution.py:83
  23.2 5.0 %collective-permute-done.4 = s32[4,1,2,64]{3,2,1,0:T(2,128)S(1)} collective-permute-done((s32[4,1,2,64]{3,2,1,0:T(2,128)S(1)}, s32[4,1,2,64]{3,2,1,0:T(2,128)S(1)}, u32[]{:S(2)}, u32[]{:S(2)}) %collective-permute-start.4) | collective-permute-done | bytes 2080 | tf_op jit(solution)/shard_map/ppermute | solution.py:83
  28.3 0.1 eq.30
  28.4 0.2 compare_convert_fusion
  28.5 14.3 %all-to-all-done = f32[16,64,256]{2,1,0:T(8,128)S(1)} async-done(((f32[16,64,256]{2,1,0:T(8,128)}), f32[16,64,256]{2,1,0:T(8,128)S(1)}, u32[]{:S(2)}, u32[]{:S(2)}) %all-to-all-start) | async-done | bytes 1048608 | tf_op jit(solution)/shard_map/all_to_all | solution.py:87
  42.8 0.3 shard_map.142
  43.1 1.6 %collective-permute-start.5 = (f32[128,256]{1,0:T(8,128)S(1)}, f32[128,256]{1,0:T(8,128)S(1)}, u32[]{:S(2)}, u32[]{:S(2)}) collective-permute-start(f32[128,256]{1,0:T(8,128)S(1)} %shard_map.142), channel_id=1, source_target_pairs={{0,1},{1,0},{2,3},{3,2},{4,5},{5,4},{6,7},{7,6},{8,9},{9,8},{10,11... | collective-permute-start | bytes 393224 | tf_op jit(solution)/shard_map/ppermute | solution.py:83
  44.7 0.1 fusion.3.picks
  44.8 0.0 copy-start.3
  44.8 0.3 shard_map.141.kept
  45.1 4.1 %collective-permute-done.5.got = f32[128,256]{1,0:T(8,128)S(1)} collective-permute-done((f32[128,256]{1,0:T(8,128)S(1)}, f32[128,256]{1,0:T(8,128)S(1)}, u32[]{:S(2)}, u32[]{:S(2)}) %collective-permute-start.5) | collective-permute-done | bytes 131104 | tf_op jit(solution)/shard_map/ppermute | solution.py:83
  49.2 0.0 copy-done.3
  49.2 1.2 %shard_map.143 = (f32[128,256]{1,0:T(8,128)}, f32[16,16,256]{2,1,0:T(8,128)}) custom-call(f32[128,256]{1,0:T(8,128)S(1)} %shard_map.141.kept, f32[128,256]{1,0:T(8,128)S(1)} %collective-permute-done.5.got, f32[128,256]{1,0:T(8,128)S(1)} %fusion.6.own, f32[128,256]{1,0:T(8,128)S(1)} %copy-done.3, bf16[256,256]{1,0:T(8,128)(2,1)S(1)} %get-tuple-element.19.w_top, ...), custom_call_target="tpu_custom_call" | custom-call | tf_op jit(solution)/shard_map/pallas_call | solution.py:38
  50.4 6.7 %all-to-all-start.1 = ((f32[16,16,256]{2,1,0:T(8,128)}), f32[16,16,256]{2,1,0:T(8,128)S(1)}, u32[]{:S(2)}, u32[]{:S(2)}) async-start(f32[16,16,256]{2,1,0:T(8,128)} %get-tuple-element.15), calls=%async_computation.1 | async-start | bytes 524288 | tf_op jit(solution)/shard_map/all_to_all | solution.py:87
  57.1 0.0 copy-done.6
  57.2 0.0 copy-done.5
  57.2 0.0 copy-start.2
  57.2 0.0 copy-done
  57.2 0.9 %copy-done.2 = f32[256,256]{1,0:T(8,128)S(1)} copy-done((f32[256,256]{1,0:T(8,128)S(1)}, f32[256,256]{1,0:T(8,128)}, u32[]{:S(2)}) %copy-start.2) | copy-done | bytes 262168
  58.1 0.3 fusion.7.own
  58.4 8.8 %all-to-all-done.1 = f32[16,16,256]{2,1,0:T(8,128)S(1)} async-done(((f32[16,16,256]{2,1,0:T(8,128)}), f32[16,16,256]{2,1,0:T(8,128)S(1)}, u32[]{:S(2)}, u32[]{:S(2)}) %all-to-all-start.1) | async-done | bytes 262176 | tf_op jit(solution)/shard_map/all_to_all | solution.py:87
  67.2 1.2 %shard_map.144 = f32[256,256]{1,0:T(8,128)} custom-call(f32[256,256]{1,0:T(8,128)S(1)} %bitcast.8, bf16[256,256]{1,0:T(8,128)(2,1)S(1)} %fusion.2.incidence, f32[256,256]{1,0:T(8,128)S(1)} %fusion.7.own, f32[256,256]{1,0:T(8,128)S(1)} %copy-done.2, bf16[256,256]{1,0:T(8,128)(2,1)S(1)} %get-tuple-element.17.w_top, bf16[256,256]{1,0:T(8,128)(2,1)S(1)} %get-tuple-element.16.w_low), custom_call_target="tpu_custom_call" | custom-call | tf_op jit(solution)/shard_map/pallas_call | solution.py:38
  (18 shorter events, 0.2 us)
Async XLA Ops:
  0.6 56.6 %copy-start = (f32[256,256]{1,0:T(8,128)S(1)}, f32[256,256]{1,0:T(8,128)}, u32[]{:S(2)}) copy-start(f32[256,256]{1,0:T(8,128)} %param.24) | copy-start | bytes 786436
  0.6 9.8 %copy-start.1 = (f32[1024,256]{1,0:T(8,128)S(1)}, f32[1024,256]{1,0:T(8,128)}, u32[]{:S(2)}) copy-start(f32[1024,256]{1,0:T(8,128)} %x.1) | copy-start | bytes 3145732
  2.4 11.3 %collective-permute-start = (s32[1,2,2,64]{3,2,1,0:T(2,128)S(1)}, s32[1,2,2,64]{3,2,1,0:T(2,128)S(1)}, u32[]{:S(2)}, u32[]{:S(2)}) collective-permute-start(s32[1,2,2,64]{3,2,1,0:T(2,128)S(1)} %get-tuple-element.30), channel_id=1, source_target_pairs={{0,8},{2,10},{4,12},{6,14},{8,0},{10,2},{12,4},{14,6},{16,24},{18,... | collective-permute-start | bytes 3080 | tf_op jit(solution)/shard_map/ppermute | solution.py:83
  5.5 8.2 %collective-permute-start.1 = (s32[1,2,2,64]{3,2,1,0:T(2,128)S(1)}, s32[1,2,2,64]{3,2,1,0:T(2,128)S(1)}, u32[]{:S(2)}, u32[]{:S(2)}) collective-permute-start(s32[1,2,2,64]{3,2,1,0:T(2,128)S(1)} %get-tuple-element.29), channel_id=1, source_target_pairs={{0,16},{2,18},{4,20},{6,22},{8,24},{10,26},{12,28},{14,30},{16,0},... | collective-permute-start | bytes 3080 | tf_op jit(solution)/shard_map/ppermute | solution.py:83
  8.0 5.7 %collective-permute-start.2 = (s32[1,2,2,64]{3,2,1,0:T(2,128)S(1)}, s32[1,2,2,64]{3,2,1,0:T(2,128)S(1)}, u32[]{:S(2)}, u32[]{:S(2)}) collective-permute-start(s32[1,2,2,64]{3,2,1,0:T(2,128)S(1)} %get-tuple-element.28), channel_id=1, source_target_pairs={{0,24},{2,26},{4,28},{6,30},{8,16},{10,18},{12,20},{14,22},{16,8},... | collective-permute-start | bytes 3080 | tf_op jit(solution)/shard_map/ppermute | solution.py:83
  9.0 1.3 %copy-start.8 = (s32[16]{0:T(128)S(1)}, s32[16]{0:T(128)}, u32[]{:S(2)}) copy-start(s32[16]{0:T(128)} %param.19) | copy-start | bytes 196
  10.5 1.0 %copy-start.4 = (f32[256,256]{1,0:T(8,128)S(1)}, f32[256,256]{1,0:T(8,128)}, u32[]{:S(2)}) copy-start(f32[256,256]{1,0:T(8,128)} %w.1) | copy-start | bytes 786436
  13.7 29.1 %all-to-all-start = ((f32[16,64,256]{2,1,0:T(8,128)}), f32[16,64,256]{2,1,0:T(8,128)S(1)}, u32[]{:S(2)}, u32[]{:S(2)}) async-start(f32[16,64,256]{2,1,0:T(8,128)} %shard_map.140), calls=%async_computation | async-start | bytes 2097152 | tf_op jit(solution)/shard_map/all_to_all | solution.py:87
  19.9 0.7 copy-start.7
  20.0 1.3 %collective-permute-start.3 = (s32[4,2,1,64]{3,2,1,0:T(1,128)S(1)}, s32[4,2,1,64]{3,2,1,0:T(1,128)S(1)}, u32[]{:S(2)}, u32[]{:S(2)}) collective-permute-start(s32[4,2,1,64]{3,2,1,0:T(1,128)S(1)} %constant_dynamic-slice_fusion), channel_id=1, source_target_pairs={{0,2},{2,0},{4,6},{6,4},{8,10},{10,8},{12,14},{14,12},{16,18},{18,... | collective-permute-start | bytes 6152 | tf_op jit(solution)/shard_map/ppermute | solution.py:83
  21.3 6.9 %collective-permute-start.4 = (s32[4,1,2,64]{3,2,1,0:T(2,128)S(1)}, s32[4,1,2,64]{3,2,1,0:T(2,128)S(1)}, u32[]{:S(2)}, u32[]{:S(2)}) collective-permute-start(s32[4,1,2,64]{3,2,1,0:T(2,128)S(1)} %fusion.4), channel_id=1, source_target_pairs={{0,4},{2,6},{4,0},{6,2},{8,12},{10,14},{12,8},{14,10},{16,20},{18,... | collective-permute-start | bytes 6152 | tf_op jit(solution)/shard_map/ppermute | solution.py:83
  43.1 6.1 %collective-permute-start.5 = (f32[128,256]{1,0:T(8,128)S(1)}, f32[128,256]{1,0:T(8,128)S(1)}, u32[]{:S(2)}, u32[]{:S(2)}) collective-permute-start(f32[128,256]{1,0:T(8,128)S(1)} %shard_map.142), channel_id=1, source_target_pairs={{0,1},{1,0},{2,3},{3,2},{4,5},{5,4},{6,7},{7,6},{8,9},{9,8},{10,11... | collective-permute-start | bytes 393224 | tf_op jit(solution)/shard_map/ppermute | solution.py:83
  44.8 4.4 %copy-start.3 = (f32[128,256]{1,0:T(8,128)S(1)}, f32[128,256]{1,0:T(8,128)}, u32[]{:S(2)}) copy-start(f32[128,256]{1,0:T(8,128)} %table.2) | copy-start | bytes 393220
  50.4 6.7 %copy-start.6 = (s32[256]{0:T(256)S(1)}, s32[256]{0:T(256)}, u32[]{:S(2)}) copy-start(s32[256]{0:T(256)} %param.20) | copy-start | bytes 3076
  50.4 6.8 %copy-start.5 = (f32[256,256]{1,0:T(8,128)S(1)}, f32[256,256]{1,0:T(8,128)}, u32[]{:S(2)}) copy-start(f32[256,256]{1,0:T(8,128)} %param.25) | copy-start | bytes 786436
  50.4 16.7 %all-to-all-start.1 = ((f32[16,16,256]{2,1,0:T(8,128)}), f32[16,16,256]{2,1,0:T(8,128)S(1)}, u32[]{:S(2)}, u32[]{:S(2)}) async-start(f32[16,16,256]{2,1,0:T(8,128)} %get-tuple-element.15), calls=%async_computation.1 | async-start | bytes 524288 | tf_op jit(solution)/shard_map/all_to_all | solution.py:87
  57.2 1.0 %copy-start.2 = (f32[256,256]{1,0:T(8,128)S(1)}, f32[256,256]{1,0:T(8,128)}, u32[]{:S(2)}) copy-start(f32[256,256]{1,0:T(8,128)} %table.3) | copy-start | bytes 786436

commit v3 on v2

v3 whole, which is shorter than its diff:
```python
import jax
import jax.numpy as jnp
from jax import lax
from jax.experimental import pallas as pl
from jax.experimental.pallas import tpu as pltpu
from jax.sharding import PartitionSpec as P

high = lax.Precision.HIGH
f32, bf16 = jnp.float32, jnp.bfloat16
LANES = 128
PAD = 8


def split(x):
    top = x.astype(bf16)
    return top, (x - top.astype(f32)).astype(bf16)


def split_outside(x):
    top = lax.reduce_precision(x, 8, 7)
    return top.astype(bf16), (x - top).astype(bf16)


def mm(a, b):
    return jnp.dot(a, b, preferred_element_type=f32)


def dot3(x, w_top, w_low):
    top, low = split(x)
    return mm(top, w_top) + (mm(low, w_top) + mm(top, w_low))


def dot2(picks, x):
    top, low = split(x)
    return mm(picks, top) + mm(picks, low)


def call(kernel, out, ins, smem=()):
    vmem = pl.BlockSpec(memory_space=pltpu.VMEM)
    scalar = pl.BlockSpec(memory_space=pltpu.SMEM)
    return pl.pallas_call(
        kernel,
        out_shape=[jax.ShapeDtypeStruct(s, f32) for s in out],
        in_specs=[scalar] * len(smem) + [vmem] * len(ins),
        out_specs=[vmem] * len(out),
        compiler_params=pltpu.CompilerParams(vmem_limit_bytes=32 * 1024 * 1024),
    )(*smem, *ins)


def lanes():
    return lax.broadcasted_iota(jnp.int32, (1, LANES), 1)


def message_kernel(place, count, tx, ids, w, p0, p1, p2, p3, q0, q1, q2, q3):
    near = place[0] & 3
    w_top, w_low = split(w[...])
    slots = q0.shape[1]
    lane = lanes()
    for m, (first, second) in enumerate(((p0, q0), (p1, q1), (p2, q2), (p3, q3))):
        c = near ^ m
        x = jnp.concatenate([tx[pl.ds(pl.multiple_of((4 * z + c) * slots, slots), slots), :] for z in range(4)], 0)
        y = jnp.maximum(dot3(x, w_top, w_low), 0.0)
        first[:, :slots, :] = y[:, :LANES].reshape(4, slots, LANES)
        second[...] = y[:, LANES:].reshape(4, slots, LANES)
        for z in range(4):
            row = ids[pl.ds(2 * z + (c >> 1), 1), :]
            turned = pltpu.roll(row, slots, 1)
            twice = jnp.where((lane >= slots).astype(jnp.int32) == (c & 1), row, turned)
            twice = jnp.where((lane & (slots - 1)) < count[4 * z + c], twice, -1).astype(f32)
            first[z, slots:, :] = jnp.broadcast_to(twice, (PAD, LANES))


def sums(place, rows, blocks, send, keep):
    mine = send.shape[1]
    slots = LANES // 2
    own = place[1]
    row = lax.broadcasted_iota(jnp.int32, (2 * mine, LANES), 0)
    target = jnp.where(row < mine, row + (1 - own) * mine, row - mine + own * mine).astype(f32)
    for z in range(4):
        picks = jnp.concatenate([(r == target).astype(bf16) for r in rows[z]], 1)
        top, low = split(jnp.concatenate([block[z, :slots, :] for block in blocks], 0))
        total = mm(picks, jnp.concatenate([top, low], 1))
        total = total[:, :LANES] + total[:, LANES:]
        send[z] = total[:mine]
        keep[z] = total[mine:]


def first_sum_kernel(place, r0, r1, r2, r3, send, keep, ids):
    slots = r0.shape[1] - PAD
    lane = lanes()
    rows = []
    for z in range(4):
        one = [block[z, pl.ds(slots, 1), :] for block in (r0, r1, r2, r3)]
        rows.append([jnp.where(lane < slots, one[i], one[i + 1]) for i in (0, 2)])
        for i in range(2):
            ids[pl.ds(2 * z + i, 1), :] = rows[z][i]
    sums(place, rows, (r0, r1, r2, r3), send, keep)


def second_sum_kernel(place, ids, r0, r1, r2, r3, send, keep):
    rows = [[ids[pl.ds(2 * z + i, 1), :] for i in range(2)] for z in range(4)]
    sums(place, rows, (r0, r1, r2, r3), send, keep)


def pair_kernel(place, keep, got, b0, b1, b2, b3):
    far = place[0] >> 2
    for k, out in enumerate((b0, b1, b2, b3)):
        out[...] = keep[far ^ k] + got[far ^ k]


def update_kernel(*refs):
    parts, (own, table, w_top, w_low, picks, new, listed) = refs[:-7], refs[-7:]
    n = len(parts) // 2
    halves = [sum(part[...] for part in side) for side in (parts[:n], parts[n:])]
    gathered = jnp.concatenate(halves, 1)
    fresh = table[...] + jnp.maximum(own[...] + dot3(gathered, w_top[...], w_low[...]), 0.0)
    new[...] = fresh
    listed[...] = dot2(picks[...], fresh).reshape(listed.shape)


def final_kernel(incoming, incidence, own, table, w_top, w_low, new):
    bought = dot2(incidence[...], incoming[...])
    new[...] = table[...] + jnp.maximum(own[...] + dot3(bought, w_top[...], w_low[...]), 0.0)


def swap(x, axis, mask, size):
    return lax.ppermute(x, axis, [(i, i ^ mask) for i in range(size)])


def spread(x):
    return lax.all_to_all(x, "hash", split_axis=0, concat_axis=0, tiled=True)


def gathered_by_permutes(place, transactions, tx_product, tx_count, w_msg, mine):
    peers = 16
    slots = transactions.shape[0] // peers
    block = (4, mine, LANES)
    out = call(
        message_kernel,
        [(4, slots + PAD, LANES)] * 4 + [(4, slots, LANES)] * 4,
        (transactions, tx_product.reshape(-1, LANES), w_msg),
        smem=(place, tx_count),
    )

    def near(blocks):
        return [blocks[0]] + [swap(blocks[m], "hash", m, peers) for m in (1, 2, 3)]

    def rest(send, keep):
        parts = call(pair_kernel, [(mine, LANES)] * 4, (keep, swap(send, "tm", 1, 2)), smem=(place,))
        return [parts[0]] + [swap(parts[k], "hash", 4 * k, peers) for k in (1, 2, 3)]

    *first, ids = call(first_sum_kernel, [block, block, (8, LANES)], near(out[:4]), smem=(place,))
    second = call(second_sum_kernel, [block, block], (ids, *near(out[4:])), smem=(place,))
    return rest(*first) + rest(*second)


def gathered_plainly(transactions, tx_product, tx_count, w_msg, mine):
    peers, pair = lax.axis_size("hash"), lax.axis_size("tm")
    width = transactions.shape[1]
    slots = transactions.shape[0] // peers
    slot_index = lax.broadcasted_iota(jnp.int32, (peers, slots), 1)
    ids = jnp.where(slot_index < tx_count[:, None], tx_product.reshape(peers, slots), -1)
    outgoing = jax.nn.relu(jnp.dot(transactions, w_msg, precision=high))
    arrived = spread(outgoing.reshape(peers, slots, width)).reshape(-1, width)
    flat = spread(ids).reshape(-1)

    def part_sum(part):
        onehot = (flat[None, :] == (part * mine + lax.iota(jnp.int32, mine))[:, None]).astype(f32)
        return jnp.dot(onehot, arrived, precision=high)

    parts = lax.map(part_sum, jnp.arange(pair)).reshape(pair * mine, width)
    total = lax.psum_scatter(parts, "tm", scatter_dimension=0, tiled=True)
    return [total[:, :LANES], total[:, LANES:]]


def local(
    transactions,
    tx_product,
    tx_count,
    products,
    customers,
    send_rows,
    send_count,
    recv_customer,
    w_msg,
    w_prod_self,
    w_prod_agg,
    w_cust_self,
    w_cust_prod,
):
    peers, pair = lax.axis_size("hash"), lax.axis_size("tm")
    width = transactions.shape[1]
    mine = products.shape[0]
    send_slots = send_rows.shape[0] // peers
    place = jnp.stack([lax.axis_index("hash"), lax.axis_index("tm")]).astype(jnp.int32)

    if peers == 16 and pair == 2:
        parts = gathered_by_permutes(place, transactions, tx_product, tx_count, w_msg, mine)
    else:
        parts = gathered_plainly(transactions, tx_product, tx_count, w_msg, mine)

    product_self = jnp.dot(products, w_prod_self, precision=high)
    customer_self = jnp.dot(customers, w_cust_self, precision=high)
    send_index = lax.broadcasted_iota(jnp.int32, (peers, send_slots), 1)
    named = jnp.where(send_index < send_count[:, None], send_rows.reshape(peers, send_slots), -1).reshape(-1)
    picks = (named[:, None] == lax.iota(jnp.int32, mine)[None, :]).astype(bf16)
    incidence = (recv_customer[None, :] == lax.iota(jnp.int32, customers.shape[0])[:, None]).astype(bf16)

    new_products, listed = call(
        update_kernel,
        [products.shape, (peers, send_slots, width)],
        (*parts, product_self, products, *split_outside(w_prod_agg), picks),
    )
    incoming = spread(listed).reshape(-1, width)
    (new_customers,) = call(
        final_kernel,
        [customers.shape],
        (incoming, incidence, customer_self, customers, *split_outside(w_cust_prod)),
    )
    return new_products, new_customers


def solution(mesh):
    rows, flat = P(("hash", "tm"), None), P(("hash", "tm"))
    placed = (rows, flat, flat, rows, rows, flat, flat, flat, P(), P(), P(), P(), P())
    return jax.shard_map(local, mesh=mesh, in_specs=placed, out_specs=(rows, rows), check_vma=False)
```

time: 68.9 us -> 63.9 us (0.927)
  waiting for transfers between devices: 32.8 us -> 30.8 us
  starting transfers between devices: 22.5 us -> 20.6 us
  other arithmetic: 1.51 us -> 0.35 us
  Pallas kernels: 5.33 us -> 6.45 us
  matrix products: 1.52 us -> 0.5 us
    all_to_all x2 -> x1, waiting for transfers between devices: 23 us -> 8.76 us  [spread(): return lax.all_to_all(x, 'hash', split_axis=0, concat_axis=0, tiled=True)]
    ppermute x6 -> x14, waiting for transfers between devices: 9.72 us -> 22.1 us  [swap(): return lax.ppermute(x, axis, [(i, i ^ mask) for i in range(size)])]
    all_to_all x2 -> x1, starting transfers between devices: 12.8 us -> 4.11 us  [spread(): return lax.all_to_all(x, 'hash', split_axis=0, concat_axis=0, tiled=True)]
    ppermute x6 -> x14, starting transfers between devices: 9.65 us -> 16.5 us  [swap(): return lax.ppermute(x, axis, [(i, i ^ mask) for i in range(size)])]
    pallas_call x4 -> x7, Pallas kernels: 3.09 us -> 6.45 us  [call(): pl.pallas_call(kernel, out_shape=[jax.ShapeDtypeStruct(s, f32) for s in o...]
    pallas_call x1 -> x0, Pallas kernels: 2.25 us -> none  [messages(): pl.pallas_call(message_kernel, grid=(steps,), out_shape=jax.ShapeDtypeStr...]
    unnamed x21 -> x26, local copies, waits for them, and re-layouts: 2.08 us -> 3.91 us
    dot_general x1, matrix products: 1.26 us -> 0.23 us  [local(): product_self = jnp.dot(products, w_prod_self, precision=high)]
  transfers between devices with their start and end apart: 8 -> 15, of which waited for: 5 -> 9; matrix products, arithmetic and copies ran while one was open for 5% -> 1% of each run, Pallas kernels for 4% -> 3%
where the time goes in v3:
time: 63.9 us; the launch traced here: 63.6 us
  waiting for transfers between devices  30.8 us (48%)
  starting transfers between devices  20.6 us (32%)
  Pallas kernels  6.45 us (10%)
  local copies, waits for them, and re-layouts  4 us (6%)
  between operations  0.84 us (1%)
    ppermute x14, waiting for transfers between devices, swap(): return lax.ppermute(x, axis, [(i, i ^ mask) for i in range(size)])  22.1 us
    ppermute x14, starting transfers between devices, swap(): return lax.ppermute(x, axis, [(i, i ^ mask) for i in range(size)])  16.5 us
    all_to_all x1, waiting for transfers between devices, spread(): return lax.all_to_all(x, 'hash', split_axis=0, concat_axis=0, tiled=True)  8.76 us
    pallas_call x7, Pallas kernels, call(): pl.pallas_call(kernel, out_shape=[jax.ShapeDtypeStruct(s, f32) for s in o...  6.45 us
    all_to_all x1, starting transfers between devices, spread(): return lax.all_to_all(x, 'hash', split_axis=0, concat_axis=0, tiled=True)  4.11 us
    unnamed x26, local copies, waits for them, and re-layouts  3.91 us
  transfers between devices with their start and end apart: 15, of which 9 were waited for; matrix products, arithmetic and copies ran while one was open for 1% of the time, Pallas kernels for 3%

profile of v3, /device:TPU:0, one launch (start us, length us, event | category | flops | bytes accessed | tf_op | source)
XLA Modules:
  0.0 63.6 jit_solution(11466028064609588745)
XLA Ops:
  0.6 0.0 copy-start
  0.7 0.1 pad_add_fusion.place
  0.7 0.6 %copy-done.5 = s32[1024]{0:T(1024)S(1)} copy-done((s32[1024]{0:T(1024)S(1)}, s32[1024]{0:T(1024)}, u32[]{:S(2)}) %copy-start.5) | copy-done | bytes 4120
  1.4 0.0 copy-done.6
  1.4 1.2 %copy-done.1 = f32[1024,256]{1,0:T(8,128)S(1)} copy-done((f32[1024,256]{1,0:T(8,128)S(1)}, f32[1024,256]{1,0:T(8,128)}, u32[]{:S(2)}) %copy-start.1) | copy-done | bytes 1048600
  2.6 0.9 %copy-done.4 = f32[256,256]{1,0:T(8,128)S(1)} copy-done((f32[256,256]{1,0:T(8,128)S(1)}, f32[256,256]{1,0:T(8,128)}, u32[]{:S(2)}) %copy-start.4) | copy-done | bytes 262168
  3.6 1.1 %shard_map.140 = (f32[4,72,128]{2,1,0:T(8,128)S(1)}, f32[4,72,128]{2,1,0:T(8,128)S(1)}, f32[4,72,128]{2,1,0:T(8,128)S(1)}, f32[4,72,128]{2,1,0:T(8,128)S(1)}, f3...) custom-call(s32[2]{0:T(128)S(1)} %pad_add_fusion.place, ...), custom_call_target="tpu_custom_call" | custom-call | tf_op jit(solution)/shard_map/pallas_call | solution.py:41
  4.7 0.5 collective-permute-start
  5.2 2.6 %collective-permute-start.1 = (f32[4,72,128]{2,1,0:T(8,128)S(1)}, f32[4,72,128]{2,1,0:T(8,128)S(1)}, u32[]{:S(2)}, u32[]{:S(2)}) collective-permute-start(f32[4,72,128]{2,1,0:T(8,128)S(1)} %get-tuple-element.27), channel_id=1, source_target_pairs={{0,4},{2,6},{4,0},{6,2},{8,12},{10,14},{12,8},{14,10},{16,20},{18,... | collective-permute-start | bytes 442376 | tf_op jit(solution)/shard_map/ppermute | solution.py:127
  7.8 0.1 collective-permute-start.2
  7.9 0.1 collective-permute-start.7
  8.0 1.9 %collective-permute-start.8 = (f32[4,64,128]{2,1,0:T(8,128)S(1)}, f32[4,64,128]{2,1,0:T(8,128)S(1)}, u32[]{:S(2)}, u32[]{:S(2)}) collective-permute-start(f32[4,64,128]{2,1,0:T(8,128)S(1)} %get-tuple-element.38), channel_id=1, source_target_pairs={{0,4},{2,6},{4,0},{6,2},{8,12},{10,14},{12,8},{14,10},{16,20},{18,... | collective-permute-start | bytes 393224 | tf_op jit(solution)/shard_map/ppermute | solution.py:127
  10.0 0.2 fusion.4.refs_8_
  10.2 2.3 %collective-permute-done.1.r2 = f32[4,72,128]{2,1,0:T(8,128)S(1)} collective-permute-done((f32[4,72,128]{2,1,0:T(8,128)S(1)}, f32[4,72,128]{2,1,0:T(8,128)S(1)}, u32[]{:S(2)}, u32[]{:S(2)}) %collective-permute-start.1) | collective-permute-done | bytes 147488 | tf_op jit(solution)/shard_map/ppermute | solution.py:127
  12.5 2.6 %collective-permute-done.2.r3 = f32[4,72,128]{2,1,0:T(8,128)S(1)} collective-permute-done((f32[4,72,128]{2,1,0:T(8,128)S(1)}, f32[4,72,128]{2,1,0:T(8,128)S(1)}, u32[]{:S(2)}, u32[]{:S(2)}) %collective-permute-start.2) | collective-permute-done | bytes 147488 | tf_op jit(solution)/shard_map/ppermute | solution.py:127
  15.1 0.8 %shard_map.141 = (f32[4,128,128]{2,1,0:T(8,128)S(1)}, f32[4,128,128]{2,1,0:T(8,128)S(1)}, f32[8,128]{1,0:T(8,128)S(1)}) custom-call(s32[2]{0:T(128)S(1)} %pad_add_fusion.place, f32[4,72,128]{2,1,0:T(8,128)S(1)} %get-tuple-element.25.r0, f32[4,72,128]{2,1,0:T(8,128)S(1)} %collective-permute-done.r1, f32[4,72,128]{2,1,0:T(8,128)S(1)} %collective-permute-done.1.r2, ...), custom_call_target="tpu_custom_call" | custom-call | tf_op jit(solution)/shard_map/pallas_call | solution.py:41
  16.0 2.5 %collective-permute-done.8.r2 = f32[4,64,128]{2,1,0:T(8,128)S(1)} collective-permute-done((f32[4,64,128]{2,1,0:T(8,128)S(1)}, f32[4,64,128]{2,1,0:T(8,128)S(1)}, u32[]{:S(2)}, u32[]{:S(2)}) %collective-permute-start.8) | collective-permute-done | bytes 131104 | tf_op jit(solution)/shard_map/ppermute | solution.py:127
  18.5 2.3 %collective-permute-done.9.r3 = f32[4,64,128]{2,1,0:T(8,128)S(1)} collective-permute-done((f32[4,64,128]{2,1,0:T(8,128)S(1)}, f32[4,64,128]{2,1,0:T(8,128)S(1)}, u32[]{:S(2)}, u32[]{:S(2)}) %collective-permute-start.9) | collective-permute-done | bytes 131104 | tf_op jit(solution)/shard_map/ppermute | solution.py:127
  20.8 0.9 %shard_map.143 = (f32[4,128,128]{2,1,0:T(8,128)S(1)}, f32[4,128,128]{2,1,0:T(8,128)S(1)}) custom-call(s32[2]{0:T(128)S(1)} %pad_add_fusion.place, f32[8,128]{1,0:T(8,128)S(1)} %get-tuple-element.35.ids, f32[4,64,128]{2,1,0:T(8,128)S(1)} %get-tuple-element.36.r0, f32[4,64,128]{2,1,0:T(8,128)S(1)} %collective-permute-done.7.r1, ...), custom_call_target="tpu_custom_call" | custom-call | tf_op jit(solution)/shard_map/pallas_call | solution.py:41
  21.6 1.7 %collective-permute-start.10 = (f32[4,128,128]{2,1,0:T(8,128)S(1)}, f32[4,128,128]{2,1,0:T(8,128)S(1)}, u32[]{:S(2)}, u32[]{:S(2)}) collective-permute-start(f32[4,128,128]{2,1,0:T(8,128)S(1)} %get-tuple-element.41), channel_id=1, source_target_pairs={{0,1},{1,0},{2,3},{3,2},{4,5},{5,4},{6,7},{7,6},{8,9},{9,8},{10,11... | collective-permute-start | bytes 786440 | tf_op jit(solution)/shard_map/ppermute | solution.py:127
  23.3 0.0 copy-start.12
  23.3 0.5 collective-permute-start.3
  23.8 0.1 copy-done.12
  24.0 0.1 iota_compare_fusion.2
  24.1 0.1 lt.15
  24.1 6.7 %collective-permute-done.10.got = f32[4,128,128]{2,1,0:T(8,128)S(1)} collective-permute-done((f32[4,128,128]{2,1,0:T(8,128)S(1)}, f32[4,128,128]{2,1,0:T(8,128)S(1)}, u32[]{:S(2)}, u32[]{:S(2)}) %collective-permute-start.10) | collective-permute-done | bytes 262176 | tf_op jit(solution)/shard_map/ppermute | solution.py:127
  30.8 0.6 shard_map.144
  31.4 0.0 copy-start.11
  31.4 1.7 %collective-permute-start.11 = (f32[128,128]{1,0:T(8,128)S(1)}, f32[128,128]{1,0:T(8,128)S(1)}, u32[]{:S(2)}, u32[]{:S(2)}) collective-permute-start(f32[128,128]{1,0:T(8,128)S(1)} %get-tuple-element.43), channel_id=1, source_target_pairs={{0,8},{2,10},{4,12},{6,14},{8,0},{10,2},{12,4},{14,6},{16,24},{18,... | collective-permute-start | bytes 196616 | tf_op jit(solution)/shard_map/ppermute | solution.py:127
  33.1 2.6 %collective-permute-start.12 = (f32[128,128]{1,0:T(8,128)S(1)}, f32[128,128]{1,0:T(8,128)S(1)}, u32[]{:S(2)}, u32[]{:S(2)}) collective-permute-start(f32[128,128]{1,0:T(8,128)S(1)} %get-tuple-element.44), channel_id=1, source_target_pairs={{0,16},{2,18},{4,20},{6,22},{8,24},{10,26},{12,28},{14,30},{16,0},... | collective-permute-start | bytes 196616 | tf_op jit(solution)/shard_map/ppermute | solution.py:127
  35.7 0.4 collective-permute-start.13
  36.1 0.0 collective-permute-done.3.got
  36.1 0.6 shard_map.142
  36.7 1.4 %collective-permute-start.4 = (f32[128,128]{1,0:T(8,128)S(1)}, f32[128,128]{1,0:T(8,128)S(1)}, u32[]{:S(2)}, u32[]{:S(2)}) collective-permute-start(f32[128,128]{1,0:T(8,128)S(1)} %get-tuple-element.32), channel_id=1, source_target_pairs={{0,8},{2,10},{4,12},{6,14},{8,0},{10,2},{12,4},{14,6},{16,24},{18,... | collective-permute-start | bytes 196616 | tf_op jit(solution)/shard_map/ppermute | solution.py:127
  38.1 2.7 %collective-permute-start.5 = (f32[128,128]{1,0:T(8,128)S(1)}, f32[128,128]{1,0:T(8,128)S(1)}, u32[]{:S(2)}, u32[]{:S(2)}) collective-permute-start(f32[128,128]{1,0:T(8,128)S(1)} %get-tuple-element.33), channel_id=1, source_target_pairs={{0,16},{2,18},{4,20},{6,22},{8,24},{10,26},{12,28},{14,30},{16,0},... | collective-permute-start | bytes 196616 | tf_op jit(solution)/shard_map/ppermute | solution.py:127
  40.8 0.0 collective-permute-done.11.refs_5_
  40.8 0.4 collective-permute-start.6
  41.1 0.1 fusion.3.refs_12_
  41.2 1.2 %collective-permute-done.13.refs_7_ = f32[128,128]{1,0:T(8,128)S(1)} collective-permute-done((f32[128,128]{1,0:T(8,128)S(1)}, f32[128,128]{1,0:T(8,128)S(1)}, u32[]{:S(2)}, u32[]{:S(2)}) %collective-permute-start.13) | collective-permute-done | bytes 65568 | tf_op jit(solution)/shard_map/ppermute | solution.py:127
  42.4 3.2 %collective-permute-done.5.refs_2_ = f32[128,128]{1,0:T(8,128)S(1)} collective-permute-done((f32[128,128]{1,0:T(8,128)S(1)}, f32[128,128]{1,0:T(8,128)S(1)}, u32[]{:S(2)}, u32[]{:S(2)}) %collective-permute-start.5) | collective-permute-done | bytes 65568 | tf_op jit(solution)/shard_map/ppermute | solution.py:127
  45.6 1.3 %collective-permute-done.6.refs_3_ = f32[128,128]{1,0:T(8,128)S(1)} collective-permute-done((f32[128,128]{1,0:T(8,128)S(1)}, f32[128,128]{1,0:T(8,128)S(1)}, u32[]{:S(2)}, u32[]{:S(2)}) %collective-permute-start.6) | collective-permute-done | bytes 65568 | tf_op jit(solution)/shard_map/ppermute | solution.py:127
  46.9 1.2 %shard_map.145 = (f32[128,256]{1,0:T(8,128)}, f32[16,16,256]{2,1,0:T(8,128)}) custom-call(f32[128,128]{1,0:T(8,128)S(1)} %get-tuple-element.31.refs_0_, f32[128,128]{1,0:T(8,128)S(1)} %collective-permute-done.4.refs_1_, f32[128,128]{1,0:T(8,128)S(1)} %collective-permute-done.5.refs_2_, f32[128,128]{1,0:T(8,128)S(1)} %collective-permute-done.6.refs_3_, ...), custom_call_target="tpu_custom_call" | custom-call | tf_op jit(solution)/shard_map/pallas_call | solution.py:41
  48.2 4.1 %all-to-all-start = ((f32[16,16,256]{2,1,0:T(8,128)}), f32[16,16,256]{2,1,0:T(8,128)S(1)}, u32[]{:S(2)}, u32[]{:S(2)}) async-start(f32[16,16,256]{2,1,0:T(8,128)} %get-tuple-element.47), calls=%async_computation | async-start | bytes 524288 | tf_op jit(solution)/shard_map/all_to_all | solution.py:131
  52.3 0.0 copy-start.2
  52.4 0.9 %copy-done.2 = f32[256,256]{1,0:T(8,128)S(1)} copy-done((f32[256,256]{1,0:T(8,128)S(1)}, f32[256,256]{1,0:T(8,128)}, u32[]{:S(2)}) %copy-start.2) | copy-done | bytes 262168
  53.3 0.3 fusion.5.own
  53.6 8.8 %all-to-all-done = f32[16,16,256]{2,1,0:T(8,128)S(1)} async-done(((f32[16,16,256]{2,1,0:T(8,128)}), f32[16,16,256]{2,1,0:T(8,128)S(1)}, u32[]{:S(2)}, u32[]{:S(2)}) %all-to-all-start) | async-done | bytes 262176 | tf_op jit(solution)/shard_map/all_to_all | solution.py:131
  62.3 1.2 %shard_map.146 = f32[256,256]{1,0:T(8,128)} custom-call(f32[256,256]{1,0:T(8,128)S(1)} %bitcast.8, bf16[256,256]{1,0:T(8,128)(2,1)S(1)} %fusion.2.incidence, f32[256,256]{1,0:T(8,128)S(1)} %fusion.5.own, f32[256,256]{1,0:T(8,128)S(1)} %copy-done.2, bf16[256,256]{1,0:T(8,128)(2,1)S(1)} %get-tuple-element.49.w_top, bf16[256,256]{1,0:T(8,128)(2,1)S(1)} %get-tuple-element.48.w_low), custom_call_target="tpu_custom_call" | custom-call | tf_op jit(solution)/shard_map/pallas_call | solution.py:41
  (25 shorter events, 0.1 us)
Async XLA Ops:
  0.6 51.8 %copy-start = (f32[256,256]{1,0:T(8,128)S(1)}, f32[256,256]{1,0:T(8,128)}, u32[]{:S(2)}) copy-start(f32[256,256]{1,0:T(8,128)} %param.24) | copy-start | bytes 786436
  0.6 0.7 %copy-start.5 = (s32[1024]{0:T(1024)S(1)}, s32[1024]{0:T(1024)}, u32[]{:S(2)}) copy-start(s32[1024]{0:T(1024)} %param.14) | copy-start | bytes 12292
  0.7 0.7 %copy-start.6 = (s32[16]{0:T(128)S(1)}, s32[16]{0:T(128)}, u32[]{:S(2)}) copy-start(s32[16]{0:T(128)} %count.1) | copy-start | bytes 196
  1.4 1.2 %copy-start.1 = (f32[1024,256]{1,0:T(8,128)S(1)}, f32[1024,256]{1,0:T(8,128)}, u32[]{:S(2)}) copy-start(f32[1024,256]{1,0:T(8,128)} %tx.1) | copy-start | bytes 3145732
  2.6 0.9 %copy-start.4 = (f32[256,256]{1,0:T(8,128)S(1)}, f32[256,256]{1,0:T(8,128)}, u32[]{:S(2)}) copy-start(f32[256,256]{1,0:T(8,128)} %w.1) | copy-start | bytes 786436
  3.6 6.4 %copy-start.3 = (f32[128,256]{1,0:T(8,128)S(1)}, f32[128,256]{1,0:T(8,128)}, u32[]{:S(2)}) copy-start(f32[128,256]{1,0:T(8,128)} %refs_9_.1) | copy-start | bytes 393220
  3.6 6.4 %copy-start.7 = (f32[256,256]{1,0:T(8,128)S(1)}, f32[256,256]{1,0:T(8,128)}, u32[]{:S(2)}) copy-start(f32[256,256]{1,0:T(8,128)} %param.22) | copy-start | bytes 786436
  4.7 5.2 %collective-permute-start = (f32[4,72,128]{2,1,0:T(8,128)S(1)}, f32[4,72,128]{2,1,0:T(8,128)S(1)}, u32[]{:S(2)}, u32[]{:S(2)}) collective-permute-start(f32[4,72,128]{2,1,0:T(8,128)S(1)} %get-tuple-element.26), channel_id=1, source_target_pairs={{0,2},{2,0},{4,6},{6,4},{8,10},{10,8},{12,14},{14,12},{16,18},{18,... | collective-permute-start | bytes 442376 | tf_op jit(solution)/shard_map/ppermute | solution.py:127
  5.2 7.3 %collective-permute-start.1 = (f32[4,72,128]{2,1,0:T(8,128)S(1)}, f32[4,72,128]{2,1,0:T(8,128)S(1)}, u32[]{:S(2)}, u32[]{:S(2)}) collective-permute-start(f32[4,72,128]{2,1,0:T(8,128)S(1)} %get-tuple-element.27), channel_id=1, source_target_pairs={{0,4},{2,6},{4,0},{6,2},{8,12},{10,14},{12,8},{14,10},{16,20},{18,... | collective-permute-start | bytes 442376 | tf_op jit(solution)/shard_map/ppermute | solution.py:127
  7.8 7.3 %collective-permute-start.2 = (f32[4,72,128]{2,1,0:T(8,128)S(1)}, f32[4,72,128]{2,1,0:T(8,128)S(1)}, u32[]{:S(2)}, u32[]{:S(2)}) collective-permute-start(f32[4,72,128]{2,1,0:T(8,128)S(1)} %get-tuple-element.28), channel_id=1, source_target_pairs={{0,6},{2,4},{4,2},{6,0},{8,14},{10,12},{12,10},{14,8},{16,22},{18,... | collective-permute-start | bytes 442376 | tf_op jit(solution)/shard_map/ppermute | solution.py:127
  7.9 8.1 %collective-permute-start.7 = (f32[4,64,128]{2,1,0:T(8,128)S(1)}, f32[4,64,128]{2,1,0:T(8,128)S(1)}, u32[]{:S(2)}, u32[]{:S(2)}) collective-permute-start(f32[4,64,128]{2,1,0:T(8,128)S(1)} %get-tuple-element.37), channel_id=1, source_target_pairs={{0,2},{2,0},{4,6},{6,4},{8,10},{10,8},{12,14},{14,12},{16,18},{18,... | collective-permute-start | bytes 393224 | tf_op jit(solution)/shard_map/ppermute | solution.py:127
  8.0 10.5 %collective-permute-start.8 = (f32[4,64,128]{2,1,0:T(8,128)S(1)}, f32[4,64,128]{2,1,0:T(8,128)S(1)}, u32[]{:S(2)}, u32[]{:S(2)}) collective-permute-start(f32[4,64,128]{2,1,0:T(8,128)S(1)} %get-tuple-element.38), channel_id=1, source_target_pairs={{0,4},{2,6},{4,0},{6,2},{8,12},{10,14},{12,8},{14,10},{16,20},{18,... | collective-permute-start | bytes 393224 | tf_op jit(solution)/shard_map/ppermute | solution.py:127
  9.9 10.8 %collective-permute-start.9 = (f32[4,64,128]{2,1,0:T(8,128)S(1)}, f32[4,64,128]{2,1,0:T(8,128)S(1)}, u32[]{:S(2)}, u32[]{:S(2)}) collective-permute-start(f32[4,64,128]{2,1,0:T(8,128)S(1)} %get-tuple-element.39), channel_id=1, source_target_pairs={{0,6},{2,4},{4,2},{6,0},{8,14},{10,12},{12,10},{14,8},{16,22},{18,... | collective-permute-start | bytes 393224 | tf_op jit(solution)/shard_map/ppermute | solution.py:127
  20.8 2.5 %copy-start.8 = (f32[256,256]{1,0:T(8,128)S(1)}, f32[256,256]{1,0:T(8,128)}, u32[]{:S(2)}) copy-start(f32[256,256]{1,0:T(8,128)} %param.23) | copy-start | bytes 786436
  21.6 9.2 %collective-permute-start.10 = (f32[4,128,128]{2,1,0:T(8,128)S(1)}, f32[4,128,128]{2,1,0:T(8,128)S(1)}, u32[]{:S(2)}, u32[]{:S(2)}) collective-permute-start(f32[4,128,128]{2,1,0:T(8,128)S(1)} %get-tuple-element.41), channel_id=1, source_target_pairs={{0,1},{1,0},{2,3},{3,2},{4,5},{5,4},{6,7},{7,6},{8,9},{9,8},{10,11... | collective-permute-start | bytes 786440 | tf_op jit(solution)/shard_map/ppermute | solution.py:127
  23.3 0.7 %copy-start.12 = (s32[16]{0:T(128)S(1)}, s32[16]{0:T(128)}, u32[]{:S(2)}) copy-start(s32[16]{0:T(128)} %param.19) | copy-start | bytes 196
  23.3 12.8 %collective-permute-start.3 = (f32[4,128,128]{2,1,0:T(8,128)S(1)}, f32[4,128,128]{2,1,0:T(8,128)S(1)}, u32[]{:S(2)}, u32[]{:S(2)}) collective-permute-start(f32[4,128,128]{2,1,0:T(8,128)S(1)} %get-tuple-element.30), channel_id=1, source_target_pairs={{0,1},{1,0},{2,3},{3,2},{4,5},{5,4},{6,7},{7,6},{8,9},{9,8},{10,11... | collective-permute-start | bytes 786440 | tf_op jit(solution)/shard_map/ppermute | solution.py:127
  31.4 1.7 %copy-start.11 = (s32[256]{0:T(256)S(1)}, s32[256]{0:T(256)}, u32[]{:S(2)}) copy-start(s32[256]{0:T(256)} %param.18) | copy-start | bytes 3076
  31.4 9.3 %collective-permute-start.11 = (f32[128,128]{1,0:T(8,128)S(1)}, f32[128,128]{1,0:T(8,128)S(1)}, u32[]{:S(2)}, u32[]{:S(2)}) collective-permute-start(f32[128,128]{1,0:T(8,128)S(1)} %get-tuple-element.43), channel_id=1, source_target_pairs={{0,8},{2,10},{4,12},{6,14},{8,0},{10,2},{12,4},{14,6},{16,24},{18,... | collective-permute-start | bytes 196616 | tf_op jit(solution)/shard_map/ppermute | solution.py:127
  33.1 8.1 %collective-permute-start.12 = (f32[128,128]{1,0:T(8,128)S(1)}, f32[128,128]{1,0:T(8,128)S(1)}, u32[]{:S(2)}, u32[]{:S(2)}) collective-permute-start(f32[128,128]{1,0:T(8,128)S(1)} %get-tuple-element.44), channel_id=1, source_target_pairs={{0,16},{2,18},{4,20},{6,22},{8,24},{10,26},{12,28},{14,30},{16,0},... | collective-permute-start | bytes 196616 | tf_op jit(solution)/shard_map/ppermute | solution.py:127
  35.7 6.7 %collective-permute-start.13 = (f32[128,128]{1,0:T(8,128)S(1)}, f32[128,128]{1,0:T(8,128)S(1)}, u32[]{:S(2)}, u32[]{:S(2)}) collective-permute-start(f32[128,128]{1,0:T(8,128)S(1)} %get-tuple-element.45), channel_id=1, source_target_pairs={{0,24},{2,26},{4,28},{6,30},{8,16},{10,18},{12,20},{14,22},{16,8},... | collective-permute-start | bytes 196616 | tf_op jit(solution)/shard_map/ppermute | solution.py:127
  36.7 5.7 %collective-permute-start.4 = (f32[128,128]{1,0:T(8,128)S(1)}, f32[128,128]{1,0:T(8,128)S(1)}, u32[]{:S(2)}, u32[]{:S(2)}) collective-permute-start(f32[128,128]{1,0:T(8,128)S(1)} %get-tuple-element.32), channel_id=1, source_target_pairs={{0,8},{2,10},{4,12},{6,14},{8,0},{10,2},{12,4},{14,6},{16,24},{18,... | collective-permute-start | bytes 196616 | tf_op jit(solution)/shard_map/ppermute | solution.py:127
  38.1 7.5 %collective-permute-start.5 = (f32[128,128]{1,0:T(8,128)S(1)}, f32[128,128]{1,0:T(8,128)S(1)}, u32[]{:S(2)}, u32[]{:S(2)}) collective-permute-start(f32[128,128]{1,0:T(8,128)S(1)} %get-tuple-element.33), channel_id=1, source_target_pairs={{0,16},{2,18},{4,20},{6,22},{8,24},{10,26},{12,28},{14,30},{16,0},... | collective-permute-start | bytes 196616 | tf_op jit(solution)/shard_map/ppermute | solution.py:127
  40.8 6.2 %collective-permute-start.6 = (f32[128,128]{1,0:T(8,128)S(1)}, f32[128,128]{1,0:T(8,128)S(1)}, u32[]{:S(2)}, u32[]{:S(2)}) collective-permute-start(f32[128,128]{1,0:T(8,128)S(1)} %get-tuple-element.34), channel_id=1, source_target_pairs={{0,24},{2,26},{4,28},{6,30},{8,16},{10,18},{12,20},{14,22},{16,8},... | collective-permute-start | bytes 196616 | tf_op jit(solution)/shard_map/ppermute | solution.py:127
  48.1 4.1 %copy-start.10 = (s32[256]{0:T(256)S(1)}, s32[256]{0:T(256)}, u32[]{:S(2)}) copy-start(s32[256]{0:T(256)} %param.20) | copy-start | bytes 3076
  48.1 4.2 %copy-start.9 = (f32[256,256]{1,0:T(8,128)S(1)}, f32[256,256]{1,0:T(8,128)}, u32[]{:S(2)}) copy-start(f32[256,256]{1,0:T(8,128)} %param.25) | copy-start | bytes 786436
  48.2 14.2 %all-to-all-start = ((f32[16,16,256]{2,1,0:T(8,128)}), f32[16,16,256]{2,1,0:T(8,128)S(1)}, u32[]{:S(2)}, u32[]{:S(2)}) async-start(f32[16,16,256]{2,1,0:T(8,128)} %get-tuple-element.47), calls=%async_computation | async-start | bytes 524288 | tf_op jit(solution)/shard_map/all_to_all | solution.py:131
  52.3 1.0 %copy-start.2 = (f32[256,256]{1,0:T(8,128)S(1)}, f32[256,256]{1,0:T(8,128)}, u32[]{:S(2)}) copy-start(f32[256,256]{1,0:T(8,128)} %table.1) | copy-start | bytes 786436

commit v4 on v3

--- a/solution.py
+++ b/solution.py
@@ -35,14 +35,15 @@
     return mm(picks, top) + mm(picks, low)
 
 
-def call(kernel, out, ins, smem=()):
+def call(kernel, out, ins, smem=(), space=pltpu.VMEM, scratch=()):
     vmem = pl.BlockSpec(memory_space=pltpu.VMEM)
     scalar = pl.BlockSpec(memory_space=pltpu.SMEM)
     return pl.pallas_call(
         kernel,
         out_shape=[jax.ShapeDtypeStruct(s, f32) for s in out],
-        in_specs=[scalar] * len(smem) + [vmem] * len(ins),
+        in_specs=[scalar] * len(smem) + [pl.BlockSpec(memory_space=space)] * len(ins),
         out_specs=[vmem] * len(out),
+        scratch_shapes=list(scratch),
         compiler_params=pltpu.CompilerParams(vmem_limit_bytes=32 * 1024 * 1024),
     )(*smem, *ins)
 
@@ -51,19 +52,28 @@
     return lax.broadcasted_iota(jnp.int32, (1, LANES), 1)
 
 
-def message_kernel(place, count, tx, ids, w, p0, p1, p2, p3, q0, q1, q2, q3):
+def message_kernel(place, count, tx, ids, w, p0, p1, p2, p3, q0, q1, q2, q3, buf, w_buf, ids_buf, sem):
     near = place[0] & 3
-    w_top, w_low = split(w[...])
     slots = q0.shape[1]
+    copies = [pltpu.make_async_copy(w, w_buf, sem.at[4]), pltpu.make_async_copy(ids, ids_buf, sem.at[5])]
+    order = (2, 3, 1, 0)
+    copies += [pltpu.make_async_copy(tx.at[:, near ^ m], buf.at[m], sem.at[m]) for m in order]
+    for copy in copies:
+        copy.start()
     lane = lanes()
-    for m, (first, second) in enumerate(((p0, q0), (p1, q1), (p2, q2), (p3, q3))):
+    copies[0].wait()
+    copies[1].wait()
+    w_top, w_low = split(w_buf[...])
+    outs = ((p0, q0), (p1, q1), (p2, q2), (p3, q3))
+    for m, copy in zip(order, copies[2:]):
+        first, second = outs[m]
         c = near ^ m
-        x = jnp.concatenate([tx[pl.ds(pl.multiple_of((4 * z + c) * slots, slots), slots), :] for z in range(4)], 0)
-        y = jnp.maximum(dot3(x, w_top, w_low), 0.0)
+        copy.wait()
+        y = jnp.maximum(dot3(buf[m].reshape(4 * slots, 2 * LANES), w_top, w_low), 0.0)
         first[:, :slots, :] = y[:, :LANES].reshape(4, slots, LANES)
         second[...] = y[:, LANES:].reshape(4, slots, LANES)
         for z in range(4):
-            row = ids[pl.ds(2 * z + (c >> 1), 1), :]
+            row = ids_buf[pl.ds(2 * z + (c >> 1), 1), :]
             turned = pltpu.roll(row, slots, 1)
             twice = jnp.where((lane >= slots).astype(jnp.int32) == (c & 1), row, turned)
             twice = jnp.where((lane & (slots - 1)) < count[4 * z + c], twice, -1).astype(f32)
@@ -135,23 +145,36 @@
     peers = 16
     slots = transactions.shape[0] // peers
     block = (4, mine, LANES)
+    width = 2 * LANES
     out = call(
         message_kernel,
         [(4, slots + PAD, LANES)] * 4 + [(4, slots, LANES)] * 4,
-        (transactions, tx_product.reshape(-1, LANES), w_msg),
+        (transactions.reshape(4, 4, slots, width), tx_product.reshape(-1, LANES), w_msg),
         smem=(place, tx_count),
+        space=pltpu.HBM,
+        scratch=[
+            pltpu.VMEM((4, 4, slots, width), f32),
+            pltpu.VMEM((width, width), f32),
+            pltpu.VMEM((peers * slots // LANES, LANES), jnp.int32),
+            pltpu.SemaphoreType.DMA((6,)),
+        ],
     )
 
     def near(blocks):
         return [blocks[0]] + [swap(blocks[m], "hash", m, peers) for m in (1, 2, 3)]
 
-    def rest(send, keep):
-        parts = call(pair_kernel, [(mine, LANES)] * 4, (keep, swap(send, "tm", 1, 2)), smem=(place,))
+    def across(keep, got):
+        parts = call(pair_kernel, [(mine, LANES)] * 4, (keep, got), smem=(place,))
         return [parts[0]] + [swap(parts[k], "hash", 4 * k, peers) for k in (1, 2, 3)]
 
-    *first, ids = call(first_sum_kernel, [block, block, (8, LANES)], near(out[:4]), smem=(place,))
-    second = call(second_sum_kernel, [block, block], (ids, *near(out[4:])), smem=(place,))
-    return rest(*first) + rest(*second)
+    first, second = near(out[:4]), near(out[4:])
+    send_p, keep_p, ids = call(first_sum_kernel, [block, block, (8, LANES)], first, smem=(place,))
+    got_p = swap(send_p, "tm", 1, 2)
+    got_p, *second = lax.optimization_barrier((got_p, *second))
+    send_q, keep_q = call(second_sum_kernel, [block, block], (ids, *second), smem=(place,))
+    got_p, send_q = lax.optimization_barrier((got_p, send_q))
+    got_q = swap(send_q, "tm", 1, 2)
+    return across(keep_p, got_p) + across(keep_q, got_q)
 
 
 def gathered_plainly(transactions, tx_product, tx_count, w_msg, mine):

time: 63.9 us -> 62.5 us (0.978)
  waiting for transfers between devices: 30.8 us -> 27.7 us
  Pallas kernels: 6.45 us -> 7.48 us
  starting transfers between devices: 20.6 us -> 21.4 us
    ppermute x14, waiting for transfers between devices: 22.1 us -> 19 us  [swap(): return lax.ppermute(x, axis, [(i, i ^ mask) for i in range(size)])]
    ppermute x14, starting transfers between devices: 16.5 us -> 17.8 us  [swap(): return lax.ppermute(x, axis, [(i, i ^ mask) for i in range(size)])]
    pallas_call x7, Pallas kernels: 6.45 us -> 7.48 us  [call(): pl.pallas_call(kernel, out_shape=[jax.ShapeDtypeStruct(s, f32) for s in o...]
  transfers between devices with their start and end apart: 15 -> 15, of which waited for: 9 -> 10; matrix products, arithmetic and copies ran while one was open for 1% -> 1% of each run, Pallas kernels for 3% -> 3%
where the time goes in v4:
time: 62.5 us; the launch traced here: 62.2 us
  waiting for transfers between devices  27.7 us (44%)
  starting transfers between devices  21.4 us (34%)
  Pallas kernels  7.48 us (12%)
  local copies, waits for them, and re-layouts  3.86 us (6%)
  between operations  0.85 us (1%)
    ppermute x14, waiting for transfers between devices, swap(): return lax.ppermute(x, axis, [(i, i ^ mask) for i in range(size)])  19 us
    ppermute x14, starting transfers between devices, swap(): return lax.ppermute(x, axis, [(i, i ^ mask) for i in range(size)])  17.8 us
    all_to_all x1, waiting for transfers between devices, spread(): return lax.all_to_all(x, 'hash', split_axis=0, concat_axis=0, tiled=True)  8.75 us
    pallas_call x7, Pallas kernels, call(): pl.pallas_call(kernel, out_shape=[jax.ShapeDtypeStruct(s, f32) for s in o...  7.48 us
    unnamed x26, local copies, waits for them, and re-layouts  3.77 us
    all_to_all x1, starting transfers between devices, spread(): return lax.all_to_all(x, 'hash', split_axis=0, concat_axis=0, tiled=True)  3.67 us
  transfers between devices with their start and end apart: 15, of which 10 were waited for; matrix products, arithmetic and copies ran while one was open for 1% of the time, Pallas kernels for 3%

profile of v4, /device:TPU:0, one launch (start us, length us, event | category | flops | bytes accessed | tf_op | source)
XLA Modules:
  0.0 62.2 jit_solution(4934658061062794414)
XLA Ops:
  0.6 0.0 copy-start
  0.7 0.1 pad_add_fusion.place
  0.7 0.6 %copy-done.5 = s32[1024]{0:T(1024)S(1)} copy-done((s32[1024]{0:T(1024)S(1)}, s32[1024]{0:T(1024)}, u32[]{:S(2)}) %copy-start.5) | copy-done | bytes 4120
  1.4 0.0 copy-done.6
  1.4 1.2 %copy-done.1 = f32[1024,256]{1,0:T(8,128)S(1)} copy-done((f32[1024,256]{1,0:T(8,128)S(1)}, f32[1024,256]{1,0:T(8,128)}, u32[]{:S(2)}) %copy-start.1) | copy-done | bytes 1048600
  2.6 0.9 %copy-done.4 = f32[256,256]{1,0:T(8,128)S(1)} copy-done((f32[256,256]{1,0:T(8,128)S(1)}, f32[256,256]{1,0:T(8,128)}, u32[]{:S(2)}) %copy-start.4) | copy-done | bytes 262168
  3.6 2.2 %shard_map.140 = (f32[4,72,128]{2,1,0:T(8,128)S(1)}, f32[4,72,128]{2,1,0:T(8,128)S(1)}, f32[4,72,128]{2,1,0:T(8,128)S(1)}, f32[4,72,128]{2,1,0:T(8,128)S(1)}, f3...) custom-call(s32[2]{0:T(128)S(1)} %pad_add_fusion.place, ...), custom_call_target="tpu_custom_call" | custom-call | tf_op jit(solution)/shard_map/pallas_call | solution.py:41
  5.7 0.5 collective-permute-start
  6.3 2.6 %collective-permute-start.1 = (f32[4,72,128]{2,1,0:T(8,128)S(1)}, f32[4,72,128]{2,1,0:T(8,128)S(1)}, u32[]{:S(2)}, u32[]{:S(2)}) collective-permute-start(f32[4,72,128]{2,1,0:T(8,128)S(1)} %get-tuple-element.34), channel_id=1, source_target_pairs={{0,4},{2,6},{4,0},{6,2},{8,12},{10,14},{12,8},{14,10},{16,20},{18,... | collective-permute-start | bytes 442376 | tf_op jit(solution)/shard_map/ppermute | solution.py:137
  8.8 0.1 collective-permute-start.2
  8.9 0.1 collective-permute-start.4
  9.0 1.9 %collective-permute-start.5 = (f32[4,64,128]{2,1,0:T(8,128)S(1)}, f32[4,64,128]{2,1,0:T(8,128)S(1)}, u32[]{:S(2)}, u32[]{:S(2)}) collective-permute-start(f32[4,64,128]{2,1,0:T(8,128)S(1)} %get-tuple-element.40), channel_id=1, source_target_pairs={{0,4},{2,6},{4,0},{6,2},{8,12},{10,14},{12,8},{14,10},{16,20},{18,... | collective-permute-start | bytes 393224 | tf_op jit(solution)/shard_map/ppermute | solution.py:137
  11.0 0.0 collective-permute-done.r1
  11.0 0.0 collective-permute-start.6
  11.0 2.5 %collective-permute-done.1.r2 = f32[4,72,128]{2,1,0:T(8,128)S(1)} collective-permute-done((f32[4,72,128]{2,1,0:T(8,128)S(1)}, f32[4,72,128]{2,1,0:T(8,128)S(1)}, u32[]{:S(2)}, u32[]{:S(2)}) %collective-permute-start.1) | collective-permute-done | bytes 147488 | tf_op jit(solution)/shard_map/ppermute | solution.py:137
  13.5 2.6 %collective-permute-done.2.r3 = f32[4,72,128]{2,1,0:T(8,128)S(1)} collective-permute-done((f32[4,72,128]{2,1,0:T(8,128)S(1)}, f32[4,72,128]{2,1,0:T(8,128)S(1)}, u32[]{:S(2)}, u32[]{:S(2)}) %collective-permute-start.2) | collective-permute-done | bytes 147488 | tf_op jit(solution)/shard_map/ppermute | solution.py:137
  16.2 0.8 %shard_map.141 = (f32[4,128,128]{2,1,0:T(8,128)S(1)}, f32[4,128,128]{2,1,0:T(8,128)S(1)}, f32[8,128]{1,0:T(8,128)S(1)}) custom-call(s32[2]{0:T(128)S(1)} %pad_add_fusion.place, f32[4,72,128]{2,1,0:T(8,128)S(1)} %get-tuple-element.32.r0, f32[4,72,128]{2,1,0:T(8,128)S(1)} %collective-permute-done.r1, f32[4,72,128]{2,1,0:T(8,128)S(1)} %collective-permute-done.1.r2, ...), custom_call_target="tpu_custom_call" | custom-call | tf_op jit(solution)/shard_map/pallas_call | solution.py:41
  17.0 0.0 copy-start.8
  17.0 1.7 %collective-permute-start.3 = (f32[4,128,128]{2,1,0:T(8,128)S(1)}, f32[4,128,128]{2,1,0:T(8,128)S(1)}, u32[]{:S(2)}, u32[]{:S(2)}) collective-permute-start(f32[4,128,128]{2,1,0:T(8,128)S(1)} %get-tuple-element.37), channel_id=1, source_target_pairs={{0,1},{1,0},{2,3},{3,2},{4,5},{5,4},{6,7},{7,6},{8,9},{9,8},{10,11... | collective-permute-start | bytes 786440 | tf_op jit(solution)/shard_map/ppermute | solution.py:137
  18.7 0.2 fusion.4.refs_8_
  19.0 0.5 collective-permute-done.5.r2
  19.5 2.3 %collective-permute-done.6.r3 = f32[4,64,128]{2,1,0:T(8,128)S(1)} collective-permute-done((f32[4,64,128]{2,1,0:T(8,128)S(1)}, f32[4,64,128]{2,1,0:T(8,128)S(1)}, u32[]{:S(2)}, u32[]{:S(2)}) %collective-permute-start.6) | collective-permute-done | bytes 131104 | tf_op jit(solution)/shard_map/ppermute | solution.py:137
  21.8 4.1 %collective-permute-done.3.got = f32[4,128,128]{2,1,0:T(8,128)S(1)} collective-permute-done((f32[4,128,128]{2,1,0:T(8,128)S(1)}, f32[4,128,128]{2,1,0:T(8,128)S(1)}, u32[]{:S(2)}, u32[]{:S(2)}) %collective-permute-start.3) | collective-permute-done | bytes 262176 | tf_op jit(solution)/shard_map/ppermute | solution.py:137
  25.9 0.9 %shard_map.142 = (f32[4,128,128]{2,1,0:T(8,128)S(1)}, f32[4,128,128]{2,1,0:T(8,128)S(1)}) custom-call(s32[2]{0:T(128)S(1)} %pad_add_fusion.place, f32[8,128]{1,0:T(8,128)S(1)} %get-tuple-element.43.ids, f32[4,64,128]{2,1,0:T(8,128)S(1)} %get-tuple-element.44.r0, f32[4,64,128]{2,1,0:T(8,128)S(1)} %collective-permute-done.4.r1, ...), custom_call_target="tpu_custom_call" | custom-call | tf_op jit(solution)/shard_map/pallas_call | solution.py:41
  26.7 0.0 copy-start.12
  26.8 1.8 %collective-permute-start.10 = (f32[4,128,128]{2,1,0:T(8,128)S(1)}, f32[4,128,128]{2,1,0:T(8,128)S(1)}, u32[]{:S(2)}, u32[]{:S(2)}) collective-permute-start(f32[4,128,128]{2,1,0:T(8,128)S(1)} %get-tuple-element.55), channel_id=1, source_target_pairs={{0,1},{1,0},{2,3},{3,2},{4,5},{5,4},{6,7},{7,6},{8,9},{9,8},{10,11... | collective-permute-start | bytes 786440 | tf_op jit(solution)/shard_map/ppermute | solution.py:137
  28.6 0.1 iota_compare_fusion.2
  28.6 0.1 lt.15
  28.7 0.6 shard_map.143
  29.3 0.0 copy-start.11
  29.3 1.6 %collective-permute-start.7 = (f32[128,128]{1,0:T(8,128)S(1)}, f32[128,128]{1,0:T(8,128)S(1)}, u32[]{:S(2)}, u32[]{:S(2)}) collective-permute-start(f32[128,128]{1,0:T(8,128)S(1)} %get-tuple-element.51), channel_id=1, source_target_pairs={{0,8},{2,10},{4,12},{6,14},{8,0},{10,2},{12,4},{14,6},{16,24},{18,... | collective-permute-start | bytes 196616 | tf_op jit(solution)/shard_map/ppermute | solution.py:137
  31.0 2.6 %collective-permute-start.8 = (f32[128,128]{1,0:T(8,128)S(1)}, f32[128,128]{1,0:T(8,128)S(1)}, u32[]{:S(2)}, u32[]{:S(2)}) collective-permute-start(f32[128,128]{1,0:T(8,128)S(1)} %get-tuple-element.52), channel_id=1, source_target_pairs={{0,16},{2,18},{4,20},{6,22},{8,24},{10,26},{12,28},{14,30},{16,0},... | collective-permute-start | bytes 196616 | tf_op jit(solution)/shard_map/ppermute | solution.py:137
  33.6 0.4 collective-permute-start.9
  33.9 1.0 %collective-permute-done.10.got = f32[4,128,128]{2,1,0:T(8,128)S(1)} collective-permute-done((f32[4,128,128]{2,1,0:T(8,128)S(1)}, f32[4,128,128]{2,1,0:T(8,128)S(1)}, u32[]{:S(2)}, u32[]{:S(2)}) %collective-permute-start.10) | collective-permute-done | bytes 262176 | tf_op jit(solution)/shard_map/ppermute | solution.py:137
  34.9 0.6 shard_map.144
  35.5 1.9 %collective-permute-start.11 = (f32[128,128]{1,0:T(8,128)S(1)}, f32[128,128]{1,0:T(8,128)S(1)}, u32[]{:S(2)}, u32[]{:S(2)}) collective-permute-start(f32[128,128]{1,0:T(8,128)S(1)} %get-tuple-element.57), channel_id=1, source_target_pairs={{0,8},{2,10},{4,12},{6,14},{8,0},{10,2},{12,4},{14,6},{16,24},{18,... | collective-permute-start | bytes 196616 | tf_op jit(solution)/shard_map/ppermute | solution.py:137
  37.3 2.6 %collective-permute-start.12 = (f32[128,128]{1,0:T(8,128)S(1)}, f32[128,128]{1,0:T(8,128)S(1)}, u32[]{:S(2)}, u32[]{:S(2)}) collective-permute-start(f32[128,128]{1,0:T(8,128)S(1)} %get-tuple-element.58), channel_id=1, source_target_pairs={{0,16},{2,18},{4,20},{6,22},{8,24},{10,26},{12,28},{14,30},{16,0},... | collective-permute-start | bytes 196616 | tf_op jit(solution)/shard_map/ppermute | solution.py:137
  39.9 0.1 fusion.3.refs_12_
  40.1 0.9 %collective-permute-done.11.refs_5_ = f32[128,128]{1,0:T(8,128)S(1)} collective-permute-done((f32[128,128]{1,0:T(8,128)S(1)}, f32[128,128]{1,0:T(8,128)S(1)}, u32[]{:S(2)}, u32[]{:S(2)}) %collective-permute-start.11) | collective-permute-done | bytes 65568 | tf_op jit(solution)/shard_map/ppermute | solution.py:137
  40.9 3.0 %collective-permute-done.12.refs_6_ = f32[128,128]{1,0:T(8,128)S(1)} collective-permute-done((f32[128,128]{1,0:T(8,128)S(1)}, f32[128,128]{1,0:T(8,128)S(1)}, u32[]{:S(2)}, u32[]{:S(2)}) %collective-permute-start.12) | collective-permute-done | bytes 65568 | tf_op jit(solution)/shard_map/ppermute | solution.py:137
  44.0 2.0 %collective-permute-done.13.refs_7_ = f32[128,128]{1,0:T(8,128)S(1)} collective-permute-done((f32[128,128]{1,0:T(8,128)S(1)}, f32[128,128]{1,0:T(8,128)S(1)}, u32[]{:S(2)}, u32[]{:S(2)}) %collective-permute-start.13) | collective-permute-done | bytes 65568 | tf_op jit(solution)/shard_map/ppermute | solution.py:137
  46.0 1.2 %shard_map.145 = (f32[128,256]{1,0:T(8,128)}, f32[16,16,256]{2,1,0:T(8,128)}) custom-call(f32[128,128]{1,0:T(8,128)S(1)} %get-tuple-element.50.refs_0_, f32[128,128]{1,0:T(8,128)S(1)} %collective-permute-done.7.refs_1_, f32[128,128]{1,0:T(8,128)S(1)} %collective-permute-done.8.refs_2_, f32[128,128]{1,0:T(8,128)S(1)} %collective-permute-done.9.refs_3_, ...), custom_call_target="tpu_custom_call" | custom-call | tf_op jit(solution)/shard_map/pallas_call | solution.py:41
  47.2 3.7 %all-to-all-start = ((f32[16,16,256]{2,1,0:T(8,128)}), f32[16,16,256]{2,1,0:T(8,128)S(1)}, u32[]{:S(2)}, u32[]{:S(2)}) async-start(f32[16,16,256]{2,1,0:T(8,128)} %get-tuple-element.61), calls=%async_computation | async-start | bytes 524288 | tf_op jit(solution)/shard_map/all_to_all | solution.py:141
  51.0 0.0 copy-start.2
  51.0 0.9 %copy-done.2 = f32[256,256]{1,0:T(8,128)S(1)} copy-done((f32[256,256]{1,0:T(8,128)S(1)}, f32[256,256]{1,0:T(8,128)}, u32[]{:S(2)}) %copy-start.2) | copy-done | bytes 262168
  51.9 0.3 fusion.5.own
  52.2 8.7 %all-to-all-done = f32[16,16,256]{2,1,0:T(8,128)S(1)} async-done(((f32[16,16,256]{2,1,0:T(8,128)}), f32[16,16,256]{2,1,0:T(8,128)S(1)}, u32[]{:S(2)}, u32[]{:S(2)}) %all-to-all-start) | async-done | bytes 262176 | tf_op jit(solution)/shard_map/all_to_all | solution.py:141
  60.9 1.2 %shard_map.146 = f32[256,256]{1,0:T(8,128)} custom-call(f32[256,256]{1,0:T(8,128)S(1)} %bitcast.10, bf16[256,256]{1,0:T(8,128)(2,1)S(1)} %fusion.2.incidence, f32[256,256]{1,0:T(8,128)S(1)} %fusion.5.own, f32[256,256]{1,0:T(8,128)S(1)} %copy-done.2, bf16[256,256]{1,0:T(8,128)(2,1)S(1)} %get-tuple-element.63.w_top, bf16[256,256]{1,0:T(8,128)(2,1)S(1)} %get-tuple-element.62.w_low), custom_call_target="tpu_custom_call" | custom-call | tf_op jit(solution)/shard_map/pallas_call | solution.py:41
  (25 shorter events, 0.1 us)
Async XLA Ops:
  0.6 50.4 %copy-start = (f32[256,256]{1,0:T(8,128)S(1)}, f32[256,256]{1,0:T(8,128)}, u32[]{:S(2)}) copy-start(f32[256,256]{1,0:T(8,128)} %param.24) | copy-start | bytes 786436
  0.6 0.7 %copy-start.5 = (s32[1024]{0:T(1024)S(1)}, s32[1024]{0:T(1024)}, u32[]{:S(2)}) copy-start(s32[1024]{0:T(1024)} %param.14) | copy-start | bytes 12292
  0.7 0.7 %copy-start.6 = (s32[16]{0:T(128)S(1)}, s32[16]{0:T(128)}, u32[]{:S(2)}) copy-start(s32[16]{0:T(128)} %count.1) | copy-start | bytes 196
  1.4 1.2 %copy-start.1 = (f32[1024,256]{1,0:T(8,128)S(1)}, f32[1024,256]{1,0:T(8,128)}, u32[]{:S(2)}) copy-start(f32[1024,256]{1,0:T(8,128)} %param.13) | copy-start | bytes 3145732
  2.6 0.9 %copy-start.4 = (f32[256,256]{1,0:T(8,128)S(1)}, f32[256,256]{1,0:T(8,128)}, u32[]{:S(2)}) copy-start(f32[256,256]{1,0:T(8,128)} %w.1) | copy-start | bytes 786436
  5.7 5.2 %collective-permute-start = (f32[4,72,128]{2,1,0:T(8,128)S(1)}, f32[4,72,128]{2,1,0:T(8,128)S(1)}, u32[]{:S(2)}, u32[]{:S(2)}) collective-permute-start(f32[4,72,128]{2,1,0:T(8,128)S(1)} %get-tuple-element.33), channel_id=1, source_target_pairs={{0,2},{2,0},{4,6},{6,4},{8,10},{10,8},{12,14},{14,12},{16,18},{18,... | collective-permute-start | bytes 442376 | tf_op jit(solution)/shard_map/ppermute | solution.py:137
  6.3 7.3 %collective-permute-start.1 = (f32[4,72,128]{2,1,0:T(8,128)S(1)}, f32[4,72,128]{2,1,0:T(8,128)S(1)}, u32[]{:S(2)}, u32[]{:S(2)}) collective-permute-start(f32[4,72,128]{2,1,0:T(8,128)S(1)} %get-tuple-element.34), channel_id=1, source_target_pairs={{0,4},{2,6},{4,0},{6,2},{8,12},{10,14},{12,8},{14,10},{16,20},{18,... | collective-permute-start | bytes 442376 | tf_op jit(solution)/shard_map/ppermute | solution.py:137
  8.8 7.3 %collective-permute-start.2 = (f32[4,72,128]{2,1,0:T(8,128)S(1)}, f32[4,72,128]{2,1,0:T(8,128)S(1)}, u32[]{:S(2)}, u32[]{:S(2)}) collective-permute-start(f32[4,72,128]{2,1,0:T(8,128)S(1)} %get-tuple-element.35), channel_id=1, source_target_pairs={{0,6},{2,4},{4,2},{6,0},{8,14},{10,12},{12,10},{14,8},{16,22},{18,... | collective-permute-start | bytes 442376 | tf_op jit(solution)/shard_map/ppermute | solution.py:137
  8.9 10.1 %collective-permute-start.4 = (f32[4,64,128]{2,1,0:T(8,128)S(1)}, f32[4,64,128]{2,1,0:T(8,128)S(1)}, u32[]{:S(2)}, u32[]{:S(2)}) collective-permute-start(f32[4,64,128]{2,1,0:T(8,128)S(1)} %get-tuple-element.39), channel_id=1, source_target_pairs={{0,2},{2,0},{4,6},{6,4},{8,10},{10,8},{12,14},{14,12},{16,18},{18,... | collective-permute-start | bytes 393224 | tf_op jit(solution)/shard_map/ppermute | solution.py:137
  9.0 10.5 %collective-permute-start.5 = (f32[4,64,128]{2,1,0:T(8,128)S(1)}, f32[4,64,128]{2,1,0:T(8,128)S(1)}, u32[]{:S(2)}, u32[]{:S(2)}) collective-permute-start(f32[4,64,128]{2,1,0:T(8,128)S(1)} %get-tuple-element.40), channel_id=1, source_target_pairs={{0,4},{2,6},{4,0},{6,2},{8,12},{10,14},{12,8},{14,10},{16,20},{18,... | collective-permute-start | bytes 393224 | tf_op jit(solution)/shard_map/ppermute | solution.py:137
  11.0 10.8 %collective-permute-start.6 = (f32[4,64,128]{2,1,0:T(8,128)S(1)}, f32[4,64,128]{2,1,0:T(8,128)S(1)}, u32[]{:S(2)}, u32[]{:S(2)}) collective-permute-start(f32[4,64,128]{2,1,0:T(8,128)S(1)} %get-tuple-element.41), channel_id=1, source_target_pairs={{0,6},{2,4},{4,2},{6,0},{8,14},{10,12},{12,10},{14,8},{16,22},{18,... | collective-permute-start | bytes 393224 | tf_op jit(solution)/shard_map/ppermute | solution.py:137
  16.2 2.5 %copy-start.3 = (f32[128,256]{1,0:T(8,128)S(1)}, f32[128,256]{1,0:T(8,128)}, u32[]{:S(2)}) copy-start(f32[128,256]{1,0:T(8,128)} %refs_9_.1) | copy-start | bytes 393220
  16.2 2.5 %copy-start.7 = (f32[256,256]{1,0:T(8,128)S(1)}, f32[256,256]{1,0:T(8,128)}, u32[]{:S(2)}) copy-start(f32[256,256]{1,0:T(8,128)} %param.22) | copy-start | bytes 786436
  17.0 1.9 %copy-start.8 = (f32[256,256]{1,0:T(8,128)S(1)}, f32[256,256]{1,0:T(8,128)}, u32[]{:S(2)}) copy-start(f32[256,256]{1,0:T(8,128)} %param.23) | copy-start | bytes 786436
  17.0 8.9 %collective-permute-start.3 = (f32[4,128,128]{2,1,0:T(8,128)S(1)}, f32[4,128,128]{2,1,0:T(8,128)S(1)}, u32[]{:S(2)}, u32[]{:S(2)}) collective-permute-start(f32[4,128,128]{2,1,0:T(8,128)S(1)} %get-tuple-element.37), channel_id=1, source_target_pairs={{0,1},{1,0},{2,3},{3,2},{4,5},{5,4},{6,7},{7,6},{8,9},{9,8},{10,11... | collective-permute-start | bytes 786440 | tf_op jit(solution)/shard_map/ppermute | solution.py:137
  26.7 1.8 %copy-start.12 = (s32[16]{0:T(128)S(1)}, s32[16]{0:T(128)}, u32[]{:S(2)}) copy-start(s32[16]{0:T(128)} %param.19) | copy-start | bytes 196
  26.8 8.1 %collective-permute-start.10 = (f32[4,128,128]{2,1,0:T(8,128)S(1)}, f32[4,128,128]{2,1,0:T(8,128)S(1)}, u32[]{:S(2)}, u32[]{:S(2)}) collective-permute-start(f32[4,128,128]{2,1,0:T(8,128)S(1)} %get-tuple-element.55), channel_id=1, source_target_pairs={{0,1},{1,0},{2,3},{3,2},{4,5},{5,4},{6,7},{7,6},{8,9},{9,8},{10,11... | collective-permute-start | bytes 786440 | tf_op jit(solution)/shard_map/ppermute | solution.py:137
  29.3 1.7 %copy-start.11 = (s32[256]{0:T(256)S(1)}, s32[256]{0:T(256)}, u32[]{:S(2)}) copy-start(s32[256]{0:T(256)} %param.18) | copy-start | bytes 3076
  29.3 10.6 %collective-permute-start.7 = (f32[128,128]{1,0:T(8,128)S(1)}, f32[128,128]{1,0:T(8,128)S(1)}, u32[]{:S(2)}, u32[]{:S(2)}) collective-permute-start(f32[128,128]{1,0:T(8,128)S(1)} %get-tuple-element.51), channel_id=1, source_target_pairs={{0,8},{2,10},{4,12},{6,14},{8,0},{10,2},{12,4},{14,6},{16,24},{18,... | collective-permute-start | bytes 196616 | tf_op jit(solution)/shard_map/ppermute | solution.py:137
  31.0 9.1 %collective-permute-start.8 = (f32[128,128]{1,0:T(8,128)S(1)}, f32[128,128]{1,0:T(8,128)S(1)}, u32[]{:S(2)}, u32[]{:S(2)}) collective-permute-start(f32[128,128]{1,0:T(8,128)S(1)} %get-tuple-element.52), channel_id=1, source_target_pairs={{0,16},{2,18},{4,20},{6,22},{8,24},{10,26},{12,28},{14,30},{16,0},... | collective-permute-start | bytes 196616 | tf_op jit(solution)/shard_map/ppermute | solution.py:137
  33.6 6.5 %collective-permute-start.9 = (f32[128,128]{1,0:T(8,128)S(1)}, f32[128,128]{1,0:T(8,128)S(1)}, u32[]{:S(2)}, u32[]{:S(2)}) collective-permute-start(f32[128,128]{1,0:T(8,128)S(1)} %get-tuple-element.53), channel_id=1, source_target_pairs={{0,24},{2,26},{4,28},{6,30},{8,16},{10,18},{12,20},{14,22},{16,8},... | collective-permute-start | bytes 196616 | tf_op jit(solution)/shard_map/ppermute | solution.py:137
  35.5 5.5 %collective-permute-start.11 = (f32[128,128]{1,0:T(8,128)S(1)}, f32[128,128]{1,0:T(8,128)S(1)}, u32[]{:S(2)}, u32[]{:S(2)}) collective-permute-start(f32[128,128]{1,0:T(8,128)S(1)} %get-tuple-element.57), channel_id=1, source_target_pairs={{0,8},{2,10},{4,12},{6,14},{8,0},{10,2},{12,4},{14,6},{16,24},{18,... | collective-permute-start | bytes 196616 | tf_op jit(solution)/shard_map/ppermute | solution.py:137
  37.3 6.6 %collective-permute-start.12 = (f32[128,128]{1,0:T(8,128)S(1)}, f32[128,128]{1,0:T(8,128)S(1)}, u32[]{:S(2)}, u32[]{:S(2)}) collective-permute-start(f32[128,128]{1,0:T(8,128)S(1)} %get-tuple-element.58), channel_id=1, source_target_pairs={{0,16},{2,18},{4,20},{6,22},{8,24},{10,26},{12,28},{14,30},{16,0},... | collective-permute-start | bytes 196616 | tf_op jit(solution)/shard_map/ppermute | solution.py:137
  39.9 6.1 %collective-permute-start.13 = (f32[128,128]{1,0:T(8,128)S(1)}, f32[128,128]{1,0:T(8,128)S(1)}, u32[]{:S(2)}, u32[]{:S(2)}) collective-permute-start(f32[128,128]{1,0:T(8,128)S(1)} %get-tuple-element.59), channel_id=1, source_target_pairs={{0,24},{2,26},{4,28},{6,30},{8,16},{10,18},{12,20},{14,22},{16,8},... | collective-permute-start | bytes 196616 | tf_op jit(solution)/shard_map/ppermute | solution.py:137
  47.2 3.7 %copy-start.10 = (s32[256]{0:T(256)S(1)}, s32[256]{0:T(256)}, u32[]{:S(2)}) copy-start(s32[256]{0:T(256)} %param.20) | copy-start | bytes 3076
  47.2 3.7 %copy-start.9 = (f32[256,256]{1,0:T(8,128)S(1)}, f32[256,256]{1,0:T(8,128)}, u32[]{:S(2)}) copy-start(f32[256,256]{1,0:T(8,128)} %param.25) | copy-start | bytes 786436
  47.2 13.7 %all-to-all-start = ((f32[16,16,256]{2,1,0:T(8,128)}), f32[16,16,256]{2,1,0:T(8,128)S(1)}, u32[]{:S(2)}, u32[]{:S(2)}) async-start(f32[16,16,256]{2,1,0:T(8,128)} %get-tuple-element.61), calls=%async_computation | async-start | bytes 524288 | tf_op jit(solution)/shard_map/all_to_all | solution.py:141
  51.0 1.0 %copy-start.2 = (f32[256,256]{1,0:T(8,128)S(1)}, f32[256,256]{1,0:T(8,128)}, u32[]{:S(2)}) copy-start(f32[256,256]{1,0:T(8,128)} %table.1) | copy-start | bytes 786436

commit v5 on v3

--- a/solution.py
+++ b/solution.py
@@ -51,68 +51,91 @@
     return lax.broadcasted_iota(jnp.int32, (1, LANES), 1)
 
 
-def message_kernel(place, count, tx, ids, w, p0, p1, p2, p3, q0, q1, q2, q3):
-    near = place[0] & 3
-    w_top, w_low = split(w[...])
-    slots = q0.shape[1]
+def message_kernel(place, count, tx, ids, w_top, w_low, own, core, l2, l3, r2, r3, b2, b3):
+    near, far = place[0] & 3, place[0] >> 2
+    slots = tx.shape[0] // 16
     lane = lanes()
-    for m, (first, second) in enumerate(((p0, q0), (p1, q1), (p2, q2), (p3, q3))):
+    top, low = w_top[...], w_low[...]
+    for m in (2, 3, 1, 0):
         c = near ^ m
-        x = jnp.concatenate([tx[pl.ds(pl.multiple_of((4 * z + c) * slots, slots), slots), :] for z in range(4)], 0)
-        y = jnp.maximum(dot3(x, w_top, w_low), 0.0)
-        first[:, :slots, :] = y[:, :LANES].reshape(4, slots, LANES)
-        second[...] = y[:, LANES:].reshape(4, slots, LANES)
-        for z in range(4):
-            row = ids[pl.ds(2 * z + (c >> 1), 1), :]
+        buckets = [4 * (far ^ k) + c for k in (2, 3, 1, 0)]
+        x = jnp.concatenate([tx[pl.ds(pl.multiple_of(b * slots, slots), slots), :] for b in buckets], 0)
+        y = jnp.maximum(dot3(x, top, low), 0.0).reshape(4, slots, 2 * LANES)
+        if m < 2:
+            outs = ((own, core)[m], 0, 0), ((own, core)[m], 0, slots), ((own, core)[m], 2, 0)
+        else:
+            outs = ((l2, l3)[m - 2], 0, 0), ((r2, r3)[m - 2], 0, 0), ((b2, b3)[m - 2], 0, 0)
+        (left, _, _), (right, _, at), (both, first, _) = outs
+        left[:2, :slots, :] = y[:2, :, :LANES]
+        right[:2, at : at + slots, :] = y[:2, :, LANES:]
+        both[first : first + 2, :slots, :] = y[2:, :, :LANES]
+        both[first : first + 2, slots : 2 * slots, :] = y[2:, :, LANES:]
+        for i, b in enumerate(buckets):
+            row = ids[pl.ds(b >> 1, 1), :]
             turned = pltpu.roll(row, slots, 1)
             twice = jnp.where((lane >= slots).astype(jnp.int32) == (c & 1), row, turned)
-            twice = jnp.where((lane & (slots - 1)) < count[4 * z + c], twice, -1).astype(f32)
-            first[z, slots:, :] = jnp.broadcast_to(twice, (PAD, LANES))
-
-
-def sums(place, rows, blocks, send, keep):
+            twice = jnp.where((lane & (slots - 1)) < count[b], twice, -1).astype(f32)
+            target, z = (left, i) if i < 2 else (both, first + i - 2)
+            target[z, target.shape[1] - PAD :, :] = jnp.broadcast_to(twice, (PAD, LANES))
+
+
+def id_rows(blocks, starts):
+    lane = lanes()
+    rows = []
+    for z in range(2):
+        one = [block[start + z, pl.ds(block.shape[1] - PAD, 1), :] for block, start in zip(blocks, starts)]
+        rows.append([jnp.where(lane < LANES // 2, one[i], one[i + 1]) for i in (0, 2)])
+    return rows
+
+
+def sums(place, rows, sides, send, keep):
     mine = send.shape[1]
     slots = LANES // 2
     own = place[1]
     row = lax.broadcasted_iota(jnp.int32, (2 * mine, LANES), 0)
     target = jnp.where(row < mine, row + (1 - own) * mine, row - mine + own * mine).astype(f32)
-    for z in range(4):
+    for z in range(2):
         picks = jnp.concatenate([(r == target).astype(bf16) for r in rows[z]], 1)
-        top, low = split(jnp.concatenate([block[z, :slots, :] for block in blocks], 0))
-        total = mm(picks, jnp.concatenate([top, low], 1))
-        total = total[:, :LANES] + total[:, LANES:]
-        send[z] = total[:mine]
-        keep[z] = total[mine:]
-
-
-def first_sum_kernel(place, r0, r1, r2, r3, send, keep, ids):
-    slots = r0.shape[1] - PAD
-    lane = lanes()
-    rows = []
-    for z in range(4):
-        one = [block[z, pl.ds(slots, 1), :] for block in (r0, r1, r2, r3)]
-        rows.append([jnp.where(lane < slots, one[i], one[i + 1]) for i in (0, 2)])
+        for side, blocks in enumerate(sides):
+            x = jnp.concatenate([block[first + z, at : at + slots, :] for block, first, at in blocks], 0)
+            total = mm(picks, jnp.concatenate(split(x), 1))
+            total = total[:, :LANES] + total[:, LANES:]
+            send[z, :, side * LANES : (side + 1) * LANES] = total[:mine]
+            keep[z, :, side * LANES : (side + 1) * LANES] = total[mine:]
+
+
+def left_kernel(place, own, core, l2, l3, send, keep, ids):
+    blocks = (own, core, l2, l3)
+    rows = id_rows(blocks, (0, 0, 0, 0))
+    for z in range(2):
         for i in range(2):
             ids[pl.ds(2 * z + i, 1), :] = rows[z][i]
-    sums(place, rows, (r0, r1, r2, r3), send, keep)
-
-
-def second_sum_kernel(place, ids, r0, r1, r2, r3, send, keep):
-    rows = [[ids[pl.ds(2 * z + i, 1), :] for i in range(2)] for z in range(4)]
-    sums(place, rows, (r0, r1, r2, r3), send, keep)
-
-
-def pair_kernel(place, keep, got, b0, b1, b2, b3):
-    far = place[0] >> 2
-    for k, out in enumerate((b0, b1, b2, b3)):
-        out[...] = keep[far ^ k] + got[far ^ k]
+    sums(place, rows, [[(block, 0, 0) for block in blocks]], send, keep)
+
+
+def right_kernel(place, ids, own, core, r2, r3, send, keep):
+    rows = [[ids[pl.ds(2 * z + i, 1), :] for i in range(2)] for z in range(2)]
+    slots = r2.shape[1]
+    sums(place, rows, [[(own, 0, slots), (core, 0, slots), (r2, 0, 0), (r3, 0, 0)]], send, keep)
+
+
+def both_kernel(place, own, core, b2, b3, send, keep):
+    blocks, starts = (own, core, b2, b3), (2, 2, 0, 0)
+    slots = LANES // 2
+    sides = [[(block, first, at) for block, first in zip(blocks, starts)] for at in (0, slots)]
+    sums(place, id_rows(blocks, starts), sides, send, keep)
+
+
+def pair_kernel(keep, got, first, second):
+    first[...] = keep[0] + got[0]
+    second[...] = keep[1] + got[1]
 
 
 def update_kernel(*refs):
     parts, (own, table, w_top, w_low, picks, new, listed) = refs[:-7], refs[-7:]
-    n = len(parts) // 2
-    halves = [sum(part[...] for part in side) for side in (parts[:n], parts[n:])]
-    gathered = jnp.concatenate(halves, 1)
+    wide = [part[...] for part in parts if part.shape[1] != LANES]
+    left, right = (sum(part[...] for part in side) for side in (parts[:2], parts[2:4]))
+    gathered = jnp.concatenate([left, right], 1) + sum(wide)
     fresh = table[...] + jnp.maximum(own[...] + dot3(gathered, w_top[...], w_low[...]), 0.0)
     new[...] = fresh
     listed[...] = dot2(picks[...], fresh).reshape(listed.shape)
@@ -134,24 +157,43 @@
 def gathered_by_permutes(place, transactions, tx_product, tx_count, w_msg, mine):
     peers = 16
     slots = transactions.shape[0] // peers
-    block = (4, mine, LANES)
-    out = call(
+    own, core, *out = call(
         message_kernel,
-        [(4, slots + PAD, LANES)] * 4 + [(4, slots, LANES)] * 4,
-        (transactions, tx_product.reshape(-1, LANES), w_msg),
+        [(4, 2 * slots + PAD, LANES)] * 2
+        + [(2, slots + PAD, LANES)] * 2
+        + [(2, slots, LANES)] * 2
+        + [(2, 2 * slots + PAD, LANES)] * 2,
+        (transactions, tx_product.reshape(-1, LANES), *split_outside(w_msg)),
         smem=(place, tx_count),
     )
+    half, whole = (2, mine, LANES), (2, mine, 2 * LANES)
 
     def near(blocks):
-        return [blocks[0]] + [swap(blocks[m], "hash", m, peers) for m in (1, 2, 3)]
-
-    def rest(send, keep):
-        parts = call(pair_kernel, [(mine, LANES)] * 4, (keep, swap(send, "tm", 1, 2)), smem=(place,))
-        return [parts[0]] + [swap(parts[k], "hash", 4 * k, peers) for k in (1, 2, 3)]
-
-    *first, ids = call(first_sum_kernel, [block, block, (8, LANES)], near(out[:4]), smem=(place,))
-    second = call(second_sum_kernel, [block, block], (ids, *near(out[4:])), smem=(place,))
-    return rest(*first) + rest(*second)
+        return [swap(block, "hash", mask, peers) for block, mask in zip(blocks, (2, 3))]
+
+    def pair(keep, got):
+        return call(pair_kernel, [keep.shape[1:]] * 2, (keep, got))
+
+    def after(value, ready):
+        return lax.optimization_barrier((*value, *ready))[: len(value)]
+
+    def across(parts):
+        return [swap(part, "hash", mask, peers) for part, mask in zip(parts, (8, 12))]
+
+    left, right = near(out[:2]), near(out[2:4])
+    core = swap(core, "hash", 1, peers)
+    both = near(after(out[4:], left))
+    send_l, keep_l, ids = call(left_kernel, [half, half, (8, LANES)], (own, core, *left), smem=(place,))
+    got_l = swap(send_l, "tm", 1, 2)
+    send_r, keep_r = call(right_kernel, [half, half], (ids, own, core, *after(right, [got_l])), smem=(place,))
+    got_r = swap(send_r, "tm", 1, 2)
+    parts_l = pair(keep_l, *after([got_l], [send_r]))
+    far_l = across(parts_l)
+    send_b, keep_b = call(both_kernel, [whole, whole], (own, core, *after(both, [got_r, *parts_l])), smem=(place,))
+    got_b = swap(send_b, "tm", 1, 2)
+    far_r = across(pair(keep_r, *after([got_r], [send_b])))
+    next_to, mine_b = pair(keep_b, *after([got_b], far_l))
+    return [*far_l, *far_r, swap(next_to, "hash", 4, peers), mine_b]
 
 
 def gathered_plainly(transactions, tx_product, tx_count, w_msg, mine):
@@ -170,7 +212,8 @@
 
     parts = lax.map(part_sum, jnp.arange(pair)).reshape(pair * mine, width)
     total = lax.psum_scatter(parts, "tm", scatter_dimension=0, tiled=True)
-    return [total[:, :LANES], total[:, LANES:]]
+    zero = jnp.zeros((mine, LANES), f32)
+    return [zero, zero, zero, zero, total]
 
 
 def local(

time: 63.9 us -> 62.5 us (0.978)
  waiting for transfers between devices: 30.8 us -> 23.5 us
  starting transfers between devices: 20.6 us -> 27 us
  local copies, waits for them, and re-layouts: 4 us -> 2.9 us
  other arithmetic: 0.35 us -> 1.38 us
    ppermute x14 -> x15, waiting for transfers between devices: 22.1 us -> 14.7 us  [swap(): return lax.ppermute(x, axis, [(i, i ^ mask) for i in range(size)])]
    ppermute x14 -> x15, starting transfers between devices: 16.5 us -> 20.5 us  [swap(): return lax.ppermute(x, axis, [(i, i ^ mask) for i in range(size)])]
    all_to_all x1, starting transfers between devices: 4.11 us -> 6.54 us  [spread(): return lax.all_to_all(x, 'hash', split_axis=0, concat_axis=0, tiled=True)]
    unnamed x26 -> x24, local copies, waits for them, and re-layouts: 3.91 us -> 2.81 us
    convert_element_type x2 -> x3, other arithmetic: 0.07 us -> 1.09 us  [split_outside(): return (top.astype(bf16), (x - top).astype(bf16))]
    pallas_call x7 -> x9, Pallas kernels: 6.45 us -> 6.05 us  [call(): pl.pallas_call(kernel, out_shape=[jax.ShapeDtypeStruct(s, f32) for s in o...]
  transfers between devices with their start and end apart: 15 -> 16, of which waited for: 9 -> 10; matrix products, arithmetic and copies ran while one was open for 1% -> 1% of each run, Pallas kernels for 3% -> 3%
where the time goes in v5:
time: 62.5 us; the launch traced here: 62.1 us
  starting transfers between devices  27 us (43%)
  waiting for transfers between devices  23.5 us (38%)
  Pallas kernels  6.05 us (10%)
  local copies, waits for them, and re-layouts  2.9 us (5%)
  other arithmetic  1.38 us (2%)
  between operations  0.82 us (1%)
    ppermute x15, starting transfers between devices, swap(): return lax.ppermute(x, axis, [(i, i ^ mask) for i in range(size)])  20.5 us
    ppermute x15, waiting for transfers between devices, swap(): return lax.ppermute(x, axis, [(i, i ^ mask) for i in range(size)])  14.7 us
    all_to_all x1, waiting for transfers between devices, spread(): return lax.all_to_all(x, 'hash', split_axis=0, concat_axis=0, tiled=True)  8.76 us
    all_to_all x1, starting transfers between devices, spread(): return lax.all_to_all(x, 'hash', split_axis=0, concat_axis=0, tiled=True)  6.54 us
    pallas_call x9, Pallas kernels, call(): pl.pallas_call(kernel, out_shape=[jax.ShapeDtypeStruct(s, f32) for s in o...  6.05 us
    unnamed x24, local copies, waits for them, and re-layouts  2.81 us
  transfers between devices with their start and end apart: 16, of which 10 were waited for; matrix products, arithmetic and copies ran while one was open for 1% of the time, Pallas kernels for 3%

profile of v5, /device:TPU:0, one launch (start us, length us, event | category | flops | bytes accessed | tf_op | source)
XLA Modules:
  0.0 62.1 jit_solution(13904122506814290264)
XLA Ops:
  0.6 0.0 copy-start
  0.7 1.0 %fusion = (bf16[256,256]{1,0:T(8,128)(2,1)S(1)}, bf16[256,256]{1,0:T(8,128)(2,1)S(1)}) fusion(f32[256,256]{1,0:T(8,128)} %param.21), kind=kLoop, calls=%fused_computation.6 | loop fusion | flops 262144 | bytes 524288 | tf_op jit(solution)/shard_map/convert_element_type | solution.py:21
  1.7 0.0 copy-start.4
  1.7 0.1 pad_add_fusion.place
  1.8 0.6 copy-done.4
  2.4 0.1 copy-done.5
  2.4 1.2 %copy-done.1 = f32[1024,256]{1,0:T(8,128)S(1)} copy-done((f32[1024,256]{1,0:T(8,128)S(1)}, f32[1024,256]{1,0:T(8,128)}, u32[]{:S(2)}) %copy-start.1) | copy-done | bytes 1048600
  3.7 1.1 %shard_map.140 = (f32[4,136,128]{2,1,0:T(8,128)S(1)}, f32[4,136,128]{2,1,0:T(8,128)S(1)}, f32[2,72,128]{2,1,0:T(8,128)S(1)}, f32[2,72,128]{2,1,0:T(8,128)S(1)}, ...) custom-call(s32[2]{0:T(128)S(1)} %pad_add_fusion.place, ...), custom_call_target="tpu_custom_call" | custom-call | tf_op jit(solution)/shard_map/pallas_call | solution.py:41
  4.8 0.5 collective-permute-start
  5.3 2.6 %collective-permute-start.1 = (f32[2,72,128]{2,1,0:T(8,128)S(1)}, f32[2,72,128]{2,1,0:T(8,128)S(1)}, u32[]{:S(2)}, u32[]{:S(2)}) collective-permute-start(f32[2,72,128]{2,1,0:T(8,128)S(1)} %get-tuple-element.36), channel_id=1, source_target_pairs={{0,4},{2,6},{4,0},{6,2},{8,12},{10,14},{12,8},{14,10},{16,20},{18,... | collective-permute-start | bytes 221192 | tf_op jit(solution)/shard_map/ppermute | solution.py:150
  7.9 0.1 collective-permute-start.2
  7.9 1.7 %collective-permute-start.4 = (f32[2,64,128]{2,1,0:T(8,128)S(1)}, f32[2,64,128]{2,1,0:T(8,128)S(1)}, u32[]{:S(2)}, u32[]{:S(2)}) collective-permute-start(f32[2,64,128]{2,1,0:T(8,128)S(1)} %get-tuple-element.41), channel_id=1, source_target_pairs={{0,4},{2,6},{4,0},{6,2},{8,12},{10,14},{12,8},{14,10},{16,20},{18,... | collective-permute-start | bytes 196616 | tf_op jit(solution)/shard_map/ppermute | solution.py:150
  9.7 1.0 %collective-permute-done.1.l2 = f32[2,72,128]{2,1,0:T(8,128)S(1)} collective-permute-done((f32[2,72,128]{2,1,0:T(8,128)S(1)}, f32[2,72,128]{2,1,0:T(8,128)S(1)}, u32[]{:S(2)}, u32[]{:S(2)}) %collective-permute-start.1) | collective-permute-done | bytes 73760 | tf_op jit(solution)/shard_map/ppermute | solution.py:150
  10.7 1.4 %collective-permute-done.2.l3 = f32[2,72,128]{2,1,0:T(8,128)S(1)} collective-permute-done((f32[2,72,128]{2,1,0:T(8,128)S(1)}, f32[2,72,128]{2,1,0:T(8,128)S(1)}, u32[]{:S(2)}, u32[]{:S(2)}) %collective-permute-start.2) | collective-permute-done | bytes 73760 | tf_op jit(solution)/shard_map/ppermute | solution.py:150
  12.1 0.8 %shard_map.141 = (f32[2,128,128]{2,1,0:T(8,128)S(1)}, f32[2,128,128]{2,1,0:T(8,128)S(1)}, f32[8,128]{1,0:T(8,128)S(1)}) custom-call(s32[2]{0:T(128)S(1)} %pad_add_fusion.place, f32[4,136,128]{2,1,0:T(8,128)S(1)} %get-tuple-element.34.own, f32[4,136,128]{2,1,0:T(8,128)S(1)} %collective-permute-done.core, f32[2,72,128]{2,1,0:T(8,128)S(1)} %collective-permute-done.1.l2, ...), custom_call_target="tpu_custom_call" | custom-call | tf_op jit(solution)/shard_map/pallas_call | solution.py:41
  12.9 1.8 %collective-permute-start.3 = (f32[2,128,128]{2,1,0:T(8,128)S(1)}, f32[2,128,128]{2,1,0:T(8,128)S(1)}, u32[]{:S(2)}, u32[]{:S(2)}) collective-permute-start(f32[2,128,128]{2,1,0:T(8,128)S(1)} %get-tuple-element.39), channel_id=1, source_target_pairs={{0,1},{1,0},{2,3},{3,2},{4,5},{5,4},{6,7},{7,6},{8,9},{9,8},{10,11... | collective-permute-start | bytes 393224 | tf_op jit(solution)/shard_map/ppermute | solution.py:150
  14.7 0.2 fusion.5.refs_6_
  15.0 1.3 %collective-permute-start.9 = (f32[2,136,128]{2,1,0:T(8,128)S(1)}, f32[2,136,128]{2,1,0:T(8,128)S(1)}, u32[]{:S(2)}, u32[]{:S(2)}) collective-permute-start(f32[2,136,128]{2,1,0:T(8,128)S(1)} %get-tuple-element.52), channel_id=1, source_target_pairs={{0,4},{2,6},{4,0},{6,2},{8,12},{10,14},{12,8},{14,10},{16,20},{18,... | collective-permute-start | bytes 417800 | tf_op jit(solution)/shard_map/ppermute | solution.py:150
  16.3 0.1 collective-permute-start.10
  16.4 0.0 collective-permute-done.4.r2
  16.4 0.0 collective-permute-done.5.r3
  16.5 2.4 %collective-permute-done.3.got = f32[2,128,128]{2,1,0:T(8,128)S(1)} collective-permute-done((f32[2,128,128]{2,1,0:T(8,128)S(1)}, f32[2,128,128]{2,1,0:T(8,128)S(1)}, u32[]{:S(2)}, u32[]{:S(2)}) %collective-permute-start.3) | collective-permute-done | bytes 131104 | tf_op jit(solution)/shard_map/ppermute | solution.py:150
  18.9 0.8 %shard_map.142 = (f32[2,128,128]{2,1,0:T(8,128)S(1)}, f32[2,128,128]{2,1,0:T(8,128)S(1)}) custom-call(s32[2]{0:T(128)S(1)} %pad_add_fusion.place, f32[8,128]{1,0:T(8,128)S(1)} %get-tuple-element.40.ids, f32[4,136,128]{2,1,0:T(8,128)S(1)} %get-tuple-element.34.own, f32[4,136,128]{2,1,0:T(8,128)S(1)} %collective-permute-done.core, ...), custom_call_target="tpu_custom_call" | custom-call | tf_op jit(solution)/shard_map/pallas_call | solution.py:41
  19.6 1.6 %collective-permute-start.8 = (f32[2,128,128]{2,1,0:T(8,128)S(1)}, f32[2,128,128]{2,1,0:T(8,128)S(1)}, u32[]{:S(2)}, u32[]{:S(2)}) collective-permute-start(f32[2,128,128]{2,1,0:T(8,128)S(1)} %get-tuple-element.45), channel_id=1, source_target_pairs={{0,1},{1,0},{2,3},{3,2},{4,5},{5,4},{6,7},{7,6},{8,9},{9,8},{10,11... | collective-permute-start | bytes 393224 | tf_op jit(solution)/shard_map/ppermute | solution.py:150
  21.3 0.3 collective-permute-done.9.b2
  21.6 1.3 %collective-permute-done.10.b3 = f32[2,136,128]{2,1,0:T(8,128)S(1)} collective-permute-done((f32[2,136,128]{2,1,0:T(8,128)S(1)}, f32[2,136,128]{2,1,0:T(8,128)S(1)}, u32[]{:S(2)}, u32[]{:S(2)}) %collective-permute-start.10) | collective-permute-done | bytes 139296 | tf_op jit(solution)/shard_map/ppermute | solution.py:150
  22.8 2.0 %collective-permute-done.8.got = f32[2,128,128]{2,1,0:T(8,128)S(1)} collective-permute-done((f32[2,128,128]{2,1,0:T(8,128)S(1)}, f32[2,128,128]{2,1,0:T(8,128)S(1)}, u32[]{:S(2)}, u32[]{:S(2)}) %collective-permute-start.8) | collective-permute-done | bytes 131104 | tf_op jit(solution)/shard_map/ppermute | solution.py:150
  24.8 0.9 %shard_map.144 = (f32[2,128,256]{2,1,0:T(8,128)S(1)}, f32[2,128,256]{2,1,0:T(8,128)S(1)}) custom-call(s32[2]{0:T(128)S(1)} %pad_add_fusion.place, f32[4,136,128]{2,1,0:T(8,128)S(1)} %get-tuple-element.34.own, f32[4,136,128]{2,1,0:T(8,128)S(1)} %collective-permute-done.core, f32[2,136,128]{2,1,0:T(8,128)S(1)} %collective-permute-done.9.b2, ...), custom_call_target="tpu_custom_call" | custom-call | tf_op jit(solution)/shard_map/pallas_call | solution.py:41
  25.7 0.0 copy-start.11
  25.7 1.4 %collective-permute-start.13 = (f32[2,128,256]{2,1,0:T(8,128)S(1)}, f32[2,128,256]{2,1,0:T(8,128)S(1)}, u32[]{:S(2)}, u32[]{:S(2)}) collective-permute-start(f32[2,128,256]{2,1,0:T(8,128)S(1)} %get-tuple-element.56), channel_id=1, source_target_pairs={{0,1},{1,0},{2,3},{3,2},{4,5},{5,4},{6,7},{7,6},{8,9},{9,8},{10,11... | collective-permute-start | bytes 786440 | tf_op jit(solution)/shard_map/ppermute | solution.py:150
  27.1 0.1 iota_compare_fusion.2
  27.2 0.1 lt.15
  27.3 2.6 %collective-permute-start.6 = (f32[128,128]{1,0:T(8,128)S(1)}, f32[128,128]{1,0:T(8,128)S(1)}, u32[]{:S(2)}, u32[]{:S(2)}) collective-permute-start(f32[128,128]{1,0:T(8,128)S(1)} %get-tuple-element.47), channel_id=1, source_target_pairs={{0,16},{2,18},{4,20},{6,22},{8,24},{10,26},{12,28},{14,30},{16,0},... | collective-permute-start | bytes 196616 | tf_op jit(solution)/shard_map/ppermute | solution.py:150
  29.9 1.4 %collective-permute-start.7 = (f32[128,128]{1,0:T(8,128)S(1)}, f32[128,128]{1,0:T(8,128)S(1)}, u32[]{:S(2)}, u32[]{:S(2)}) collective-permute-start(f32[128,128]{1,0:T(8,128)S(1)} %get-tuple-element.48), channel_id=1, source_target_pairs={{0,24},{2,26},{4,28},{6,30},{8,16},{10,18},{12,20},{14,22},{16,8},... | collective-permute-start | bytes 196616 | tf_op jit(solution)/shard_map/ppermute | solution.py:150
  31.3 1.7 %collective-permute-start.11 = (f32[128,128]{1,0:T(8,128)S(1)}, f32[128,128]{1,0:T(8,128)S(1)}, u32[]{:S(2)}, u32[]{:S(2)}) collective-permute-start(f32[128,128]{1,0:T(8,128)S(1)} %get-tuple-element.58), channel_id=1, source_target_pairs={{0,16},{2,18},{4,20},{6,22},{8,24},{10,26},{12,28},{14,30},{16,0},... | collective-permute-start | bytes 196616 | tf_op jit(solution)/shard_map/ppermute | solution.py:150
  33.0 0.9 %collective-permute-start.12 = (f32[128,128]{1,0:T(8,128)S(1)}, f32[128,128]{1,0:T(8,128)S(1)}, u32[]{:S(2)}, u32[]{:S(2)}) collective-permute-start(f32[128,128]{1,0:T(8,128)S(1)} %get-tuple-element.59), channel_id=1, source_target_pairs={{0,24},{2,26},{4,28},{6,30},{8,16},{10,18},{12,20},{14,22},{16,8},... | collective-permute-start | bytes 196616 | tf_op jit(solution)/shard_map/ppermute | solution.py:150
  33.9 3.5 %collective-permute-done.6.refs_0_ = f32[128,128]{1,0:T(8,128)S(1)} collective-permute-done((f32[128,128]{1,0:T(8,128)S(1)}, f32[128,128]{1,0:T(8,128)S(1)}, u32[]{:S(2)}, u32[]{:S(2)}) %collective-permute-start.6) | collective-permute-done | bytes 65568 | tf_op jit(solution)/shard_map/ppermute | solution.py:150
  37.5 2.6 %collective-permute-start.14 = (f32[128,256]{1,0:T(8,128)S(1)}, f32[128,256]{1,0:T(8,128)S(1)}, u32[]{:S(2)}, u32[]{:S(2)}) collective-permute-start(f32[128,256]{1,0:T(8,128)S(1)} %get-tuple-element.62), channel_id=1, source_target_pairs={{0,8},{2,10},{4,12},{6,14},{8,0},{10,2},{12,4},{14,6},{16,24},{18,... | collective-permute-start | bytes 393224 | tf_op jit(solution)/shard_map/ppermute | solution.py:150
  40.1 0.1 fusion.4.refs_10_
  40.2 0.2 collective-permute-done.11.refs_2_
  40.4 2.6 %collective-permute-done.14.refs_4_ = f32[128,256]{1,0:T(8,128)S(1)} collective-permute-done((f32[128,256]{1,0:T(8,128)S(1)}, f32[128,256]{1,0:T(8,128)S(1)}, u32[]{:S(2)}, u32[]{:S(2)}) %collective-permute-start.14) | collective-permute-done | bytes 131104 | tf_op jit(solution)/shard_map/ppermute | solution.py:150
  43.1 1.2 %shard_map.147 = (f32[128,256]{1,0:T(8,128)}, f32[16,16,256]{2,1,0:T(8,128)}) custom-call(f32[128,128]{1,0:T(8,128)S(1)} %collective-permute-done.6.refs_0_, f32[128,128]{1,0:T(8,128)S(1)} %collective-permute-done.7.refs_1_, f32[128,128]{1,0:T(8,128)S(1)} %collective-permute-done.11.refs_2_, f32[128,128]{1,0:T(8,128)S(1)} %collective-permute-done.12.refs_3_, ...), custom_call_target="tpu_custom_call" | custom-call | tf_op jit(solution)/shard_map/pallas_call | solution.py:41
  44.3 6.5 %all-to-all-start = ((f32[16,16,256]{2,1,0:T(8,128)}), f32[16,16,256]{2,1,0:T(8,128)S(1)}, u32[]{:S(2)}, u32[]{:S(2)}) async-start(f32[16,16,256]{2,1,0:T(8,128)} %get-tuple-element.65), calls=%async_computation | async-start | bytes 524288 | tf_op jit(solution)/shard_map/all_to_all | solution.py:154
  50.9 0.0 copy-start.2
  50.9 0.9 %copy-done.2 = f32[256,256]{1,0:T(8,128)S(1)} copy-done((f32[256,256]{1,0:T(8,128)S(1)}, f32[256,256]{1,0:T(8,128)}, u32[]{:S(2)}) %copy-start.2) | copy-done | bytes 262168
  51.8 0.3 fusion.6.own
  52.1 8.8 %all-to-all-done = f32[16,16,256]{2,1,0:T(8,128)S(1)} async-done(((f32[16,16,256]{2,1,0:T(8,128)}), f32[16,16,256]{2,1,0:T(8,128)S(1)}, u32[]{:S(2)}, u32[]{:S(2)}) %all-to-all-start) | async-done | bytes 262176 | tf_op jit(solution)/shard_map/all_to_all | solution.py:154
  60.9 1.2 %shard_map.148 = f32[256,256]{1,0:T(8,128)} custom-call(f32[256,256]{1,0:T(8,128)S(1)} %bitcast.8, bf16[256,256]{1,0:T(8,128)(2,1)S(1)} %fusion.3.incidence, f32[256,256]{1,0:T(8,128)S(1)} %fusion.6.own, f32[256,256]{1,0:T(8,128)S(1)} %copy-done.2, bf16[256,256]{1,0:T(8,128)(2,1)S(1)} %get-tuple-element.67.w_top, bf16[256,256]{1,0:T(8,128)(2,1)S(1)} %get-tuple-element.66.w_low), custom_call_target="tpu_custom_call" | custom-call | tf_op jit(solution)/shard_map/pallas_call | solution.py:41
  (28 shorter events, 0.2 us)
Async XLA Ops:
  0.6 50.3 %copy-start = (f32[256,256]{1,0:T(8,128)S(1)}, f32[256,256]{1,0:T(8,128)}, u32[]{:S(2)}) copy-start(f32[256,256]{1,0:T(8,128)} %param.24) | copy-start | bytes 786436
  1.7 0.7 %copy-start.4 = (s32[1024]{0:T(1024)S(1)}, s32[1024]{0:T(1024)}, u32[]{:S(2)}) copy-start(s32[1024]{0:T(1024)} %param.14) | copy-start | bytes 12292
  1.8 0.7 %copy-start.5 = (s32[16]{0:T(128)S(1)}, s32[16]{0:T(128)}, u32[]{:S(2)}) copy-start(s32[16]{0:T(128)} %count.1) | copy-start | bytes 196
  2.4 1.2 %copy-start.1 = (f32[1024,256]{1,0:T(8,128)S(1)}, f32[1024,256]{1,0:T(8,128)}, u32[]{:S(2)}) copy-start(f32[1024,256]{1,0:T(8,128)} %tx.1) | copy-start | bytes 3145732
  4.8 7.3 %collective-permute-start = (f32[4,136,128]{2,1,0:T(8,128)S(1)}, f32[4,136,128]{2,1,0:T(8,128)S(1)}, u32[]{:S(2)}, u32[]{:S(2)}) collective-permute-start(f32[4,136,128]{2,1,0:T(8,128)S(1)} %get-tuple-element.35), channel_id=1, source_target_pairs={{0,2},{2,0},{4,6},{6,4},{8,10},{10,8},{12,14},{14,12},{16,18},{18,... | collective-permute-start | bytes 835592 | tf_op jit(solution)/shard_map/ppermute | solution.py:150
  5.3 5.4 %collective-permute-start.1 = (f32[2,72,128]{2,1,0:T(8,128)S(1)}, f32[2,72,128]{2,1,0:T(8,128)S(1)}, u32[]{:S(2)}, u32[]{:S(2)}) collective-permute-start(f32[2,72,128]{2,1,0:T(8,128)S(1)} %get-tuple-element.36), channel_id=1, source_target_pairs={{0,4},{2,6},{4,0},{6,2},{8,12},{10,14},{12,8},{14,10},{16,20},{18,... | collective-permute-start | bytes 221192 | tf_op jit(solution)/shard_map/ppermute | solution.py:150
  7.9 4.2 %collective-permute-start.2 = (f32[2,72,128]{2,1,0:T(8,128)S(1)}, f32[2,72,128]{2,1,0:T(8,128)S(1)}, u32[]{:S(2)}, u32[]{:S(2)}) collective-permute-start(f32[2,72,128]{2,1,0:T(8,128)S(1)} %get-tuple-element.37), channel_id=1, source_target_pairs={{0,6},{2,4},{4,2},{6,0},{8,14},{10,12},{12,10},{14,8},{16,22},{18,... | collective-permute-start | bytes 221192 | tf_op jit(solution)/shard_map/ppermute | solution.py:150
  7.9 8.5 %collective-permute-start.4 = (f32[2,64,128]{2,1,0:T(8,128)S(1)}, f32[2,64,128]{2,1,0:T(8,128)S(1)}, u32[]{:S(2)}, u32[]{:S(2)}) collective-permute-start(f32[2,64,128]{2,1,0:T(8,128)S(1)} %get-tuple-element.41), channel_id=1, source_target_pairs={{0,4},{2,6},{4,0},{6,2},{8,12},{10,14},{12,8},{14,10},{16,20},{18,... | collective-permute-start | bytes 196616 | tf_op jit(solution)/shard_map/ppermute | solution.py:150
  9.7 6.8 %collective-permute-start.5 = (f32[2,64,128]{2,1,0:T(8,128)S(1)}, f32[2,64,128]{2,1,0:T(8,128)S(1)}, u32[]{:S(2)}, u32[]{:S(2)}) collective-permute-start(f32[2,64,128]{2,1,0:T(8,128)S(1)} %get-tuple-element.42), channel_id=1, source_target_pairs={{0,6},{2,4},{4,2},{6,0},{8,14},{10,12},{12,10},{14,8},{16,22},{18,... | collective-permute-start | bytes 196616 | tf_op jit(solution)/shard_map/ppermute | solution.py:150
  12.1 2.6 %copy-start.3 = (f32[128,256]{1,0:T(8,128)S(1)}, f32[128,256]{1,0:T(8,128)}, u32[]{:S(2)}) copy-start(f32[128,256]{1,0:T(8,128)} %refs_7_.1) | copy-start | bytes 393220
  12.1 2.6 %copy-start.6 = (f32[256,256]{1,0:T(8,128)S(1)}, f32[256,256]{1,0:T(8,128)}, u32[]{:S(2)}) copy-start(f32[256,256]{1,0:T(8,128)} %param.22) | copy-start | bytes 786436
  12.9 6.0 %collective-permute-start.3 = (f32[2,128,128]{2,1,0:T(8,128)S(1)}, f32[2,128,128]{2,1,0:T(8,128)S(1)}, u32[]{:S(2)}, u32[]{:S(2)}) collective-permute-start(f32[2,128,128]{2,1,0:T(8,128)S(1)} %get-tuple-element.39), channel_id=1, source_target_pairs={{0,1},{1,0},{2,3},{3,2},{4,5},{5,4},{6,7},{7,6},{8,9},{9,8},{10,11... | collective-permute-start | bytes 393224 | tf_op jit(solution)/shard_map/ppermute | solution.py:150
  15.0 6.6 %collective-permute-start.9 = (f32[2,136,128]{2,1,0:T(8,128)S(1)}, f32[2,136,128]{2,1,0:T(8,128)S(1)}, u32[]{:S(2)}, u32[]{:S(2)}) collective-permute-start(f32[2,136,128]{2,1,0:T(8,128)S(1)} %get-tuple-element.52), channel_id=1, source_target_pairs={{0,4},{2,6},{4,0},{6,2},{8,12},{10,14},{12,8},{14,10},{16,20},{18,... | collective-permute-start | bytes 417800 | tf_op jit(solution)/shard_map/ppermute | solution.py:150
  16.3 6.5 %collective-permute-start.10 = (f32[2,136,128]{2,1,0:T(8,128)S(1)}, f32[2,136,128]{2,1,0:T(8,128)S(1)}, u32[]{:S(2)}, u32[]{:S(2)}) collective-permute-start(f32[2,136,128]{2,1,0:T(8,128)S(1)} %get-tuple-element.53), channel_id=1, source_target_pairs={{0,6},{2,4},{4,2},{6,0},{8,14},{10,12},{12,10},{14,8},{16,22},{18,... | collective-permute-start | bytes 417800 | tf_op jit(solution)/shard_map/ppermute | solution.py:150
  18.9 2.4 %copy-start.7 = (f32[256,256]{1,0:T(8,128)S(1)}, f32[256,256]{1,0:T(8,128)}, u32[]{:S(2)}) copy-start(f32[256,256]{1,0:T(8,128)} %param.23) | copy-start | bytes 786436
  19.6 5.2 %collective-permute-start.8 = (f32[2,128,128]{2,1,0:T(8,128)S(1)}, f32[2,128,128]{2,1,0:T(8,128)S(1)}, u32[]{:S(2)}, u32[]{:S(2)}) collective-permute-start(f32[2,128,128]{2,1,0:T(8,128)S(1)} %get-tuple-element.45), channel_id=1, source_target_pairs={{0,1},{1,0},{2,3},{3,2},{4,5},{5,4},{6,7},{7,6},{8,9},{9,8},{10,11... | collective-permute-start | bytes 393224 | tf_op jit(solution)/shard_map/ppermute | solution.py:150
  25.7 1.5 %copy-start.11 = (s32[16]{0:T(128)S(1)}, s32[16]{0:T(128)}, u32[]{:S(2)}) copy-start(s32[16]{0:T(128)} %param.19) | copy-start | bytes 196
  25.7 11.7 %collective-permute-start.13 = (f32[2,128,256]{2,1,0:T(8,128)S(1)}, f32[2,128,256]{2,1,0:T(8,128)S(1)}, u32[]{:S(2)}, u32[]{:S(2)}) collective-permute-start(f32[2,128,256]{2,1,0:T(8,128)S(1)} %get-tuple-element.56), channel_id=1, source_target_pairs={{0,1},{1,0},{2,3},{3,2},{4,5},{5,4},{6,7},{7,6},{8,9},{9,8},{10,11... | collective-permute-start | bytes 786440 | tf_op jit(solution)/shard_map/ppermute | solution.py:150
  27.2 4.0 %copy-start.10 = (s32[256]{0:T(256)S(1)}, s32[256]{0:T(256)}, u32[]{:S(2)}) copy-start(s32[256]{0:T(256)} %param.18) | copy-start | bytes 3076
  27.3 10.1 %collective-permute-start.6 = (f32[128,128]{1,0:T(8,128)S(1)}, f32[128,128]{1,0:T(8,128)S(1)}, u32[]{:S(2)}, u32[]{:S(2)}) collective-permute-start(f32[128,128]{1,0:T(8,128)S(1)} %get-tuple-element.47), channel_id=1, source_target_pairs={{0,16},{2,18},{4,20},{6,22},{8,24},{10,26},{12,28},{14,30},{16,0},... | collective-permute-start | bytes 196616 | tf_op jit(solution)/shard_map/ppermute | solution.py:150
  29.9 7.5 %collective-permute-start.7 = (f32[128,128]{1,0:T(8,128)S(1)}, f32[128,128]{1,0:T(8,128)S(1)}, u32[]{:S(2)}, u32[]{:S(2)}) collective-permute-start(f32[128,128]{1,0:T(8,128)S(1)} %get-tuple-element.48), channel_id=1, source_target_pairs={{0,24},{2,26},{4,28},{6,30},{8,16},{10,18},{12,20},{14,22},{16,8},... | collective-permute-start | bytes 196616 | tf_op jit(solution)/shard_map/ppermute | solution.py:150
  31.3 9.1 %collective-permute-start.11 = (f32[128,128]{1,0:T(8,128)S(1)}, f32[128,128]{1,0:T(8,128)S(1)}, u32[]{:S(2)}, u32[]{:S(2)}) collective-permute-start(f32[128,128]{1,0:T(8,128)S(1)} %get-tuple-element.58), channel_id=1, source_target_pairs={{0,16},{2,18},{4,20},{6,22},{8,24},{10,26},{12,28},{14,30},{16,0},... | collective-permute-start | bytes 196616 | tf_op jit(solution)/shard_map/ppermute | solution.py:150
  33.0 7.4 %collective-permute-start.12 = (f32[128,128]{1,0:T(8,128)S(1)}, f32[128,128]{1,0:T(8,128)S(1)}, u32[]{:S(2)}, u32[]{:S(2)}) collective-permute-start(f32[128,128]{1,0:T(8,128)S(1)} %get-tuple-element.59), channel_id=1, source_target_pairs={{0,24},{2,26},{4,28},{6,30},{8,16},{10,18},{12,20},{14,22},{16,8},... | collective-permute-start | bytes 196616 | tf_op jit(solution)/shard_map/ppermute | solution.py:150
  37.5 5.6 %collective-permute-start.14 = (f32[128,256]{1,0:T(8,128)S(1)}, f32[128,256]{1,0:T(8,128)S(1)}, u32[]{:S(2)}, u32[]{:S(2)}) collective-permute-start(f32[128,256]{1,0:T(8,128)S(1)} %get-tuple-element.62), channel_id=1, source_target_pairs={{0,8},{2,10},{4,12},{6,14},{8,0},{10,2},{12,4},{14,6},{16,24},{18,... | collective-permute-start | bytes 393224 | tf_op jit(solution)/shard_map/ppermute | solution.py:150
  44.3 6.6 %copy-start.9 = (s32[256]{0:T(256)S(1)}, s32[256]{0:T(256)}, u32[]{:S(2)}) copy-start(s32[256]{0:T(256)} %param.20) | copy-start | bytes 3076
  44.3 6.6 %copy-start.8 = (f32[256,256]{1,0:T(8,128)S(1)}, f32[256,256]{1,0:T(8,128)}, u32[]{:S(2)}) copy-start(f32[256,256]{1,0:T(8,128)} %param.25) | copy-start | bytes 786436
  44.3 16.6 %all-to-all-start = ((f32[16,16,256]{2,1,0:T(8,128)}), f32[16,16,256]{2,1,0:T(8,128)S(1)}, u32[]{:S(2)}, u32[]{:S(2)}) async-start(f32[16,16,256]{2,1,0:T(8,128)} %get-tuple-element.65), calls=%async_computation | async-start | bytes 524288 | tf_op jit(solution)/shard_map/all_to_all | solution.py:154
  50.9 1.0 %copy-start.2 = (f32[256,256]{1,0:T(8,128)S(1)}, f32[256,256]{1,0:T(8,128)}, u32[]{:S(2)}) copy-start(f32[256,256]{1,0:T(8,128)} %table.1) | copy-start | bytes 786436

commit v6 on v5

--- a/solution.py
+++ b/solution.py
@@ -1,3 +1,5 @@
+import functools
+
 import jax
 import jax.numpy as jnp
 from jax import lax
@@ -131,18 +133,32 @@
     second[...] = keep[1] + got[1]
 
 
-def update_kernel(*refs):
-    parts, (own, table, w_top, w_low, picks, new, listed) = refs[:-7], refs[-7:]
+def update_kernel(n, *refs):
+    parts, (own, table, w_top, w_low, picks), (new, *outs) = refs[:n], refs[n : n + 5], refs[n + 5 :]
     wide = [part[...] for part in parts if part.shape[1] != LANES]
     left, right = (sum(part[...] for part in side) for side in (parts[:2], parts[2:4]))
     gathered = jnp.concatenate([left, right], 1) + sum(wide)
     fresh = table[...] + jnp.maximum(own[...] + dot3(gathered, w_top[...], w_low[...]), 0.0)
     new[...] = fresh
-    listed[...] = dot2(picks[...], fresh).reshape(listed.shape)
-
-
-def final_kernel(incoming, incidence, own, table, w_top, w_low, new):
-    bought = dot2(incidence[...], incoming[...])
+    listed = dot2(picks[...], fresh)
+    at = 0
+    for out in outs:
+        rows = out.shape[0] * out.shape[1]
+        out[...] = listed[at : at + rows].reshape(out.shape)
+        at += rows
+
+
+def turn_kernel(start, own, core, third, fourth, first, second):
+    for i, out in enumerate((first, second)):
+        for m, (block, at) in enumerate(((own, start), (core, start), (third, 0), (fourth, 0))):
+            out[m] = block[at + i]
+
+
+def final_kernel(incidence, own, table, w_top, w_low, *refs):
+    incoming, new = refs[:-1], refs[-1]
+    width = table.shape[1]
+    rows = jnp.concatenate([block[...].reshape(-1, width) for block in incoming], 0)
+    bought = dot2(incidence[...], rows)
     new[...] = table[...] + jnp.maximum(own[...] + dot3(bought, w_top[...], w_low[...]), 0.0)
 
 
@@ -191,9 +207,31 @@
     far_l = across(parts_l)
     send_b, keep_b = call(both_kernel, [whole, whole], (own, core, *after(both, [got_r, *parts_l])), smem=(place,))
     got_b = swap(send_b, "tm", 1, 2)
-    far_r = across(pair(keep_r, *after([got_r], [send_b])))
-    next_to, mine_b = pair(keep_b, *after([got_b], far_l))
-    return [*far_l, *far_r, swap(next_to, "hash", 4, peers), mine_b]
+    parts_r = pair(keep_r, *after([got_r], [send_b]))
+    next_to, mine_b = pair(keep_b, *after([got_b], [*far_l, *parts_r]))
+    return [*far_l, *across(parts_r), swap(next_to, "hash", 4, peers), mine_b]
+
+
+def pick(x, i, axis):
+    return lax.dynamic_index_in_dim(x, i, axis, keepdims=True)
+
+
+def by_distance(x, place, zs):
+    x = x.reshape(4, 4, -1)
+    x = jnp.concatenate([pick(x, (place[0] >> 2) ^ k, 0) for k in zs], 0)
+    return jnp.concatenate([pick(x, (place[0] & 3) ^ m, 1) for m in range(4)], 1)
+
+
+def deliver(own, core, a2, a3, b2, b3):
+    peers = 16
+    turned = [(4, *own.shape[1:])] * 2
+    a2, a3 = swap(a2, "hash", 2, peers), swap(a3, "hash", 3, peers)
+    core = swap(core, "hash", 1, peers)
+    b2, b3 = swap(b2, "hash", 2, peers), swap(b3, "hash", 3, peers)
+    two, three = call(functools.partial(turn_kernel, 0), turned, (own, core, a2, a3))
+    two, three = swap(two, "hash", 8, peers), swap(three, "hash", 12, peers)
+    one, here = call(functools.partial(turn_kernel, 2), turned, (own, core, b2, b3))
+    return [two, three, swap(one, "hash", 4, peers), here]
 
 
 def gathered_plainly(transactions, tx_product, tx_count, w_msg, mine):
@@ -245,20 +283,31 @@
     product_self = jnp.dot(products, w_prod_self, precision=high)
     customer_self = jnp.dot(customers, w_cust_self, precision=high)
     send_index = lax.broadcasted_iota(jnp.int32, (peers, send_slots), 1)
-    named = jnp.where(send_index < send_count[:, None], send_rows.reshape(peers, send_slots), -1).reshape(-1)
-    picks = (named[:, None] == lax.iota(jnp.int32, mine)[None, :]).astype(bf16)
-    incidence = (recv_customer[None, :] == lax.iota(jnp.int32, customers.shape[0])[:, None]).astype(bf16)
-
-    new_products, listed = call(
-        update_kernel,
-        [products.shape, (peers, send_slots, width)],
+    named = jnp.where(send_index < send_count[:, None], send_rows.reshape(peers, send_slots), -1)
+    receivers = recv_customer.reshape(peers, send_slots)
+    near = peers == 16 and pair == 2
+    if near:
+        order = (2, 3, 1, 0)
+        named = by_distance(named, place, order).transpose(1, 0, 2)
+        receivers = by_distance(receivers, place, order)
+    picks = (named.reshape(-1)[:, None] == lax.iota(jnp.int32, mine)[None, :]).astype(bf16)
+    incidence = (receivers.reshape(-1)[None, :] == lax.iota(jnp.int32, customers.shape[0])[:, None]).astype(bf16)
+
+    counts = (4, 4, 2, 2, 2, 2) if near else (peers,)
+    new_products, *listed = call(
+        functools.partial(update_kernel, len(parts)),
+        [products.shape] + [(n, send_slots, width) for n in counts],
         (*parts, product_self, products, *split_outside(w_prod_agg), picks),
     )
-    incoming = spread(listed).reshape(-1, width)
+    if near:
+        own, core, a2, b2, a3, b3 = listed
+        incoming = deliver(own, core, a2, a3, b2, b3)
+    else:
+        incoming = [spread(listed[0])]
     (new_customers,) = call(
         final_kernel,
         [customers.shape],
-        (incoming, incidence, customer_self, customers, *split_outside(w_cust_prod)),
+        (incidence, customer_self, customers, *split_outside(w_cust_prod), *incoming),
     )
     return new_products, new_customers
 

time: 62.5 us -> 62.3 us (level)
  local copies, waits for them, and re-layouts: 2.9 us -> 6.52 us
  waiting for transfers between devices: 23.5 us -> 20.5 us
    all_to_all x1 -> x0, waiting for transfers between devices: 8.76 us -> none  [spread(): return lax.all_to_all(x, 'hash', split_axis=0, concat_axis=0, tiled=True)]
    all_to_all x1 -> x0, starting transfers between devices: 6.54 us -> none  [spread(): return lax.all_to_all(x, 'hash', split_axis=0, concat_axis=0, tiled=True)]
    ppermute x15 -> x23, starting transfers between devices: 20.5 us -> 26.4 us  [swap(): return lax.ppermute(x, axis, [(i, i ^ mask) for i in range(size)])]
    ppermute x15 -> x23, waiting for transfers between devices: 14.7 us -> 20.5 us  [swap(): return lax.ppermute(x, axis, [(i, i ^ mask) for i in range(size)])]
    unnamed x24, local copies, waits for them, and re-layouts: 2.81 us -> 6.07 us
    pallas_call x9 -> x11, Pallas kernels: 6.05 us -> 5.8 us  [call(): pl.pallas_call(kernel, out_shape=[jax.ShapeDtypeStruct(s, f32) for s in o...]
  transfers between devices with their start and end apart: 16 -> 23, of which waited for: 10 -> 12; matrix products, arithmetic and copies ran while one was open for 1% -> 2% of each run, Pallas kernels for 3% -> 3%
where the time goes in v6:
time: 62.3 us; the launch traced here: 61.9 us
  starting transfers between devices  26.4 us (42%)
  waiting for transfers between devices  20.5 us (33%)
  local copies, waits for them, and re-layouts  6.52 us (10%)
  Pallas kernels  5.8 us (9%)
  other arithmetic  1.41 us (2%)
  between operations  0.83 us (1%)
    ppermute x23, starting transfers between devices, swap(): return lax.ppermute(x, axis, [(i, i ^ mask) for i in range(size)])  26.4 us
    ppermute x23, waiting for transfers between devices, swap(): return lax.ppermute(x, axis, [(i, i ^ mask) for i in range(size)])  20.5 us
    unnamed x24, local copies, waits for them, and re-layouts  6.07 us
    pallas_call x11, Pallas kernels, call(): pl.pallas_call(kernel, out_shape=[jax.ShapeDtypeStruct(s, f32) for s in o...  5.8 us
  transfers between devices with their start and end apart: 23, of which 12 were waited for; matrix products, arithmetic and copies ran while one was open for 2% of the time, Pallas kernels for 3%

profile of v6, /device:TPU:0, one launch (start us, length us, event | category | flops | bytes accessed | tf_op | source)
XLA Modules:
  0.0 61.9 jit_solution(4871216737809679705)
XLA Ops:
  0.7 1.0 %fusion = (bf16[256,256]{1,0:T(8,128)(2,1)S(1)}, bf16[256,256]{1,0:T(8,128)(2,1)S(1)}) fusion(f32[256,256]{1,0:T(8,128)} %param.21), kind=kLoop, calls=%fused_computation.6 | loop fusion | flops 262144 | bytes 524288 | tf_op jit(solution)/shard_map/convert_element_type | solution.py:23
  1.8 0.6 copy-done.4
  2.4 1.2 %copy-done.1 = f32[1024,256]{1,0:T(8,128)S(1)} copy-done((f32[1024,256]{1,0:T(8,128)S(1)}, f32[1024,256]{1,0:T(8,128)}, u32[]{:S(2)}) %copy-start.1) | copy-done | bytes 1048600
  3.7 1.1 %shard_map.140 = (f32[4,136,128]{2,1,0:T(8,128)S(1)}, f32[4,136,128]{2,1,0:T(8,128)S(1)}, f32[2,72,128]{2,1,0:T(8,128)S(1)}, f32[2,72,128]{2,1,0:T(8,128)S(1)}, ...) custom-call(s32[2]{0:T(128)S(1)} %pad_add_fusion.3.place, ...), custom_call_target="tpu_custom_call" | custom-call | tf_op jit(solution)/shard_map/pallas_call | solution.py:43
  4.8 0.5 collective-permute-start
  5.3 2.6 %collective-permute-start.1 = (f32[2,72,128]{2,1,0:T(8,128)S(1)}, f32[2,72,128]{2,1,0:T(8,128)S(1)}, u32[]{:S(2)}, u32[]{:S(2)}) collective-permute-start(f32[2,72,128]{2,1,0:T(8,128)S(1)} %get-tuple-element.45), channel_id=1, source_target_pairs={{0,4},{2,6},{4,0},{6,2},{8,12},{10,14},{12,8},{14,10},{16,20},{18,... | collective-permute-start | bytes 221192 | tf_op jit(solution)/shard_map/ppermute | solution.py:166
  8.0 1.7 %collective-permute-start.4 = (f32[2,64,128]{2,1,0:T(8,128)S(1)}, f32[2,64,128]{2,1,0:T(8,128)S(1)}, u32[]{:S(2)}, u32[]{:S(2)}) collective-permute-start(f32[2,64,128]{2,1,0:T(8,128)S(1)} %get-tuple-element.50), channel_id=1, source_target_pairs={{0,4},{2,6},{4,0},{6,2},{8,12},{10,14},{12,8},{14,10},{16,20},{18,... | collective-permute-start | bytes 196616 | tf_op jit(solution)/shard_map/ppermute | solution.py:166
  9.7 0.2 fusion.6.refs_6_
  10.0 0.7 %copy-done.2 = f32[256,256]{1,0:T(8,128)S(1)} copy-done((f32[256,256]{1,0:T(8,128)S(1)}, f32[256,256]{1,0:T(8,128)}, u32[]{:S(2)}) %copy-start.2) | copy-done | bytes 262168
  10.6 0.3 fusion.7.own
  10.9 0.7 %copy-done.7 = f32[256,256]{1,0:T(8,128)S(1)} copy-done((f32[256,256]{1,0:T(8,128)S(1)}, f32[256,256]{1,0:T(8,128)}, u32[]{:S(2)}) %copy-start.7) | copy-done | bytes 262168
  11.6 0.9 %copy-done.8 = f32[256,256]{1,0:T(8,128)S(1)} copy-done((f32[256,256]{1,0:T(8,128)S(1)}, f32[256,256]{1,0:T(8,128)}, u32[]{:S(2)}) %copy-start.8) | copy-done | bytes 262168
  12.6 0.6 %copy-done.9 = s32[256]{0:T(256)S(1)} copy-done((s32[256]{0:T(256)S(1)}, s32[256]{0:T(256)}, u32[]{:S(2)}) %copy-start.9) | copy-done | bytes 1048
  13.3 0.6 copy-done.11
  14.0 0.8 %shard_map.141 = (f32[2,128,128]{2,1,0:T(8,128)S(1)}, f32[2,128,128]{2,1,0:T(8,128)S(1)}, f32[8,128]{1,0:T(8,128)S(1)}) custom-call(s32[2]{0:T(128)S(1)} %pad_add_fusion.3.place, f32[4,136,128]{2,1,0:T(8,128)S(1)} %get-tuple-element.43.own, f32[4,136,128]{2,1,0:T(8,128)S(1)} %collective-permute-done.core, f32[2,72,128]{2,1,0:T(8,128)S(1)} %collective-permute-done.1.l2, ...), custom_call_target="tpu_custom_call" | custom-call | tf_op jit(solution)/shard_map/pallas_call | solution.py:43
  14.8 1.6 %collective-permute-start.3 = (f32[2,128,128]{2,1,0:T(8,128)S(1)}, f32[2,128,128]{2,1,0:T(8,128)S(1)}, u32[]{:S(2)}, u32[]{:S(2)}) collective-permute-start(f32[2,128,128]{2,1,0:T(8,128)S(1)} %get-tuple-element.48), channel_id=1, source_target_pairs={{0,1},{1,0},{2,3},{3,2},{4,5},{5,4},{6,7},{7,6},{8,9},{9,8},{10,11... | collective-permute-start | bytes 393224 | tf_op jit(solution)/shard_map/ppermute | solution.py:166
  16.4 0.7 %copy-done.10 = s32[256]{0:T(256)S(1)} copy-done((s32[256]{0:T(256)S(1)}, s32[256]{0:T(256)}, u32[]{:S(2)}) %copy-start.10) | copy-done | bytes 1048
  17.2 1.1 %collective-permute-start.9 = (f32[2,136,128]{2,1,0:T(8,128)S(1)}, f32[2,136,128]{2,1,0:T(8,128)S(1)}, u32[]{:S(2)}, u32[]{:S(2)}) collective-permute-start(f32[2,136,128]{2,1,0:T(8,128)S(1)} %get-tuple-element.61), channel_id=1, source_target_pairs={{0,4},{2,6},{4,0},{6,2},{8,12},{10,14},{12,8},{14,10},{16,20},{18,... | collective-permute-start | bytes 417800 | tf_op jit(solution)/shard_map/ppermute | solution.py:166
  18.3 0.1 collective-permute-start.10
  18.4 1.9 %collective-permute-done.3.got = f32[2,128,128]{2,1,0:T(8,128)S(1)} collective-permute-done((f32[2,128,128]{2,1,0:T(8,128)S(1)}, f32[2,128,128]{2,1,0:T(8,128)S(1)}, u32[]{:S(2)}, u32[]{:S(2)}) %collective-permute-start.3) | collective-permute-done | bytes 131104 | tf_op jit(solution)/shard_map/ppermute | solution.py:166
  20.3 0.8 %shard_map.142 = (f32[2,128,128]{2,1,0:T(8,128)S(1)}, f32[2,128,128]{2,1,0:T(8,128)S(1)}) custom-call(s32[2]{0:T(128)S(1)} %pad_add_fusion.3.place, f32[8,128]{1,0:T(8,128)S(1)} %get-tuple-element.49.ids, f32[4,136,128]{2,1,0:T(8,128)S(1)} %get-tuple-element.43.own, f32[4,136,128]{2,1,0:T(8,128)S(1)} %collective-permute-done.core, ...), custom_call_target="tpu_custom_call" | custom-call | tf_op jit(solution)/shard_map/pallas_call | solution.py:43
  21.1 1.6 %collective-permute-start.8 = (f32[2,128,128]{2,1,0:T(8,128)S(1)}, f32[2,128,128]{2,1,0:T(8,128)S(1)}, u32[]{:S(2)}, u32[]{:S(2)}) collective-permute-start(f32[2,128,128]{2,1,0:T(8,128)S(1)} %get-tuple-element.54), channel_id=1, source_target_pairs={{0,1},{1,0},{2,3},{3,2},{4,5},{5,4},{6,7},{7,6},{8,9},{9,8},{10,11... | collective-permute-start | bytes 393224 | tf_op jit(solution)/shard_map/ppermute | solution.py:166
  22.7 1.1 %collective-permute-done.9.b2 = f32[2,136,128]{2,1,0:T(8,128)S(1)} collective-permute-done((f32[2,136,128]{2,1,0:T(8,128)S(1)}, f32[2,136,128]{2,1,0:T(8,128)S(1)}, u32[]{:S(2)}, u32[]{:S(2)}) %collective-permute-start.9) | collective-permute-done | bytes 139296 | tf_op jit(solution)/shard_map/ppermute | solution.py:166
  23.8 0.7 %collective-permute-done.10.b3 = f32[2,136,128]{2,1,0:T(8,128)S(1)} collective-permute-done((f32[2,136,128]{2,1,0:T(8,128)S(1)}, f32[2,136,128]{2,1,0:T(8,128)S(1)}, u32[]{:S(2)}, u32[]{:S(2)}) %collective-permute-start.10) | collective-permute-done | bytes 139296 | tf_op jit(solution)/shard_map/ppermute | solution.py:166
  24.5 1.6 %collective-permute-done.8.got = f32[2,128,128]{2,1,0:T(8,128)S(1)} collective-permute-done((f32[2,128,128]{2,1,0:T(8,128)S(1)}, f32[2,128,128]{2,1,0:T(8,128)S(1)}, u32[]{:S(2)}, u32[]{:S(2)}) %collective-permute-start.8) | collective-permute-done | bytes 131104 | tf_op jit(solution)/shard_map/ppermute | solution.py:166
  26.1 0.8 %shard_map.144 = (f32[2,128,256]{2,1,0:T(8,128)S(1)}, f32[2,128,256]{2,1,0:T(8,128)S(1)}) custom-call(s32[2]{0:T(128)S(1)} %pad_add_fusion.3.place, f32[4,136,128]{2,1,0:T(8,128)S(1)} %get-tuple-element.43.own, f32[4,136,128]{2,1,0:T(8,128)S(1)} %collective-permute-done.core, f32[2,136,128]{2,1,0:T(8,128)S(1)} %collective-permute-done.9.b2, ...), custom_call_target="tpu_custom_call" | custom-call | tf_op jit(solution)/shard_map/pallas_call | solution.py:43
  26.9 1.6 %collective-permute-start.13 = (f32[2,128,256]{2,1,0:T(8,128)S(1)}, f32[2,128,256]{2,1,0:T(8,128)S(1)}, u32[]{:S(2)}, u32[]{:S(2)}) collective-permute-start(f32[2,128,256]{2,1,0:T(8,128)S(1)} %get-tuple-element.65), channel_id=1, source_target_pairs={{0,1},{1,0},{2,3},{3,2},{4,5},{5,4},{6,7},{7,6},{8,9},{9,8},{10,11... | collective-permute-start | bytes 786440 | tf_op jit(solution)/shard_map/ppermute | solution.py:166
  28.6 2.6 %collective-permute-start.6 = (f32[128,128]{1,0:T(8,128)S(1)}, f32[128,128]{1,0:T(8,128)S(1)}, u32[]{:S(2)}, u32[]{:S(2)}) collective-permute-start(f32[128,128]{1,0:T(8,128)S(1)} %get-tuple-element.56), channel_id=1, source_target_pairs={{0,16},{2,18},{4,20},{6,22},{8,24},{10,26},{12,28},{14,30},{16,0},... | collective-permute-start | bytes 196616 | tf_op jit(solution)/shard_map/ppermute | solution.py:166
  31.2 1.3 %collective-permute-start.7 = (f32[128,128]{1,0:T(8,128)S(1)}, f32[128,128]{1,0:T(8,128)S(1)}, u32[]{:S(2)}, u32[]{:S(2)}) collective-permute-start(f32[128,128]{1,0:T(8,128)S(1)} %get-tuple-element.57), channel_id=1, source_target_pairs={{0,24},{2,26},{4,28},{6,30},{8,16},{10,18},{12,20},{14,22},{16,8},... | collective-permute-start | bytes 196616 | tf_op jit(solution)/shard_map/ppermute | solution.py:166
  32.6 0.1 fusion.4.refs_10_
  32.7 2.8 %collective-permute-done.6.refs_0_ = f32[128,128]{1,0:T(8,128)S(1)} collective-permute-done((f32[128,128]{1,0:T(8,128)S(1)}, f32[128,128]{1,0:T(8,128)S(1)}, u32[]{:S(2)}, u32[]{:S(2)}) %collective-permute-start.6) | collective-permute-done | bytes 65568 | tf_op jit(solution)/shard_map/ppermute | solution.py:166
  35.5 1.8 %collective-permute-done.7.refs_1_ = f32[128,128]{1,0:T(8,128)S(1)} collective-permute-done((f32[128,128]{1,0:T(8,128)S(1)}, f32[128,128]{1,0:T(8,128)S(1)}, u32[]{:S(2)}, u32[]{:S(2)}) %collective-permute-start.7) | collective-permute-done | bytes 65568 | tf_op jit(solution)/shard_map/ppermute | solution.py:166
  37.5 1.9 %collective-permute-start.11 = (f32[128,128]{1,0:T(8,128)S(1)}, f32[128,128]{1,0:T(8,128)S(1)}, u32[]{:S(2)}, u32[]{:S(2)}) collective-permute-start(f32[128,128]{1,0:T(8,128)S(1)} %get-tuple-element.67), channel_id=1, source_target_pairs={{0,16},{2,18},{4,20},{6,22},{8,24},{10,26},{12,28},{14,30},{16,0},... | collective-permute-start | bytes 196616 | tf_op jit(solution)/shard_map/ppermute | solution.py:166
  39.4 2.4 %collective-permute-start.12 = (f32[128,128]{1,0:T(8,128)S(1)}, f32[128,128]{1,0:T(8,128)S(1)}, u32[]{:S(2)}, u32[]{:S(2)}) collective-permute-start(f32[128,128]{1,0:T(8,128)S(1)} %get-tuple-element.68), channel_id=1, source_target_pairs={{0,24},{2,26},{4,28},{6,30},{8,16},{10,18},{12,20},{14,22},{16,8},... | collective-permute-start | bytes 196616 | tf_op jit(solution)/shard_map/ppermute | solution.py:166
  41.9 1.5 %collective-permute-done.11.refs_2_ = f32[128,128]{1,0:T(8,128)S(1)} collective-permute-done((f32[128,128]{1,0:T(8,128)S(1)}, f32[128,128]{1,0:T(8,128)S(1)}, u32[]{:S(2)}, u32[]{:S(2)}) %collective-permute-start.11) | collective-permute-done | bytes 65568 | tf_op jit(solution)/shard_map/ppermute | solution.py:166
  43.4 2.2 %collective-permute-done.12.refs_3_ = f32[128,128]{1,0:T(8,128)S(1)} collective-permute-done((f32[128,128]{1,0:T(8,128)S(1)}, f32[128,128]{1,0:T(8,128)S(1)}, u32[]{:S(2)}, u32[]{:S(2)}) %collective-permute-start.12) | collective-permute-done | bytes 65568 | tf_op jit(solution)/shard_map/ppermute | solution.py:166
  45.5 0.9 %shard_map.147 = (f32[128,256]{1,0:T(8,128)}, f32[4,16,256]{2,1,0:T(8,128)S(1)}, f32[4,16,256]{2,1,0:T(8,128)S(1)}, f32[2,16,256]{2,1,0:T(8,128)S(1)}, f32[2,16,...) custom-call(f32[128,128]{1,0:T(8,128)S(1)} %collective-permute-done.6.refs_0_, ...), custom_call_target="tpu_custom_call" | custom-call | tf_op jit(solution)/shard_map/pallas_call | solution.py:43
  46.5 1.7 %collective-permute-start.16 = (f32[2,16,256]{2,1,0:T(8,128)S(1)}, f32[2,16,256]{2,1,0:T(8,128)S(1)}, u32[]{:S(2)}, u32[]{:S(2)}) collective-permute-start(f32[2,16,256]{2,1,0:T(8,128)S(1)} %get-tuple-element.76), channel_id=1, source_target_pairs={{0,4},{2,6},{4,0},{6,2},{8,12},{10,14},{12,8},{14,10},{16,20},{18,... | collective-permute-start | bytes 98312 | tf_op jit(solution)/shard_map/ppermute | solution.py:166
  48.2 0.2 collective-permute-start.17
  48.4 1.7 %collective-permute-start.20 = (f32[2,16,256]{2,1,0:T(8,128)S(1)}, f32[2,16,256]{2,1,0:T(8,128)S(1)}, u32[]{:S(2)}, u32[]{:S(2)}) collective-permute-start(f32[2,16,256]{2,1,0:T(8,128)S(1)} %get-tuple-element.80), channel_id=1, source_target_pairs={{0,4},{2,6},{4,0},{6,2},{8,12},{10,14},{12,8},{14,10},{16,20},{18,... | collective-permute-start | bytes 98312 | tf_op jit(solution)/shard_map/ppermute | solution.py:166
  50.2 0.2 collective-permute-done.16.third
  50.4 1.1 %collective-permute-done.17.fourth = f32[2,16,256]{2,1,0:T(8,128)S(1)} collective-permute-done((f32[2,16,256]{2,1,0:T(8,128)S(1)}, f32[2,16,256]{2,1,0:T(8,128)S(1)}, u32[]{:S(2)}, u32[]{:S(2)}) %collective-permute-start.17) | collective-permute-done | bytes 32800 | tf_op jit(solution)/shard_map/ppermute | solution.py:166
  51.6 0.4 collective-permute-start.18
  51.9 2.2 %collective-permute-start.19 = (f32[4,16,256]{2,1,0:T(8,128)S(1)}, f32[4,16,256]{2,1,0:T(8,128)S(1)}, u32[]{:S(2)}, u32[]{:S(2)}) collective-permute-start(f32[4,16,256]{2,1,0:T(8,128)S(1)} %get-tuple-element.79), channel_id=1, source_target_pairs={{0,24},{2,26},{4,28},{6,30},{8,16},{10,18},{12,20},{14,22},{16,8},... | collective-permute-start | bytes 196616 | tf_op jit(solution)/shard_map/ppermute | solution.py:166
  54.1 1.1 %collective-permute-start.22 = (f32[4,16,256]{2,1,0:T(8,128)S(1)}, f32[4,16,256]{2,1,0:T(8,128)S(1)}, u32[]{:S(2)}, u32[]{:S(2)}) collective-permute-start(f32[4,16,256]{2,1,0:T(8,128)S(1)} %get-tuple-element.82), channel_id=1, source_target_pairs={{0,8},{2,10},{4,12},{6,14},{8,0},{10,2},{12,4},{14,6},{16,24},{18,... | collective-permute-start | bytes 196616 | tf_op jit(solution)/shard_map/ppermute | solution.py:166
  55.2 4.1 %collective-permute-done.18.refs_0_ = f32[4,16,256]{2,1,0:T(8,128)S(1)} collective-permute-done((f32[4,16,256]{2,1,0:T(8,128)S(1)}, f32[4,16,256]{2,1,0:T(8,128)S(1)}, u32[]{:S(2)}, u32[]{:S(2)}) %collective-permute-start.18) | collective-permute-done | bytes 65568 | tf_op jit(solution)/shard_map/ppermute | solution.py:166
  59.4 1.3 %collective-permute-done.22.refs_2_ = f32[4,16,256]{2,1,0:T(8,128)S(1)} collective-permute-done((f32[4,16,256]{2,1,0:T(8,128)S(1)}, f32[4,16,256]{2,1,0:T(8,128)S(1)}, u32[]{:S(2)}, u32[]{:S(2)}) %collective-permute-start.22) | collective-permute-done | bytes 65568 | tf_op jit(solution)/shard_map/ppermute | solution.py:166
  60.7 1.2 %shard_map.150 = f32[256,256]{1,0:T(8,128)} custom-call(bf16[256,256]{1,0:T(8,128)(2,1)S(1)} %fusion.3.incidence, f32[256,256]{1,0:T(8,128)S(1)} %fusion.7.own, f32[256,256]{1,0:T(8,128)S(1)} %copy-done.2, bf16[256,256]{1,0:T(8,128)(2,1)S(1)} %get-tuple-element.85.w_top, bf16[256,256]{1,0:T(8,128)(2,1)S(1)} %get-tuple-element.84.w_low, ...), custom_call_target="tpu_custom_call" | custom-call | tf_op jit(solution)/shard_map/pallas_call | solution.py:43
  (55 shorter events, 1.1 us)
Async XLA Ops:
  0.6 9.3 %copy-start = (f32[256,256]{1,0:T(8,128)S(1)}, f32[256,256]{1,0:T(8,128)}, u32[]{:S(2)}) copy-start(f32[256,256]{1,0:T(8,128)} %param.24) | copy-start | bytes 786436
  1.7 0.7 %copy-start.4 = (s32[1024]{0:T(1024)S(1)}, s32[1024]{0:T(1024)}, u32[]{:S(2)}) copy-start(s32[1024]{0:T(1024)} %param.14) | copy-start | bytes 12292
  1.8 0.7 %copy-start.5 = (s32[16]{0:T(128)S(1)}, s32[16]{0:T(128)}, u32[]{:S(2)}) copy-start(s32[16]{0:T(128)} %count.1) | copy-start | bytes 196
  2.4 1.2 %copy-start.1 = (f32[1024,256]{1,0:T(8,128)S(1)}, f32[1024,256]{1,0:T(8,128)}, u32[]{:S(2)}) copy-start(f32[1024,256]{1,0:T(8,128)} %tx.1) | copy-start | bytes 3145732
  3.6 6.1 %copy-start.3 = (f32[128,256]{1,0:T(8,128)S(1)}, f32[128,256]{1,0:T(8,128)}, u32[]{:S(2)}) copy-start(f32[128,256]{1,0:T(8,128)} %refs_7_.1) | copy-start | bytes 393220
  3.7 6.1 %copy-start.6 = (f32[256,256]{1,0:T(8,128)S(1)}, f32[256,256]{1,0:T(8,128)}, u32[]{:S(2)}) copy-start(f32[256,256]{1,0:T(8,128)} %param.22) | copy-start | bytes 786436
  4.8 9.2 %collective-permute-start = (f32[4,136,128]{2,1,0:T(8,128)S(1)}, f32[4,136,128]{2,1,0:T(8,128)S(1)}, u32[]{:S(2)}, u32[]{:S(2)}) collective-permute-start(f32[4,136,128]{2,1,0:T(8,128)S(1)} %get-tuple-element.44), channel_id=1, source_target_pairs={{0,2},{2,0},{4,6},{6,4},{8,10},{10,8},{12,14},{14,12},{16,18},{18,... | collective-permute-start | bytes 835592 | tf_op jit(solution)/shard_map/ppermute | solution.py:166
  5.3 8.6 %collective-permute-start.1 = (f32[2,72,128]{2,1,0:T(8,128)S(1)}, f32[2,72,128]{2,1,0:T(8,128)S(1)}, u32[]{:S(2)}, u32[]{:S(2)}) collective-permute-start(f32[2,72,128]{2,1,0:T(8,128)S(1)} %get-tuple-element.45), channel_id=1, source_target_pairs={{0,4},{2,6},{4,0},{6,2},{8,12},{10,14},{12,8},{14,10},{16,20},{18,... | collective-permute-start | bytes 221192 | tf_op jit(solution)/shard_map/ppermute | solution.py:166
  7.9 6.1 %collective-permute-start.2 = (f32[2,72,128]{2,1,0:T(8,128)S(1)}, f32[2,72,128]{2,1,0:T(8,128)S(1)}, u32[]{:S(2)}, u32[]{:S(2)}) collective-permute-start(f32[2,72,128]{2,1,0:T(8,128)S(1)} %get-tuple-element.46), channel_id=1, source_target_pairs={{0,6},{2,4},{4,2},{6,0},{8,14},{10,12},{12,10},{14,8},{16,22},{18,... | collective-permute-start | bytes 221192 | tf_op jit(solution)/shard_map/ppermute | solution.py:166
  8.0 10.4 %collective-permute-start.4 = (f32[2,64,128]{2,1,0:T(8,128)S(1)}, f32[2,64,128]{2,1,0:T(8,128)S(1)}, u32[]{:S(2)}, u32[]{:S(2)}) collective-permute-start(f32[2,64,128]{2,1,0:T(8,128)S(1)} %get-tuple-element.50), channel_id=1, source_target_pairs={{0,4},{2,6},{4,0},{6,2},{8,12},{10,14},{12,8},{14,10},{16,20},{18,... | collective-permute-start | bytes 196616 | tf_op jit(solution)/shard_map/ppermute | solution.py:166
  9.7 0.9 %copy-start.2 = (f32[256,256]{1,0:T(8,128)S(1)}, f32[256,256]{1,0:T(8,128)}, u32[]{:S(2)}) copy-start(f32[256,256]{1,0:T(8,128)} %table.1) | copy-start | bytes 786436
  9.7 8.7 %collective-permute-start.5 = (f32[2,64,128]{2,1,0:T(8,128)S(1)}, f32[2,64,128]{2,1,0:T(8,128)S(1)}, u32[]{:S(2)}, u32[]{:S(2)}) collective-permute-start(f32[2,64,128]{2,1,0:T(8,128)S(1)} %get-tuple-element.51), channel_id=1, source_target_pairs={{0,6},{2,4},{4,2},{6,0},{8,14},{10,12},{12,10},{14,8},{16,22},{18,... | collective-permute-start | bytes 196616 | tf_op jit(solution)/shard_map/ppermute | solution.py:166
  10.6 0.9 %copy-start.7 = (f32[256,256]{1,0:T(8,128)S(1)}, f32[256,256]{1,0:T(8,128)}, u32[]{:S(2)}) copy-start(f32[256,256]{1,0:T(8,128)} %param.23) | copy-start | bytes 786436
  11.6 0.9 %copy-start.8 = (f32[256,256]{1,0:T(8,128)S(1)}, f32[256,256]{1,0:T(8,128)}, u32[]{:S(2)}) copy-start(f32[256,256]{1,0:T(8,128)} %param.25) | copy-start | bytes 786436
  12.5 0.7 %copy-start.9 = (s32[256]{0:T(256)S(1)}, s32[256]{0:T(256)}, u32[]{:S(2)}) copy-start(s32[256]{0:T(256)} %param.18) | copy-start | bytes 3076
  13.2 0.7 %copy-start.11 = (s32[16]{0:T(128)S(1)}, s32[16]{0:T(128)}, u32[]{:S(2)}) copy-start(s32[16]{0:T(128)} %param.19) | copy-start | bytes 196
  14.8 5.5 %collective-permute-start.3 = (f32[2,128,128]{2,1,0:T(8,128)S(1)}, f32[2,128,128]{2,1,0:T(8,128)S(1)}, u32[]{:S(2)}, u32[]{:S(2)}) collective-permute-start(f32[2,128,128]{2,1,0:T(8,128)S(1)} %get-tuple-element.48), channel_id=1, source_target_pairs={{0,1},{1,0},{2,3},{3,2},{4,5},{5,4},{6,7},{7,6},{8,9},{9,8},{10,11... | collective-permute-start | bytes 393224 | tf_op jit(solution)/shard_map/ppermute | solution.py:166
  16.4 0.7 %copy-start.10 = (s32[256]{0:T(256)S(1)}, s32[256]{0:T(256)}, u32[]{:S(2)}) copy-start(s32[256]{0:T(256)} %param.20) | copy-start | bytes 3076
  17.2 6.6 %collective-permute-start.9 = (f32[2,136,128]{2,1,0:T(8,128)S(1)}, f32[2,136,128]{2,1,0:T(8,128)S(1)}, u32[]{:S(2)}, u32[]{:S(2)}) collective-permute-start(f32[2,136,128]{2,1,0:T(8,128)S(1)} %get-tuple-element.61), channel_id=1, source_target_pairs={{0,4},{2,6},{4,0},{6,2},{8,12},{10,14},{12,8},{14,10},{16,20},{18,... | collective-permute-start | bytes 417800 | tf_op jit(solution)/shard_map/ppermute | solution.py:166
  18.3 6.2 %collective-permute-start.10 = (f32[2,136,128]{2,1,0:T(8,128)S(1)}, f32[2,136,128]{2,1,0:T(8,128)S(1)}, u32[]{:S(2)}, u32[]{:S(2)}) collective-permute-start(f32[2,136,128]{2,1,0:T(8,128)S(1)} %get-tuple-element.62), channel_id=1, source_target_pairs={{0,6},{2,4},{4,2},{6,0},{8,14},{10,12},{12,10},{14,8},{16,22},{18,... | collective-permute-start | bytes 417800 | tf_op jit(solution)/shard_map/ppermute | solution.py:166
  21.1 5.0 %collective-permute-start.8 = (f32[2,128,128]{2,1,0:T(8,128)S(1)}, f32[2,128,128]{2,1,0:T(8,128)S(1)}, u32[]{:S(2)}, u32[]{:S(2)}) collective-permute-start(f32[2,128,128]{2,1,0:T(8,128)S(1)} %get-tuple-element.54), channel_id=1, source_target_pairs={{0,1},{1,0},{2,3},{3,2},{4,5},{5,4},{6,7},{7,6},{8,9},{9,8},{10,11... | collective-permute-start | bytes 393224 | tf_op jit(solution)/shard_map/ppermute | solution.py:166
  26.9 10.4 %collective-permute-start.13 = (f32[2,128,256]{2,1,0:T(8,128)S(1)}, f32[2,128,256]{2,1,0:T(8,128)S(1)}, u32[]{:S(2)}, u32[]{:S(2)}) collective-permute-start(f32[2,128,256]{2,1,0:T(8,128)S(1)} %get-tuple-element.65), channel_id=1, source_target_pairs={{0,1},{1,0},{2,3},{3,2},{4,5},{5,4},{6,7},{7,6},{8,9},{9,8},{10,11... | collective-permute-start | bytes 786440 | tf_op jit(solution)/shard_map/ppermute | solution.py:166
  28.6 6.9 %collective-permute-start.6 = (f32[128,128]{1,0:T(8,128)S(1)}, f32[128,128]{1,0:T(8,128)S(1)}, u32[]{:S(2)}, u32[]{:S(2)}) collective-permute-start(f32[128,128]{1,0:T(8,128)S(1)} %get-tuple-element.56), channel_id=1, source_target_pairs={{0,16},{2,18},{4,20},{6,22},{8,24},{10,26},{12,28},{14,30},{16,0},... | collective-permute-start | bytes 196616 | tf_op jit(solution)/shard_map/ppermute | solution.py:166
  31.2 6.1 %collective-permute-start.7 = (f32[128,128]{1,0:T(8,128)S(1)}, f32[128,128]{1,0:T(8,128)S(1)}, u32[]{:S(2)}, u32[]{:S(2)}) collective-permute-start(f32[128,128]{1,0:T(8,128)S(1)} %get-tuple-element.57), channel_id=1, source_target_pairs={{0,24},{2,26},{4,28},{6,30},{8,16},{10,18},{12,20},{14,22},{16,8},... | collective-permute-start | bytes 196616 | tf_op jit(solution)/shard_map/ppermute | solution.py:166
  37.4 8.2 %collective-permute-start.14 = (f32[128,256]{1,0:T(8,128)S(1)}, f32[128,256]{1,0:T(8,128)S(1)}, u32[]{:S(2)}, u32[]{:S(2)}) collective-permute-start(f32[128,256]{1,0:T(8,128)S(1)} %get-tuple-element.71), channel_id=1, source_target_pairs={{0,8},{2,10},{4,12},{6,14},{8,0},{10,2},{12,4},{14,6},{16,24},{18,... | collective-permute-start | bytes 393224 | tf_op jit(solution)/shard_map/ppermute | solution.py:166
  37.5 5.9 %collective-permute-start.11 = (f32[128,128]{1,0:T(8,128)S(1)}, f32[128,128]{1,0:T(8,128)S(1)}, u32[]{:S(2)}, u32[]{:S(2)}) collective-permute-start(f32[128,128]{1,0:T(8,128)S(1)} %get-tuple-element.67), channel_id=1, source_target_pairs={{0,16},{2,18},{4,20},{6,22},{8,24},{10,26},{12,28},{14,30},{16,0},... | collective-permute-start | bytes 196616 | tf_op jit(solution)/shard_map/ppermute | solution.py:166
  39.4 6.1 %collective-permute-start.12 = (f32[128,128]{1,0:T(8,128)S(1)}, f32[128,128]{1,0:T(8,128)S(1)}, u32[]{:S(2)}, u32[]{:S(2)}) collective-permute-start(f32[128,128]{1,0:T(8,128)S(1)} %get-tuple-element.68), channel_id=1, source_target_pairs={{0,24},{2,26},{4,28},{6,30},{8,16},{10,18},{12,20},{14,22},{16,8},... | collective-permute-start | bytes 196616 | tf_op jit(solution)/shard_map/ppermute | solution.py:166
  46.5 5.1 %collective-permute-start.15 = (f32[4,16,256]{2,1,0:T(8,128)S(1)}, f32[4,16,256]{2,1,0:T(8,128)S(1)}, u32[]{:S(2)}, u32[]{:S(2)}) collective-permute-start(f32[4,16,256]{2,1,0:T(8,128)S(1)} %get-tuple-element.75), channel_id=1, source_target_pairs={{0,2},{2,0},{4,6},{6,4},{8,10},{10,8},{12,14},{14,12},{16,18},{18,... | collective-permute-start | bytes 196616 | tf_op jit(solution)/shard_map/ppermute | solution.py:166
  46.5 3.9 %collective-permute-start.16 = (f32[2,16,256]{2,1,0:T(8,128)S(1)}, f32[2,16,256]{2,1,0:T(8,128)S(1)}, u32[]{:S(2)}, u32[]{:S(2)}) collective-permute-start(f32[2,16,256]{2,1,0:T(8,128)S(1)} %get-tuple-element.76), channel_id=1, source_target_pairs={{0,4},{2,6},{4,0},{6,2},{8,12},{10,14},{12,8},{14,10},{16,20},{18,... | collective-permute-start | bytes 98312 | tf_op jit(solution)/shard_map/ppermute | solution.py:166
  48.2 3.3 %collective-permute-start.17 = (f32[2,16,256]{2,1,0:T(8,128)S(1)}, f32[2,16,256]{2,1,0:T(8,128)S(1)}, u32[]{:S(2)}, u32[]{:S(2)}) collective-permute-start(f32[2,16,256]{2,1,0:T(8,128)S(1)} %get-tuple-element.77), channel_id=1, source_target_pairs={{0,6},{2,4},{4,2},{6,0},{8,14},{10,12},{12,10},{14,8},{16,22},{18,... | collective-permute-start | bytes 98312 | tf_op jit(solution)/shard_map/ppermute | solution.py:166
  48.4 5.7 %collective-permute-start.20 = (f32[2,16,256]{2,1,0:T(8,128)S(1)}, f32[2,16,256]{2,1,0:T(8,128)S(1)}, u32[]{:S(2)}, u32[]{:S(2)}) collective-permute-start(f32[2,16,256]{2,1,0:T(8,128)S(1)} %get-tuple-element.80), channel_id=1, source_target_pairs={{0,4},{2,6},{4,0},{6,2},{8,12},{10,14},{12,8},{14,10},{16,20},{18,... | collective-permute-start | bytes 98312 | tf_op jit(solution)/shard_map/ppermute | solution.py:166
  50.1 4.0 %collective-permute-start.21 = (f32[2,16,256]{2,1,0:T(8,128)S(1)}, f32[2,16,256]{2,1,0:T(8,128)S(1)}, u32[]{:S(2)}, u32[]{:S(2)}) collective-permute-start(f32[2,16,256]{2,1,0:T(8,128)S(1)} %get-tuple-element.81), channel_id=1, source_target_pairs={{0,6},{2,4},{4,2},{6,0},{8,14},{10,12},{12,10},{14,8},{16,22},{18,... | collective-permute-start | bytes 98312 | tf_op jit(solution)/shard_map/ppermute | solution.py:166
  51.6 7.8 %collective-permute-start.18 = (f32[4,16,256]{2,1,0:T(8,128)S(1)}, f32[4,16,256]{2,1,0:T(8,128)S(1)}, u32[]{:S(2)}, u32[]{:S(2)}) collective-permute-start(f32[4,16,256]{2,1,0:T(8,128)S(1)} %get-tuple-element.78), channel_id=1, source_target_pairs={{0,16},{2,18},{4,20},{6,22},{8,24},{10,26},{12,28},{14,30},{16,0},... | collective-permute-start | bytes 196616 | tf_op jit(solution)/shard_map/ppermute | solution.py:166
  51.9 7.5 %collective-permute-start.19 = (f32[4,16,256]{2,1,0:T(8,128)S(1)}, f32[4,16,256]{2,1,0:T(8,128)S(1)}, u32[]{:S(2)}, u32[]{:S(2)}) collective-permute-start(f32[4,16,256]{2,1,0:T(8,128)S(1)} %get-tuple-element.79), channel_id=1, source_target_pairs={{0,24},{2,26},{4,28},{6,30},{8,16},{10,18},{12,20},{14,22},{16,8},... | collective-permute-start | bytes 196616 | tf_op jit(solution)/shard_map/ppermute | solution.py:166
  54.1 6.6 %collective-permute-start.22 = (f32[4,16,256]{2,1,0:T(8,128)S(1)}, f32[4,16,256]{2,1,0:T(8,128)S(1)}, u32[]{:S(2)}, u32[]{:S(2)}) collective-permute-start(f32[4,16,256]{2,1,0:T(8,128)S(1)} %get-tuple-element.82), channel_id=1, source_target_pairs={{0,8},{2,10},{4,12},{6,14},{8,0},{10,2},{12,4},{14,6},{16,24},{18,... | collective-permute-start | bytes 196616 | tf_op jit(solution)/shard_map/ppermute | solution.py:166

commit v7 on v6

--- a/solution.py
+++ b/solution.py
@@ -53,7 +53,7 @@
     return lax.broadcasted_iota(jnp.int32, (1, LANES), 1)
 
 
-def message_kernel(place, count, tx, ids, w_top, w_low, own, core, l2, l3, r2, r3, b2, b3):
+def message_kernel(place, count, tx, ids, w_top, w_low, own, core, l2, l3, r2, r3):
     near, far = place[0] & 3, place[0] >> 2
     slots = tx.shape[0] // 16
     lane = lanes()
@@ -62,81 +62,90 @@
         c = near ^ m
         buckets = [4 * (far ^ k) + c for k in (2, 3, 1, 0)]
         x = jnp.concatenate([tx[pl.ds(pl.multiple_of(b * slots, slots), slots), :] for b in buckets], 0)
-        y = jnp.maximum(dot3(x, top, low), 0.0).reshape(4, slots, 2 * LANES)
-        if m < 2:
-            outs = ((own, core)[m], 0, 0), ((own, core)[m], 0, slots), ((own, core)[m], 2, 0)
-        else:
-            outs = ((l2, l3)[m - 2], 0, 0), ((r2, r3)[m - 2], 0, 0), ((b2, b3)[m - 2], 0, 0)
-        (left, _, _), (right, _, at), (both, first, _) = outs
-        left[:2, :slots, :] = y[:2, :, :LANES]
-        right[:2, at : at + slots, :] = y[:2, :, LANES:]
-        both[first : first + 2, :slots, :] = y[2:, :, :LANES]
-        both[first : first + 2, slots : 2 * slots, :] = y[2:, :, LANES:]
+        y = jnp.maximum(dot3(x, top, low), 0.0)
         for i, b in enumerate(buckets):
             row = ids[pl.ds(b >> 1, 1), :]
             turned = pltpu.roll(row, slots, 1)
             twice = jnp.where((lane >= slots).astype(jnp.int32) == (c & 1), row, turned)
             twice = jnp.where((lane & (slots - 1)) < count[b], twice, -1).astype(f32)
-            target, z = (left, i) if i < 2 else (both, first + i - 2)
-            target[z, target.shape[1] - PAD :, :] = jnp.broadcast_to(twice, (PAD, LANES))
-
-
-def id_rows(blocks, starts):
+            twice = jnp.broadcast_to(twice, (PAD, LANES))
+            left, right = y[i * slots : (i + 1) * slots, :LANES], y[i * slots : (i + 1) * slots, LANES:]
+            if m < 2:
+                out = (own, core)[m]
+                out[i, :slots, :] = left
+                out[i, slots : 2 * slots, :] = right
+                out[i, 2 * slots :, :] = twice
+            elif i < 3:
+                first, second = (l2, l3)[m - 2], (r2, r3)[m - 2]
+                first[i, :slots, :] = left
+                first[i, slots:, :] = twice
+                second[i * slots : (i + 1) * slots, :] = right
+            else:
+                out = (r2, r3)[m - 2]
+                out[3 * slots : 4 * slots, :] = left
+                out[4 * slots : 5 * slots, :] = right
+                out[5 * slots :, :] = twice
+
+
+def targets(place, mine):
+    row = lax.broadcasted_iota(jnp.int32, (2 * mine, LANES), 0)
+    own = place[1]
+    return jnp.where(row < mine, row + (1 - own) * mine, row - mine + own * mine).astype(f32)
+
+
+def joined(one):
     lane = lanes()
-    rows = []
-    for z in range(2):
-        one = [block[start + z, pl.ds(block.shape[1] - PAD, 1), :] for block, start in zip(blocks, starts)]
-        rows.append([jnp.where(lane < LANES // 2, one[i], one[i + 1]) for i in (0, 2)])
-    return rows
-
-
-def sums(place, rows, sides, send, keep):
+    return [jnp.where(lane < LANES // 2, one[i], one[i + 1]) for i in (0, 2)]
+
+
+def bucket_sum(rows, target, blocks, send, keep, at):
     mine = send.shape[1]
+    picks = jnp.concatenate([(r == target).astype(bf16) for r in rows], 1)
+    total = mm(picks, jnp.concatenate(split(jnp.concatenate(blocks, 0)), 1))
+    total = total[:, :LANES] + total[:, LANES:]
+    send[at] = total[:mine]
+    keep[at] = total[mine:]
+
+
+def left_kernel(place, own, core, l2, l3, send, keep, ids):
+    target = targets(place, send.shape[1])
+    senders = (own, core, l2, l3)
     slots = LANES // 2
-    own = place[1]
-    row = lax.broadcasted_iota(jnp.int32, (2 * mine, LANES), 0)
-    target = jnp.where(row < mine, row + (1 - own) * mine, row - mine + own * mine).astype(f32)
-    for z in range(2):
-        picks = jnp.concatenate([(r == target).astype(bf16) for r in rows[z]], 1)
-        for side, blocks in enumerate(sides):
-            x = jnp.concatenate([block[first + z, at : at + slots, :] for block, first, at in blocks], 0)
-            total = mm(picks, jnp.concatenate(split(x), 1))
-            total = total[:, :LANES] + total[:, LANES:]
-            send[z, :, side * LANES : (side + 1) * LANES] = total[:mine]
-            keep[z, :, side * LANES : (side + 1) * LANES] = total[mine:]
-
-
-def left_kernel(place, own, core, l2, l3, send, keep, ids):
-    blocks = (own, core, l2, l3)
-    rows = id_rows(blocks, (0, 0, 0, 0))
-    for z in range(2):
+    for z in range(3):
+        rows = joined([block[z, pl.ds(block.shape[1] - PAD, 1), :] for block in senders])
         for i in range(2):
-            ids[pl.ds(2 * z + i, 1), :] = rows[z][i]
-    sums(place, rows, [[(block, 0, 0) for block in blocks]], send, keep)
-
-
-def right_kernel(place, ids, own, core, r2, r3, send, keep):
-    rows = [[ids[pl.ds(2 * z + i, 1), :] for i in range(2)] for z in range(2)]
-    slots = r2.shape[1]
-    sums(place, rows, [[(own, 0, slots), (core, 0, slots), (r2, 0, 0), (r3, 0, 0)]], send, keep)
-
-
-def both_kernel(place, own, core, b2, b3, send, keep):
-    blocks, starts = (own, core, b2, b3), (2, 2, 0, 0)
+            ids[pl.ds(2 * z + i, 1), :] = rows[i]
+        bucket_sum(rows, target, [block[z, :slots, :] for block in senders], send, keep, z)
+
+
+def rest_kernel(place, ids, own, core, r2, r3, send, keep):
+    target = targets(place, send.shape[1])
     slots = LANES // 2
-    sides = [[(block, first, at) for block, first in zip(blocks, starts)] for at in (0, slots)]
-    sums(place, id_rows(blocks, starts), sides, send, keep)
-
-
-def pair_kernel(keep, got, first, second):
-    first[...] = keep[0] + got[0]
-    second[...] = keep[1] + got[1]
+    for z in range(3):
+        rows = [ids[pl.ds(2 * z + i, 1), :] for i in range(2)]
+        blocks = [block[z, slots : 2 * slots, :] for block in (own, core)]
+        blocks += [block[z * slots : (z + 1) * slots, :] for block in (r2, r3)]
+        bucket_sum(rows, target, blocks, send, keep, z)
+    one = [block[3, pl.ds(2 * slots, 1), :] for block in (own, core)]
+    rows = joined(one + [block[pl.ds(5 * slots, 1), :] for block in (r2, r3)])
+    for side in range(2):
+        blocks = [block[3, side * slots : (side + 1) * slots, :] for block in (own, core)]
+        blocks += [block[(3 + side) * slots : (4 + side) * slots, :] for block in (r2, r3)]
+        bucket_sum(rows, target, blocks, send, keep, 3 + side)
+
+
+def pair_kernel(keep, got, *outs):
+    for i in range(3):
+        outs[i][...] = keep[i] + got[i]
+    for own in outs[3:]:
+        own[:, :LANES] = keep[3] + got[3]
+        own[:, LANES:] = keep[4] + got[4]
 
 
 def update_kernel(n, *refs):
     parts, (own, table, w_top, w_low, picks), (new, *outs) = refs[:n], refs[n : n + 5], refs[n + 5 :]
     wide = [part[...] for part in parts if part.shape[1] != LANES]
-    left, right = (sum(part[...] for part in side) for side in (parts[:2], parts[2:4]))
+    left, right = (sum(part[...] for part in side) for side in (parts[:3], parts[3:6]))
     gathered = jnp.concatenate([left, right], 1) + sum(wide)
     fresh = table[...] + jnp.maximum(own[...] + dot3(gathered, w_top[...], w_low[...]), 0.0)
     new[...] = fresh
@@ -173,43 +182,33 @@
 def gathered_by_permutes(place, transactions, tx_product, tx_count, w_msg, mine):
     peers = 16
     slots = transactions.shape[0] // peers
-    own, core, *out = call(
+    own, core, l2, l3, r2, r3 = call(
         message_kernel,
-        [(4, 2 * slots + PAD, LANES)] * 2
-        + [(2, slots + PAD, LANES)] * 2
-        + [(2, slots, LANES)] * 2
-        + [(2, 2 * slots + PAD, LANES)] * 2,
+        [(4, 2 * slots + PAD, LANES)] * 2 + [(3, slots + PAD, LANES)] * 2 + [(5 * slots + PAD, LANES)] * 2,
         (transactions, tx_product.reshape(-1, LANES), *split_outside(w_msg)),
         smem=(place, tx_count),
     )
-    half, whole = (2, mine, LANES), (2, mine, 2 * LANES)
+    left, rest, part = (3, mine, LANES), (5, mine, LANES), (mine, LANES)
 
     def near(blocks):
         return [swap(block, "hash", mask, peers) for block, mask in zip(blocks, (2, 3))]
 
-    def pair(keep, got):
-        return call(pair_kernel, [keep.shape[1:]] * 2, (keep, got))
+    def across(parts):
+        return [swap(part, "hash", mask, peers) for part, mask in zip(parts, (8, 12, 4))]
 
     def after(value, ready):
         return lax.optimization_barrier((*value, *ready))[: len(value)]
 
-    def across(parts):
-        return [swap(part, "hash", mask, peers) for part, mask in zip(parts, (8, 12))]
-
-    left, right = near(out[:2]), near(out[2:4])
+    first = near((l2, l3))
     core = swap(core, "hash", 1, peers)
-    both = near(after(out[4:], left))
-    send_l, keep_l, ids = call(left_kernel, [half, half, (8, LANES)], (own, core, *left), smem=(place,))
+    second = near(after((r2, r3), first))
+    send_l, keep_l, ids = call(left_kernel, [left, left, (8, LANES)], (own, core, *first), smem=(place,))
     got_l = swap(send_l, "tm", 1, 2)
-    send_r, keep_r = call(right_kernel, [half, half], (ids, own, core, *after(right, [got_l])), smem=(place,))
+    send_r, keep_r = call(rest_kernel, [rest, rest], (ids, own, core, *after(second, [got_l])), smem=(place,))
     got_r = swap(send_r, "tm", 1, 2)
-    parts_l = pair(keep_l, *after([got_l], [send_r]))
-    far_l = across(parts_l)
-    send_b, keep_b = call(both_kernel, [whole, whole], (own, core, *after(both, [got_r, *parts_l])), smem=(place,))
-    got_b = swap(send_b, "tm", 1, 2)
-    parts_r = pair(keep_r, *after([got_r], [send_b]))
-    next_to, mine_b = pair(keep_b, *after([got_b], [*far_l, *parts_r]))
-    return [*far_l, *across(parts_r), swap(next_to, "hash", 4, peers), mine_b]
+    far_l = across(call(pair_kernel, [part] * 3, (keep_l, *after([got_l], [send_r]))))
+    *parts_r, whole = call(pair_kernel, [part] * 3 + [(mine, 2 * LANES)], (keep_r, *after([got_r], far_l)))
+    return [*far_l, *across(parts_r), whole]
 
 
 def pick(x, i, axis):
@@ -251,7 +250,7 @@
     parts = lax.map(part_sum, jnp.arange(pair)).reshape(pair * mine, width)
     total = lax.psum_scatter(parts, "tm", scatter_dimension=0, tiled=True)
     zero = jnp.zeros((mine, LANES), f32)
-    return [zero, zero, zero, zero, total]
+    return [zero] * 6 + [total]
 
 
 def local(

time: 62.3 us -> 61.1 us (0.981)
  waiting for transfers between devices: 20.5 us -> 25.1 us
  starting transfers between devices: 26.4 us -> 23 us
  local copies, waits for them, and re-layouts: 6.52 us -> 4.79 us
  Pallas kernels: 5.8 us -> 5.1 us
    ppermute x23 -> x21, waiting for transfers between devices: 20.5 us -> 25.1 us  [swap(): return lax.ppermute(x, axis, [(i, i ^ mask) for i in range(size)])]
    ppermute x23 -> x21, starting transfers between devices: 26.4 us -> 23 us  [swap(): return lax.ppermute(x, axis, [(i, i ^ mask) for i in range(size)])]
    unnamed x24, local copies, waits for them, and re-layouts: 6.07 us -> 4.32 us
    pallas_call x11 -> x9, Pallas kernels: 5.8 us -> 5.1 us  [call(): pl.pallas_call(kernel, out_shape=[jax.ShapeDtypeStruct(s, f32) for s in o...]
  transfers between devices with their start and end apart: 23 -> 21, of which waited for: 12 -> 14; matrix products, arithmetic and copies ran while one was open for 2% -> 2% of each run, Pallas kernels for 3% -> 1%
where the time goes in v7:
time: 61.1 us; the launch traced here: 60.8 us
  waiting for transfers between devices  25.1 us (41%)
  starting transfers between devices  23 us (38%)
  Pallas kernels  5.1 us (8%)
  local copies, waits for them, and re-layouts  4.79 us (8%)
  other arithmetic  1.42 us (2%)
  between operations  0.86 us (1%)
    ppermute x21, waiting for transfers between devices, swap(): return lax.ppermute(x, axis, [(i, i ^ mask) for i in range(size)])  25.1 us
    ppermute x21, starting transfers between devices, swap(): return lax.ppermute(x, axis, [(i, i ^ mask) for i in range(size)])  23 us
    pallas_call x9, Pallas kernels, call(): pl.pallas_call(kernel, out_shape=[jax.ShapeDtypeStruct(s, f32) for s in o...  5.1 us
    unnamed x24, local copies, waits for them, and re-layouts  4.32 us
  transfers between devices with their start and end apart: 21, of which 14 were waited for; matrix products, arithmetic and copies ran while one was open for 2% of the time, Pallas kernels for 1%

profile of v7, /device:TPU:0, one launch (start us, length us, event | category | flops | bytes accessed | tf_op | source)
XLA Modules:
  0.0 60.8 jit_solution(3236842013980137504)
XLA Ops:
  0.7 1.0 %fusion = (bf16[256,256]{1,0:T(8,128)(2,1)S(1)}, bf16[256,256]{1,0:T(8,128)(2,1)S(1)}) fusion(f32[256,256]{1,0:T(8,128)} %param.21), kind=kLoop, calls=%fused_computation.6 | loop fusion | flops 262144 | bytes 524288 | tf_op jit(solution)/shard_map/convert_element_type | solution.py:23
  1.8 0.6 copy-done.4
  2.4 1.2 %copy-done.1 = f32[1024,256]{1,0:T(8,128)S(1)} copy-done((f32[1024,256]{1,0:T(8,128)S(1)}, f32[1024,256]{1,0:T(8,128)}, u32[]{:S(2)}) %copy-start.1) | copy-done | bytes 1048600
  3.7 1.1 %shard_map.140 = (f32[4,136,128]{2,1,0:T(8,128)S(1)}, f32[4,136,128]{2,1,0:T(8,128)S(1)}, f32[3,72,128]{2,1,0:T(8,128)S(1)}, f32[3,72,128]{2,1,0:T(8,128)S(1)}, ...) custom-call(s32[2]{0:T(128)S(1)} %pad_add_fusion.3.place, s32[16]{0:T(128)S(1)} %copy-done.5, f32[1024,256]{1,0:T(8,128)S(1)} %copy-done.1, ...), custom_call_target="tpu_custom_call" | custom-call | tf_op jit(solution)/shard_map/pallas_call | solution.py:43
  4.8 0.5 collective-permute-start
  5.3 2.6 %collective-permute-start.1 = (f32[3,72,128]{2,1,0:T(8,128)S(1)}, f32[3,72,128]{2,1,0:T(8,128)S(1)}, u32[]{:S(2)}, u32[]{:S(2)}) collective-permute-start(f32[3,72,128]{2,1,0:T(8,128)S(1)} %get-tuple-element.39), channel_id=1, source_target_pairs={{0,4},{2,6},{4,0},{6,2},{8,12},{10,14},{12,8},{14,10},{16,20},{18,... | collective-permute-start | bytes 331784 | tf_op jit(solution)/shard_map/ppermute | solution.py:175
  8.0 0.6 %copy-done.9 = s32[256]{0:T(256)S(1)} copy-done((s32[256]{0:T(256)S(1)}, s32[256]{0:T(256)}, u32[]{:S(2)}) %copy-start.9) | copy-done | bytes 1048
  8.7 0.6 copy-done.10
  9.4 0.6 copy-done.11
  10.1 0.2 fusion.6.refs_7_
  10.4 0.6 %copy-done.2 = f32[256,256]{1,0:T(8,128)S(1)} copy-done((f32[256,256]{1,0:T(8,128)S(1)}, f32[256,256]{1,0:T(8,128)}, u32[]{:S(2)}) %copy-start.2) | copy-done | bytes 262168
  11.0 0.3 fusion.7.own
  11.5 0.3 collective-permute-done.1.l2
  11.8 1.8 %collective-permute-done.2.l3 = f32[3,72,128]{2,1,0:T(8,128)S(1)} collective-permute-done((f32[3,72,128]{2,1,0:T(8,128)S(1)}, f32[3,72,128]{2,1,0:T(8,128)S(1)}, u32[]{:S(2)}, u32[]{:S(2)}) %collective-permute-start.2) | collective-permute-done | bytes 110624 | tf_op jit(solution)/shard_map/ppermute | solution.py:175
  13.6 1.6 %collective-permute-start.4 = (f32[328,128]{1,0:T(8,128)S(1)}, f32[328,128]{1,0:T(8,128)S(1)}, u32[]{:S(2)}, u32[]{:S(2)}) collective-permute-start(f32[328,128]{1,0:T(8,128)S(1)} %get-tuple-element.46), channel_id=1, source_target_pairs={{0,4},{2,6},{4,0},{6,2},{8,12},{10,14},{12,8},{14,10},{16,20},{18,... | collective-permute-start | bytes 503816 | tf_op jit(solution)/shard_map/ppermute | solution.py:175
  15.2 0.8 %shard_map.141 = (f32[3,128,128]{2,1,0:T(8,128)S(1)}, f32[3,128,128]{2,1,0:T(8,128)S(1)}, f32[8,128]{1,0:T(8,128)S(1)}) custom-call(s32[2]{0:T(128)S(1)} %pad_add_fusion.3.place, f32[4,136,128]{2,1,0:T(8,128)S(1)} %get-tuple-element.37.own, f32[4,136,128]{2,1,0:T(8,128)S(1)} %collective-permute-done.core, f32[3,72,128]{2,1,0:T(8,128)S(1)} %collective-permute-done.1.l2, ...), custom_call_target="tpu_custom_call" | custom-call | tf_op jit(solution)/shard_map/pallas_call | solution.py:43
  16.0 1.7 %collective-permute-start.3 = (f32[3,128,128]{2,1,0:T(8,128)S(1)}, f32[3,128,128]{2,1,0:T(8,128)S(1)}, u32[]{:S(2)}, u32[]{:S(2)}) collective-permute-start(f32[3,128,128]{2,1,0:T(8,128)S(1)} %get-tuple-element.42), channel_id=1, source_target_pairs={{0,1},{1,0},{2,3},{3,2},{4,5},{5,4},{6,7},{7,6},{8,9},{9,8},{10,11... | collective-permute-start | bytes 589832 | tf_op jit(solution)/shard_map/ppermute | solution.py:175
  17.8 3.0 %collective-permute-done.4.r2 = f32[328,128]{1,0:T(8,128)S(1)} collective-permute-done((f32[328,128]{1,0:T(8,128)S(1)}, f32[328,128]{1,0:T(8,128)S(1)}, u32[]{:S(2)}, u32[]{:S(2)}) %collective-permute-start.4) | collective-permute-done | bytes 167968 | tf_op jit(solution)/shard_map/ppermute | solution.py:175
  20.8 2.0 %collective-permute-done.5.r3 = f32[328,128]{1,0:T(8,128)S(1)} collective-permute-done((f32[328,128]{1,0:T(8,128)S(1)}, f32[328,128]{1,0:T(8,128)S(1)}, u32[]{:S(2)}, u32[]{:S(2)}) %collective-permute-start.5) | collective-permute-done | bytes 167968 | tf_op jit(solution)/shard_map/ppermute | solution.py:175
  22.8 0.7 %collective-permute-done.3.got = f32[3,128,128]{2,1,0:T(8,128)S(1)} collective-permute-done((f32[3,128,128]{2,1,0:T(8,128)S(1)}, f32[3,128,128]{2,1,0:T(8,128)S(1)}, u32[]{:S(2)}, u32[]{:S(2)}) %collective-permute-start.3) | collective-permute-done | bytes 196640 | tf_op jit(solution)/shard_map/ppermute | solution.py:175
  23.5 0.9 %shard_map.142 = (f32[5,128,128]{2,1,0:T(8,128)S(1)}, f32[5,128,128]{2,1,0:T(8,128)S(1)}) custom-call(s32[2]{0:T(128)S(1)} %pad_add_fusion.3.place, f32[8,128]{1,0:T(8,128)S(1)} %get-tuple-element.43.ids, f32[4,136,128]{2,1,0:T(8,128)S(1)} %get-tuple-element.37.own, f32[4,136,128]{2,1,0:T(8,128)S(1)} %collective-permute-done.core, ...), custom_call_target="tpu_custom_call" | custom-call | tf_op jit(solution)/shard_map/pallas_call | solution.py:43
  24.4 1.7 %collective-permute-start.9 = (f32[5,128,128]{2,1,0:T(8,128)S(1)}, f32[5,128,128]{2,1,0:T(8,128)S(1)}, u32[]{:S(2)}, u32[]{:S(2)}) collective-permute-start(f32[5,128,128]{2,1,0:T(8,128)S(1)} %get-tuple-element.50), channel_id=1, source_target_pairs={{0,1},{1,0},{2,3},{3,2},{4,5},{5,4},{6,7},{7,6},{8,9},{9,8},{10,11... | collective-permute-start | bytes 983048 | tf_op jit(solution)/shard_map/ppermute | solution.py:175
  26.0 0.1 fusion.4.refs_11_
  26.2 2.6 %collective-permute-start.6 = (f32[128,128]{1,0:T(8,128)S(1)}, f32[128,128]{1,0:T(8,128)S(1)}, u32[]{:S(2)}, u32[]{:S(2)}) collective-permute-start(f32[128,128]{1,0:T(8,128)S(1)} %get-tuple-element.52), channel_id=1, source_target_pairs={{0,16},{2,18},{4,20},{6,22},{8,24},{10,26},{12,28},{14,30},{16,0},... | collective-permute-start | bytes 196616 | tf_op jit(solution)/shard_map/ppermute | solution.py:175
  28.8 1.4 %collective-permute-start.7 = (f32[128,128]{1,0:T(8,128)S(1)}, f32[128,128]{1,0:T(8,128)S(1)}, u32[]{:S(2)}, u32[]{:S(2)}) collective-permute-start(f32[128,128]{1,0:T(8,128)S(1)} %get-tuple-element.53), channel_id=1, source_target_pairs={{0,24},{2,26},{4,28},{6,30},{8,16},{10,18},{12,20},{14,22},{16,8},... | collective-permute-start | bytes 196616 | tf_op jit(solution)/shard_map/ppermute | solution.py:175
  30.2 0.2 collective-permute-start.8
  30.4 3.2 %collective-permute-done.6.refs_0_ = f32[128,128]{1,0:T(8,128)S(1)} collective-permute-done((f32[128,128]{1,0:T(8,128)S(1)}, f32[128,128]{1,0:T(8,128)S(1)}, u32[]{:S(2)}, u32[]{:S(2)}) %collective-permute-start.6) | collective-permute-done | bytes 65568 | tf_op jit(solution)/shard_map/ppermute | solution.py:175
  33.6 1.4 %collective-permute-done.7.refs_1_ = f32[128,128]{1,0:T(8,128)S(1)} collective-permute-done((f32[128,128]{1,0:T(8,128)S(1)}, f32[128,128]{1,0:T(8,128)S(1)}, u32[]{:S(2)}, u32[]{:S(2)}) %collective-permute-start.7) | collective-permute-done | bytes 65568 | tf_op jit(solution)/shard_map/ppermute | solution.py:175
  35.0 0.1 collective-permute-done.8.refs_2_
  35.2 2.7 %collective-permute-start.10 = (f32[128,128]{1,0:T(8,128)S(1)}, f32[128,128]{1,0:T(8,128)S(1)}, u32[]{:S(2)}, u32[]{:S(2)}) collective-permute-start(f32[128,128]{1,0:T(8,128)S(1)} %get-tuple-element.57), channel_id=1, source_target_pairs={{0,16},{2,18},{4,20},{6,22},{8,24},{10,26},{12,28},{14,30},{16,0},... | collective-permute-start | bytes 196616 | tf_op jit(solution)/shard_map/ppermute | solution.py:175
  37.9 0.6 collective-permute-start.11
  38.5 0.3 collective-permute-start.12
  38.8 3.8 %collective-permute-done.10.refs_3_ = f32[128,128]{1,0:T(8,128)S(1)} collective-permute-done((f32[128,128]{1,0:T(8,128)S(1)}, f32[128,128]{1,0:T(8,128)S(1)}, u32[]{:S(2)}, u32[]{:S(2)}) %collective-permute-start.10) | collective-permute-done | bytes 65568 | tf_op jit(solution)/shard_map/ppermute | solution.py:175
  42.6 1.5 %collective-permute-done.11.refs_4_ = f32[128,128]{1,0:T(8,128)S(1)} collective-permute-done((f32[128,128]{1,0:T(8,128)S(1)}, f32[128,128]{1,0:T(8,128)S(1)}, u32[]{:S(2)}, u32[]{:S(2)}) %collective-permute-start.11) | collective-permute-done | bytes 65568 | tf_op jit(solution)/shard_map/ppermute | solution.py:175
  44.1 0.9 %shard_map.145 = (f32[128,256]{1,0:T(8,128)}, f32[4,16,256]{2,1,0:T(8,128)S(1)}, f32[4,16,256]{2,1,0:T(8,128)S(1)}, f32[2,16,256]{2,1,0:T(8,128)S(1)}, f32[2,16,...) custom-call(f32[128,128]{1,0:T(8,128)S(1)} %collective-permute-done.6.refs_0_, ...), custom_call_target="tpu_custom_call" | custom-call | tf_op jit(solution)/shard_map/pallas_call | solution.py:43
  45.0 1.5 %collective-permute-start.14 = (f32[2,16,256]{2,1,0:T(8,128)S(1)}, f32[2,16,256]{2,1,0:T(8,128)S(1)}, u32[]{:S(2)}, u32[]{:S(2)}) collective-permute-start(f32[2,16,256]{2,1,0:T(8,128)S(1)} %get-tuple-element.64), channel_id=1, source_target_pairs={{0,4},{2,6},{4,0},{6,2},{8,12},{10,14},{12,8},{14,10},{16,20},{18,... | collective-permute-start | bytes 98312 | tf_op jit(solution)/shard_map/ppermute | solution.py:175
  46.5 0.4 collective-permute-start.15
  46.9 1.5 %collective-permute-start.18 = (f32[2,16,256]{2,1,0:T(8,128)S(1)}, f32[2,16,256]{2,1,0:T(8,128)S(1)}, u32[]{:S(2)}, u32[]{:S(2)}) collective-permute-start(f32[2,16,256]{2,1,0:T(8,128)S(1)} %get-tuple-element.68), channel_id=1, source_target_pairs={{0,4},{2,6},{4,0},{6,2},{8,12},{10,14},{12,8},{14,10},{16,20},{18,... | collective-permute-start | bytes 98312 | tf_op jit(solution)/shard_map/ppermute | solution.py:175
  48.4 0.1 collective-permute-start.19
  48.5 0.1 eq.34
  48.6 0.3 collective-permute-done.14.third
  48.9 0.9 %collective-permute-done.15.fourth = f32[2,16,256]{2,1,0:T(8,128)S(1)} collective-permute-done((f32[2,16,256]{2,1,0:T(8,128)S(1)}, f32[2,16,256]{2,1,0:T(8,128)S(1)}, u32[]{:S(2)}, u32[]{:S(2)}) %collective-permute-start.15) | collective-permute-done | bytes 32800 | tf_op jit(solution)/shard_map/ppermute | solution.py:175
  49.9 1.6 %collective-permute-start.16 = (f32[4,16,256]{2,1,0:T(8,128)S(1)}, f32[4,16,256]{2,1,0:T(8,128)S(1)}, u32[]{:S(2)}, u32[]{:S(2)}) collective-permute-start(f32[4,16,256]{2,1,0:T(8,128)S(1)} %get-tuple-element.66), channel_id=1, source_target_pairs={{0,16},{2,18},{4,20},{6,22},{8,24},{10,26},{12,28},{14,30},{16,0},... | collective-permute-start | bytes 196616 | tf_op jit(solution)/shard_map/ppermute | solution.py:175
  51.5 1.5 %collective-permute-start.17 = (f32[4,16,256]{2,1,0:T(8,128)S(1)}, f32[4,16,256]{2,1,0:T(8,128)S(1)}, u32[]{:S(2)}, u32[]{:S(2)}) collective-permute-start(f32[4,16,256]{2,1,0:T(8,128)S(1)} %get-tuple-element.67), channel_id=1, source_target_pairs={{0,24},{2,26},{4,28},{6,30},{8,16},{10,18},{12,20},{14,22},{16,8},... | collective-permute-start | bytes 196616 | tf_op jit(solution)/shard_map/ppermute | solution.py:175
  52.9 0.6 collective-permute-start.20
  53.6 4.8 %collective-permute-done.16.refs_0_ = f32[4,16,256]{2,1,0:T(8,128)S(1)} collective-permute-done((f32[4,16,256]{2,1,0:T(8,128)S(1)}, f32[4,16,256]{2,1,0:T(8,128)S(1)}, u32[]{:S(2)}, u32[]{:S(2)}) %collective-permute-start.16) | collective-permute-done | bytes 65568 | tf_op jit(solution)/shard_map/ppermute | solution.py:175
  58.3 1.2 %collective-permute-done.20.refs_2_ = f32[4,16,256]{2,1,0:T(8,128)S(1)} collective-permute-done((f32[4,16,256]{2,1,0:T(8,128)S(1)}, f32[4,16,256]{2,1,0:T(8,128)S(1)}, u32[]{:S(2)}, u32[]{:S(2)}) %collective-permute-start.20) | collective-permute-done | bytes 65568 | tf_op jit(solution)/shard_map/ppermute | solution.py:175
  59.6 1.2 %shard_map.148 = f32[256,256]{1,0:T(8,128)} custom-call(bf16[256,256]{1,0:T(8,128)(2,1)S(1)} %fusion.3.incidence, f32[256,256]{1,0:T(8,128)S(1)} %fusion.7.own, f32[256,256]{1,0:T(8,128)S(1)} %copy-done.2, bf16[256,256]{1,0:T(8,128)(2,1)S(1)} %get-tuple-element.73.w_top, bf16[256,256]{1,0:T(8,128)(2,1)S(1)} %get-tuple-element.72.w_low, ...), custom_call_target="tpu_custom_call" | custom-call | tf_op jit(solution)/shard_map/pallas_call | solution.py:43
  (49 shorter events, 0.9 us)
Async XLA Ops:
  0.6 9.8 %copy-start = (f32[256,256]{1,0:T(8,128)S(1)}, f32[256,256]{1,0:T(8,128)}, u32[]{:S(2)}) copy-start(f32[256,256]{1,0:T(8,128)} %param.24) | copy-start | bytes 786436
  1.7 0.7 %copy-start.4 = (s32[1024]{0:T(1024)S(1)}, s32[1024]{0:T(1024)}, u32[]{:S(2)}) copy-start(s32[1024]{0:T(1024)} %param.14) | copy-start | bytes 12292
  1.8 0.7 %copy-start.5 = (s32[16]{0:T(128)S(1)}, s32[16]{0:T(128)}, u32[]{:S(2)}) copy-start(s32[16]{0:T(128)} %count.1) | copy-start | bytes 196
  2.4 1.2 %copy-start.1 = (f32[1024,256]{1,0:T(8,128)S(1)}, f32[1024,256]{1,0:T(8,128)}, u32[]{:S(2)}) copy-start(f32[1024,256]{1,0:T(8,128)} %tx.1) | copy-start | bytes 3145732
  3.6 4.3 %copy-start.6 = (f32[256,256]{1,0:T(8,128)S(1)}, f32[256,256]{1,0:T(8,128)}, u32[]{:S(2)}) copy-start(f32[256,256]{1,0:T(8,128)} %param.23) | copy-start | bytes 786436
  4.8 10.4 %collective-permute-start = (f32[4,136,128]{2,1,0:T(8,128)S(1)}, f32[4,136,128]{2,1,0:T(8,128)S(1)}, u32[]{:S(2)}, u32[]{:S(2)}) collective-permute-start(f32[4,136,128]{2,1,0:T(8,128)S(1)} %get-tuple-element.38), channel_id=1, source_target_pairs={{0,2},{2,0},{4,6},{6,4},{8,10},{10,8},{12,14},{14,12},{16,18},{18,... | collective-permute-start | bytes 835592 | tf_op jit(solution)/shard_map/ppermute | solution.py:175
  5.3 6.5 %collective-permute-start.1 = (f32[3,72,128]{2,1,0:T(8,128)S(1)}, f32[3,72,128]{2,1,0:T(8,128)S(1)}, u32[]{:S(2)}, u32[]{:S(2)}) collective-permute-start(f32[3,72,128]{2,1,0:T(8,128)S(1)} %get-tuple-element.39), channel_id=1, source_target_pairs={{0,4},{2,6},{4,0},{6,2},{8,12},{10,14},{12,8},{14,10},{16,20},{18,... | collective-permute-start | bytes 331784 | tf_op jit(solution)/shard_map/ppermute | solution.py:175
  7.9 5.8 %collective-permute-start.2 = (f32[3,72,128]{2,1,0:T(8,128)S(1)}, f32[3,72,128]{2,1,0:T(8,128)S(1)}, u32[]{:S(2)}, u32[]{:S(2)}) collective-permute-start(f32[3,72,128]{2,1,0:T(8,128)S(1)} %get-tuple-element.40), channel_id=1, source_target_pairs={{0,6},{2,4},{4,2},{6,0},{8,14},{10,12},{12,10},{14,8},{16,22},{18,... | collective-permute-start | bytes 331784 | tf_op jit(solution)/shard_map/ppermute | solution.py:175
  8.0 0.7 %copy-start.9 = (s32[256]{0:T(256)S(1)}, s32[256]{0:T(256)}, u32[]{:S(2)}) copy-start(s32[256]{0:T(256)} %param.20) | copy-start | bytes 3076
  8.0 2.1 %copy-start.3 = (f32[128,256]{1,0:T(8,128)S(1)}, f32[128,256]{1,0:T(8,128)}, u32[]{:S(2)}) copy-start(f32[128,256]{1,0:T(8,128)} %refs_8_.1) | copy-start | bytes 393220
  8.0 2.1 %copy-start.7 = (f32[256,256]{1,0:T(8,128)S(1)}, f32[256,256]{1,0:T(8,128)}, u32[]{:S(2)}) copy-start(f32[256,256]{1,0:T(8,128)} %param.22) | copy-start | bytes 786436
  8.6 0.7 %copy-start.10 = (s32[256]{0:T(256)S(1)}, s32[256]{0:T(256)}, u32[]{:S(2)}) copy-start(s32[256]{0:T(256)} %param.18) | copy-start | bytes 3076
  9.3 0.7 %copy-start.11 = (s32[16]{0:T(128)S(1)}, s32[16]{0:T(128)}, u32[]{:S(2)}) copy-start(s32[16]{0:T(128)} %param.19) | copy-start | bytes 196
  10.1 1.0 %copy-start.2 = (f32[256,256]{1,0:T(8,128)S(1)}, f32[256,256]{1,0:T(8,128)}, u32[]{:S(2)}) copy-start(f32[256,256]{1,0:T(8,128)} %table.1) | copy-start | bytes 786436
  13.6 7.1 %collective-permute-start.4 = (f32[328,128]{1,0:T(8,128)S(1)}, f32[328,128]{1,0:T(8,128)S(1)}, u32[]{:S(2)}, u32[]{:S(2)}) collective-permute-start(f32[328,128]{1,0:T(8,128)S(1)} %get-tuple-element.46), channel_id=1, source_target_pairs={{0,4},{2,6},{4,0},{6,2},{8,12},{10,14},{12,8},{14,10},{16,20},{18,... | collective-permute-start | bytes 503816 | tf_op jit(solution)/shard_map/ppermute | solution.py:175
  15.2 7.6 %collective-permute-start.5 = (f32[328,128]{1,0:T(8,128)S(1)}, f32[328,128]{1,0:T(8,128)S(1)}, u32[]{:S(2)}, u32[]{:S(2)}) collective-permute-start(f32[328,128]{1,0:T(8,128)S(1)} %get-tuple-element.47), channel_id=1, source_target_pairs={{0,6},{2,4},{4,2},{6,0},{8,14},{10,12},{12,10},{14,8},{16,22},{18,... | collective-permute-start | bytes 503816 | tf_op jit(solution)/shard_map/ppermute | solution.py:175
  15.2 2.5 %copy-start.8 = (f32[256,256]{1,0:T(8,128)S(1)}, f32[256,256]{1,0:T(8,128)}, u32[]{:S(2)}) copy-start(f32[256,256]{1,0:T(8,128)} %param.25) | copy-start | bytes 786436
  16.0 7.4 %collective-permute-start.3 = (f32[3,128,128]{2,1,0:T(8,128)S(1)}, f32[3,128,128]{2,1,0:T(8,128)S(1)}, u32[]{:S(2)}, u32[]{:S(2)}) collective-permute-start(f32[3,128,128]{2,1,0:T(8,128)S(1)} %get-tuple-element.42), channel_id=1, source_target_pairs={{0,1},{1,0},{2,3},{3,2},{4,5},{5,4},{6,7},{7,6},{8,9},{9,8},{10,11... | collective-permute-start | bytes 589832 | tf_op jit(solution)/shard_map/ppermute | solution.py:175
  24.4 10.8 %collective-permute-start.9 = (f32[5,128,128]{2,1,0:T(8,128)S(1)}, f32[5,128,128]{2,1,0:T(8,128)S(1)}, u32[]{:S(2)}, u32[]{:S(2)}) collective-permute-start(f32[5,128,128]{2,1,0:T(8,128)S(1)} %get-tuple-element.50), channel_id=1, source_target_pairs={{0,1},{1,0},{2,3},{3,2},{4,5},{5,4},{6,7},{7,6},{8,9},{9,8},{10,11... | collective-permute-start | bytes 983048 | tf_op jit(solution)/shard_map/ppermute | solution.py:175
  26.2 7.4 %collective-permute-start.6 = (f32[128,128]{1,0:T(8,128)S(1)}, f32[128,128]{1,0:T(8,128)S(1)}, u32[]{:S(2)}, u32[]{:S(2)}) collective-permute-start(f32[128,128]{1,0:T(8,128)S(1)} %get-tuple-element.52), channel_id=1, source_target_pairs={{0,16},{2,18},{4,20},{6,22},{8,24},{10,26},{12,28},{14,30},{16,0},... | collective-permute-start | bytes 196616 | tf_op jit(solution)/shard_map/ppermute | solution.py:175
  28.8 6.2 %collective-permute-start.7 = (f32[128,128]{1,0:T(8,128)S(1)}, f32[128,128]{1,0:T(8,128)S(1)}, u32[]{:S(2)}, u32[]{:S(2)}) collective-permute-start(f32[128,128]{1,0:T(8,128)S(1)} %get-tuple-element.53), channel_id=1, source_target_pairs={{0,24},{2,26},{4,28},{6,30},{8,16},{10,18},{12,20},{14,22},{16,8},... | collective-permute-start | bytes 196616 | tf_op jit(solution)/shard_map/ppermute | solution.py:175
  30.2 5.0 %collective-permute-start.8 = (f32[128,128]{1,0:T(8,128)S(1)}, f32[128,128]{1,0:T(8,128)S(1)}, u32[]{:S(2)}, u32[]{:S(2)}) collective-permute-start(f32[128,128]{1,0:T(8,128)S(1)} %get-tuple-element.54), channel_id=1, source_target_pairs={{0,8},{2,10},{4,12},{6,14},{8,0},{10,2},{12,4},{14,6},{16,24},{18,... | collective-permute-start | bytes 196616 | tf_op jit(solution)/shard_map/ppermute | solution.py:175
  35.2 7.4 %collective-permute-start.10 = (f32[128,128]{1,0:T(8,128)S(1)}, f32[128,128]{1,0:T(8,128)S(1)}, u32[]{:S(2)}, u32[]{:S(2)}) collective-permute-start(f32[128,128]{1,0:T(8,128)S(1)} %get-tuple-element.57), channel_id=1, source_target_pairs={{0,16},{2,18},{4,20},{6,22},{8,24},{10,26},{12,28},{14,30},{16,0},... | collective-permute-start | bytes 196616 | tf_op jit(solution)/shard_map/ppermute | solution.py:175
  37.9 6.2 %collective-permute-start.11 = (f32[128,128]{1,0:T(8,128)S(1)}, f32[128,128]{1,0:T(8,128)S(1)}, u32[]{:S(2)}, u32[]{:S(2)}) collective-permute-start(f32[128,128]{1,0:T(8,128)S(1)} %get-tuple-element.58), channel_id=1, source_target_pairs={{0,24},{2,26},{4,28},{6,30},{8,16},{10,18},{12,20},{14,22},{16,8},... | collective-permute-start | bytes 196616 | tf_op jit(solution)/shard_map/ppermute | solution.py:175
  38.5 5.6 %collective-permute-start.12 = (f32[128,128]{1,0:T(8,128)S(1)}, f32[128,128]{1,0:T(8,128)S(1)}, u32[]{:S(2)}, u32[]{:S(2)}) collective-permute-start(f32[128,128]{1,0:T(8,128)S(1)} %get-tuple-element.59), channel_id=1, source_target_pairs={{0,8},{2,10},{4,12},{6,14},{8,0},{10,2},{12,4},{14,6},{16,24},{18,... | collective-permute-start | bytes 196616 | tf_op jit(solution)/shard_map/ppermute | solution.py:175
  45.0 4.9 %collective-permute-start.13 = (f32[4,16,256]{2,1,0:T(8,128)S(1)}, f32[4,16,256]{2,1,0:T(8,128)S(1)}, u32[]{:S(2)}, u32[]{:S(2)}) collective-permute-start(f32[4,16,256]{2,1,0:T(8,128)S(1)} %get-tuple-element.63), channel_id=1, source_target_pairs={{0,2},{2,0},{4,6},{6,4},{8,10},{10,8},{12,14},{14,12},{16,18},{18,... | collective-permute-start | bytes 196616 | tf_op jit(solution)/shard_map/ppermute | solution.py:175
  45.0 3.9 %collective-permute-start.14 = (f32[2,16,256]{2,1,0:T(8,128)S(1)}, f32[2,16,256]{2,1,0:T(8,128)S(1)}, u32[]{:S(2)}, u32[]{:S(2)}) collective-permute-start(f32[2,16,256]{2,1,0:T(8,128)S(1)} %get-tuple-element.64), channel_id=1, source_target_pairs={{0,4},{2,6},{4,0},{6,2},{8,12},{10,14},{12,8},{14,10},{16,20},{18,... | collective-permute-start | bytes 98312 | tf_op jit(solution)/shard_map/ppermute | solution.py:175
  46.5 3.3 %collective-permute-start.15 = (f32[2,16,256]{2,1,0:T(8,128)S(1)}, f32[2,16,256]{2,1,0:T(8,128)S(1)}, u32[]{:S(2)}, u32[]{:S(2)}) collective-permute-start(f32[2,16,256]{2,1,0:T(8,128)S(1)} %get-tuple-element.65), channel_id=1, source_target_pairs={{0,6},{2,4},{4,2},{6,0},{8,14},{10,12},{12,10},{14,8},{16,22},{18,... | collective-permute-start | bytes 98312 | tf_op jit(solution)/shard_map/ppermute | solution.py:175
  46.9 6.0 %collective-permute-start.18 = (f32[2,16,256]{2,1,0:T(8,128)S(1)}, f32[2,16,256]{2,1,0:T(8,128)S(1)}, u32[]{:S(2)}, u32[]{:S(2)}) collective-permute-start(f32[2,16,256]{2,1,0:T(8,128)S(1)} %get-tuple-element.68), channel_id=1, source_target_pairs={{0,4},{2,6},{4,0},{6,2},{8,12},{10,14},{12,8},{14,10},{16,20},{18,... | collective-permute-start | bytes 98312 | tf_op jit(solution)/shard_map/ppermute | solution.py:175
  48.4 4.5 %collective-permute-start.19 = (f32[2,16,256]{2,1,0:T(8,128)S(1)}, f32[2,16,256]{2,1,0:T(8,128)S(1)}, u32[]{:S(2)}, u32[]{:S(2)}) collective-permute-start(f32[2,16,256]{2,1,0:T(8,128)S(1)} %get-tuple-element.69), channel_id=1, source_target_pairs={{0,6},{2,4},{4,2},{6,0},{8,14},{10,12},{12,10},{14,8},{16,22},{18,... | collective-permute-start | bytes 98312 | tf_op jit(solution)/shard_map/ppermute | solution.py:175
  49.9 8.4 %collective-permute-start.16 = (f32[4,16,256]{2,1,0:T(8,128)S(1)}, f32[4,16,256]{2,1,0:T(8,128)S(1)}, u32[]{:S(2)}, u32[]{:S(2)}) collective-permute-start(f32[4,16,256]{2,1,0:T(8,128)S(1)} %get-tuple-element.66), channel_id=1, source_target_pairs={{0,16},{2,18},{4,20},{6,22},{8,24},{10,26},{12,28},{14,30},{16,0},... | collective-permute-start | bytes 196616 | tf_op jit(solution)/shard_map/ppermute | solution.py:175
  51.5 6.9 %collective-permute-start.17 = (f32[4,16,256]{2,1,0:T(8,128)S(1)}, f32[4,16,256]{2,1,0:T(8,128)S(1)}, u32[]{:S(2)}, u32[]{:S(2)}) collective-permute-start(f32[4,16,256]{2,1,0:T(8,128)S(1)} %get-tuple-element.67), channel_id=1, source_target_pairs={{0,24},{2,26},{4,28},{6,30},{8,16},{10,18},{12,20},{14,22},{16,8},... | collective-permute-start | bytes 196616 | tf_op jit(solution)/shard_map/ppermute | solution.py:175
  52.9 6.6 %collective-permute-start.20 = (f32[4,16,256]{2,1,0:T(8,128)S(1)}, f32[4,16,256]{2,1,0:T(8,128)S(1)}, u32[]{:S(2)}, u32[]{:S(2)}) collective-permute-start(f32[4,16,256]{2,1,0:T(8,128)S(1)} %get-tuple-element.70), channel_id=1, source_target_pairs={{0,8},{2,10},{4,12},{6,14},{8,0},{10,2},{12,4},{14,6},{16,24},{18,... | collective-permute-start | bytes 196616 | tf_op jit(solution)/shard_map/ppermute | solution.py:175

commit v8 on v7

--- a/solution.py
+++ b/solution.py
@@ -157,10 +157,11 @@
         at += rows
 
 
-def turn_kernel(start, own, core, third, fourth, first, second):
-    for i, out in enumerate((first, second)):
-        for m, (block, at) in enumerate(((own, start), (core, start), (third, 0), (fourth, 0))):
-            out[m] = block[at + i]
+def turn_kernel(*refs):
+    blocks, outs = refs[:4], refs[4:]
+    for i, out in enumerate(outs):
+        for m, block in enumerate(blocks):
+            out[m] = block[i]
 
 
 def final_kernel(incidence, own, table, w_top, w_low, *refs):
@@ -173,6 +174,10 @@
 
 def swap(x, axis, mask, size):
     return lax.ppermute(x, axis, [(i, i ^ mask) for i in range(size)])
+
+
+def after(value, ready):
+    return lax.optimization_barrier((*value, *ready))[: len(value)]
 
 
 def spread(x):
@@ -196,9 +201,6 @@
     def across(parts):
         return [swap(part, "hash", mask, peers) for part, mask in zip(parts, (8, 12, 4))]
 
-    def after(value, ready):
-        return lax.optimization_barrier((*value, *ready))[: len(value)]
-
     first = near((l2, l3))
     core = swap(core, "hash", 1, peers)
     second = near(after((r2, r3), first))
@@ -221,16 +223,11 @@
     return jnp.concatenate([pick(x, (place[0] & 3) ^ m, 1) for m in range(4)], 1)
 
 
-def deliver(own, core, a2, a3, b2, b3):
+def deliver(*blocks):
     peers = 16
-    turned = [(4, *own.shape[1:])] * 2
-    a2, a3 = swap(a2, "hash", 2, peers), swap(a3, "hash", 3, peers)
-    core = swap(core, "hash", 1, peers)
-    b2, b3 = swap(b2, "hash", 2, peers), swap(b3, "hash", 3, peers)
-    two, three = call(functools.partial(turn_kernel, 0), turned, (own, core, a2, a3))
-    two, three = swap(two, "hash", 8, peers), swap(three, "hash", 12, peers)
-    one, here = call(functools.partial(turn_kernel, 2), turned, (own, core, b2, b3))
-    return [two, three, swap(one, "hash", 4, peers), here]
+    near = [blocks[0]] + [swap(blocks[m], "hash", m, peers) for m in (1, 2, 3)]
+    two, three, one, own = call(turn_kernel, [blocks[0].shape] * 4, near)
+    return [swap(two, "hash", 8, peers), swap(three, "hash", 12, peers), swap(one, "hash", 4, peers), own]
 
 
 def gathered_plainly(transactions, tx_product, tx_count, w_msg, mine):
@@ -292,15 +289,14 @@
     picks = (named.reshape(-1)[:, None] == lax.iota(jnp.int32, mine)[None, :]).astype(bf16)
     incidence = (receivers.reshape(-1)[None, :] == lax.iota(jnp.int32, customers.shape[0])[:, None]).astype(bf16)
 
-    counts = (4, 4, 2, 2, 2, 2) if near else (peers,)
+    counts = (4, 4, 4, 4) if near else (peers,)
     new_products, *listed = call(
         functools.partial(update_kernel, len(parts)),
         [products.shape] + [(n, send_slots, width) for n in counts],
         (*parts, product_self, products, *split_outside(w_prod_agg), picks),
     )
     if near:
-        own, core, a2, b2, a3, b3 = listed
-        incoming = deliver(own, core, a2, a3, b2, b3)
+        incoming = deliver(*listed)
     else:
         incoming = [spread(listed[0])]
     (new_customers,) = call(

time: 61.1 us -> 61.4 us (level)
  waiting for transfers between devices: 25.1 us -> 27.1 us
  starting transfers between devices: 23 us -> 21.3 us
    ppermute x21 -> x19, waiting for transfers between devices: 25.1 us -> 27.1 us  [swap(): return lax.ppermute(x, axis, [(i, i ^ mask) for i in range(size)])]
    ppermute x21 -> x19, starting transfers between devices: 23 us -> 21.3 us  [swap(): return lax.ppermute(x, axis, [(i, i ^ mask) for i in range(size)])]
    pallas_call x9 -> x8, Pallas kernels: 5.1 us -> 5.1 us  [call(): pl.pallas_call(kernel, out_shape=[jax.ShapeDtypeStruct(s, f32) for s in o...]
  transfers between devices with their start and end apart: 21 -> 19, of which waited for: 14 -> 14; matrix products, arithmetic and copies ran while one was open for 2% -> 2% of each run, Pallas kernels for 1% -> 1%
where the time goes in v8:
time: 61.4 us; the launch traced here: 61.1 us
  waiting for transfers between devices  27.1 us (44%)
  starting transfers between devices  21.3 us (35%)
  Pallas kernels  5.1 us (8%)
  local copies, waits for them, and re-layouts  4.79 us (8%)
  other arithmetic  1.42 us (2%)
  between operations  0.85 us (1%)
    ppermute x19, waiting for transfers between devices, swap(): return lax.ppermute(x, axis, [(i, i ^ mask) for i in range(size)])  27.1 us
    ppermute x19, starting transfers between devices, swap(): return lax.ppermute(x, axis, [(i, i ^ mask) for i in range(size)])  21.3 us
    pallas_call x8, Pallas kernels, call(): pl.pallas_call(kernel, out_shape=[jax.ShapeDtypeStruct(s, f32) for s in o...  5.1 us
    unnamed x24, local copies, waits for them, and re-layouts  4.32 us
  transfers between devices with their start and end apart: 19, of which 14 were waited for; matrix products, arithmetic and copies ran while one was open for 2% of the time, Pallas kernels for 1%

profile of v8, /device:TPU:0, one launch (start us, length us, event | category | flops | bytes accessed | tf_op | source)
XLA Modules:
  0.0 61.1 jit_solution(17420721667286663294)
XLA Ops:
  0.7 1.0 %fusion = (bf16[256,256]{1,0:T(8,128)(2,1)S(1)}, bf16[256,256]{1,0:T(8,128)(2,1)S(1)}) fusion(f32[256,256]{1,0:T(8,128)} %param.21), kind=kLoop, calls=%fused_computation.6 | loop fusion | flops 262144 | bytes 524288 | tf_op jit(solution)/shard_map/convert_element_type | solution.py:23
  1.8 0.6 copy-done.4
  2.4 1.2 %copy-done.1 = f32[1024,256]{1,0:T(8,128)S(1)} copy-done((f32[1024,256]{1,0:T(8,128)S(1)}, f32[1024,256]{1,0:T(8,128)}, u32[]{:S(2)}) %copy-start.1) | copy-done | bytes 1048600
  3.7 1.1 %shard_map.140 = (f32[4,136,128]{2,1,0:T(8,128)S(1)}, f32[4,136,128]{2,1,0:T(8,128)S(1)}, f32[3,72,128]{2,1,0:T(8,128)S(1)}, f32[3,72,128]{2,1,0:T(8,128)S(1)}, ...) custom-call(s32[2]{0:T(128)S(1)} %pad_add_fusion.3.place, s32[16]{0:T(128)S(1)} %copy-done.5, f32[1024,256]{1,0:T(8,128)S(1)} %copy-done.1, ...), custom_call_target="tpu_custom_call" | custom-call | tf_op jit(solution)/shard_map/pallas_call | solution.py:43
  4.8 0.5 collective-permute-start
  5.3 2.6 %collective-permute-start.1 = (f32[3,72,128]{2,1,0:T(8,128)S(1)}, f32[3,72,128]{2,1,0:T(8,128)S(1)}, u32[]{:S(2)}, u32[]{:S(2)}) collective-permute-start(f32[3,72,128]{2,1,0:T(8,128)S(1)} %get-tuple-element.37), channel_id=1, source_target_pairs={{0,4},{2,6},{4,0},{6,2},{8,12},{10,14},{12,8},{14,10},{16,20},{18,... | collective-permute-start | bytes 331784 | tf_op jit(solution)/shard_map/ppermute | solution.py:176
  8.0 0.6 %copy-done.9 = s32[256]{0:T(256)S(1)} copy-done((s32[256]{0:T(256)S(1)}, s32[256]{0:T(256)}, u32[]{:S(2)}) %copy-start.9) | copy-done | bytes 1048
  8.6 0.1 reshape_reshape.3
  8.7 0.6 copy-done.10
  9.3 0.1 reshape.22
  9.4 0.6 copy-done.11
  10.1 0.2 fusion.6.refs_7_
  10.4 0.6 %copy-done.2 = f32[256,256]{1,0:T(8,128)S(1)} copy-done((f32[256,256]{1,0:T(8,128)S(1)}, f32[256,256]{1,0:T(8,128)}, u32[]{:S(2)}) %copy-start.2) | copy-done | bytes 262168
  11.0 0.3 fusion.7.own
  11.5 0.3 collective-permute-done.1.l2
  11.8 1.8 %collective-permute-done.2.l3 = f32[3,72,128]{2,1,0:T(8,128)S(1)} collective-permute-done((f32[3,72,128]{2,1,0:T(8,128)S(1)}, f32[3,72,128]{2,1,0:T(8,128)S(1)}, u32[]{:S(2)}, u32[]{:S(2)}) %collective-permute-start.2) | collective-permute-done | bytes 110624 | tf_op jit(solution)/shard_map/ppermute | solution.py:176
  13.6 1.6 %collective-permute-start.4 = (f32[328,128]{1,0:T(8,128)S(1)}, f32[328,128]{1,0:T(8,128)S(1)}, u32[]{:S(2)}, u32[]{:S(2)}) collective-permute-start(f32[328,128]{1,0:T(8,128)S(1)} %get-tuple-element.44), channel_id=1, source_target_pairs={{0,4},{2,6},{4,0},{6,2},{8,12},{10,14},{12,8},{14,10},{16,20},{18,... | collective-permute-start | bytes 503816 | tf_op jit(solution)/shard_map/ppermute | solution.py:176
  15.2 0.8 %shard_map.141 = (f32[3,128,128]{2,1,0:T(8,128)S(1)}, f32[3,128,128]{2,1,0:T(8,128)S(1)}, f32[8,128]{1,0:T(8,128)S(1)}) custom-call(s32[2]{0:T(128)S(1)} %pad_add_fusion.3.place, f32[4,136,128]{2,1,0:T(8,128)S(1)} %get-tuple-element.35.own, f32[4,136,128]{2,1,0:T(8,128)S(1)} %collective-permute-done.core, f32[3,72,128]{2,1,0:T(8,128)S(1)} %collective-permute-done.1.l2, ...), custom_call_target="tpu_custom_call" | custom-call | tf_op jit(solution)/shard_map/pallas_call | solution.py:43
  16.0 1.7 %collective-permute-start.3 = (f32[3,128,128]{2,1,0:T(8,128)S(1)}, f32[3,128,128]{2,1,0:T(8,128)S(1)}, u32[]{:S(2)}, u32[]{:S(2)}) collective-permute-start(f32[3,128,128]{2,1,0:T(8,128)S(1)} %get-tuple-element.40), channel_id=1, source_target_pairs={{0,1},{1,0},{2,3},{3,2},{4,5},{5,4},{6,7},{7,6},{8,9},{9,8},{10,11... | collective-permute-start | bytes 589832 | tf_op jit(solution)/shard_map/ppermute | solution.py:176
  17.8 3.0 %collective-permute-done.4.r2 = f32[328,128]{1,0:T(8,128)S(1)} collective-permute-done((f32[328,128]{1,0:T(8,128)S(1)}, f32[328,128]{1,0:T(8,128)S(1)}, u32[]{:S(2)}, u32[]{:S(2)}) %collective-permute-start.4) | collective-permute-done | bytes 167968 | tf_op jit(solution)/shard_map/ppermute | solution.py:176
  20.8 2.0 %collective-permute-done.5.r3 = f32[328,128]{1,0:T(8,128)S(1)} collective-permute-done((f32[328,128]{1,0:T(8,128)S(1)}, f32[328,128]{1,0:T(8,128)S(1)}, u32[]{:S(2)}, u32[]{:S(2)}) %collective-permute-start.5) | collective-permute-done | bytes 167968 | tf_op jit(solution)/shard_map/ppermute | solution.py:176
  22.8 0.7 %collective-permute-done.3.got = f32[3,128,128]{2,1,0:T(8,128)S(1)} collective-permute-done((f32[3,128,128]{2,1,0:T(8,128)S(1)}, f32[3,128,128]{2,1,0:T(8,128)S(1)}, u32[]{:S(2)}, u32[]{:S(2)}) %collective-permute-start.3) | collective-permute-done | bytes 196640 | tf_op jit(solution)/shard_map/ppermute | solution.py:176
  23.5 0.9 %shard_map.142 = (f32[5,128,128]{2,1,0:T(8,128)S(1)}, f32[5,128,128]{2,1,0:T(8,128)S(1)}) custom-call(s32[2]{0:T(128)S(1)} %pad_add_fusion.3.place, f32[8,128]{1,0:T(8,128)S(1)} %get-tuple-element.41.ids, f32[4,136,128]{2,1,0:T(8,128)S(1)} %get-tuple-element.35.own, f32[4,136,128]{2,1,0:T(8,128)S(1)} %collective-permute-done.core, ...), custom_call_target="tpu_custom_call" | custom-call | tf_op jit(solution)/shard_map/pallas_call | solution.py:43
  24.4 1.7 %collective-permute-start.9 = (f32[5,128,128]{2,1,0:T(8,128)S(1)}, f32[5,128,128]{2,1,0:T(8,128)S(1)}, u32[]{:S(2)}, u32[]{:S(2)}) collective-permute-start(f32[5,128,128]{2,1,0:T(8,128)S(1)} %get-tuple-element.48), channel_id=1, source_target_pairs={{0,1},{1,0},{2,3},{3,2},{4,5},{5,4},{6,7},{7,6},{8,9},{9,8},{10,11... | collective-permute-start | bytes 983048 | tf_op jit(solution)/shard_map/ppermute | solution.py:176
  26.0 0.1 fusion.4.refs_11_
  26.2 2.6 %collective-permute-start.6 = (f32[128,128]{1,0:T(8,128)S(1)}, f32[128,128]{1,0:T(8,128)S(1)}, u32[]{:S(2)}, u32[]{:S(2)}) collective-permute-start(f32[128,128]{1,0:T(8,128)S(1)} %get-tuple-element.50), channel_id=1, source_target_pairs={{0,16},{2,18},{4,20},{6,22},{8,24},{10,26},{12,28},{14,30},{16,0},... | collective-permute-start | bytes 196616 | tf_op jit(solution)/shard_map/ppermute | solution.py:176
  28.8 1.4 %collective-permute-start.7 = (f32[128,128]{1,0:T(8,128)S(1)}, f32[128,128]{1,0:T(8,128)S(1)}, u32[]{:S(2)}, u32[]{:S(2)}) collective-permute-start(f32[128,128]{1,0:T(8,128)S(1)} %get-tuple-element.51), channel_id=1, source_target_pairs={{0,24},{2,26},{4,28},{6,30},{8,16},{10,18},{12,20},{14,22},{16,8},... | collective-permute-start | bytes 196616 | tf_op jit(solution)/shard_map/ppermute | solution.py:176
  30.2 0.2 collective-permute-start.8
  30.4 3.2 %collective-permute-done.6.refs_0_ = f32[128,128]{1,0:T(8,128)S(1)} collective-permute-done((f32[128,128]{1,0:T(8,128)S(1)}, f32[128,128]{1,0:T(8,128)S(1)}, u32[]{:S(2)}, u32[]{:S(2)}) %collective-permute-start.6) | collective-permute-done | bytes 65568 | tf_op jit(solution)/shard_map/ppermute | solution.py:176
  33.6 1.4 %collective-permute-done.7.refs_1_ = f32[128,128]{1,0:T(8,128)S(1)} collective-permute-done((f32[128,128]{1,0:T(8,128)S(1)}, f32[128,128]{1,0:T(8,128)S(1)}, u32[]{:S(2)}, u32[]{:S(2)}) %collective-permute-start.7) | collective-permute-done | bytes 65568 | tf_op jit(solution)/shard_map/ppermute | solution.py:176
  35.0 0.1 collective-permute-done.8.refs_2_
  35.2 2.7 %collective-permute-start.10 = (f32[128,128]{1,0:T(8,128)S(1)}, f32[128,128]{1,0:T(8,128)S(1)}, u32[]{:S(2)}, u32[]{:S(2)}) collective-permute-start(f32[128,128]{1,0:T(8,128)S(1)} %get-tuple-element.55), channel_id=1, source_target_pairs={{0,16},{2,18},{4,20},{6,22},{8,24},{10,26},{12,28},{14,30},{16,0},... | collective-permute-start | bytes 196616 | tf_op jit(solution)/shard_map/ppermute | solution.py:176
  37.9 0.6 collective-permute-start.11
  38.5 0.3 collective-permute-start.12
  38.8 3.8 %collective-permute-done.10.refs_3_ = f32[128,128]{1,0:T(8,128)S(1)} collective-permute-done((f32[128,128]{1,0:T(8,128)S(1)}, f32[128,128]{1,0:T(8,128)S(1)}, u32[]{:S(2)}, u32[]{:S(2)}) %collective-permute-start.10) | collective-permute-done | bytes 65568 | tf_op jit(solution)/shard_map/ppermute | solution.py:176
  42.6 1.5 %collective-permute-done.11.refs_4_ = f32[128,128]{1,0:T(8,128)S(1)} collective-permute-done((f32[128,128]{1,0:T(8,128)S(1)}, f32[128,128]{1,0:T(8,128)S(1)}, u32[]{:S(2)}, u32[]{:S(2)}) %collective-permute-start.11) | collective-permute-done | bytes 65568 | tf_op jit(solution)/shard_map/ppermute | solution.py:176
  44.1 0.9 %shard_map.145 = (f32[128,256]{1,0:T(8,128)}, f32[4,16,256]{2,1,0:T(8,128)S(1)}, f32[4,16,256]{2,1,0:T(8,128)S(1)}, f32[4,16,256]{2,1,0:T(8,128)S(1)}, f32[4,16,256]{2,1,0:T(8,128)S(1)}) custom-call(f32[128,128]{1,0:T(8,128)S(1)} %collective-permute-done.6.refs_0_, f32[128,128]{1,0:T(8,128)S(1)} %collective-permute-done.7.refs_1_, ...), custom_call_target="tpu_custom_call" | custom-call | tf_op jit(solution)/shard_map/pallas_call | solution.py:43
  45.0 1.5 %collective-permute-start.14 = (f32[4,16,256]{2,1,0:T(8,128)S(1)}, f32[4,16,256]{2,1,0:T(8,128)S(1)}, u32[]{:S(2)}, u32[]{:S(2)}) collective-permute-start(f32[4,16,256]{2,1,0:T(8,128)S(1)} %get-tuple-element.62), channel_id=1, source_target_pairs={{0,4},{2,6},{4,0},{6,2},{8,12},{10,14},{12,8},{14,10},{16,20},{18,... | collective-permute-start | bytes 196616 | tf_op jit(solution)/shard_map/ppermute | solution.py:176
  46.5 0.4 collective-permute-start.15
  46.9 0.1 eq.34
  47.0 2.6 %collective-permute-done.14.refs_2_ = f32[4,16,256]{2,1,0:T(8,128)S(1)} collective-permute-done((f32[4,16,256]{2,1,0:T(8,128)S(1)}, f32[4,16,256]{2,1,0:T(8,128)S(1)}, u32[]{:S(2)}, u32[]{:S(2)}) %collective-permute-start.14) | collective-permute-done | bytes 65568 | tf_op jit(solution)/shard_map/ppermute | solution.py:176
  49.6 1.1 %collective-permute-done.15.refs_3_ = f32[4,16,256]{2,1,0:T(8,128)S(1)} collective-permute-done((f32[4,16,256]{2,1,0:T(8,128)S(1)}, f32[4,16,256]{2,1,0:T(8,128)S(1)}, u32[]{:S(2)}, u32[]{:S(2)}) %collective-permute-start.15) | collective-permute-done | bytes 65568 | tf_op jit(solution)/shard_map/ppermute | solution.py:176
  50.6 1.6 %collective-permute-start.16 = (f32[4,16,256]{2,1,0:T(8,128)S(1)}, f32[4,16,256]{2,1,0:T(8,128)S(1)}, u32[]{:S(2)}, u32[]{:S(2)}) collective-permute-start(f32[4,16,256]{2,1,0:T(8,128)S(1)} %get-tuple-element.64), channel_id=1, source_target_pairs={{0,16},{2,18},{4,20},{6,22},{8,24},{10,26},{12,28},{14,30},{16,0},... | collective-permute-start | bytes 196616 | tf_op jit(solution)/shard_map/ppermute | solution.py:176
  52.2 1.4 %collective-permute-start.17 = (f32[4,16,256]{2,1,0:T(8,128)S(1)}, f32[4,16,256]{2,1,0:T(8,128)S(1)}, u32[]{:S(2)}, u32[]{:S(2)}) collective-permute-start(f32[4,16,256]{2,1,0:T(8,128)S(1)} %get-tuple-element.65), channel_id=1, source_target_pairs={{0,24},{2,26},{4,28},{6,30},{8,16},{10,18},{12,20},{14,22},{16,8},... | collective-permute-start | bytes 196616 | tf_op jit(solution)/shard_map/ppermute | solution.py:176
  53.6 0.6 collective-permute-start.18
  54.2 4.5 %collective-permute-done.16.refs_0_ = f32[4,16,256]{2,1,0:T(8,128)S(1)} collective-permute-done((f32[4,16,256]{2,1,0:T(8,128)S(1)}, f32[4,16,256]{2,1,0:T(8,128)S(1)}, u32[]{:S(2)}, u32[]{:S(2)}) %collective-permute-start.16) | collective-permute-done | bytes 65568 | tf_op jit(solution)/shard_map/ppermute | solution.py:176
  58.7 1.2 %collective-permute-done.18.refs_2_ = f32[4,16,256]{2,1,0:T(8,128)S(1)} collective-permute-done((f32[4,16,256]{2,1,0:T(8,128)S(1)}, f32[4,16,256]{2,1,0:T(8,128)S(1)}, u32[]{:S(2)}, u32[]{:S(2)}) %collective-permute-start.18) | collective-permute-done | bytes 65568 | tf_op jit(solution)/shard_map/ppermute | solution.py:176
  59.9 1.2 %shard_map.147 = f32[256,256]{1,0:T(8,128)} custom-call(bf16[256,256]{1,0:T(8,128)(2,1)S(1)} %fusion.3.incidence, f32[256,256]{1,0:T(8,128)S(1)} %fusion.7.own, f32[256,256]{1,0:T(8,128)S(1)} %copy-done.2, bf16[256,256]{1,0:T(8,128)(2,1)S(1)} %get-tuple-element.69.w_top, bf16[256,256]{1,0:T(8,128)(2,1)S(1)} %get-tuple-element.68.w_low, ...), custom_call_target="tpu_custom_call" | custom-call | tf_op jit(solution)/shard_map/pallas_call | solution.py:43
  (44 shorter events, 0.8 us)
Async XLA Ops:
  0.6 9.8 %copy-start = (f32[256,256]{1,0:T(8,128)S(1)}, f32[256,256]{1,0:T(8,128)}, u32[]{:S(2)}) copy-start(f32[256,256]{1,0:T(8,128)} %param.24) | copy-start | bytes 786436
  1.7 0.7 %copy-start.4 = (s32[1024]{0:T(1024)S(1)}, s32[1024]{0:T(1024)}, u32[]{:S(2)}) copy-start(s32[1024]{0:T(1024)} %param.14) | copy-start | bytes 12292
  1.8 0.7 %copy-start.5 = (s32[16]{0:T(128)S(1)}, s32[16]{0:T(128)}, u32[]{:S(2)}) copy-start(s32[16]{0:T(128)} %count.1) | copy-start | bytes 196
  2.4 1.2 %copy-start.1 = (f32[1024,256]{1,0:T(8,128)S(1)}, f32[1024,256]{1,0:T(8,128)}, u32[]{:S(2)}) copy-start(f32[1024,256]{1,0:T(8,128)} %tx.1) | copy-start | bytes 3145732
  3.6 4.3 %copy-start.6 = (f32[256,256]{1,0:T(8,128)S(1)}, f32[256,256]{1,0:T(8,128)}, u32[]{:S(2)}) copy-start(f32[256,256]{1,0:T(8,128)} %param.23) | copy-start | bytes 786436
  4.8 10.4 %collective-permute-start = (f32[4,136,128]{2,1,0:T(8,128)S(1)}, f32[4,136,128]{2,1,0:T(8,128)S(1)}, u32[]{:S(2)}, u32[]{:S(2)}) collective-permute-start(f32[4,136,128]{2,1,0:T(8,128)S(1)} %get-tuple-element.36), channel_id=1, source_target_pairs={{0,2},{2,0},{4,6},{6,4},{8,10},{10,8},{12,14},{14,12},{16,18},{18,... | collective-permute-start | bytes 835592 | tf_op jit(solution)/shard_map/ppermute | solution.py:176
  5.3 6.5 %collective-permute-start.1 = (f32[3,72,128]{2,1,0:T(8,128)S(1)}, f32[3,72,128]{2,1,0:T(8,128)S(1)}, u32[]{:S(2)}, u32[]{:S(2)}) collective-permute-start(f32[3,72,128]{2,1,0:T(8,128)S(1)} %get-tuple-element.37), channel_id=1, source_target_pairs={{0,4},{2,6},{4,0},{6,2},{8,12},{10,14},{12,8},{14,10},{16,20},{18,... | collective-permute-start | bytes 331784 | tf_op jit(solution)/shard_map/ppermute | solution.py:176
  7.9 5.8 %collective-permute-start.2 = (f32[3,72,128]{2,1,0:T(8,128)S(1)}, f32[3,72,128]{2,1,0:T(8,128)S(1)}, u32[]{:S(2)}, u32[]{:S(2)}) collective-permute-start(f32[3,72,128]{2,1,0:T(8,128)S(1)} %get-tuple-element.38), channel_id=1, source_target_pairs={{0,6},{2,4},{4,2},{6,0},{8,14},{10,12},{12,10},{14,8},{16,22},{18,... | collective-permute-start | bytes 331784 | tf_op jit(solution)/shard_map/ppermute | solution.py:176
  8.0 0.7 %copy-start.9 = (s32[256]{0:T(256)S(1)}, s32[256]{0:T(256)}, u32[]{:S(2)}) copy-start(s32[256]{0:T(256)} %param.20) | copy-start | bytes 3076
  8.0 2.1 %copy-start.3 = (f32[128,256]{1,0:T(8,128)S(1)}, f32[128,256]{1,0:T(8,128)}, u32[]{:S(2)}) copy-start(f32[128,256]{1,0:T(8,128)} %refs_8_.1) | copy-start | bytes 393220
  8.0 2.1 %copy-start.7 = (f32[256,256]{1,0:T(8,128)S(1)}, f32[256,256]{1,0:T(8,128)}, u32[]{:S(2)}) copy-start(f32[256,256]{1,0:T(8,128)} %param.22) | copy-start | bytes 786436
  8.6 0.7 %copy-start.10 = (s32[256]{0:T(256)S(1)}, s32[256]{0:T(256)}, u32[]{:S(2)}) copy-start(s32[256]{0:T(256)} %param.18) | copy-start | bytes 3076
  9.3 0.7 %copy-start.11 = (s32[16]{0:T(128)S(1)}, s32[16]{0:T(128)}, u32[]{:S(2)}) copy-start(s32[16]{0:T(128)} %param.19) | copy-start | bytes 196
  10.1 1.0 %copy-start.2 = (f32[256,256]{1,0:T(8,128)S(1)}, f32[256,256]{1,0:T(8,128)}, u32[]{:S(2)}) copy-start(f32[256,256]{1,0:T(8,128)} %table.1) | copy-start | bytes 786436
  13.6 7.1 %collective-permute-start.4 = (f32[328,128]{1,0:T(8,128)S(1)}, f32[328,128]{1,0:T(8,128)S(1)}, u32[]{:S(2)}, u32[]{:S(2)}) collective-permute-start(f32[328,128]{1,0:T(8,128)S(1)} %get-tuple-element.44), channel_id=1, source_target_pairs={{0,4},{2,6},{4,0},{6,2},{8,12},{10,14},{12,8},{14,10},{16,20},{18,... | collective-permute-start | bytes 503816 | tf_op jit(solution)/shard_map/ppermute | solution.py:176
  15.2 7.6 %collective-permute-start.5 = (f32[328,128]{1,0:T(8,128)S(1)}, f32[328,128]{1,0:T(8,128)S(1)}, u32[]{:S(2)}, u32[]{:S(2)}) collective-permute-start(f32[328,128]{1,0:T(8,128)S(1)} %get-tuple-element.45), channel_id=1, source_target_pairs={{0,6},{2,4},{4,2},{6,0},{8,14},{10,12},{12,10},{14,8},{16,22},{18,... | collective-permute-start | bytes 503816 | tf_op jit(solution)/shard_map/ppermute | solution.py:176
  15.2 2.5 %copy-start.8 = (f32[256,256]{1,0:T(8,128)S(1)}, f32[256,256]{1,0:T(8,128)}, u32[]{:S(2)}) copy-start(f32[256,256]{1,0:T(8,128)} %param.25) | copy-start | bytes 786436
  16.0 7.4 %collective-permute-start.3 = (f32[3,128,128]{2,1,0:T(8,128)S(1)}, f32[3,128,128]{2,1,0:T(8,128)S(1)}, u32[]{:S(2)}, u32[]{:S(2)}) collective-permute-start(f32[3,128,128]{2,1,0:T(8,128)S(1)} %get-tuple-element.40), channel_id=1, source_target_pairs={{0,1},{1,0},{2,3},{3,2},{4,5},{5,4},{6,7},{7,6},{8,9},{9,8},{10,11... | collective-permute-start | bytes 589832 | tf_op jit(solution)/shard_map/ppermute | solution.py:176
  24.4 10.8 %collective-permute-start.9 = (f32[5,128,128]{2,1,0:T(8,128)S(1)}, f32[5,128,128]{2,1,0:T(8,128)S(1)}, u32[]{:S(2)}, u32[]{:S(2)}) collective-permute-start(f32[5,128,128]{2,1,0:T(8,128)S(1)} %get-tuple-element.48), channel_id=1, source_target_pairs={{0,1},{1,0},{2,3},{3,2},{4,5},{5,4},{6,7},{7,6},{8,9},{9,8},{10,11... | collective-permute-start | bytes 983048 | tf_op jit(solution)/shard_map/ppermute | solution.py:176
  26.2 7.4 %collective-permute-start.6 = (f32[128,128]{1,0:T(8,128)S(1)}, f32[128,128]{1,0:T(8,128)S(1)}, u32[]{:S(2)}, u32[]{:S(2)}) collective-permute-start(f32[128,128]{1,0:T(8,128)S(1)} %get-tuple-element.50), channel_id=1, source_target_pairs={{0,16},{2,18},{4,20},{6,22},{8,24},{10,26},{12,28},{14,30},{16,0},... | collective-permute-start | bytes 196616 | tf_op jit(solution)/shard_map/ppermute | solution.py:176
  28.8 6.2 %collective-permute-start.7 = (f32[128,128]{1,0:T(8,128)S(1)}, f32[128,128]{1,0:T(8,128)S(1)}, u32[]{:S(2)}, u32[]{:S(2)}) collective-permute-start(f32[128,128]{1,0:T(8,128)S(1)} %get-tuple-element.51), channel_id=1, source_target_pairs={{0,24},{2,26},{4,28},{6,30},{8,16},{10,18},{12,20},{14,22},{16,8},... | collective-permute-start | bytes 196616 | tf_op jit(solution)/shard_map/ppermute | solution.py:176
  30.2 5.0 %collective-permute-start.8 = (f32[128,128]{1,0:T(8,128)S(1)}, f32[128,128]{1,0:T(8,128)S(1)}, u32[]{:S(2)}, u32[]{:S(2)}) collective-permute-start(f32[128,128]{1,0:T(8,128)S(1)} %get-tuple-element.52), channel_id=1, source_target_pairs={{0,8},{2,10},{4,12},{6,14},{8,0},{10,2},{12,4},{14,6},{16,24},{18,... | collective-permute-start | bytes 196616 | tf_op jit(solution)/shard_map/ppermute | solution.py:176
  35.2 7.4 %collective-permute-start.10 = (f32[128,128]{1,0:T(8,128)S(1)}, f32[128,128]{1,0:T(8,128)S(1)}, u32[]{:S(2)}, u32[]{:S(2)}) collective-permute-start(f32[128,128]{1,0:T(8,128)S(1)} %get-tuple-element.55), channel_id=1, source_target_pairs={{0,16},{2,18},{4,20},{6,22},{8,24},{10,26},{12,28},{14,30},{16,0},... | collective-permute-start | bytes 196616 | tf_op jit(solution)/shard_map/ppermute | solution.py:176
  37.9 6.2 %collective-permute-start.11 = (f32[128,128]{1,0:T(8,128)S(1)}, f32[128,128]{1,0:T(8,128)S(1)}, u32[]{:S(2)}, u32[]{:S(2)}) collective-permute-start(f32[128,128]{1,0:T(8,128)S(1)} %get-tuple-element.56), channel_id=1, source_target_pairs={{0,24},{2,26},{4,28},{6,30},{8,16},{10,18},{12,20},{14,22},{16,8},... | collective-permute-start | bytes 196616 | tf_op jit(solution)/shard_map/ppermute | solution.py:176
  38.5 5.6 %collective-permute-start.12 = (f32[128,128]{1,0:T(8,128)S(1)}, f32[128,128]{1,0:T(8,128)S(1)}, u32[]{:S(2)}, u32[]{:S(2)}) collective-permute-start(f32[128,128]{1,0:T(8,128)S(1)} %get-tuple-element.57), channel_id=1, source_target_pairs={{0,8},{2,10},{4,12},{6,14},{8,0},{10,2},{12,4},{14,6},{16,24},{18,... | collective-permute-start | bytes 196616 | tf_op jit(solution)/shard_map/ppermute | solution.py:176
  45.0 2.0 %collective-permute-start.13 = (f32[4,16,256]{2,1,0:T(8,128)S(1)}, f32[4,16,256]{2,1,0:T(8,128)S(1)}, u32[]{:S(2)}, u32[]{:S(2)}) collective-permute-start(f32[4,16,256]{2,1,0:T(8,128)S(1)} %get-tuple-element.61), channel_id=1, source_target_pairs={{0,2},{2,0},{4,6},{6,4},{8,10},{10,8},{12,14},{14,12},{16,18},{18,... | collective-permute-start | bytes 196616 | tf_op jit(solution)/shard_map/ppermute | solution.py:176
  45.0 4.5 %collective-permute-start.14 = (f32[4,16,256]{2,1,0:T(8,128)S(1)}, f32[4,16,256]{2,1,0:T(8,128)S(1)}, u32[]{:S(2)}, u32[]{:S(2)}) collective-permute-start(f32[4,16,256]{2,1,0:T(8,128)S(1)} %get-tuple-element.62), channel_id=1, source_target_pairs={{0,4},{2,6},{4,0},{6,2},{8,12},{10,14},{12,8},{14,10},{16,20},{18,... | collective-permute-start | bytes 196616 | tf_op jit(solution)/shard_map/ppermute | solution.py:176
  46.5 4.1 %collective-permute-start.15 = (f32[4,16,256]{2,1,0:T(8,128)S(1)}, f32[4,16,256]{2,1,0:T(8,128)S(1)}, u32[]{:S(2)}, u32[]{:S(2)}) collective-permute-start(f32[4,16,256]{2,1,0:T(8,128)S(1)} %get-tuple-element.63), channel_id=1, source_target_pairs={{0,6},{2,4},{4,2},{6,0},{8,14},{10,12},{12,10},{14,8},{16,22},{18,... | collective-permute-start | bytes 196616 | tf_op jit(solution)/shard_map/ppermute | solution.py:176
  50.6 8.1 %collective-permute-start.16 = (f32[4,16,256]{2,1,0:T(8,128)S(1)}, f32[4,16,256]{2,1,0:T(8,128)S(1)}, u32[]{:S(2)}, u32[]{:S(2)}) collective-permute-start(f32[4,16,256]{2,1,0:T(8,128)S(1)} %get-tuple-element.64), channel_id=1, source_target_pairs={{0,16},{2,18},{4,20},{6,22},{8,24},{10,26},{12,28},{14,30},{16,0},... | collective-permute-start | bytes 196616 | tf_op jit(solution)/shard_map/ppermute | solution.py:176
  52.2 6.5 %collective-permute-start.17 = (f32[4,16,256]{2,1,0:T(8,128)S(1)}, f32[4,16,256]{2,1,0:T(8,128)S(1)}, u32[]{:S(2)}, u32[]{:S(2)}) collective-permute-start(f32[4,16,256]{2,1,0:T(8,128)S(1)} %get-tuple-element.65), channel_id=1, source_target_pairs={{0,24},{2,26},{4,28},{6,30},{8,16},{10,18},{12,20},{14,22},{16,8},... | collective-permute-start | bytes 196616 | tf_op jit(solution)/shard_map/ppermute | solution.py:176
  53.6 6.2 %collective-permute-start.18 = (f32[4,16,256]{2,1,0:T(8,128)S(1)}, f32[4,16,256]{2,1,0:T(8,128)S(1)}, u32[]{:S(2)}, u32[]{:S(2)}) collective-permute-start(f32[4,16,256]{2,1,0:T(8,128)S(1)} %get-tuple-element.66), channel_id=1, source_target_pairs={{0,8},{2,10},{4,12},{6,14},{8,0},{10,2},{12,4},{14,6},{16,24},{18,... | collective-permute-start | bytes 196616 | tf_op jit(solution)/shard_map/ppermute | solution.py:176

commit v9 on v8

--- a/solution.py
+++ b/solution.py
@@ -75,16 +75,16 @@
                 out[i, :slots, :] = left
                 out[i, slots : 2 * slots, :] = right
                 out[i, 2 * slots :, :] = twice
-            elif i < 3:
+            elif i < 2:
                 first, second = (l2, l3)[m - 2], (r2, r3)[m - 2]
                 first[i, :slots, :] = left
                 first[i, slots:, :] = twice
                 second[i * slots : (i + 1) * slots, :] = right
             else:
-                out = (r2, r3)[m - 2]
-                out[3 * slots : 4 * slots, :] = left
-                out[4 * slots : 5 * slots, :] = right
-                out[5 * slots :, :] = twice
+                out, at = (r2, r3)[m - 2], 2 * slots + (i - 2) * (2 * slots + PAD)
+                out[at : at + slots, :] = left
+                out[at + slots : at + 2 * slots, :] = right
+                out[at + 2 * slots : at + 2 * slots + PAD, :] = twice
 
 
 def targets(place, mine):
@@ -111,7 +111,7 @@
     target = targets(place, send.shape[1])
     senders = (own, core, l2, l3)
     slots = LANES // 2
-    for z in range(3):
+    for z in range(2):
         rows = joined([block[z, pl.ds(block.shape[1] - PAD, 1), :] for block in senders])
         for i in range(2):
             ids[pl.ds(2 * z + i, 1), :] = rows[i]
@@ -121,31 +121,33 @@
 def rest_kernel(place, ids, own, core, r2, r3, send, keep):
     target = targets(place, send.shape[1])
     slots = LANES // 2
-    for z in range(3):
+    for z in range(2):
         rows = [ids[pl.ds(2 * z + i, 1), :] for i in range(2)]
         blocks = [block[z, slots : 2 * slots, :] for block in (own, core)]
         blocks += [block[z * slots : (z + 1) * slots, :] for block in (r2, r3)]
         bucket_sum(rows, target, blocks, send, keep, z)
-    one = [block[3, pl.ds(2 * slots, 1), :] for block in (own, core)]
-    rows = joined(one + [block[pl.ds(5 * slots, 1), :] for block in (r2, r3)])
-    for side in range(2):
-        blocks = [block[3, side * slots : (side + 1) * slots, :] for block in (own, core)]
-        blocks += [block[(3 + side) * slots : (4 + side) * slots, :] for block in (r2, r3)]
-        bucket_sum(rows, target, blocks, send, keep, 3 + side)
+    for z in (2, 3):
+        at = 2 * slots + (z - 2) * (2 * slots + PAD)
+        one = [block[z, pl.ds(2 * slots, 1), :] for block in (own, core)]
+        rows = joined(one + [block[pl.ds(at + 2 * slots, 1), :] for block in (r2, r3)])
+        for side in range(2):
+            blocks = [block[z, side * slots : (side + 1) * slots, :] for block in (own, core)]
+            blocks += [block[at + side * slots : at + (side + 1) * slots, :] for block in (r2, r3)]
+            bucket_sum(rows, target, blocks, send, keep, 2 * z - 2 + side)
 
 
 def pair_kernel(keep, got, *outs):
-    for i in range(3):
+    for i in range(2):
         outs[i][...] = keep[i] + got[i]
-    for own in outs[3:]:
-        own[:, :LANES] = keep[3] + got[3]
-        own[:, LANES:] = keep[4] + got[4]
+    for i, out in enumerate(outs[2:]):
+        out[:, :LANES] = keep[2 * i + 2] + got[2 * i + 2]
+        out[:, LANES:] = keep[2 * i + 3] + got[2 * i + 3]
 
 
 def update_kernel(n, *refs):
     parts, (own, table, w_top, w_low, picks), (new, *outs) = refs[:n], refs[n : n + 5], refs[n + 5 :]
     wide = [part[...] for part in parts if part.shape[1] != LANES]
-    left, right = (sum(part[...] for part in side) for side in (parts[:3], parts[3:6]))
+    left, right = (sum(part[...] for part in side) for side in (parts[:2], parts[2:4]))
     gathered = jnp.concatenate([left, right], 1) + sum(wide)
     fresh = table[...] + jnp.maximum(own[...] + dot3(gathered, w_top[...], w_low[...]), 0.0)
     new[...] = fresh
@@ -189,28 +191,28 @@
     slots = transactions.shape[0] // peers
     own, core, l2, l3, r2, r3 = call(
         message_kernel,
-        [(4, 2 * slots + PAD, LANES)] * 2 + [(3, slots + PAD, LANES)] * 2 + [(5 * slots + PAD, LANES)] * 2,
+        [(4, 2 * slots + PAD, LANES)] * 2 + [(2, slots + PAD, LANES)] * 2 + [(6 * slots + 2 * PAD, LANES)] * 2,
         (transactions, tx_product.reshape(-1, LANES), *split_outside(w_msg)),
         smem=(place, tx_count),
     )
-    left, rest, part = (3, mine, LANES), (5, mine, LANES), (mine, LANES)
+    left, rest, part, wide = (2, mine, LANES), (6, mine, LANES), (mine, LANES), (mine, 2 * LANES)
 
     def near(blocks):
         return [swap(block, "hash", mask, peers) for block, mask in zip(blocks, (2, 3))]
 
     def across(parts):
-        return [swap(part, "hash", mask, peers) for part, mask in zip(parts, (8, 12, 4))]
+        return [swap(part, "hash", mask, peers) for part, mask in zip(parts, (8, 12))]
 
     first = near((l2, l3))
     core = swap(core, "hash", 1, peers)
-    second = near(after((r2, r3), first))
+    second = near((r2, r3))
     send_l, keep_l, ids = call(left_kernel, [left, left, (8, LANES)], (own, core, *first), smem=(place,))
     got_l = swap(send_l, "tm", 1, 2)
     send_r, keep_r = call(rest_kernel, [rest, rest], (ids, own, core, *after(second, [got_l])), smem=(place,))
     got_r = swap(send_r, "tm", 1, 2)
-    far_l = across(call(pair_kernel, [part] * 3, (keep_l, *after([got_l], [send_r]))))
-    *parts_r, whole = call(pair_kernel, [part] * 3 + [(mine, 2 * LANES)], (keep_r, *after([got_r], far_l)))
-    return [*far_l, *across(parts_r), whole]
+    far_l = across(call(pair_kernel, [part] * 2, (keep_l, *after([got_l], [send_r]))))
+    *parts_r, next_to, whole = call(pair_kernel, [part] * 2 + [wide] * 2, (keep_r, *after([got_r], far_l)))
+    return [*far_l, *across(parts_r), swap(next_to, "hash", 4, peers), whole]
 
 
 def pick(x, i, axis):
@@ -247,7 +249,7 @@
     parts = lax.map(part_sum, jnp.arange(pair)).reshape(pair * mine, width)
     total = lax.psum_scatter(parts, "tm", scatter_dimension=0, tiled=True)
     zero = jnp.zeros((mine, LANES), f32)
-    return [zero] * 6 + [total]
+    return [zero] * 4 + [total]
 
 
 def local(

time: 61.4 us -> 61 us (level)
  waiting for transfers between devices: 27.1 us -> 25.6 us
  starting transfers between devices: 21.3 us -> 22.4 us
    ppermute x19 -> x18, waiting for transfers between devices: 27.1 us -> 25.6 us  [swap(): return lax.ppermute(x, axis, [(i, i ^ mask) for i in range(size)])]
    ppermute x19 -> x18, starting transfers between devices: 21.3 us -> 22.4 us  [swap(): return lax.ppermute(x, axis, [(i, i ^ mask) for i in range(size)])]
  transfers between devices with their start and end apart: 19 -> 18, of which waited for: 14 -> 11; matrix products, arithmetic and copies ran while one was open for 2% -> 2% of each run, Pallas kernels for 1% -> 1%
where the time goes in v9:
time: 61 us; the launch traced here: 60.7 us
  waiting for transfers between devices  25.6 us (42%)
  starting transfers between devices  22.4 us (37%)
  Pallas kernels  5.12 us (8%)
  local copies, waits for them, and re-layouts  4.84 us (8%)
  other arithmetic  1.42 us (2%)
  between operations  0.86 us (1%)
    ppermute x18, waiting for transfers between devices, swap(): return lax.ppermute(x, axis, [(i, i ^ mask) for i in range(size)])  25.6 us
    ppermute x18, starting transfers between devices, swap(): return lax.ppermute(x, axis, [(i, i ^ mask) for i in range(size)])  22.4 us
    pallas_call x8, Pallas kernels, call(): pl.pallas_call(kernel, out_shape=[jax.ShapeDtypeStruct(s, f32) for s in o...  5.12 us
    unnamed x24, local copies, waits for them, and re-layouts  4.37 us
  transfers between devices with their start and end apart: 18, of which 11 were waited for; matrix products, arithmetic and copies ran while one was open for 2% of the time, Pallas kernels for 1%

profile of v9, /device:TPU:0, one launch (start us, length us, event | category | flops | bytes accessed | tf_op | source)
XLA Modules:
  0.0 60.7 jit_solution(6576151009525875086)
XLA Ops:
  0.7 1.0 %fusion = (bf16[256,256]{1,0:T(8,128)(2,1)S(1)}, bf16[256,256]{1,0:T(8,128)(2,1)S(1)}) fusion(f32[256,256]{1,0:T(8,128)} %param.21), kind=kLoop, calls=%fused_computation.6 | loop fusion | flops 262144 | bytes 524288 | tf_op jit(solution)/shard_map/convert_element_type | solution.py:23
  1.7 0.1 pad_add_fusion.3.place
  1.8 0.6 copy-done.4
  2.4 1.2 %copy-done.1 = f32[1024,256]{1,0:T(8,128)S(1)} copy-done((f32[1024,256]{1,0:T(8,128)S(1)}, f32[1024,256]{1,0:T(8,128)}, u32[]{:S(2)}) %copy-start.1) | copy-done | bytes 1048600
  3.7 1.1 %shard_map.140 = (f32[4,136,128]{2,1,0:T(8,128)S(1)}, f32[4,136,128]{2,1,0:T(8,128)S(1)}, f32[2,72,128]{2,1,0:T(8,128)S(1)}, f32[2,72,128]{2,1,0:T(8,128)S(1)}, ...) custom-call(s32[2]{0:T(128)S(1)} %pad_add_fusion.3.place, s32[16]{0:T(128)S(1)} %copy-done.5, f32[1024,256]{1,0:T(8,128)S(1)} %copy-done.1, ...), custom_call_target="tpu_custom_call" | custom-call | tf_op jit(solution)/shard_map/pallas_call | solution.py:43
  4.8 0.5 collective-permute-start
  5.3 2.6 %collective-permute-start.1 = (f32[2,72,128]{2,1,0:T(8,128)S(1)}, f32[2,72,128]{2,1,0:T(8,128)S(1)}, u32[]{:S(2)}, u32[]{:S(2)}) collective-permute-start(f32[2,72,128]{2,1,0:T(8,128)S(1)} %get-tuple-element.34), channel_id=1, source_target_pairs={{0,4},{2,6},{4,0},{6,2},{8,12},{10,14},{12,8},{14,10},{16,20},{18,... | collective-permute-start | bytes 221192 | tf_op jit(solution)/shard_map/ppermute | solution.py:178
  7.9 0.1 collective-permute-start.2
  8.0 1.7 %collective-permute-start.4 = (f32[400,128]{1,0:T(8,128)S(1)}, f32[400,128]{1,0:T(8,128)S(1)}, u32[]{:S(2)}, u32[]{:S(2)}) collective-permute-start(f32[400,128]{1,0:T(8,128)S(1)} %get-tuple-element.39), channel_id=1, source_target_pairs={{0,4},{2,6},{4,0},{6,2},{8,12},{10,14},{12,8},{14,10},{16,20},{18,... | collective-permute-start | bytes 614408 | tf_op jit(solution)/shard_map/ppermute | solution.py:178
  9.7 0.7 %copy-done.9 = s32[256]{0:T(256)S(1)} copy-done((s32[256]{0:T(256)S(1)}, s32[256]{0:T(256)}, u32[]{:S(2)}) %copy-start.9) | copy-done | bytes 1048
  10.4 0.1 reshape_reshape.3
  10.5 0.6 copy-done.10
  11.1 0.1 reshape.22
  11.1 0.6 copy-done.11
  11.7 0.1 lt.45
  11.8 0.2 fusion.6.refs_6_
  12.1 0.1 fusion.5
  12.1 0.6 %copy-done.2 = f32[256,256]{1,0:T(8,128)S(1)} copy-done((f32[256,256]{1,0:T(8,128)S(1)}, f32[256,256]{1,0:T(8,128)}, u32[]{:S(2)}) %copy-start.2) | copy-done | bytes 262168
  12.8 0.3 fusion.7.own
  13.1 0.1 eq.30
  13.3 0.8 %shard_map.141 = (f32[2,128,128]{2,1,0:T(8,128)S(1)}, f32[2,128,128]{2,1,0:T(8,128)S(1)}, f32[8,128]{1,0:T(8,128)S(1)}) custom-call(s32[2]{0:T(128)S(1)} %pad_add_fusion.3.place, f32[4,136,128]{2,1,0:T(8,128)S(1)} %get-tuple-element.32.own, f32[4,136,128]{2,1,0:T(8,128)S(1)} %collective-permute-done.core, f32[2,72,128]{2,1,0:T(8,128)S(1)} %collective-permute-done.1.l2, ...), custom_call_target="tpu_custom_call" | custom-call | tf_op jit(solution)/shard_map/pallas_call | solution.py:43
  14.1 1.8 %collective-permute-start.3 = (f32[2,128,128]{2,1,0:T(8,128)S(1)}, f32[2,128,128]{2,1,0:T(8,128)S(1)}, u32[]{:S(2)}, u32[]{:S(2)}) collective-permute-start(f32[2,128,128]{2,1,0:T(8,128)S(1)} %get-tuple-element.37), channel_id=1, source_target_pairs={{0,1},{1,0},{2,3},{3,2},{4,5},{5,4},{6,7},{7,6},{8,9},{9,8},{10,11... | collective-permute-start | bytes 393224 | tf_op jit(solution)/shard_map/ppermute | solution.py:178
  15.9 1.3 %collective-permute-done.4.r2 = f32[400,128]{1,0:T(8,128)S(1)} collective-permute-done((f32[400,128]{1,0:T(8,128)S(1)}, f32[400,128]{1,0:T(8,128)S(1)}, u32[]{:S(2)}, u32[]{:S(2)}) %collective-permute-start.4) | collective-permute-done | bytes 204832 | tf_op jit(solution)/shard_map/ppermute | solution.py:178
  17.2 3.7 %collective-permute-done.5.r3 = f32[400,128]{1,0:T(8,128)S(1)} collective-permute-done((f32[400,128]{1,0:T(8,128)S(1)}, f32[400,128]{1,0:T(8,128)S(1)}, u32[]{:S(2)}, u32[]{:S(2)}) %collective-permute-start.5) | collective-permute-done | bytes 204832 | tf_op jit(solution)/shard_map/ppermute | solution.py:178
  20.9 0.9 %shard_map.142 = (f32[6,128,128]{2,1,0:T(8,128)S(1)}, f32[6,128,128]{2,1,0:T(8,128)S(1)}) custom-call(s32[2]{0:T(128)S(1)} %pad_add_fusion.3.place, f32[8,128]{1,0:T(8,128)S(1)} %get-tuple-element.38.ids, f32[4,136,128]{2,1,0:T(8,128)S(1)} %get-tuple-element.32.own, f32[4,136,128]{2,1,0:T(8,128)S(1)} %collective-permute-done.core, ...), custom_call_target="tpu_custom_call" | custom-call | tf_op jit(solution)/shard_map/pallas_call | solution.py:43
  21.8 1.9 %collective-permute-start.8 = (f32[6,128,128]{2,1,0:T(8,128)S(1)}, f32[6,128,128]{2,1,0:T(8,128)S(1)}, u32[]{:S(2)}, u32[]{:S(2)}) collective-permute-start(f32[6,128,128]{2,1,0:T(8,128)S(1)} %get-tuple-element.43), channel_id=1, source_target_pairs={{0,1},{1,0},{2,3},{3,2},{4,5},{5,4},{6,7},{7,6},{8,9},{9,8},{10,11... | collective-permute-start | bytes 1179656 | tf_op jit(solution)/shard_map/ppermute | solution.py:178
  23.8 2.6 %collective-permute-start.6 = (f32[128,128]{1,0:T(8,128)S(1)}, f32[128,128]{1,0:T(8,128)S(1)}, u32[]{:S(2)}, u32[]{:S(2)}) collective-permute-start(f32[128,128]{1,0:T(8,128)S(1)} %get-tuple-element.45), channel_id=1, source_target_pairs={{0,16},{2,18},{4,20},{6,22},{8,24},{10,26},{12,28},{14,30},{16,0},... | collective-permute-start | bytes 196616 | tf_op jit(solution)/shard_map/ppermute | solution.py:178
  26.4 1.4 %collective-permute-start.7 = (f32[128,128]{1,0:T(8,128)S(1)}, f32[128,128]{1,0:T(8,128)S(1)}, u32[]{:S(2)}, u32[]{:S(2)}) collective-permute-start(f32[128,128]{1,0:T(8,128)S(1)} %get-tuple-element.46), channel_id=1, source_target_pairs={{0,24},{2,26},{4,28},{6,30},{8,16},{10,18},{12,20},{14,22},{16,8},... | collective-permute-start | bytes 196616 | tf_op jit(solution)/shard_map/ppermute | solution.py:178
  27.8 0.1 fusion.4.refs_10_
  27.9 3.3 %collective-permute-done.6.refs_0_ = f32[128,128]{1,0:T(8,128)S(1)} collective-permute-done((f32[128,128]{1,0:T(8,128)S(1)}, f32[128,128]{1,0:T(8,128)S(1)}, u32[]{:S(2)}, u32[]{:S(2)}) %collective-permute-start.6) | collective-permute-done | bytes 65568 | tf_op jit(solution)/shard_map/ppermute | solution.py:178
  31.2 1.4 %collective-permute-done.7.refs_1_ = f32[128,128]{1,0:T(8,128)S(1)} collective-permute-done((f32[128,128]{1,0:T(8,128)S(1)}, f32[128,128]{1,0:T(8,128)S(1)}, u32[]{:S(2)}, u32[]{:S(2)}) %collective-permute-start.7) | collective-permute-done | bytes 65568 | tf_op jit(solution)/shard_map/ppermute | solution.py:178
  32.6 0.5 collective-permute-done.8.got
  33.1 1.8 %collective-permute-start.11 = (f32[128,256]{1,0:T(8,128)S(1)}, f32[128,256]{1,0:T(8,128)S(1)}, u32[]{:S(2)}, u32[]{:S(2)}) collective-permute-start(f32[128,256]{1,0:T(8,128)S(1)} %get-tuple-element.51), channel_id=1, source_target_pairs={{0,8},{2,10},{4,12},{6,14},{8,0},{10,2},{12,4},{14,6},{16,24},{18,... | collective-permute-start | bytes 393224 | tf_op jit(solution)/shard_map/ppermute | solution.py:178
  35.0 2.6 %collective-permute-start.9 = (f32[128,128]{1,0:T(8,128)S(1)}, f32[128,128]{1,0:T(8,128)S(1)}, u32[]{:S(2)}, u32[]{:S(2)}) collective-permute-start(f32[128,128]{1,0:T(8,128)S(1)} %get-tuple-element.49), channel_id=1, source_target_pairs={{0,16},{2,18},{4,20},{6,22},{8,24},{10,26},{12,28},{14,30},{16,0},... | collective-permute-start | bytes 196616 | tf_op jit(solution)/shard_map/ppermute | solution.py:178
  37.6 3.2 %collective-permute-done.9.refs_2_ = f32[128,128]{1,0:T(8,128)S(1)} collective-permute-done((f32[128,128]{1,0:T(8,128)S(1)}, f32[128,128]{1,0:T(8,128)S(1)}, u32[]{:S(2)}, u32[]{:S(2)}) %collective-permute-start.9) | collective-permute-done | bytes 65568 | tf_op jit(solution)/shard_map/ppermute | solution.py:178
  40.8 2.8 %collective-permute-done.10.refs_3_ = f32[128,128]{1,0:T(8,128)S(1)} collective-permute-done((f32[128,128]{1,0:T(8,128)S(1)}, f32[128,128]{1,0:T(8,128)S(1)}, u32[]{:S(2)}, u32[]{:S(2)}) %collective-permute-start.10) | collective-permute-done | bytes 65568 | tf_op jit(solution)/shard_map/ppermute | solution.py:178
  43.6 0.9 %shard_map.145 = (f32[128,256]{1,0:T(8,128)}, f32[4,16,256]{2,1,0:T(8,128)S(1)}, f32[4,16,256]{2,1,0:T(8,128)S(1)}, f32[4,16,256]{2,1,0:T(8,128)S(1)}, f32[4,16,256]{2,1,0:T(8,128)S(1)}) custom-call(f32[128,128]{1,0:T(8,128)S(1)} %collective-permute-done.6.refs_0_, f32[128,128]{1,0:T(8,128)S(1)} %collective-permute-done.7.refs_1_, ...), custom_call_target="tpu_custom_call" | custom-call | tf_op jit(solution)/shard_map/pallas_call | solution.py:43
  44.6 1.5 %collective-permute-start.13 = (f32[4,16,256]{2,1,0:T(8,128)S(1)}, f32[4,16,256]{2,1,0:T(8,128)S(1)}, u32[]{:S(2)}, u32[]{:S(2)}) collective-permute-start(f32[4,16,256]{2,1,0:T(8,128)S(1)} %get-tuple-element.56), channel_id=1, source_target_pairs={{0,4},{2,6},{4,0},{6,2},{8,12},{10,14},{12,8},{14,10},{16,20},{18,... | collective-permute-start | bytes 196616 | tf_op jit(solution)/shard_map/ppermute | solution.py:178
  46.1 0.4 collective-permute-start.14
  46.5 0.1 eq.34
  46.5 2.6 %collective-permute-done.13.refs_2_ = f32[4,16,256]{2,1,0:T(8,128)S(1)} collective-permute-done((f32[4,16,256]{2,1,0:T(8,128)S(1)}, f32[4,16,256]{2,1,0:T(8,128)S(1)}, u32[]{:S(2)}, u32[]{:S(2)}) %collective-permute-start.13) | collective-permute-done | bytes 65568 | tf_op jit(solution)/shard_map/ppermute | solution.py:178
  49.1 1.1 %collective-permute-done.14.refs_3_ = f32[4,16,256]{2,1,0:T(8,128)S(1)} collective-permute-done((f32[4,16,256]{2,1,0:T(8,128)S(1)}, f32[4,16,256]{2,1,0:T(8,128)S(1)}, u32[]{:S(2)}, u32[]{:S(2)}) %collective-permute-start.14) | collective-permute-done | bytes 65568 | tf_op jit(solution)/shard_map/ppermute | solution.py:178
  50.2 1.2 %collective-permute-start.15 = (f32[4,16,256]{2,1,0:T(8,128)S(1)}, f32[4,16,256]{2,1,0:T(8,128)S(1)}, u32[]{:S(2)}, u32[]{:S(2)}) collective-permute-start(f32[4,16,256]{2,1,0:T(8,128)S(1)} %get-tuple-element.58), channel_id=1, source_target_pairs={{0,16},{2,18},{4,20},{6,22},{8,24},{10,26},{12,28},{14,30},{16,0},... | collective-permute-start | bytes 196616 | tf_op jit(solution)/shard_map/ppermute | solution.py:178
  51.4 1.9 %collective-permute-start.16 = (f32[4,16,256]{2,1,0:T(8,128)S(1)}, f32[4,16,256]{2,1,0:T(8,128)S(1)}, u32[]{:S(2)}, u32[]{:S(2)}) collective-permute-start(f32[4,16,256]{2,1,0:T(8,128)S(1)} %get-tuple-element.59), channel_id=1, source_target_pairs={{0,24},{2,26},{4,28},{6,30},{8,16},{10,18},{12,20},{14,22},{16,8},... | collective-permute-start | bytes 196616 | tf_op jit(solution)/shard_map/ppermute | solution.py:178
  53.3 0.5 collective-permute-start.17
  53.8 4.5 %collective-permute-done.15.refs_0_ = f32[4,16,256]{2,1,0:T(8,128)S(1)} collective-permute-done((f32[4,16,256]{2,1,0:T(8,128)S(1)}, f32[4,16,256]{2,1,0:T(8,128)S(1)}, u32[]{:S(2)}, u32[]{:S(2)}) %collective-permute-start.15) | collective-permute-done | bytes 65568 | tf_op jit(solution)/shard_map/ppermute | solution.py:178
  58.3 1.1 %collective-permute-done.17.refs_2_ = f32[4,16,256]{2,1,0:T(8,128)S(1)} collective-permute-done((f32[4,16,256]{2,1,0:T(8,128)S(1)}, f32[4,16,256]{2,1,0:T(8,128)S(1)}, u32[]{:S(2)}, u32[]{:S(2)}) %collective-permute-start.17) | collective-permute-done | bytes 65568 | tf_op jit(solution)/shard_map/ppermute | solution.py:178
  59.5 1.2 %shard_map.147 = f32[256,256]{1,0:T(8,128)} custom-call(bf16[256,256]{1,0:T(8,128)(2,1)S(1)} %fusion.3.incidence, f32[256,256]{1,0:T(8,128)S(1)} %fusion.7.own, f32[256,256]{1,0:T(8,128)S(1)} %copy-done.2, bf16[256,256]{1,0:T(8,128)(2,1)S(1)} %get-tuple-element.63.w_top, bf16[256,256]{1,0:T(8,128)(2,1)S(1)} %get-tuple-element.62.w_low, ...), custom_call_target="tpu_custom_call" | custom-call | tf_op jit(solution)/shard_map/pallas_call | solution.py:43
  (42 shorter events, 0.4 us)
Async XLA Ops:
  0.6 11.5 %copy-start = (f32[256,256]{1,0:T(8,128)S(1)}, f32[256,256]{1,0:T(8,128)}, u32[]{:S(2)}) copy-start(f32[256,256]{1,0:T(8,128)} %param.24) | copy-start | bytes 786436
  1.7 0.7 %copy-start.4 = (s32[1024]{0:T(1024)S(1)}, s32[1024]{0:T(1024)}, u32[]{:S(2)}) copy-start(s32[1024]{0:T(1024)} %param.14) | copy-start | bytes 12292
  1.8 0.7 %copy-start.5 = (s32[16]{0:T(128)S(1)}, s32[16]{0:T(128)}, u32[]{:S(2)}) copy-start(s32[16]{0:T(128)} %count.1) | copy-start | bytes 196
  2.4 1.2 %copy-start.1 = (f32[1024,256]{1,0:T(8,128)S(1)}, f32[1024,256]{1,0:T(8,128)}, u32[]{:S(2)}) copy-start(f32[1024,256]{1,0:T(8,128)} %tx.1) | copy-start | bytes 3145732
  3.6 8.1 %copy-start.3 = (f32[128,256]{1,0:T(8,128)S(1)}, f32[128,256]{1,0:T(8,128)}, u32[]{:S(2)}) copy-start(f32[128,256]{1,0:T(8,128)} %refs_7_.1) | copy-start | bytes 393220
  3.7 8.1 %copy-start.6 = (f32[256,256]{1,0:T(8,128)S(1)}, f32[256,256]{1,0:T(8,128)}, u32[]{:S(2)}) copy-start(f32[256,256]{1,0:T(8,128)} %param.22) | copy-start | bytes 786436
  4.8 8.4 %collective-permute-start = (f32[4,136,128]{2,1,0:T(8,128)S(1)}, f32[4,136,128]{2,1,0:T(8,128)S(1)}, u32[]{:S(2)}, u32[]{:S(2)}) collective-permute-start(f32[4,136,128]{2,1,0:T(8,128)S(1)} %get-tuple-element.33), channel_id=1, source_target_pairs={{0,2},{2,0},{4,6},{6,4},{8,10},{10,8},{12,14},{14,12},{16,18},{18,... | collective-permute-start | bytes 835592 | tf_op jit(solution)/shard_map/ppermute | solution.py:178
  5.3 7.9 %collective-permute-start.1 = (f32[2,72,128]{2,1,0:T(8,128)S(1)}, f32[2,72,128]{2,1,0:T(8,128)S(1)}, u32[]{:S(2)}, u32[]{:S(2)}) collective-permute-start(f32[2,72,128]{2,1,0:T(8,128)S(1)} %get-tuple-element.34), channel_id=1, source_target_pairs={{0,4},{2,6},{4,0},{6,2},{8,12},{10,14},{12,8},{14,10},{16,20},{18,... | collective-permute-start | bytes 221192 | tf_op jit(solution)/shard_map/ppermute | solution.py:178
  7.9 5.4 %collective-permute-start.2 = (f32[2,72,128]{2,1,0:T(8,128)S(1)}, f32[2,72,128]{2,1,0:T(8,128)S(1)}, u32[]{:S(2)}, u32[]{:S(2)}) collective-permute-start(f32[2,72,128]{2,1,0:T(8,128)S(1)} %get-tuple-element.35), channel_id=1, source_target_pairs={{0,6},{2,4},{4,2},{6,0},{8,14},{10,12},{12,10},{14,8},{16,22},{18,... | collective-permute-start | bytes 221192 | tf_op jit(solution)/shard_map/ppermute | solution.py:178
  8.0 9.2 %collective-permute-start.4 = (f32[400,128]{1,0:T(8,128)S(1)}, f32[400,128]{1,0:T(8,128)S(1)}, u32[]{:S(2)}, u32[]{:S(2)}) collective-permute-start(f32[400,128]{1,0:T(8,128)S(1)} %get-tuple-element.39), channel_id=1, source_target_pairs={{0,4},{2,6},{4,0},{6,2},{8,12},{10,14},{12,8},{14,10},{16,20},{18,... | collective-permute-start | bytes 614408 | tf_op jit(solution)/shard_map/ppermute | solution.py:178
  9.7 11.2 %collective-permute-start.5 = (f32[400,128]{1,0:T(8,128)S(1)}, f32[400,128]{1,0:T(8,128)S(1)}, u32[]{:S(2)}, u32[]{:S(2)}) collective-permute-start(f32[400,128]{1,0:T(8,128)S(1)} %get-tuple-element.40), channel_id=1, source_target_pairs={{0,6},{2,4},{4,2},{6,0},{8,14},{10,12},{12,10},{14,8},{16,22},{18,... | collective-permute-start | bytes 614408 | tf_op jit(solution)/shard_map/ppermute | solution.py:178
  9.7 0.7 %copy-start.9 = (s32[256]{0:T(256)S(1)}, s32[256]{0:T(256)}, u32[]{:S(2)}) copy-start(s32[256]{0:T(256)} %param.20) | copy-start | bytes 3076
  10.4 0.7 %copy-start.10 = (s32[256]{0:T(256)S(1)}, s32[256]{0:T(256)}, u32[]{:S(2)}) copy-start(s32[256]{0:T(256)} %param.18) | copy-start | bytes 3076
  11.1 0.7 %copy-start.11 = (s32[16]{0:T(128)S(1)}, s32[16]{0:T(128)}, u32[]{:S(2)}) copy-start(s32[16]{0:T(128)} %param.19) | copy-start | bytes 196
  11.8 1.0 %copy-start.2 = (f32[256,256]{1,0:T(8,128)S(1)}, f32[256,256]{1,0:T(8,128)}, u32[]{:S(2)}) copy-start(f32[256,256]{1,0:T(8,128)} %table.1) | copy-start | bytes 786436
  13.3 2.6 %copy-start.7 = (f32[256,256]{1,0:T(8,128)S(1)}, f32[256,256]{1,0:T(8,128)}, u32[]{:S(2)}) copy-start(f32[256,256]{1,0:T(8,128)} %param.23) | copy-start | bytes 786436
  14.1 6.8 %collective-permute-start.3 = (f32[2,128,128]{2,1,0:T(8,128)S(1)}, f32[2,128,128]{2,1,0:T(8,128)S(1)}, u32[]{:S(2)}, u32[]{:S(2)}) collective-permute-start(f32[2,128,128]{2,1,0:T(8,128)S(1)} %get-tuple-element.37), channel_id=1, source_target_pairs={{0,1},{1,0},{2,3},{3,2},{4,5},{5,4},{6,7},{7,6},{8,9},{9,8},{10,11... | collective-permute-start | bytes 393224 | tf_op jit(solution)/shard_map/ppermute | solution.py:178
  20.9 2.8 %copy-start.8 = (f32[256,256]{1,0:T(8,128)S(1)}, f32[256,256]{1,0:T(8,128)}, u32[]{:S(2)}) copy-start(f32[256,256]{1,0:T(8,128)} %param.25) | copy-start | bytes 786436
  21.8 11.3 %collective-permute-start.8 = (f32[6,128,128]{2,1,0:T(8,128)S(1)}, f32[6,128,128]{2,1,0:T(8,128)S(1)}, u32[]{:S(2)}, u32[]{:S(2)}) collective-permute-start(f32[6,128,128]{2,1,0:T(8,128)S(1)} %get-tuple-element.43), channel_id=1, source_target_pairs={{0,1},{1,0},{2,3},{3,2},{4,5},{5,4},{6,7},{7,6},{8,9},{9,8},{10,11... | collective-permute-start | bytes 1179656 | tf_op jit(solution)/shard_map/ppermute | solution.py:178
  23.8 7.4 %collective-permute-start.6 = (f32[128,128]{1,0:T(8,128)S(1)}, f32[128,128]{1,0:T(8,128)S(1)}, u32[]{:S(2)}, u32[]{:S(2)}) collective-permute-start(f32[128,128]{1,0:T(8,128)S(1)} %get-tuple-element.45), channel_id=1, source_target_pairs={{0,16},{2,18},{4,20},{6,22},{8,24},{10,26},{12,28},{14,30},{16,0},... | collective-permute-start | bytes 196616 | tf_op jit(solution)/shard_map/ppermute | solution.py:178
  26.4 6.2 %collective-permute-start.7 = (f32[128,128]{1,0:T(8,128)S(1)}, f32[128,128]{1,0:T(8,128)S(1)}, u32[]{:S(2)}, u32[]{:S(2)}) collective-permute-start(f32[128,128]{1,0:T(8,128)S(1)} %get-tuple-element.46), channel_id=1, source_target_pairs={{0,24},{2,26},{4,28},{6,30},{8,16},{10,18},{12,20},{14,22},{16,8},... | collective-permute-start | bytes 196616 | tf_op jit(solution)/shard_map/ppermute | solution.py:178
  33.1 10.5 %collective-permute-start.11 = (f32[128,256]{1,0:T(8,128)S(1)}, f32[128,256]{1,0:T(8,128)S(1)}, u32[]{:S(2)}, u32[]{:S(2)}) collective-permute-start(f32[128,256]{1,0:T(8,128)S(1)} %get-tuple-element.51), channel_id=1, source_target_pairs={{0,8},{2,10},{4,12},{6,14},{8,0},{10,2},{12,4},{14,6},{16,24},{18,... | collective-permute-start | bytes 393224 | tf_op jit(solution)/shard_map/ppermute | solution.py:178
  35.0 5.9 %collective-permute-start.9 = (f32[128,128]{1,0:T(8,128)S(1)}, f32[128,128]{1,0:T(8,128)S(1)}, u32[]{:S(2)}, u32[]{:S(2)}) collective-permute-start(f32[128,128]{1,0:T(8,128)S(1)} %get-tuple-element.49), channel_id=1, source_target_pairs={{0,16},{2,18},{4,20},{6,22},{8,24},{10,26},{12,28},{14,30},{16,0},... | collective-permute-start | bytes 196616 | tf_op jit(solution)/shard_map/ppermute | solution.py:178
  37.6 6.1 %collective-permute-start.10 = (f32[128,128]{1,0:T(8,128)S(1)}, f32[128,128]{1,0:T(8,128)S(1)}, u32[]{:S(2)}, u32[]{:S(2)}) collective-permute-start(f32[128,128]{1,0:T(8,128)S(1)} %get-tuple-element.50), channel_id=1, source_target_pairs={{0,24},{2,26},{4,28},{6,30},{8,16},{10,18},{12,20},{14,22},{16,8},... | collective-permute-start | bytes 196616 | tf_op jit(solution)/shard_map/ppermute | solution.py:178
  44.6 2.0 %collective-permute-start.12 = (f32[4,16,256]{2,1,0:T(8,128)S(1)}, f32[4,16,256]{2,1,0:T(8,128)S(1)}, u32[]{:S(2)}, u32[]{:S(2)}) collective-permute-start(f32[4,16,256]{2,1,0:T(8,128)S(1)} %get-tuple-element.55), channel_id=1, source_target_pairs={{0,2},{2,0},{4,6},{6,4},{8,10},{10,8},{12,14},{14,12},{16,18},{18,... | collective-permute-start | bytes 196616 | tf_op jit(solution)/shard_map/ppermute | solution.py:178
  44.6 4.6 %collective-permute-start.13 = (f32[4,16,256]{2,1,0:T(8,128)S(1)}, f32[4,16,256]{2,1,0:T(8,128)S(1)}, u32[]{:S(2)}, u32[]{:S(2)}) collective-permute-start(f32[4,16,256]{2,1,0:T(8,128)S(1)} %get-tuple-element.56), channel_id=1, source_target_pairs={{0,4},{2,6},{4,0},{6,2},{8,12},{10,14},{12,8},{14,10},{16,20},{18,... | collective-permute-start | bytes 196616 | tf_op jit(solution)/shard_map/ppermute | solution.py:178
  46.1 4.1 %collective-permute-start.14 = (f32[4,16,256]{2,1,0:T(8,128)S(1)}, f32[4,16,256]{2,1,0:T(8,128)S(1)}, u32[]{:S(2)}, u32[]{:S(2)}) collective-permute-start(f32[4,16,256]{2,1,0:T(8,128)S(1)} %get-tuple-element.57), channel_id=1, source_target_pairs={{0,6},{2,4},{4,2},{6,0},{8,14},{10,12},{12,10},{14,8},{16,22},{18,... | collective-permute-start | bytes 196616 | tf_op jit(solution)/shard_map/ppermute | solution.py:178
  50.2 8.1 %collective-permute-start.15 = (f32[4,16,256]{2,1,0:T(8,128)S(1)}, f32[4,16,256]{2,1,0:T(8,128)S(1)}, u32[]{:S(2)}, u32[]{:S(2)}) collective-permute-start(f32[4,16,256]{2,1,0:T(8,128)S(1)} %get-tuple-element.58), channel_id=1, source_target_pairs={{0,16},{2,18},{4,20},{6,22},{8,24},{10,26},{12,28},{14,30},{16,0},... | collective-permute-start | bytes 196616 | tf_op jit(solution)/shard_map/ppermute | solution.py:178
  51.4 6.9 %collective-permute-start.16 = (f32[4,16,256]{2,1,0:T(8,128)S(1)}, f32[4,16,256]{2,1,0:T(8,128)S(1)}, u32[]{:S(2)}, u32[]{:S(2)}) collective-permute-start(f32[4,16,256]{2,1,0:T(8,128)S(1)} %get-tuple-element.59), channel_id=1, source_target_pairs={{0,24},{2,26},{4,28},{6,30},{8,16},{10,18},{12,20},{14,22},{16,8},... | collective-permute-start | bytes 196616 | tf_op jit(solution)/shard_map/ppermute | solution.py:178
  53.3 6.2 %collective-permute-start.17 = (f32[4,16,256]{2,1,0:T(8,128)S(1)}, f32[4,16,256]{2,1,0:T(8,128)S(1)}, u32[]{:S(2)}, u32[]{:S(2)}) collective-permute-start(f32[4,16,256]{2,1,0:T(8,128)S(1)} %get-tuple-element.60), channel_id=1, source_target_pairs={{0,8},{2,10},{4,12},{6,14},{8,0},{10,2},{12,4},{14,6},{16,24},{18,... | collective-permute-start | bytes 196616 | tf_op jit(solution)/shard_map/ppermute | solution.py:178

commit v10 on v9

--- a/solution.py
+++ b/solution.py
@@ -137,17 +137,17 @@
 
 
 def pair_kernel(keep, got, *outs):
-    for i in range(2):
-        outs[i][...] = keep[i] + got[i]
-    for i, out in enumerate(outs[2:]):
-        out[:, :LANES] = keep[2 * i + 2] + got[2 * i + 2]
-        out[:, LANES:] = keep[2 * i + 3] + got[2 * i + 3]
+    for i, out in enumerate(outs[:4]):
+        out[...] = keep[i] + got[i]
+    for own in outs[4:]:
+        own[:, :LANES] = keep[4] + got[4]
+        own[:, LANES:] = keep[5] + got[5]
 
 
 def update_kernel(n, *refs):
     parts, (own, table, w_top, w_low, picks), (new, *outs) = refs[:n], refs[n : n + 5], refs[n + 5 :]
     wide = [part[...] for part in parts if part.shape[1] != LANES]
-    left, right = (sum(part[...] for part in side) for side in (parts[:2], parts[2:4]))
+    left, right = (sum(part[...] for part in side) for side in ((*parts[:2], parts[4]), (*parts[2:4], parts[5])))
     gathered = jnp.concatenate([left, right], 1) + sum(wide)
     fresh = table[...] + jnp.maximum(own[...] + dot3(gathered, w_top[...], w_low[...]), 0.0)
     new[...] = fresh
@@ -211,8 +211,9 @@
     send_r, keep_r = call(rest_kernel, [rest, rest], (ids, own, core, *after(second, [got_l])), smem=(place,))
     got_r = swap(send_r, "tm", 1, 2)
     far_l = across(call(pair_kernel, [part] * 2, (keep_l, *after([got_l], [send_r]))))
-    *parts_r, next_to, whole = call(pair_kernel, [part] * 2 + [wide] * 2, (keep_r, *after([got_r], far_l)))
-    return [*far_l, *across(parts_r), swap(next_to, "hash", 4, peers), whole]
+    *parts_r, near_l, near_r, whole = call(pair_kernel, [part] * 4 + [wide], (keep_r, *after([got_r], far_l)))
+    far_r = across(parts_r)
+    return [*far_l, *far_r, swap(near_l, "hash", 4, peers), swap(near_r, "hash", 4, peers), whole]
 
 
 def pick(x, i, axis):
@@ -249,7 +250,7 @@
     parts = lax.map(part_sum, jnp.arange(pair)).reshape(pair * mine, width)
     total = lax.psum_scatter(parts, "tm", scatter_dimension=0, tiled=True)
     zero = jnp.zeros((mine, LANES), f32)
-    return [zero] * 4 + [total]
+    return [zero] * 6 + [total]
 
 
 def local(

time: 61 us -> 60.4 us (level)
  starting transfers between devices: 22.4 us -> 24.5 us
  waiting for transfers between devices: 25.6 us -> 23.6 us
  local copies, waits for them, and re-layouts: 4.84 us -> 4.15 us
    ppermute x18 -> x19, starting transfers between devices: 22.4 us -> 24.5 us  [swap(): return lax.ppermute(x, axis, [(i, i ^ mask) for i in range(size)])]
    ppermute x18 -> x19, waiting for transfers between devices: 25.6 us -> 23.6 us  [swap(): return lax.ppermute(x, axis, [(i, i ^ mask) for i in range(size)])]
    unnamed x24, local copies, waits for them, and re-layouts: 4.37 us -> 3.7 us
  transfers between devices with their start and end apart: 18 -> 19, of which waited for: 11 -> 11; matrix products, arithmetic and copies ran while one was open for 2% -> 2% of each run, Pallas kernels for 1% -> 1%
where the time goes in v10:
time: 60.4 us; the launch traced here: 60.1 us
  starting transfers between devices  24.5 us (41%)
  waiting for transfers between devices  23.6 us (39%)
  Pallas kernels  5.1 us (8%)
  local copies, waits for them, and re-layouts  4.15 us (7%)
  other arithmetic  1.42 us (2%)
  between operations  0.9 us (1%)
    ppermute x19, starting transfers between devices, swap(): return lax.ppermute(x, axis, [(i, i ^ mask) for i in range(size)])  24.5 us
    ppermute x19, waiting for transfers between devices, swap(): return lax.ppermute(x, axis, [(i, i ^ mask) for i in range(size)])  23.6 us
    pallas_call x8, Pallas kernels, call(): pl.pallas_call(kernel, out_shape=[jax.ShapeDtypeStruct(s, f32) for s in o...  5.1 us
    unnamed x24, local copies, waits for them, and re-layouts  3.7 us
  transfers between devices with their start and end apart: 19, of which 11 were waited for; matrix products, arithmetic and copies ran while one was open for 2% of the time, Pallas kernels for 1%

profile of v10, /device:TPU:0, one launch (start us, length us, event | category | flops | bytes accessed | tf_op | source)
XLA Modules:
  0.0 60.1 jit_solution(7566716908140050765)
XLA Ops:
  0.7 1.0 %fusion = (bf16[256,256]{1,0:T(8,128)(2,1)S(1)}, bf16[256,256]{1,0:T(8,128)(2,1)S(1)}) fusion(f32[256,256]{1,0:T(8,128)} %param.21), kind=kLoop, calls=%fused_computation.6 | loop fusion | flops 262144 | bytes 524288 | tf_op jit(solution)/shard_map/convert_element_type | solution.py:23
  1.7 0.1 pad_add_fusion.3.place
  1.8 0.6 copy-done.4
  2.4 1.2 %copy-done.1 = f32[1024,256]{1,0:T(8,128)S(1)} copy-done((f32[1024,256]{1,0:T(8,128)S(1)}, f32[1024,256]{1,0:T(8,128)}, u32[]{:S(2)}) %copy-start.1) | copy-done | bytes 1048600
  3.7 1.1 %shard_map.140 = (f32[4,136,128]{2,1,0:T(8,128)S(1)}, f32[4,136,128]{2,1,0:T(8,128)S(1)}, f32[2,72,128]{2,1,0:T(8,128)S(1)}, f32[2,72,128]{2,1,0:T(8,128)S(1)}, ...) custom-call(s32[2]{0:T(128)S(1)} %pad_add_fusion.3.place, s32[16]{0:T(128)S(1)} %copy-done.5, f32[1024,256]{1,0:T(8,128)S(1)} %copy-done.1, ...), custom_call_target="tpu_custom_call" | custom-call | tf_op jit(solution)/shard_map/pallas_call | solution.py:43
  4.8 0.5 collective-permute-start
  5.3 2.6 %collective-permute-start.1 = (f32[2,72,128]{2,1,0:T(8,128)S(1)}, f32[2,72,128]{2,1,0:T(8,128)S(1)}, u32[]{:S(2)}, u32[]{:S(2)}) collective-permute-start(f32[2,72,128]{2,1,0:T(8,128)S(1)} %get-tuple-element.35), channel_id=1, source_target_pairs={{0,4},{2,6},{4,0},{6,2},{8,12},{10,14},{12,8},{14,10},{16,20},{18,... | collective-permute-start | bytes 221192 | tf_op jit(solution)/shard_map/ppermute | solution.py:178
  8.0 1.7 %collective-permute-start.4 = (f32[400,128]{1,0:T(8,128)S(1)}, f32[400,128]{1,0:T(8,128)S(1)}, u32[]{:S(2)}, u32[]{:S(2)}) collective-permute-start(f32[400,128]{1,0:T(8,128)S(1)} %get-tuple-element.40), channel_id=1, source_target_pairs={{0,4},{2,6},{4,0},{6,2},{8,12},{10,14},{12,8},{14,10},{16,20},{18,... | collective-permute-start | bytes 614408 | tf_op jit(solution)/shard_map/ppermute | solution.py:178
  9.8 0.6 %copy-done.9 = s32[256]{0:T(256)S(1)} copy-done((s32[256]{0:T(256)S(1)}, s32[256]{0:T(256)}, u32[]{:S(2)}) %copy-start.9) | copy-done | bytes 1048
  10.4 0.1 reshape_reshape.3
  10.5 0.6 copy-done.10
  11.1 0.1 reshape.22
  11.1 0.6 copy-done.11
  11.7 0.1 lt.45
  11.8 0.2 fusion.6.refs_7_
  12.1 0.1 fusion.5
  12.2 0.1 eq.30
  12.4 0.8 %shard_map.141 = (f32[2,128,128]{2,1,0:T(8,128)S(1)}, f32[2,128,128]{2,1,0:T(8,128)S(1)}, f32[8,128]{1,0:T(8,128)S(1)}) custom-call(s32[2]{0:T(128)S(1)} %pad_add_fusion.3.place, f32[4,136,128]{2,1,0:T(8,128)S(1)} %get-tuple-element.33.own, f32[4,136,128]{2,1,0:T(8,128)S(1)} %collective-permute-done.core, f32[2,72,128]{2,1,0:T(8,128)S(1)} %collective-permute-done.1.l2, ...), custom_call_target="tpu_custom_call" | custom-call | tf_op jit(solution)/shard_map/pallas_call | solution.py:43
  13.1 1.8 %collective-permute-start.3 = (f32[2,128,128]{2,1,0:T(8,128)S(1)}, f32[2,128,128]{2,1,0:T(8,128)S(1)}, u32[]{:S(2)}, u32[]{:S(2)}) collective-permute-start(f32[2,128,128]{2,1,0:T(8,128)S(1)} %get-tuple-element.38), channel_id=1, source_target_pairs={{0,1},{1,0},{2,3},{3,2},{4,5},{5,4},{6,7},{7,6},{8,9},{9,8},{10,11... | collective-permute-start | bytes 393224 | tf_op jit(solution)/shard_map/ppermute | solution.py:178
  14.9 2.2 %collective-permute-done.4.r2 = f32[400,128]{1,0:T(8,128)S(1)} collective-permute-done((f32[400,128]{1,0:T(8,128)S(1)}, f32[400,128]{1,0:T(8,128)S(1)}, u32[]{:S(2)}, u32[]{:S(2)}) %collective-permute-start.4) | collective-permute-done | bytes 204832 | tf_op jit(solution)/shard_map/ppermute | solution.py:178
  17.2 3.7 %collective-permute-done.5.r3 = f32[400,128]{1,0:T(8,128)S(1)} collective-permute-done((f32[400,128]{1,0:T(8,128)S(1)}, f32[400,128]{1,0:T(8,128)S(1)}, u32[]{:S(2)}, u32[]{:S(2)}) %collective-permute-start.5) | collective-permute-done | bytes 204832 | tf_op jit(solution)/shard_map/ppermute | solution.py:178
  20.9 0.9 %shard_map.142 = (f32[6,128,128]{2,1,0:T(8,128)S(1)}, f32[6,128,128]{2,1,0:T(8,128)S(1)}) custom-call(s32[2]{0:T(128)S(1)} %pad_add_fusion.3.place, f32[8,128]{1,0:T(8,128)S(1)} %get-tuple-element.39.ids, f32[4,136,128]{2,1,0:T(8,128)S(1)} %get-tuple-element.33.own, f32[4,136,128]{2,1,0:T(8,128)S(1)} %collective-permute-done.core, ...), custom_call_target="tpu_custom_call" | custom-call | tf_op jit(solution)/shard_map/pallas_call | solution.py:43
  21.8 1.9 %collective-permute-start.8 = (f32[6,128,128]{2,1,0:T(8,128)S(1)}, f32[6,128,128]{2,1,0:T(8,128)S(1)}, u32[]{:S(2)}, u32[]{:S(2)}) collective-permute-start(f32[6,128,128]{2,1,0:T(8,128)S(1)} %get-tuple-element.44), channel_id=1, source_target_pairs={{0,1},{1,0},{2,3},{3,2},{4,5},{5,4},{6,7},{7,6},{8,9},{9,8},{10,11... | collective-permute-start | bytes 1179656 | tf_op jit(solution)/shard_map/ppermute | solution.py:178
  23.7 0.1 fusion.4.refs_11_
  23.8 0.3 fusion.7.own
  24.1 2.6 %collective-permute-start.6 = (f32[128,128]{1,0:T(8,128)S(1)}, f32[128,128]{1,0:T(8,128)S(1)}, u32[]{:S(2)}, u32[]{:S(2)}) collective-permute-start(f32[128,128]{1,0:T(8,128)S(1)} %get-tuple-element.46), channel_id=1, source_target_pairs={{0,16},{2,18},{4,20},{6,22},{8,24},{10,26},{12,28},{14,30},{16,0},... | collective-permute-start | bytes 196616 | tf_op jit(solution)/shard_map/ppermute | solution.py:178
  26.7 1.3 %collective-permute-start.7 = (f32[128,128]{1,0:T(8,128)S(1)}, f32[128,128]{1,0:T(8,128)S(1)}, u32[]{:S(2)}, u32[]{:S(2)}) collective-permute-start(f32[128,128]{1,0:T(8,128)S(1)} %get-tuple-element.47), channel_id=1, source_target_pairs={{0,24},{2,26},{4,28},{6,30},{8,16},{10,18},{12,20},{14,22},{16,8},... | collective-permute-start | bytes 196616 | tf_op jit(solution)/shard_map/ppermute | solution.py:178
  28.1 3.4 %collective-permute-done.6.refs_0_ = f32[128,128]{1,0:T(8,128)S(1)} collective-permute-done((f32[128,128]{1,0:T(8,128)S(1)}, f32[128,128]{1,0:T(8,128)S(1)}, u32[]{:S(2)}, u32[]{:S(2)}) %collective-permute-start.6) | collective-permute-done | bytes 65568 | tf_op jit(solution)/shard_map/ppermute | solution.py:178
  31.5 1.4 %collective-permute-done.7.refs_1_ = f32[128,128]{1,0:T(8,128)S(1)} collective-permute-done((f32[128,128]{1,0:T(8,128)S(1)}, f32[128,128]{1,0:T(8,128)S(1)}, u32[]{:S(2)}, u32[]{:S(2)}) %collective-permute-start.7) | collective-permute-done | bytes 65568 | tf_op jit(solution)/shard_map/ppermute | solution.py:178
  32.9 0.2 collective-permute-done.8.got
  33.1 2.9 %collective-permute-start.9 = (f32[128,128]{1,0:T(8,128)S(1)}, f32[128,128]{1,0:T(8,128)S(1)}, u32[]{:S(2)}, u32[]{:S(2)}) collective-permute-start(f32[128,128]{1,0:T(8,128)S(1)} %get-tuple-element.50), channel_id=1, source_target_pairs={{0,16},{2,18},{4,20},{6,22},{8,24},{10,26},{12,28},{14,30},{16,0},... | collective-permute-start | bytes 196616 | tf_op jit(solution)/shard_map/ppermute | solution.py:178
  36.0 1.3 %collective-permute-start.10 = (f32[128,128]{1,0:T(8,128)S(1)}, f32[128,128]{1,0:T(8,128)S(1)}, u32[]{:S(2)}, u32[]{:S(2)}) collective-permute-start(f32[128,128]{1,0:T(8,128)S(1)} %get-tuple-element.51), channel_id=1, source_target_pairs={{0,24},{2,26},{4,28},{6,30},{8,16},{10,18},{12,20},{14,22},{16,8},... | collective-permute-start | bytes 196616 | tf_op jit(solution)/shard_map/ppermute | solution.py:178
  37.3 0.2 collective-permute-start.11
  37.6 1.8 %collective-permute-start.12 = (f32[128,128]{1,0:T(8,128)S(1)}, f32[128,128]{1,0:T(8,128)S(1)}, u32[]{:S(2)}, u32[]{:S(2)}) collective-permute-start(f32[128,128]{1,0:T(8,128)S(1)} %get-tuple-element.53), channel_id=1, source_target_pairs={{0,8},{2,10},{4,12},{6,14},{8,0},{10,2},{12,4},{14,6},{16,24},{18,... | collective-permute-start | bytes 196616 | tf_op jit(solution)/shard_map/ppermute | solution.py:178
  39.4 3.1 %collective-permute-done.10.refs_3_ = f32[128,128]{1,0:T(8,128)S(1)} collective-permute-done((f32[128,128]{1,0:T(8,128)S(1)}, f32[128,128]{1,0:T(8,128)S(1)}, u32[]{:S(2)}, u32[]{:S(2)}) %collective-permute-start.10) | collective-permute-done | bytes 65568 | tf_op jit(solution)/shard_map/ppermute | solution.py:178
  42.5 0.5 collective-permute-done.12.refs_5_
  43.0 0.9 %shard_map.145 = (f32[128,256]{1,0:T(8,128)}, f32[4,16,256]{2,1,0:T(8,128)S(1)}, f32[4,16,256]{2,1,0:T(8,128)S(1)}, f32[4,16,256]{2,1,0:T(8,128)S(1)}, f32[4,16,256]{2,1,0:T(8,128)S(1)}) custom-call(f32[128,128]{1,0:T(8,128)S(1)} %collective-permute-done.6.refs_0_, f32[128,128]{1,0:T(8,128)S(1)} %collective-permute-done.7.refs_1_, ...), custom_call_target="tpu_custom_call" | custom-call | tf_op jit(solution)/shard_map/pallas_call | solution.py:43
  43.9 1.5 %collective-permute-start.14 = (f32[4,16,256]{2,1,0:T(8,128)S(1)}, f32[4,16,256]{2,1,0:T(8,128)S(1)}, u32[]{:S(2)}, u32[]{:S(2)}) collective-permute-start(f32[4,16,256]{2,1,0:T(8,128)S(1)} %get-tuple-element.58), channel_id=1, source_target_pairs={{0,4},{2,6},{4,0},{6,2},{8,12},{10,14},{12,8},{14,10},{16,20},{18,... | collective-permute-start | bytes 196616 | tf_op jit(solution)/shard_map/ppermute | solution.py:178
  45.4 0.4 collective-permute-start.15
  45.8 0.1 eq.34
  45.9 2.6 %collective-permute-done.14.refs_2_ = f32[4,16,256]{2,1,0:T(8,128)S(1)} collective-permute-done((f32[4,16,256]{2,1,0:T(8,128)S(1)}, f32[4,16,256]{2,1,0:T(8,128)S(1)}, u32[]{:S(2)}, u32[]{:S(2)}) %collective-permute-start.14) | collective-permute-done | bytes 65568 | tf_op jit(solution)/shard_map/ppermute | solution.py:178
  48.5 1.1 %collective-permute-done.15.refs_3_ = f32[4,16,256]{2,1,0:T(8,128)S(1)} collective-permute-done((f32[4,16,256]{2,1,0:T(8,128)S(1)}, f32[4,16,256]{2,1,0:T(8,128)S(1)}, u32[]{:S(2)}, u32[]{:S(2)}) %collective-permute-start.15) | collective-permute-done | bytes 65568 | tf_op jit(solution)/shard_map/ppermute | solution.py:178
  49.6 1.7 %collective-permute-start.16 = (f32[4,16,256]{2,1,0:T(8,128)S(1)}, f32[4,16,256]{2,1,0:T(8,128)S(1)}, u32[]{:S(2)}, u32[]{:S(2)}) collective-permute-start(f32[4,16,256]{2,1,0:T(8,128)S(1)} %get-tuple-element.60), channel_id=1, source_target_pairs={{0,16},{2,18},{4,20},{6,22},{8,24},{10,26},{12,28},{14,30},{16,0},... | collective-permute-start | bytes 196616 | tf_op jit(solution)/shard_map/ppermute | solution.py:178
  51.3 1.7 %collective-permute-start.17 = (f32[4,16,256]{2,1,0:T(8,128)S(1)}, f32[4,16,256]{2,1,0:T(8,128)S(1)}, u32[]{:S(2)}, u32[]{:S(2)}) collective-permute-start(f32[4,16,256]{2,1,0:T(8,128)S(1)} %get-tuple-element.61), channel_id=1, source_target_pairs={{0,24},{2,26},{4,28},{6,30},{8,16},{10,18},{12,20},{14,22},{16,8},... | collective-permute-start | bytes 196616 | tf_op jit(solution)/shard_map/ppermute | solution.py:178
  53.0 0.5 collective-permute-start.18
  53.5 4.6 %collective-permute-done.16.refs_0_ = f32[4,16,256]{2,1,0:T(8,128)S(1)} collective-permute-done((f32[4,16,256]{2,1,0:T(8,128)S(1)}, f32[4,16,256]{2,1,0:T(8,128)S(1)}, u32[]{:S(2)}, u32[]{:S(2)}) %collective-permute-start.16) | collective-permute-done | bytes 65568 | tf_op jit(solution)/shard_map/ppermute | solution.py:178
  58.1 0.8 %collective-permute-done.18.refs_2_ = f32[4,16,256]{2,1,0:T(8,128)S(1)} collective-permute-done((f32[4,16,256]{2,1,0:T(8,128)S(1)}, f32[4,16,256]{2,1,0:T(8,128)S(1)}, u32[]{:S(2)}, u32[]{:S(2)}) %collective-permute-start.18) | collective-permute-done | bytes 65568 | tf_op jit(solution)/shard_map/ppermute | solution.py:178
  58.9 1.2 %shard_map.147 = f32[256,256]{1,0:T(8,128)} custom-call(bf16[256,256]{1,0:T(8,128)(2,1)S(1)} %fusion.3.incidence, f32[256,256]{1,0:T(8,128)S(1)} %fusion.7.own, f32[256,256]{1,0:T(8,128)S(1)} %copy-done.2, bf16[256,256]{1,0:T(8,128)(2,1)S(1)} %get-tuple-element.65.w_top, bf16[256,256]{1,0:T(8,128)(2,1)S(1)} %get-tuple-element.64.w_low, ...), custom_call_target="tpu_custom_call" | custom-call | tf_op jit(solution)/shard_map/pallas_call | solution.py:43
  (44 shorter events, 0.5 us)
Async XLA Ops:
  0.6 23.1 %copy-start = (f32[256,256]{1,0:T(8,128)S(1)}, f32[256,256]{1,0:T(8,128)}, u32[]{:S(2)}) copy-start(f32[256,256]{1,0:T(8,128)} %param.24) | copy-start | bytes 786436
  1.7 0.7 %copy-start.4 = (s32[1024]{0:T(1024)S(1)}, s32[1024]{0:T(1024)}, u32[]{:S(2)}) copy-start(s32[1024]{0:T(1024)} %param.14) | copy-start | bytes 12292
  1.8 0.7 %copy-start.5 = (s32[16]{0:T(128)S(1)}, s32[16]{0:T(128)}, u32[]{:S(2)}) copy-start(s32[16]{0:T(128)} %count.1) | copy-start | bytes 196
  2.4 1.2 %copy-start.1 = (f32[1024,256]{1,0:T(8,128)S(1)}, f32[1024,256]{1,0:T(8,128)}, u32[]{:S(2)}) copy-start(f32[1024,256]{1,0:T(8,128)} %tx.1) | copy-start | bytes 3145732
  3.6 6.1 %copy-start.6 = (f32[256,256]{1,0:T(8,128)S(1)}, f32[256,256]{1,0:T(8,128)}, u32[]{:S(2)}) copy-start(f32[256,256]{1,0:T(8,128)} %param.23) | copy-start | bytes 786436
  4.8 7.5 %collective-permute-start = (f32[4,136,128]{2,1,0:T(8,128)S(1)}, f32[4,136,128]{2,1,0:T(8,128)S(1)}, u32[]{:S(2)}, u32[]{:S(2)}) collective-permute-start(f32[4,136,128]{2,1,0:T(8,128)S(1)} %get-tuple-element.34), channel_id=1, source_target_pairs={{0,2},{2,0},{4,6},{6,4},{8,10},{10,8},{12,14},{14,12},{16,18},{18,... | collective-permute-start | bytes 835592 | tf_op jit(solution)/shard_map/ppermute | solution.py:178
  5.3 7.0 %collective-permute-start.1 = (f32[2,72,128]{2,1,0:T(8,128)S(1)}, f32[2,72,128]{2,1,0:T(8,128)S(1)}, u32[]{:S(2)}, u32[]{:S(2)}) collective-permute-start(f32[2,72,128]{2,1,0:T(8,128)S(1)} %get-tuple-element.35), channel_id=1, source_target_pairs={{0,4},{2,6},{4,0},{6,2},{8,12},{10,14},{12,8},{14,10},{16,20},{18,... | collective-permute-start | bytes 221192 | tf_op jit(solution)/shard_map/ppermute | solution.py:178
  7.9 4.4 %collective-permute-start.2 = (f32[2,72,128]{2,1,0:T(8,128)S(1)}, f32[2,72,128]{2,1,0:T(8,128)S(1)}, u32[]{:S(2)}, u32[]{:S(2)}) collective-permute-start(f32[2,72,128]{2,1,0:T(8,128)S(1)} %get-tuple-element.36), channel_id=1, source_target_pairs={{0,6},{2,4},{4,2},{6,0},{8,14},{10,12},{12,10},{14,8},{16,22},{18,... | collective-permute-start | bytes 221192 | tf_op jit(solution)/shard_map/ppermute | solution.py:178
  8.0 9.2 %collective-permute-start.4 = (f32[400,128]{1,0:T(8,128)S(1)}, f32[400,128]{1,0:T(8,128)S(1)}, u32[]{:S(2)}, u32[]{:S(2)}) collective-permute-start(f32[400,128]{1,0:T(8,128)S(1)} %get-tuple-element.40), channel_id=1, source_target_pairs={{0,4},{2,6},{4,0},{6,2},{8,12},{10,14},{12,8},{14,10},{16,20},{18,... | collective-permute-start | bytes 614408 | tf_op jit(solution)/shard_map/ppermute | solution.py:178
  9.7 11.2 %collective-permute-start.5 = (f32[400,128]{1,0:T(8,128)S(1)}, f32[400,128]{1,0:T(8,128)S(1)}, u32[]{:S(2)}, u32[]{:S(2)}) collective-permute-start(f32[400,128]{1,0:T(8,128)S(1)} %get-tuple-element.41), channel_id=1, source_target_pairs={{0,6},{2,4},{4,2},{6,0},{8,14},{10,12},{12,10},{14,8},{16,22},{18,... | collective-permute-start | bytes 614408 | tf_op jit(solution)/shard_map/ppermute | solution.py:178
  9.7 0.7 %copy-start.9 = (s32[256]{0:T(256)S(1)}, s32[256]{0:T(256)}, u32[]{:S(2)}) copy-start(s32[256]{0:T(256)} %param.20) | copy-start | bytes 3076
  9.7 2.1 %copy-start.3 = (f32[128,256]{1,0:T(8,128)S(1)}, f32[128,256]{1,0:T(8,128)}, u32[]{:S(2)}) copy-start(f32[128,256]{1,0:T(8,128)} %refs_8_.1) | copy-start | bytes 393220
  9.7 2.1 %copy-start.7 = (f32[256,256]{1,0:T(8,128)S(1)}, f32[256,256]{1,0:T(8,128)}, u32[]{:S(2)}) copy-start(f32[256,256]{1,0:T(8,128)} %param.22) | copy-start | bytes 786436
  10.4 0.7 %copy-start.10 = (s32[256]{0:T(256)S(1)}, s32[256]{0:T(256)}, u32[]{:S(2)}) copy-start(s32[256]{0:T(256)} %param.18) | copy-start | bytes 3076
  11.1 0.7 %copy-start.11 = (s32[16]{0:T(128)S(1)}, s32[16]{0:T(128)}, u32[]{:S(2)}) copy-start(s32[16]{0:T(128)} %param.19) | copy-start | bytes 196
  12.3 2.6 %copy-start.8 = (f32[256,256]{1,0:T(8,128)S(1)}, f32[256,256]{1,0:T(8,128)}, u32[]{:S(2)}) copy-start(f32[256,256]{1,0:T(8,128)} %param.25) | copy-start | bytes 786436
  13.1 7.7 %collective-permute-start.3 = (f32[2,128,128]{2,1,0:T(8,128)S(1)}, f32[2,128,128]{2,1,0:T(8,128)S(1)}, u32[]{:S(2)}, u32[]{:S(2)}) collective-permute-start(f32[2,128,128]{2,1,0:T(8,128)S(1)} %get-tuple-element.38), channel_id=1, source_target_pairs={{0,1},{1,0},{2,3},{3,2},{4,5},{5,4},{6,7},{7,6},{8,9},{9,8},{10,11... | collective-permute-start | bytes 393224 | tf_op jit(solution)/shard_map/ppermute | solution.py:178
  20.9 2.9 %copy-start.2 = (f32[256,256]{1,0:T(8,128)S(1)}, f32[256,256]{1,0:T(8,128)}, u32[]{:S(2)}) copy-start(f32[256,256]{1,0:T(8,128)} %table.1) | copy-start | bytes 786436
  21.8 11.2 %collective-permute-start.8 = (f32[6,128,128]{2,1,0:T(8,128)S(1)}, f32[6,128,128]{2,1,0:T(8,128)S(1)}, u32[]{:S(2)}, u32[]{:S(2)}) collective-permute-start(f32[6,128,128]{2,1,0:T(8,128)S(1)} %get-tuple-element.44), channel_id=1, source_target_pairs={{0,1},{1,0},{2,3},{3,2},{4,5},{5,4},{6,7},{7,6},{8,9},{9,8},{10,11... | collective-permute-start | bytes 1179656 | tf_op jit(solution)/shard_map/ppermute | solution.py:178
  24.1 7.4 %collective-permute-start.6 = (f32[128,128]{1,0:T(8,128)S(1)}, f32[128,128]{1,0:T(8,128)S(1)}, u32[]{:S(2)}, u32[]{:S(2)}) collective-permute-start(f32[128,128]{1,0:T(8,128)S(1)} %get-tuple-element.46), channel_id=1, source_target_pairs={{0,16},{2,18},{4,20},{6,22},{8,24},{10,26},{12,28},{14,30},{16,0},... | collective-permute-start | bytes 196616 | tf_op jit(solution)/shard_map/ppermute | solution.py:178
  26.7 6.2 %collective-permute-start.7 = (f32[128,128]{1,0:T(8,128)S(1)}, f32[128,128]{1,0:T(8,128)S(1)}, u32[]{:S(2)}, u32[]{:S(2)}) collective-permute-start(f32[128,128]{1,0:T(8,128)S(1)} %get-tuple-element.47), channel_id=1, source_target_pairs={{0,24},{2,26},{4,28},{6,30},{8,16},{10,18},{12,20},{14,22},{16,8},... | collective-permute-start | bytes 196616 | tf_op jit(solution)/shard_map/ppermute | solution.py:178
  33.1 6.2 %collective-permute-start.9 = (f32[128,128]{1,0:T(8,128)S(1)}, f32[128,128]{1,0:T(8,128)S(1)}, u32[]{:S(2)}, u32[]{:S(2)}) collective-permute-start(f32[128,128]{1,0:T(8,128)S(1)} %get-tuple-element.50), channel_id=1, source_target_pairs={{0,16},{2,18},{4,20},{6,22},{8,24},{10,26},{12,28},{14,30},{16,0},... | collective-permute-start | bytes 196616 | tf_op jit(solution)/shard_map/ppermute | solution.py:178
  36.0 6.5 %collective-permute-start.10 = (f32[128,128]{1,0:T(8,128)S(1)}, f32[128,128]{1,0:T(8,128)S(1)}, u32[]{:S(2)}, u32[]{:S(2)}) collective-permute-start(f32[128,128]{1,0:T(8,128)S(1)} %get-tuple-element.51), channel_id=1, source_target_pairs={{0,24},{2,26},{4,28},{6,30},{8,16},{10,18},{12,20},{14,22},{16,8},... | collective-permute-start | bytes 196616 | tf_op jit(solution)/shard_map/ppermute | solution.py:178
  37.3 5.2 %collective-permute-start.11 = (f32[128,128]{1,0:T(8,128)S(1)}, f32[128,128]{1,0:T(8,128)S(1)}, u32[]{:S(2)}, u32[]{:S(2)}) collective-permute-start(f32[128,128]{1,0:T(8,128)S(1)} %get-tuple-element.52), channel_id=1, source_target_pairs={{0,8},{2,10},{4,12},{6,14},{8,0},{10,2},{12,4},{14,6},{16,24},{18,... | collective-permute-start | bytes 196616 | tf_op jit(solution)/shard_map/ppermute | solution.py:178
  37.6 5.4 %collective-permute-start.12 = (f32[128,128]{1,0:T(8,128)S(1)}, f32[128,128]{1,0:T(8,128)S(1)}, u32[]{:S(2)}, u32[]{:S(2)}) collective-permute-start(f32[128,128]{1,0:T(8,128)S(1)} %get-tuple-element.53), channel_id=1, source_target_pairs={{0,8},{2,10},{4,12},{6,14},{8,0},{10,2},{12,4},{14,6},{16,24},{18,... | collective-permute-start | bytes 196616 | tf_op jit(solution)/shard_map/ppermute | solution.py:178
  43.9 2.0 %collective-permute-start.13 = (f32[4,16,256]{2,1,0:T(8,128)S(1)}, f32[4,16,256]{2,1,0:T(8,128)S(1)}, u32[]{:S(2)}, u32[]{:S(2)}) collective-permute-start(f32[4,16,256]{2,1,0:T(8,128)S(1)} %get-tuple-element.57), channel_id=1, source_target_pairs={{0,2},{2,0},{4,6},{6,4},{8,10},{10,8},{12,14},{14,12},{16,18},{18,... | collective-permute-start | bytes 196616 | tf_op jit(solution)/shard_map/ppermute | solution.py:178
  43.9 4.6 %collective-permute-start.14 = (f32[4,16,256]{2,1,0:T(8,128)S(1)}, f32[4,16,256]{2,1,0:T(8,128)S(1)}, u32[]{:S(2)}, u32[]{:S(2)}) collective-permute-start(f32[4,16,256]{2,1,0:T(8,128)S(1)} %get-tuple-element.58), channel_id=1, source_target_pairs={{0,4},{2,6},{4,0},{6,2},{8,12},{10,14},{12,8},{14,10},{16,20},{18,... | collective-permute-start | bytes 196616 | tf_op jit(solution)/shard_map/ppermute | solution.py:178
  45.4 4.1 %collective-permute-start.15 = (f32[4,16,256]{2,1,0:T(8,128)S(1)}, f32[4,16,256]{2,1,0:T(8,128)S(1)}, u32[]{:S(2)}, u32[]{:S(2)}) collective-permute-start(f32[4,16,256]{2,1,0:T(8,128)S(1)} %get-tuple-element.59), channel_id=1, source_target_pairs={{0,6},{2,4},{4,2},{6,0},{8,14},{10,12},{12,10},{14,8},{16,22},{18,... | collective-permute-start | bytes 196616 | tf_op jit(solution)/shard_map/ppermute | solution.py:178
  49.6 8.5 %collective-permute-start.16 = (f32[4,16,256]{2,1,0:T(8,128)S(1)}, f32[4,16,256]{2,1,0:T(8,128)S(1)}, u32[]{:S(2)}, u32[]{:S(2)}) collective-permute-start(f32[4,16,256]{2,1,0:T(8,128)S(1)} %get-tuple-element.60), channel_id=1, source_target_pairs={{0,16},{2,18},{4,20},{6,22},{8,24},{10,26},{12,28},{14,30},{16,0},... | collective-permute-start | bytes 196616 | tf_op jit(solution)/shard_map/ppermute | solution.py:178
  51.3 6.8 %collective-permute-start.17 = (f32[4,16,256]{2,1,0:T(8,128)S(1)}, f32[4,16,256]{2,1,0:T(8,128)S(1)}, u32[]{:S(2)}, u32[]{:S(2)}) collective-permute-start(f32[4,16,256]{2,1,0:T(8,128)S(1)} %get-tuple-element.61), channel_id=1, source_target_pairs={{0,24},{2,26},{4,28},{6,30},{8,16},{10,18},{12,20},{14,22},{16,8},... | collective-permute-start | bytes 196616 | tf_op jit(solution)/shard_map/ppermute | solution.py:178
  53.0 5.9 %collective-permute-start.18 = (f32[4,16,256]{2,1,0:T(8,128)S(1)}, f32[4,16,256]{2,1,0:T(8,128)S(1)}, u32[]{:S(2)}, u32[]{:S(2)}) collective-permute-start(f32[4,16,256]{2,1,0:T(8,128)S(1)} %get-tuple-element.62), channel_id=1, source_target_pairs={{0,8},{2,10},{4,12},{6,14},{8,0},{10,2},{12,4},{14,6},{16,24},{18,... | collective-permute-start | bytes 196616 | tf_op jit(solution)/shard_map/ppermute | solution.py:178

commit v11 on v10

--- a/solution.py
+++ b/solution.py
@@ -68,23 +68,24 @@
             turned = pltpu.roll(row, slots, 1)
             twice = jnp.where((lane >= slots).astype(jnp.int32) == (c & 1), row, turned)
             twice = jnp.where((lane & (slots - 1)) < count[b], twice, -1).astype(f32)
-            twice = jnp.broadcast_to(twice, (PAD, LANES))
             left, right = y[i * slots : (i + 1) * slots, :LANES], y[i * slots : (i + 1) * slots, LANES:]
             if m < 2:
                 out = (own, core)[m]
                 out[i, :slots, :] = left
                 out[i, slots : 2 * slots, :] = right
-                out[i, 2 * slots :, :] = twice
-            elif i < 2:
-                first, second = (l2, l3)[m - 2], (r2, r3)[m - 2]
-                first[i, :slots, :] = left
-                first[i, slots:, :] = twice
+                out[i, 2 * slots :, :] = jnp.broadcast_to(twice, (PAD, LANES))
+                continue
+            first, second = (l2, l3)[m - 2], (r2, r3)[m - 2]
+            if i == 0:
+                first[2 * slots :, :] = jnp.broadcast_to(twice, (PAD, LANES))
+            first[2 * slots + i : 2 * slots + i + 1, :] = twice
+            if i < 2:
+                first[i * slots : (i + 1) * slots, :] = left
                 second[i * slots : (i + 1) * slots, :] = right
             else:
-                out, at = (r2, r3)[m - 2], 2 * slots + (i - 2) * (2 * slots + PAD)
-                out[at : at + slots, :] = left
-                out[at + slots : at + 2 * slots, :] = right
-                out[at + 2 * slots : at + 2 * slots + PAD, :] = twice
+                at = 2 * (i - 1) * slots
+                second[at : at + slots, :] = left
+                second[at + slots : at + 2 * slots, :] = right
 
 
 def targets(place, mine):
@@ -109,31 +110,27 @@
 
 def left_kernel(place, own, core, l2, l3, send, keep, ids):
     target = targets(place, send.shape[1])
-    senders = (own, core, l2, l3)
     slots = LANES // 2
-    for z in range(2):
-        rows = joined([block[z, pl.ds(block.shape[1] - PAD, 1), :] for block in senders])
+    for z in range(4):
+        one = [block[z, pl.ds(2 * slots, 1), :] for block in (own, core)]
+        rows = joined(one + [block[pl.ds(2 * slots + z, 1), :] for block in (l2, l3)])
         for i in range(2):
             ids[pl.ds(2 * z + i, 1), :] = rows[i]
-        bucket_sum(rows, target, [block[z, :slots, :] for block in senders], send, keep, z)
+        if z < 2:
+            blocks = [block[z, :slots, :] for block in (own, core)]
+            blocks += [block[z * slots : (z + 1) * slots, :] for block in (l2, l3)]
+            bucket_sum(rows, target, blocks, send, keep, z)
 
 
 def rest_kernel(place, ids, own, core, r2, r3, send, keep):
     target = targets(place, send.shape[1])
     slots = LANES // 2
-    for z in range(2):
+    jobs = [(0, 1), (1, 1), (2, 0), (2, 1), (3, 0), (3, 1)]
+    for at, (z, side) in enumerate(jobs):
         rows = [ids[pl.ds(2 * z + i, 1), :] for i in range(2)]
-        blocks = [block[z, slots : 2 * slots, :] for block in (own, core)]
-        blocks += [block[z * slots : (z + 1) * slots, :] for block in (r2, r3)]
-        bucket_sum(rows, target, blocks, send, keep, z)
-    for z in (2, 3):
-        at = 2 * slots + (z - 2) * (2 * slots + PAD)
-        one = [block[z, pl.ds(2 * slots, 1), :] for block in (own, core)]
-        rows = joined(one + [block[pl.ds(at + 2 * slots, 1), :] for block in (r2, r3)])
-        for side in range(2):
-            blocks = [block[z, side * slots : (side + 1) * slots, :] for block in (own, core)]
-            blocks += [block[at + side * slots : at + (side + 1) * slots, :] for block in (r2, r3)]
-            bucket_sum(rows, target, blocks, send, keep, 2 * z - 2 + side)
+        blocks = [block[z, side * slots : (side + 1) * slots, :] for block in (own, core)]
+        blocks += [block[at * slots : (at + 1) * slots, :] for block in (r2, r3)]
+        bucket_sum(rows, target, blocks, send, keep, at)
 
 
 def pair_kernel(keep, got, *outs):
@@ -191,7 +188,7 @@
     slots = transactions.shape[0] // peers
     own, core, l2, l3, r2, r3 = call(
         message_kernel,
-        [(4, 2 * slots + PAD, LANES)] * 2 + [(2, slots + PAD, LANES)] * 2 + [(6 * slots + 2 * PAD, LANES)] * 2,
+        [(4, 2 * slots + PAD, LANES)] * 2 + [(2 * slots + PAD, LANES)] * 2 + [(6 * slots, LANES)] * 2,
         (transactions, tx_product.reshape(-1, LANES), *split_outside(w_msg)),
         smem=(place, tx_count),
     )

time: 60.4 us -> 59.8 us (0.990)
  no operation moved by 1% of the time
where the time goes in v11:
time: 59.8 us; the launch traced here: 59.6 us
  starting transfers between devices  24.2 us (40%)
  waiting for transfers between devices  23.3 us (39%)
  Pallas kernels  5.1 us (9%)
  local copies, waits for them, and re-layouts  4.15 us (7%)
  other arithmetic  1.42 us (2%)
  between operations  0.9 us (2%)
    ppermute x19, starting transfers between devices, swap(): return lax.ppermute(x, axis, [(i, i ^ mask) for i in range(size)])  24.2 us
    ppermute x19, waiting for transfers between devices, swap(): return lax.ppermute(x, axis, [(i, i ^ mask) for i in range(size)])  23.3 us
    pallas_call x8, Pallas kernels, call(): pl.pallas_call(kernel, out_shape=[jax.ShapeDtypeStruct(s, f32) for s in o...  5.1 us
    unnamed x24, local copies, waits for them, and re-layouts  3.7 us
  transfers between devices with their start and end apart: 19, of which 11 were waited for; matrix products, arithmetic and copies ran while one was open for 2% of the time, Pallas kernels for 1%

profile of v11, /device:TPU:0, one launch (start us, length us, event | category | flops | bytes accessed | tf_op | source)
XLA Modules:
  0.0 59.6 jit_solution(7467529801348398342)
XLA Ops:
  0.7 1.0 %fusion = (bf16[256,256]{1,0:T(8,128)(2,1)S(1)}, bf16[256,256]{1,0:T(8,128)(2,1)S(1)}) fusion(f32[256,256]{1,0:T(8,128)} %param.21), kind=kLoop, calls=%fused_computation.6 | loop fusion | flops 262144 | bytes 524288 | tf_op jit(solution)/shard_map/convert_element_type | solution.py:23
  1.7 0.1 pad_add_fusion.3.place
  1.8 0.6 %copy-done.4 = s32[1024]{0:T(1024)S(1)} copy-done((s32[1024]{0:T(1024)S(1)}, s32[1024]{0:T(1024)}, u32[]{:S(2)}) %copy-start.4) | copy-done | bytes 4120
  2.4 1.2 %copy-done.1 = f32[1024,256]{1,0:T(8,128)S(1)} copy-done((f32[1024,256]{1,0:T(8,128)S(1)}, f32[1024,256]{1,0:T(8,128)}, u32[]{:S(2)}) %copy-start.1) | copy-done | bytes 1048600
  3.7 1.1 %shard_map.140 = (f32[4,136,128]{2,1,0:T(8,128)S(1)}, f32[4,136,128]{2,1,0:T(8,128)S(1)}, f32[136,128]{1,0:T(8,128)S(1)}, f32[136,128]{1,0:T(8,128)S(1)}, f32[38...) custom-call(s32[2]{0:T(128)S(1)} %pad_add_fusion.3.place, s32[16]{0:T(128)S(1)} %copy-done.5, f32[1024,256]{1,0:T(8,128)S(1)} %copy-done.1, ...), custom_call_target="tpu_custom_call" | custom-call | tf_op jit(solution)/shard_map/pallas_call | solution.py:43
  4.8 0.5 collective-permute-start
  5.3 2.6 %collective-permute-start.1 = (f32[136,128]{1,0:T(8,128)S(1)}, f32[136,128]{1,0:T(8,128)S(1)}, u32[]{:S(2)}, u32[]{:S(2)}) collective-permute-start(f32[136,128]{1,0:T(8,128)S(1)} %get-tuple-element.35), channel_id=1, source_target_pairs={{0,4},{2,6},{4,0},{6,2},{8,12},{10,14},{12,8},{14,10},{16,20},{18,... | collective-permute-start | bytes 208904 | tf_op jit(solution)/shard_map/ppermute | solution.py:175
  8.0 1.7 %collective-permute-start.4 = (f32[384,128]{1,0:T(8,128)S(1)}, f32[384,128]{1,0:T(8,128)S(1)}, u32[]{:S(2)}, u32[]{:S(2)}) collective-permute-start(f32[384,128]{1,0:T(8,128)S(1)} %get-tuple-element.40), channel_id=1, source_target_pairs={{0,4},{2,6},{4,0},{6,2},{8,12},{10,14},{12,8},{14,10},{16,20},{18,... | collective-permute-start | bytes 589832 | tf_op jit(solution)/shard_map/ppermute | solution.py:175
  9.8 0.6 %copy-done.9 = s32[256]{0:T(256)S(1)} copy-done((s32[256]{0:T(256)S(1)}, s32[256]{0:T(256)}, u32[]{:S(2)}) %copy-start.9) | copy-done | bytes 1048
  10.4 0.1 reshape_reshape.3
  10.5 0.6 copy-done.10
  11.1 0.1 reshape.22
  11.1 0.6 copy-done.11
  11.7 0.1 lt.45
  11.8 0.2 fusion.6.refs_7_
  12.1 0.1 fusion.5
  12.2 0.1 eq.30
  12.4 0.8 %shard_map.141 = (f32[2,128,128]{2,1,0:T(8,128)S(1)}, f32[2,128,128]{2,1,0:T(8,128)S(1)}, f32[8,128]{1,0:T(8,128)S(1)}) custom-call(s32[2]{0:T(128)S(1)} %pad_add_fusion.3.place, f32[4,136,128]{2,1,0:T(8,128)S(1)} %get-tuple-element.33.own, f32[4,136,128]{2,1,0:T(8,128)S(1)} %collective-permute-done.core, f32[136,128]{1,0:T(8,128)S(1)} %collective-permute-done.1.l2, ...), custom_call_target="tpu_custom_call" | custom-call | tf_op jit(solution)/shard_map/pallas_call | solution.py:43
  13.1 1.8 %collective-permute-start.3 = (f32[2,128,128]{2,1,0:T(8,128)S(1)}, f32[2,128,128]{2,1,0:T(8,128)S(1)}, u32[]{:S(2)}, u32[]{:S(2)}) collective-permute-start(f32[2,128,128]{2,1,0:T(8,128)S(1)} %get-tuple-element.38), channel_id=1, source_target_pairs={{0,1},{1,0},{2,3},{3,2},{4,5},{5,4},{6,7},{7,6},{8,9},{9,8},{10,11... | collective-permute-start | bytes 393224 | tf_op jit(solution)/shard_map/ppermute | solution.py:175
  15.0 2.0 %collective-permute-done.4.r2 = f32[384,128]{1,0:T(8,128)S(1)} collective-permute-done((f32[384,128]{1,0:T(8,128)S(1)}, f32[384,128]{1,0:T(8,128)S(1)}, u32[]{:S(2)}, u32[]{:S(2)}) %collective-permute-start.4) | collective-permute-done | bytes 196640 | tf_op jit(solution)/shard_map/ppermute | solution.py:175
  16.9 3.5 %collective-permute-done.5.r3 = f32[384,128]{1,0:T(8,128)S(1)} collective-permute-done((f32[384,128]{1,0:T(8,128)S(1)}, f32[384,128]{1,0:T(8,128)S(1)}, u32[]{:S(2)}, u32[]{:S(2)}) %collective-permute-start.5) | collective-permute-done | bytes 196640 | tf_op jit(solution)/shard_map/ppermute | solution.py:175
  20.5 0.9 %shard_map.142 = (f32[6,128,128]{2,1,0:T(8,128)S(1)}, f32[6,128,128]{2,1,0:T(8,128)S(1)}) custom-call(s32[2]{0:T(128)S(1)} %pad_add_fusion.3.place, f32[8,128]{1,0:T(8,128)S(1)} %get-tuple-element.39.ids, f32[4,136,128]{2,1,0:T(8,128)S(1)} %get-tuple-element.33.own, f32[4,136,128]{2,1,0:T(8,128)S(1)} %collective-permute-done.core, ...), custom_call_target="tpu_custom_call" | custom-call | tf_op jit(solution)/shard_map/pallas_call | solution.py:43
  21.4 1.7 %collective-permute-start.8 = (f32[6,128,128]{2,1,0:T(8,128)S(1)}, f32[6,128,128]{2,1,0:T(8,128)S(1)}, u32[]{:S(2)}, u32[]{:S(2)}) collective-permute-start(f32[6,128,128]{2,1,0:T(8,128)S(1)} %get-tuple-element.44), channel_id=1, source_target_pairs={{0,1},{1,0},{2,3},{3,2},{4,5},{5,4},{6,7},{7,6},{8,9},{9,8},{10,11... | collective-permute-start | bytes 1179656 | tf_op jit(solution)/shard_map/ppermute | solution.py:175
  23.1 0.1 fusion.4.refs_11_
  23.2 0.3 fusion.7.own
  23.5 2.6 %collective-permute-start.6 = (f32[128,128]{1,0:T(8,128)S(1)}, f32[128,128]{1,0:T(8,128)S(1)}, u32[]{:S(2)}, u32[]{:S(2)}) collective-permute-start(f32[128,128]{1,0:T(8,128)S(1)} %get-tuple-element.46), channel_id=1, source_target_pairs={{0,16},{2,18},{4,20},{6,22},{8,24},{10,26},{12,28},{14,30},{16,0},... | collective-permute-start | bytes 196616 | tf_op jit(solution)/shard_map/ppermute | solution.py:175
  26.1 1.3 %collective-permute-start.7 = (f32[128,128]{1,0:T(8,128)S(1)}, f32[128,128]{1,0:T(8,128)S(1)}, u32[]{:S(2)}, u32[]{:S(2)}) collective-permute-start(f32[128,128]{1,0:T(8,128)S(1)} %get-tuple-element.47), channel_id=1, source_target_pairs={{0,24},{2,26},{4,28},{6,30},{8,16},{10,18},{12,20},{14,22},{16,8},... | collective-permute-start | bytes 196616 | tf_op jit(solution)/shard_map/ppermute | solution.py:175
  27.5 3.5 %collective-permute-done.6.refs_0_ = f32[128,128]{1,0:T(8,128)S(1)} collective-permute-done((f32[128,128]{1,0:T(8,128)S(1)}, f32[128,128]{1,0:T(8,128)S(1)}, u32[]{:S(2)}, u32[]{:S(2)}) %collective-permute-start.6) | collective-permute-done | bytes 65568 | tf_op jit(solution)/shard_map/ppermute | solution.py:175
  30.9 1.4 %collective-permute-done.7.refs_1_ = f32[128,128]{1,0:T(8,128)S(1)} collective-permute-done((f32[128,128]{1,0:T(8,128)S(1)}, f32[128,128]{1,0:T(8,128)S(1)}, u32[]{:S(2)}, u32[]{:S(2)}) %collective-permute-start.7) | collective-permute-done | bytes 65568 | tf_op jit(solution)/shard_map/ppermute | solution.py:175
  32.3 0.3 collective-permute-done.8.got
  32.7 2.7 %collective-permute-start.9 = (f32[128,128]{1,0:T(8,128)S(1)}, f32[128,128]{1,0:T(8,128)S(1)}, u32[]{:S(2)}, u32[]{:S(2)}) collective-permute-start(f32[128,128]{1,0:T(8,128)S(1)} %get-tuple-element.50), channel_id=1, source_target_pairs={{0,16},{2,18},{4,20},{6,22},{8,24},{10,26},{12,28},{14,30},{16,0},... | collective-permute-start | bytes 196616 | tf_op jit(solution)/shard_map/ppermute | solution.py:175
  35.4 1.3 %collective-permute-start.10 = (f32[128,128]{1,0:T(8,128)S(1)}, f32[128,128]{1,0:T(8,128)S(1)}, u32[]{:S(2)}, u32[]{:S(2)}) collective-permute-start(f32[128,128]{1,0:T(8,128)S(1)} %get-tuple-element.51), channel_id=1, source_target_pairs={{0,24},{2,26},{4,28},{6,30},{8,16},{10,18},{12,20},{14,22},{16,8},... | collective-permute-start | bytes 196616 | tf_op jit(solution)/shard_map/ppermute | solution.py:175
  36.7 0.2 collective-permute-start.11
  37.0 1.8 %collective-permute-start.12 = (f32[128,128]{1,0:T(8,128)S(1)}, f32[128,128]{1,0:T(8,128)S(1)}, u32[]{:S(2)}, u32[]{:S(2)}) collective-permute-start(f32[128,128]{1,0:T(8,128)S(1)} %get-tuple-element.53), channel_id=1, source_target_pairs={{0,8},{2,10},{4,12},{6,14},{8,0},{10,2},{12,4},{14,6},{16,24},{18,... | collective-permute-start | bytes 196616 | tf_op jit(solution)/shard_map/ppermute | solution.py:175
  38.8 3.2 %collective-permute-done.10.refs_3_ = f32[128,128]{1,0:T(8,128)S(1)} collective-permute-done((f32[128,128]{1,0:T(8,128)S(1)}, f32[128,128]{1,0:T(8,128)S(1)}, u32[]{:S(2)}, u32[]{:S(2)}) %collective-permute-start.10) | collective-permute-done | bytes 65568 | tf_op jit(solution)/shard_map/ppermute | solution.py:175
  42.0 0.4 collective-permute-done.12.refs_5_
  42.4 0.9 %shard_map.145 = (f32[128,256]{1,0:T(8,128)}, f32[4,16,256]{2,1,0:T(8,128)S(1)}, f32[4,16,256]{2,1,0:T(8,128)S(1)}, f32[4,16,256]{2,1,0:T(8,128)S(1)}, f32[4,16,256]{2,1,0:T(8,128)S(1)}) custom-call(f32[128,128]{1,0:T(8,128)S(1)} %collective-permute-done.6.refs_0_, f32[128,128]{1,0:T(8,128)S(1)} %collective-permute-done.7.refs_1_, ...), custom_call_target="tpu_custom_call" | custom-call | tf_op jit(solution)/shard_map/pallas_call | solution.py:43
  43.3 1.5 %collective-permute-start.14 = (f32[4,16,256]{2,1,0:T(8,128)S(1)}, f32[4,16,256]{2,1,0:T(8,128)S(1)}, u32[]{:S(2)}, u32[]{:S(2)}) collective-permute-start(f32[4,16,256]{2,1,0:T(8,128)S(1)} %get-tuple-element.58), channel_id=1, source_target_pairs={{0,4},{2,6},{4,0},{6,2},{8,12},{10,14},{12,8},{14,10},{16,20},{18,... | collective-permute-start | bytes 196616 | tf_op jit(solution)/shard_map/ppermute | solution.py:175
  44.9 0.3 collective-permute-start.15
  45.2 0.1 eq.34
  45.3 2.5 %collective-permute-done.14.refs_2_ = f32[4,16,256]{2,1,0:T(8,128)S(1)} collective-permute-done((f32[4,16,256]{2,1,0:T(8,128)S(1)}, f32[4,16,256]{2,1,0:T(8,128)S(1)}, u32[]{:S(2)}, u32[]{:S(2)}) %collective-permute-start.14) | collective-permute-done | bytes 65568 | tf_op jit(solution)/shard_map/ppermute | solution.py:175
  47.8 1.1 %collective-permute-done.15.refs_3_ = f32[4,16,256]{2,1,0:T(8,128)S(1)} collective-permute-done((f32[4,16,256]{2,1,0:T(8,128)S(1)}, f32[4,16,256]{2,1,0:T(8,128)S(1)}, u32[]{:S(2)}, u32[]{:S(2)}) %collective-permute-start.15) | collective-permute-done | bytes 65568 | tf_op jit(solution)/shard_map/ppermute | solution.py:175
  49.0 1.7 %collective-permute-start.16 = (f32[4,16,256]{2,1,0:T(8,128)S(1)}, f32[4,16,256]{2,1,0:T(8,128)S(1)}, u32[]{:S(2)}, u32[]{:S(2)}) collective-permute-start(f32[4,16,256]{2,1,0:T(8,128)S(1)} %get-tuple-element.60), channel_id=1, source_target_pairs={{0,16},{2,18},{4,20},{6,22},{8,24},{10,26},{12,28},{14,30},{16,0},... | collective-permute-start | bytes 196616 | tf_op jit(solution)/shard_map/ppermute | solution.py:175
  50.7 1.8 %collective-permute-start.17 = (f32[4,16,256]{2,1,0:T(8,128)S(1)}, f32[4,16,256]{2,1,0:T(8,128)S(1)}, u32[]{:S(2)}, u32[]{:S(2)}) collective-permute-start(f32[4,16,256]{2,1,0:T(8,128)S(1)} %get-tuple-element.61), channel_id=1, source_target_pairs={{0,24},{2,26},{4,28},{6,30},{8,16},{10,18},{12,20},{14,22},{16,8},... | collective-permute-start | bytes 196616 | tf_op jit(solution)/shard_map/ppermute | solution.py:175
  52.4 0.5 collective-permute-start.18
  53.0 4.5 %collective-permute-done.16.refs_0_ = f32[4,16,256]{2,1,0:T(8,128)S(1)} collective-permute-done((f32[4,16,256]{2,1,0:T(8,128)S(1)}, f32[4,16,256]{2,1,0:T(8,128)S(1)}, u32[]{:S(2)}, u32[]{:S(2)}) %collective-permute-start.16) | collective-permute-done | bytes 65568 | tf_op jit(solution)/shard_map/ppermute | solution.py:175
  57.5 0.8 %collective-permute-done.18.refs_2_ = f32[4,16,256]{2,1,0:T(8,128)S(1)} collective-permute-done((f32[4,16,256]{2,1,0:T(8,128)S(1)}, f32[4,16,256]{2,1,0:T(8,128)S(1)}, u32[]{:S(2)}, u32[]{:S(2)}) %collective-permute-start.18) | collective-permute-done | bytes 65568 | tf_op jit(solution)/shard_map/ppermute | solution.py:175
  58.3 1.2 %shard_map.147 = f32[256,256]{1,0:T(8,128)} custom-call(bf16[256,256]{1,0:T(8,128)(2,1)S(1)} %fusion.3.incidence, f32[256,256]{1,0:T(8,128)S(1)} %fusion.7.own, f32[256,256]{1,0:T(8,128)S(1)} %copy-done.2, bf16[256,256]{1,0:T(8,128)(2,1)S(1)} %get-tuple-element.65.w_top, bf16[256,256]{1,0:T(8,128)(2,1)S(1)} %get-tuple-element.64.w_low, ...), custom_call_target="tpu_custom_call" | custom-call | tf_op jit(solution)/shard_map/pallas_call | solution.py:43
  (44 shorter events, 0.5 us)
Async XLA Ops:
  0.6 22.5 %copy-start = (f32[256,256]{1,0:T(8,128)S(1)}, f32[256,256]{1,0:T(8,128)}, u32[]{:S(2)}) copy-start(f32[256,256]{1,0:T(8,128)} %param.24) | copy-start | bytes 786436
  1.7 0.7 %copy-start.4 = (s32[1024]{0:T(1024)S(1)}, s32[1024]{0:T(1024)}, u32[]{:S(2)}) copy-start(s32[1024]{0:T(1024)} %param.14) | copy-start | bytes 12292
  1.8 0.7 %copy-start.5 = (s32[16]{0:T(128)S(1)}, s32[16]{0:T(128)}, u32[]{:S(2)}) copy-start(s32[16]{0:T(128)} %count.1) | copy-start | bytes 196
  2.4 1.2 %copy-start.1 = (f32[1024,256]{1,0:T(8,128)S(1)}, f32[1024,256]{1,0:T(8,128)}, u32[]{:S(2)}) copy-start(f32[1024,256]{1,0:T(8,128)} %tx.1) | copy-start | bytes 3145732
  3.6 6.1 %copy-start.6 = (f32[256,256]{1,0:T(8,128)S(1)}, f32[256,256]{1,0:T(8,128)}, u32[]{:S(2)}) copy-start(f32[256,256]{1,0:T(8,128)} %param.23) | copy-start | bytes 786436
  4.8 7.5 %collective-permute-start = (f32[4,136,128]{2,1,0:T(8,128)S(1)}, f32[4,136,128]{2,1,0:T(8,128)S(1)}, u32[]{:S(2)}, u32[]{:S(2)}) collective-permute-start(f32[4,136,128]{2,1,0:T(8,128)S(1)} %get-tuple-element.34), channel_id=1, source_target_pairs={{0,2},{2,0},{4,6},{6,4},{8,10},{10,8},{12,14},{14,12},{16,18},{18,... | collective-permute-start | bytes 835592 | tf_op jit(solution)/shard_map/ppermute | solution.py:175
  5.3 7.0 %collective-permute-start.1 = (f32[136,128]{1,0:T(8,128)S(1)}, f32[136,128]{1,0:T(8,128)S(1)}, u32[]{:S(2)}, u32[]{:S(2)}) collective-permute-start(f32[136,128]{1,0:T(8,128)S(1)} %get-tuple-element.35), channel_id=1, source_target_pairs={{0,4},{2,6},{4,0},{6,2},{8,12},{10,14},{12,8},{14,10},{16,20},{18,... | collective-permute-start | bytes 208904 | tf_op jit(solution)/shard_map/ppermute | solution.py:175
  7.9 4.4 %collective-permute-start.2 = (f32[136,128]{1,0:T(8,128)S(1)}, f32[136,128]{1,0:T(8,128)S(1)}, u32[]{:S(2)}, u32[]{:S(2)}) collective-permute-start(f32[136,128]{1,0:T(8,128)S(1)} %get-tuple-element.36), channel_id=1, source_target_pairs={{0,6},{2,4},{4,2},{6,0},{8,14},{10,12},{12,10},{14,8},{16,22},{18,... | collective-permute-start | bytes 208904 | tf_op jit(solution)/shard_map/ppermute | solution.py:175
  8.0 9.0 %collective-permute-start.4 = (f32[384,128]{1,0:T(8,128)S(1)}, f32[384,128]{1,0:T(8,128)S(1)}, u32[]{:S(2)}, u32[]{:S(2)}) collective-permute-start(f32[384,128]{1,0:T(8,128)S(1)} %get-tuple-element.40), channel_id=1, source_target_pairs={{0,4},{2,6},{4,0},{6,2},{8,12},{10,14},{12,8},{14,10},{16,20},{18,... | collective-permute-start | bytes 589832 | tf_op jit(solution)/shard_map/ppermute | solution.py:175
  9.7 10.8 %collective-permute-start.5 = (f32[384,128]{1,0:T(8,128)S(1)}, f32[384,128]{1,0:T(8,128)S(1)}, u32[]{:S(2)}, u32[]{:S(2)}) collective-permute-start(f32[384,128]{1,0:T(8,128)S(1)} %get-tuple-element.41), channel_id=1, source_target_pairs={{0,6},{2,4},{4,2},{6,0},{8,14},{10,12},{12,10},{14,8},{16,22},{18,... | collective-permute-start | bytes 589832 | tf_op jit(solution)/shard_map/ppermute | solution.py:175
  9.7 0.7 %copy-start.9 = (s32[256]{0:T(256)S(1)}, s32[256]{0:T(256)}, u32[]{:S(2)}) copy-start(s32[256]{0:T(256)} %param.20) | copy-start | bytes 3076
  9.7 2.1 %copy-start.3 = (f32[128,256]{1,0:T(8,128)S(1)}, f32[128,256]{1,0:T(8,128)}, u32[]{:S(2)}) copy-start(f32[128,256]{1,0:T(8,128)} %refs_8_.1) | copy-start | bytes 393220
  9.7 2.1 %copy-start.7 = (f32[256,256]{1,0:T(8,128)S(1)}, f32[256,256]{1,0:T(8,128)}, u32[]{:S(2)}) copy-start(f32[256,256]{1,0:T(8,128)} %param.22) | copy-start | bytes 786436
  10.4 0.7 %copy-start.10 = (s32[256]{0:T(256)S(1)}, s32[256]{0:T(256)}, u32[]{:S(2)}) copy-start(s32[256]{0:T(256)} %param.18) | copy-start | bytes 3076
  11.1 0.7 %copy-start.11 = (s32[16]{0:T(128)S(1)}, s32[16]{0:T(128)}, u32[]{:S(2)}) copy-start(s32[16]{0:T(128)} %param.19) | copy-start | bytes 196
  12.3 2.6 %copy-start.8 = (f32[256,256]{1,0:T(8,128)S(1)}, f32[256,256]{1,0:T(8,128)}, u32[]{:S(2)}) copy-start(f32[256,256]{1,0:T(8,128)} %param.25) | copy-start | bytes 786436
  13.1 7.3 %collective-permute-start.3 = (f32[2,128,128]{2,1,0:T(8,128)S(1)}, f32[2,128,128]{2,1,0:T(8,128)S(1)}, u32[]{:S(2)}, u32[]{:S(2)}) collective-permute-start(f32[2,128,128]{2,1,0:T(8,128)S(1)} %get-tuple-element.38), channel_id=1, source_target_pairs={{0,1},{1,0},{2,3},{3,2},{4,5},{5,4},{6,7},{7,6},{8,9},{9,8},{10,11... | collective-permute-start | bytes 393224 | tf_op jit(solution)/shard_map/ppermute | solution.py:175
  20.4 2.7 %copy-start.2 = (f32[256,256]{1,0:T(8,128)S(1)}, f32[256,256]{1,0:T(8,128)}, u32[]{:S(2)}) copy-start(f32[256,256]{1,0:T(8,128)} %table.1) | copy-start | bytes 786436
  21.4 11.3 %collective-permute-start.8 = (f32[6,128,128]{2,1,0:T(8,128)S(1)}, f32[6,128,128]{2,1,0:T(8,128)S(1)}, u32[]{:S(2)}, u32[]{:S(2)}) collective-permute-start(f32[6,128,128]{2,1,0:T(8,128)S(1)} %get-tuple-element.44), channel_id=1, source_target_pairs={{0,1},{1,0},{2,3},{3,2},{4,5},{5,4},{6,7},{7,6},{8,9},{9,8},{10,11... | collective-permute-start | bytes 1179656 | tf_op jit(solution)/shard_map/ppermute | solution.py:175
  23.5 7.5 %collective-permute-start.6 = (f32[128,128]{1,0:T(8,128)S(1)}, f32[128,128]{1,0:T(8,128)S(1)}, u32[]{:S(2)}, u32[]{:S(2)}) collective-permute-start(f32[128,128]{1,0:T(8,128)S(1)} %get-tuple-element.46), channel_id=1, source_target_pairs={{0,16},{2,18},{4,20},{6,22},{8,24},{10,26},{12,28},{14,30},{16,0},... | collective-permute-start | bytes 196616 | tf_op jit(solution)/shard_map/ppermute | solution.py:175
  26.1 6.2 %collective-permute-start.7 = (f32[128,128]{1,0:T(8,128)S(1)}, f32[128,128]{1,0:T(8,128)S(1)}, u32[]{:S(2)}, u32[]{:S(2)}) collective-permute-start(f32[128,128]{1,0:T(8,128)S(1)} %get-tuple-element.47), channel_id=1, source_target_pairs={{0,24},{2,26},{4,28},{6,30},{8,16},{10,18},{12,20},{14,22},{16,8},... | collective-permute-start | bytes 196616 | tf_op jit(solution)/shard_map/ppermute | solution.py:175
  32.7 6.1 %collective-permute-start.9 = (f32[128,128]{1,0:T(8,128)S(1)}, f32[128,128]{1,0:T(8,128)S(1)}, u32[]{:S(2)}, u32[]{:S(2)}) collective-permute-start(f32[128,128]{1,0:T(8,128)S(1)} %get-tuple-element.50), channel_id=1, source_target_pairs={{0,16},{2,18},{4,20},{6,22},{8,24},{10,26},{12,28},{14,30},{16,0},... | collective-permute-start | bytes 196616 | tf_op jit(solution)/shard_map/ppermute | solution.py:175
  35.4 6.6 %collective-permute-start.10 = (f32[128,128]{1,0:T(8,128)S(1)}, f32[128,128]{1,0:T(8,128)S(1)}, u32[]{:S(2)}, u32[]{:S(2)}) collective-permute-start(f32[128,128]{1,0:T(8,128)S(1)} %get-tuple-element.51), channel_id=1, source_target_pairs={{0,24},{2,26},{4,28},{6,30},{8,16},{10,18},{12,20},{14,22},{16,8},... | collective-permute-start | bytes 196616 | tf_op jit(solution)/shard_map/ppermute | solution.py:175
  36.7 5.3 %collective-permute-start.11 = (f32[128,128]{1,0:T(8,128)S(1)}, f32[128,128]{1,0:T(8,128)S(1)}, u32[]{:S(2)}, u32[]{:S(2)}) collective-permute-start(f32[128,128]{1,0:T(8,128)S(1)} %get-tuple-element.52), channel_id=1, source_target_pairs={{0,8},{2,10},{4,12},{6,14},{8,0},{10,2},{12,4},{14,6},{16,24},{18,... | collective-permute-start | bytes 196616 | tf_op jit(solution)/shard_map/ppermute | solution.py:175
  37.0 5.4 %collective-permute-start.12 = (f32[128,128]{1,0:T(8,128)S(1)}, f32[128,128]{1,0:T(8,128)S(1)}, u32[]{:S(2)}, u32[]{:S(2)}) collective-permute-start(f32[128,128]{1,0:T(8,128)S(1)} %get-tuple-element.53), channel_id=1, source_target_pairs={{0,8},{2,10},{4,12},{6,14},{8,0},{10,2},{12,4},{14,6},{16,24},{18,... | collective-permute-start | bytes 196616 | tf_op jit(solution)/shard_map/ppermute | solution.py:175
  43.3 2.0 %collective-permute-start.13 = (f32[4,16,256]{2,1,0:T(8,128)S(1)}, f32[4,16,256]{2,1,0:T(8,128)S(1)}, u32[]{:S(2)}, u32[]{:S(2)}) collective-permute-start(f32[4,16,256]{2,1,0:T(8,128)S(1)} %get-tuple-element.57), channel_id=1, source_target_pairs={{0,2},{2,0},{4,6},{6,4},{8,10},{10,8},{12,14},{14,12},{16,18},{18,... | collective-permute-start | bytes 196616 | tf_op jit(solution)/shard_map/ppermute | solution.py:175
  43.3 4.5 %collective-permute-start.14 = (f32[4,16,256]{2,1,0:T(8,128)S(1)}, f32[4,16,256]{2,1,0:T(8,128)S(1)}, u32[]{:S(2)}, u32[]{:S(2)}) collective-permute-start(f32[4,16,256]{2,1,0:T(8,128)S(1)} %get-tuple-element.58), channel_id=1, source_target_pairs={{0,4},{2,6},{4,0},{6,2},{8,12},{10,14},{12,8},{14,10},{16,20},{18,... | collective-permute-start | bytes 196616 | tf_op jit(solution)/shard_map/ppermute | solution.py:175
  44.9 4.1 %collective-permute-start.15 = (f32[4,16,256]{2,1,0:T(8,128)S(1)}, f32[4,16,256]{2,1,0:T(8,128)S(1)}, u32[]{:S(2)}, u32[]{:S(2)}) collective-permute-start(f32[4,16,256]{2,1,0:T(8,128)S(1)} %get-tuple-element.59), channel_id=1, source_target_pairs={{0,6},{2,4},{4,2},{6,0},{8,14},{10,12},{12,10},{14,8},{16,22},{18,... | collective-permute-start | bytes 196616 | tf_op jit(solution)/shard_map/ppermute | solution.py:175
  49.0 8.5 %collective-permute-start.16 = (f32[4,16,256]{2,1,0:T(8,128)S(1)}, f32[4,16,256]{2,1,0:T(8,128)S(1)}, u32[]{:S(2)}, u32[]{:S(2)}) collective-permute-start(f32[4,16,256]{2,1,0:T(8,128)S(1)} %get-tuple-element.60), channel_id=1, source_target_pairs={{0,16},{2,18},{4,20},{6,22},{8,24},{10,26},{12,28},{14,30},{16,0},... | collective-permute-start | bytes 196616 | tf_op jit(solution)/shard_map/ppermute | solution.py:175
  50.7 6.8 %collective-permute-start.17 = (f32[4,16,256]{2,1,0:T(8,128)S(1)}, f32[4,16,256]{2,1,0:T(8,128)S(1)}, u32[]{:S(2)}, u32[]{:S(2)}) collective-permute-start(f32[4,16,256]{2,1,0:T(8,128)S(1)} %get-tuple-element.61), channel_id=1, source_target_pairs={{0,24},{2,26},{4,28},{6,30},{8,16},{10,18},{12,20},{14,22},{16,8},... | collective-permute-start | bytes 196616 | tf_op jit(solution)/shard_map/ppermute | solution.py:175
  52.4 5.9 %collective-permute-start.18 = (f32[4,16,256]{2,1,0:T(8,128)S(1)}, f32[4,16,256]{2,1,0:T(8,128)S(1)}, u32[]{:S(2)}, u32[]{:S(2)}) collective-permute-start(f32[4,16,256]{2,1,0:T(8,128)S(1)} %get-tuple-element.62), channel_id=1, source_target_pairs={{0,8},{2,10},{4,12},{6,14},{8,0},{10,2},{12,4},{14,6},{16,24},{18,... | collective-permute-start | bytes 196616 | tf_op jit(solution)/shard_map/ppermute | solution.py:175
